TPU v7x, 32 devices: a whole 2x2x4 slice. The times are simulated.
32 devices in a mesh: dom: 8 (over z, x), sub: 4 (over y, core).
Axes of the slice: x: 2, y: 2, z: 4, core: 2. Of those that a mesh axis runs over, the one named last changes fastest.
Arguments:
- segments: float32 [4096, 9, 128], P(('dom', 'sub')), may hold values from -6 to 6
- send_tiles: int32 [32, 32, 16], P(('dom', 'sub')), may hold values from 0 to 127
- pair_local: int32 [32, 512], P(('dom', 'sub')), may hold values from 0 to 127
- pair_remote: int32 [32, 512], P(('dom', 'sub')), may hold values from 0 to 511, each once within a row
- pair_count: int32 [32], P(('dom', 'sub')), may hold values from 64 to 512, as said below
- tile_cell: int32 [4096], P(('dom', 'sub')), may hold values from 0 to 63
Outputs:
- forces: float32 [4096, 3, 128], P(('dom', 'sub'))
Inputs may be any that keep to these rules, and one draw needn't show every extreme that they name: `send_tiles`: every slot names a tile; each device sends exactly 16 tiles to every device. `pair_remote`: each device's row names every one of its 512 received slots once. `pair_count`: some device holds 512 live pairs.
All inputs are finite; a program needn't handle non-finite values.
Results may differ from a plain program's by a relative error of at most 0.00018.
Values sent between devices are 32-bit elements; how exact they have to be, the bound alone decides.
No kernel may reach another device: no remote copies, remote signals or barrier semaphores. Data moves between devices by JAX's collectives and lax.ppermute only.
A program may use at most 64 MiB of HBM per device.

v0:
```python
import jax
import jax.numpy as jnp
from jax import lax
from jax.sharding import PartitionSpec as P

BLOCK = 64
NCELL = 64


core_square = 0.25


def interact(near_block, far_block, live_mask):
    apart = near_block[:, 0:3, :, None] - far_block[:, 0:3, None, :]
    spread = jnp.sum(apart * apart, axis=1) + core_square
    inverse = lax.rsqrt(spread)
    inverse = inverse * inverse * inverse
    burgers_dot = jnp.sum(near_block[:, 3:6, :, None] * far_block[:, 3:6, None, :], axis=1)
    cross_first = jnp.sum(near_block[:, 3:6, :, None] * far_block[:, 6:9, None, :], axis=1)
    cross_second = jnp.sum(far_block[:, 3:6, None, :] * near_block[:, 6:9, :, None], axis=1)
    coupling = (burgers_dot + cross_first * cross_second) * inverse * live_mask[:, None, None]
    weighted = apart * coupling[:, None]
    return (jnp.sum(weighted, axis=3), -jnp.sum(weighted, axis=2))


def far_field(segments, tile_cell, moment_sums, total_segments):
    moments = moment_sums.reshape(NCELL, 3, 3) / jnp.sqrt(jnp.float32(total_segments))
    moments = 0.5 * (moments + jnp.transpose(moments, (0, 2, 1)))
    cells = jnp.arange(NCELL).astype(jnp.float32)
    weights = 8.0 / (8.0 + jnp.abs(cells[:, None] - cells[None, :]))
    stress = jnp.dot(weights, moments.reshape(NCELL, 9), precision=lax.Precision.HIGHEST)
    onehot = (tile_cell[:, None] == jnp.arange(NCELL)[None, :]).astype(jnp.float32)
    tile_stress = jnp.dot(onehot, stress, precision=lax.Precision.HIGHEST).reshape(-1, 3, 3)
    traction = jnp.sum(tile_stress[:, :, :, None] * segments[:, None, 3:6, :], axis=2)
    lines = segments[:, 6:9, :]
    return jnp.stack(
        [
            traction[:, 1] * lines[:, 2] - traction[:, 2] * lines[:, 1],
            traction[:, 2] * lines[:, 0] - traction[:, 0] * lines[:, 2],
            traction[:, 0] * lines[:, 1] - traction[:, 1] * lines[:, 0],
        ],
        axis=1,
    )


def local_moments(segments, tile_cell):
    outer = jnp.sum(segments[:, 3:6, None, :] * segments[:, None, 6:9, :], axis=3).reshape(-1, 9)
    onehot = (jnp.arange(NCELL)[:, None] == tile_cell[None, :]).astype(jnp.float32)
    return jnp.dot(onehot, outer, precision=lax.Precision.HIGHEST)


def on_device(segments, send_tiles, pair_local, pair_remote, pair_count, tile_cell):
    width = segments.shape[2]
    peers = send_tiles.shape[1]
    slots = send_tiles.shape[2]
    n_dom = lax.axis_size("dom")
    n_sub = lax.axis_size("sub")
    outgoing = segments[send_tiles[0]]
    arrived = lax.all_to_all(outgoing, ("dom", "sub"), split_axis=0, concat_axis=0, tiled=True)
    arrived = arrived.reshape(peers * slots, 9, width)
    moment_sums = lax.psum(local_moments(segments, tile_cell), ("dom", "sub"))
    live_total = pair_count[0]
    local_blocks = pair_local[0].reshape(-1, BLOCK)
    remote_blocks = pair_remote[0].reshape(-1, BLOCK)
    block_numbers = jnp.arange(local_blocks.shape[0])

    def advance(carry, inputs):
        near_forces, far_forces = carry
        local_ids, remote_ids, block_number = inputs
        position = block_number * BLOCK + jnp.arange(BLOCK)
        live_mask = (position < live_total).astype(jnp.float32)
        near_part, far_part = interact(segments[local_ids], arrived[remote_ids], live_mask)
        return (
            (near_forces.at[local_ids].add(near_part), far_forces.at[remote_ids].add(far_part)),
            None,
        )

    start_near = jnp.zeros((segments.shape[0], 3, width), jnp.float32)
    start_far = jnp.zeros((peers * slots, 3, width), jnp.float32)
    totals, unused = lax.scan(
        advance, (start_near, start_far), (local_blocks, remote_blocks, block_numbers)
    )
    near_forces, far_forces = totals
    returned = lax.all_to_all(
        far_forces.reshape(peers, slots, 3, width),
        ("dom", "sub"),
        split_axis=0,
        concat_axis=0,
        tiled=True,
    )
    returned = returned.reshape(peers * slots, 3, width)
    pair_forces = near_forces.at[send_tiles[0].reshape(-1)].add(returned)
    total_segments = segments.shape[0] * width * n_dom * n_sub
    return pair_forces + far_field(segments, tile_cell, moment_sums, total_segments)


def solution(mesh):
    in_specs = (
        P(("dom", "sub"), None, None),
        P(("dom", "sub"), None, None),
        P(("dom", "sub"), None),
        P(("dom", "sub"), None),
        P(("dom", "sub")),
        P(("dom", "sub")),
    )
    out_specs = P(("dom", "sub"), None, None)
    return jax.shard_map(
        on_device, mesh=mesh, in_specs=in_specs, out_specs=out_specs, check_vma=False
    )
```

profile of v0, /device:TPU:0, one launch (start us, length us, event | category | flops | bytes accessed | tf_op | source)
XLA Modules:
  0.0 508.5 jit_solution(5766471118104586138)
XLA Ops:
  0.9 4.6 gather_fusion.2
  7.1 7.4 %all-to-all-start = ((f32[32,16,9,128]{3,1,2,0:T(8,128)}), f32[32,16,9,128]{3,1,2,0:T(8,128)}, u32[]{:S(2)}, u32[]{:S(2)}) async-start(f32[32,16,9,128]{3,1,2,0:T(8,128)} %copy.64), calls=%async_computation | async-start | bytes 4718592 | tf_op jit(solution)/shard_map/all_to_all | solution.py:59
  15.3 74.4 %psum.7 = f32[64,9]{0,1:T(8,128)S(1)} all-reduce(f32[64,9]{0,1:T(8,128)S(1)} %fusion.10), channel_id=1, replica_groups=mesh['dom'=8,'sub'=4] {'dom','sub'}, use_global_device_ids=true, to_apply=%region_11.12 | all-reduce | flops 576 | bytes 4608 | tf_op jit(solution)/shard_map/psum | solution.py:61
  93.3 3.4 copy.67
  97.9 365.9 %while.12 = (s32[]{:T(128)}, f32[128,3,128]{2,1,0:T(4,128)S(1)}, f32[512,3,128]{2,1,0:T(4,128)}, s32[8,64]{1,0:T(8,128)S(1)}, f32[128,9,128]{2,1,0:T(8,128)S(1)}...) while((s32[]{:T(128)}, f32[128,3,128]{2,1,0:T(4,128)S(1)}, ...), condition=%wide.region_9.10_spmd, body=%wide.region_0.9_spmd.sunk | while | flops 44067392 | bytes 62860460 | solution.py:80
  101.5 13.1 %multiply_reduce_fusion.6 = (f32[64,128,128]{2,1,0:T(8,128)}, f32[64,128,128]{2,1,0:T(8,128)}, f32[64,128,128]{2,1,0:T(8,128)}) fusion(f32[64,3,128]{2,1,0:T(4,128)S(1)} %get-tuple-element.202, f32[64,3,128]{2,1,0:T(4,128)S(1)} %get-tuple-element.203, f32[64,3,128]{2,1,0:T(4,128)S(1)} %get-tuple-element.204, f32[64,3,128]{2,1,0:T(4,128)S(1)} %get-tuple-element.205), kind=kLoop, calls=%fused_computation.11.clone.1 | loop fusion | flops 15728640 | bytes 12976128 | tf_op jit(solution)/shard_map/while/body/eval_jaxpr/reduce_sum | solution.py:20
  114.6 4.1 fusion.33
  120.6 5.6 %fusion.34 = f32[64,128,128]{2,1,0:T(8,128)S(1)} fusion(f32[64,128,128]{2,1,0:T(8,128)S(1)} %fusion.33, f32[64,128,128]{2,1,0:T(8,128)} %get-tuple-element.206, f32[64,128,128]{2,1,0:T(8,128)} %get-tuple-element.207, f32[64,128,128]{2,1,0:T(8,128)S(1)} %copy-done.1, f32[64]{0:T(128)S(1)} %compare_convert_fusion.2), kind=kLoop, calls=%fused_computation.16.clone.1 | loop fusion | flops 7340032 | bytes 20971776 | tf_op jit(solution)/shard_map/while/body/eval_jaxpr/mul | solution.py:21
  126.1 8.0 %fusion.35 = (f32[64,3,128]{2,1,0:T(4,128)S(1)}, f32[64,3,128]{2,1,0:T(4,128)S(1)}) fusion(f32[64,128,128]{2,1,0:T(8,128)S(1)} %fusion.34, f32[64,3,128]{2,1,0:T(4,128)S(1)} %get-tuple-element.200, f32[64,3,128]{2,1,0:T(4,128)S(1)} %get-tuple-element.201), kind=kLoop, calls=%fused_computation.8.clone.1 | loop fusion | flops 12533760 | bytes 4587520 | tf_op jit(solution)/shard_map/while/body/eval_jaxpr/reduce_sum | solution.py:23
  134.2 6.7 %scatter_fusion.1 = f32[512,3,128]{2,1,0:T(4,128)} fusion(f32[512,3,128]{2,1,0:T(4,128)} %get-tuple-element.224, s32[64]{0:T(128)S(1)} %get-tuple-element.199, f32[64,3,128]{2,1,0:T(4,128)S(1)} %neg.4), kind=kCustom, calls=%fused_computation.4.clone.1 | custom fusion | flops 24576 | bytes 295168 | tf_op jit(solution)/shard_map/while/body/eval_jaxpr/scatter-add | solution.py:74
  147.3 13.1 %multiply_reduce_fusion.6 = (f32[64,128,128]{2,1,0:T(8,128)}, f32[64,128,128]{2,1,0:T(8,128)}, f32[64,128,128]{2,1,0:T(8,128)}) fusion(f32[64,3,128]{2,1,0:T(4,128)S(1)} %get-tuple-element.202, f32[64,3,128]{2,1,0:T(4,128)S(1)} %get-tuple-element.203, f32[64,3,128]{2,1,0:T(4,128)S(1)} %get-tuple-element.204, f32[64,3,128]{2,1,0:T(4,128)S(1)} %get-tuple-element.205), kind=kLoop, calls=%fused_computation.11.clone.1 | loop fusion | flops 15728640 | bytes 12976128 | tf_op jit(solution)/shard_map/while/body/eval_jaxpr/reduce_sum | solution.py:20
  160.4 4.1 fusion.33
  166.3 5.6 %fusion.34 = f32[64,128,128]{2,1,0:T(8,128)S(1)} fusion(f32[64,128,128]{2,1,0:T(8,128)S(1)} %fusion.33, f32[64,128,128]{2,1,0:T(8,128)} %get-tuple-element.206, f32[64,128,128]{2,1,0:T(8,128)} %get-tuple-element.207, f32[64,128,128]{2,1,0:T(8,128)S(1)} %copy-done.1, f32[64]{0:T(128)S(1)} %compare_convert_fusion.2), kind=kLoop, calls=%fused_computation.16.clone.1 | loop fusion | flops 7340032 | bytes 20971776 | tf_op jit(solution)/shard_map/while/body/eval_jaxpr/mul | solution.py:21
  171.9 8.0 %fusion.35 = (f32[64,3,128]{2,1,0:T(4,128)S(1)}, f32[64,3,128]{2,1,0:T(4,128)S(1)}) fusion(f32[64,128,128]{2,1,0:T(8,128)S(1)} %fusion.34, f32[64,3,128]{2,1,0:T(4,128)S(1)} %get-tuple-element.200, f32[64,3,128]{2,1,0:T(4,128)S(1)} %get-tuple-element.201), kind=kLoop, calls=%fused_computation.8.clone.1 | loop fusion | flops 12533760 | bytes 4587520 | tf_op jit(solution)/shard_map/while/body/eval_jaxpr/reduce_sum | solution.py:23
  179.9 6.7 %scatter_fusion.1 = f32[512,3,128]{2,1,0:T(4,128)} fusion(f32[512,3,128]{2,1,0:T(4,128)} %get-tuple-element.224, s32[64]{0:T(128)S(1)} %get-tuple-element.199, f32[64,3,128]{2,1,0:T(4,128)S(1)} %neg.4), kind=kCustom, calls=%fused_computation.4.clone.1 | custom fusion | flops 24576 | bytes 295168 | tf_op jit(solution)/shard_map/while/body/eval_jaxpr/scatter-add | solution.py:74
  193.0 13.1 %multiply_reduce_fusion.6 = (f32[64,128,128]{2,1,0:T(8,128)}, f32[64,128,128]{2,1,0:T(8,128)}, f32[64,128,128]{2,1,0:T(8,128)}) fusion(f32[64,3,128]{2,1,0:T(4,128)S(1)} %get-tuple-element.202, f32[64,3,128]{2,1,0:T(4,128)S(1)} %get-tuple-element.203, f32[64,3,128]{2,1,0:T(4,128)S(1)} %get-tuple-element.204, f32[64,3,128]{2,1,0:T(4,128)S(1)} %get-tuple-element.205), kind=kLoop, calls=%fused_computation.11.clone.1 | loop fusion | flops 15728640 | bytes 12976128 | tf_op jit(solution)/shard_map/while/body/eval_jaxpr/reduce_sum | solution.py:20
  206.1 4.1 fusion.33
  212.0 5.6 %fusion.34 = f32[64,128,128]{2,1,0:T(8,128)S(1)} fusion(f32[64,128,128]{2,1,0:T(8,128)S(1)} %fusion.33, f32[64,128,128]{2,1,0:T(8,128)} %get-tuple-element.206, f32[64,128,128]{2,1,0:T(8,128)} %get-tuple-element.207, f32[64,128,128]{2,1,0:T(8,128)S(1)} %copy-done.1, f32[64]{0:T(128)S(1)} %compare_convert_fusion.2), kind=kLoop, calls=%fused_computation.16.clone.1 | loop fusion | flops 7340032 | bytes 20971776 | tf_op jit(solution)/shard_map/while/body/eval_jaxpr/mul | solution.py:21
  217.6 8.0 %fusion.35 = (f32[64,3,128]{2,1,0:T(4,128)S(1)}, f32[64,3,128]{2,1,0:T(4,128)S(1)}) fusion(f32[64,128,128]{2,1,0:T(8,128)S(1)} %fusion.34, f32[64,3,128]{2,1,0:T(4,128)S(1)} %get-tuple-element.200, f32[64,3,128]{2,1,0:T(4,128)S(1)} %get-tuple-element.201), kind=kLoop, calls=%fused_computation.8.clone.1 | loop fusion | flops 12533760 | bytes 4587520 | tf_op jit(solution)/shard_map/while/body/eval_jaxpr/reduce_sum | solution.py:23
  225.6 6.7 %scatter_fusion.1 = f32[512,3,128]{2,1,0:T(4,128)} fusion(f32[512,3,128]{2,1,0:T(4,128)} %get-tuple-element.224, s32[64]{0:T(128)S(1)} %get-tuple-element.199, f32[64,3,128]{2,1,0:T(4,128)S(1)} %neg.4), kind=kCustom, calls=%fused_computation.4.clone.1 | custom fusion | flops 24576 | bytes 295168 | tf_op jit(solution)/shard_map/while/body/eval_jaxpr/scatter-add | solution.py:74
  238.8 13.1 %multiply_reduce_fusion.6 = (f32[64,128,128]{2,1,0:T(8,128)}, f32[64,128,128]{2,1,0:T(8,128)}, f32[64,128,128]{2,1,0:T(8,128)}) fusion(f32[64,3,128]{2,1,0:T(4,128)S(1)} %get-tuple-element.202, f32[64,3,128]{2,1,0:T(4,128)S(1)} %get-tuple-element.203, f32[64,3,128]{2,1,0:T(4,128)S(1)} %get-tuple-element.204, f32[64,3,128]{2,1,0:T(4,128)S(1)} %get-tuple-element.205), kind=kLoop, calls=%fused_computation.11.clone.1 | loop fusion | flops 15728640 | bytes 12976128 | tf_op jit(solution)/shard_map/while/body/eval_jaxpr/reduce_sum | solution.py:20
  251.8 4.1 fusion.33
  257.8 5.6 %fusion.34 = f32[64,128,128]{2,1,0:T(8,128)S(1)} fusion(f32[64,128,128]{2,1,0:T(8,128)S(1)} %fusion.33, f32[64,128,128]{2,1,0:T(8,128)} %get-tuple-element.206, f32[64,128,128]{2,1,0:T(8,128)} %get-tuple-element.207, f32[64,128,128]{2,1,0:T(8,128)S(1)} %copy-done.1, f32[64]{0:T(128)S(1)} %compare_convert_fusion.2), kind=kLoop, calls=%fused_computation.16.clone.1 | loop fusion | flops 7340032 | bytes 20971776 | tf_op jit(solution)/shard_map/while/body/eval_jaxpr/mul | solution.py:21
  263.4 8.0 %fusion.35 = (f32[64,3,128]{2,1,0:T(4,128)S(1)}, f32[64,3,128]{2,1,0:T(4,128)S(1)}) fusion(f32[64,128,128]{2,1,0:T(8,128)S(1)} %fusion.34, f32[64,3,128]{2,1,0:T(4,128)S(1)} %get-tuple-element.200, f32[64,3,128]{2,1,0:T(4,128)S(1)} %get-tuple-element.201), kind=kLoop, calls=%fused_computation.8.clone.1 | loop fusion | flops 12533760 | bytes 4587520 | tf_op jit(solution)/shard_map/while/body/eval_jaxpr/reduce_sum | solution.py:23
  271.4 6.8 %scatter_fusion.1 = f32[512,3,128]{2,1,0:T(4,128)} fusion(f32[512,3,128]{2,1,0:T(4,128)} %get-tuple-element.224, s32[64]{0:T(128)S(1)} %get-tuple-element.199, f32[64,3,128]{2,1,0:T(4,128)S(1)} %neg.4), kind=kCustom, calls=%fused_computation.4.clone.1 | custom fusion | flops 24576 | bytes 295168 | tf_op jit(solution)/shard_map/while/body/eval_jaxpr/scatter-add | solution.py:74
  284.6 13.1 %multiply_reduce_fusion.6 = (f32[64,128,128]{2,1,0:T(8,128)}, f32[64,128,128]{2,1,0:T(8,128)}, f32[64,128,128]{2,1,0:T(8,128)}) fusion(f32[64,3,128]{2,1,0:T(4,128)S(1)} %get-tuple-element.202, f32[64,3,128]{2,1,0:T(4,128)S(1)} %get-tuple-element.203, f32[64,3,128]{2,1,0:T(4,128)S(1)} %get-tuple-element.204, f32[64,3,128]{2,1,0:T(4,128)S(1)} %get-tuple-element.205), kind=kLoop, calls=%fused_computation.11.clone.1 | loop fusion | flops 15728640 | bytes 12976128 | tf_op jit(solution)/shard_map/while/body/eval_jaxpr/reduce_sum | solution.py:20
  297.6 4.1 fusion.33
  303.6 5.6 %fusion.34 = f32[64,128,128]{2,1,0:T(8,128)S(1)} fusion(f32[64,128,128]{2,1,0:T(8,128)S(1)} %fusion.33, f32[64,128,128]{2,1,0:T(8,128)} %get-tuple-element.206, f32[64,128,128]{2,1,0:T(8,128)} %get-tuple-element.207, f32[64,128,128]{2,1,0:T(8,128)S(1)} %copy-done.1, f32[64]{0:T(128)S(1)} %compare_convert_fusion.2), kind=kLoop, calls=%fused_computation.16.clone.1 | loop fusion | flops 7340032 | bytes 20971776 | tf_op jit(solution)/shard_map/while/body/eval_jaxpr/mul | solution.py:21
  309.2 8.0 %fusion.35 = (f32[64,3,128]{2,1,0:T(4,128)S(1)}, f32[64,3,128]{2,1,0:T(4,128)S(1)}) fusion(f32[64,128,128]{2,1,0:T(8,128)S(1)} %fusion.34, f32[64,3,128]{2,1,0:T(4,128)S(1)} %get-tuple-element.200, f32[64,3,128]{2,1,0:T(4,128)S(1)} %get-tuple-element.201), kind=kLoop, calls=%fused_computation.8.clone.1 | loop fusion | flops 12533760 | bytes 4587520 | tf_op jit(solution)/shard_map/while/body/eval_jaxpr/reduce_sum | solution.py:23
  317.2 6.7 %scatter_fusion.1 = f32[512,3,128]{2,1,0:T(4,128)} fusion(f32[512,3,128]{2,1,0:T(4,128)} %get-tuple-element.224, s32[64]{0:T(128)S(1)} %get-tuple-element.199, f32[64,3,128]{2,1,0:T(4,128)S(1)} %neg.4), kind=kCustom, calls=%fused_computation.4.clone.1 | custom fusion | flops 24576 | bytes 295168 | tf_op jit(solution)/shard_map/while/body/eval_jaxpr/scatter-add | solution.py:74
  330.3 13.1 %multiply_reduce_fusion.6 = (f32[64,128,128]{2,1,0:T(8,128)}, f32[64,128,128]{2,1,0:T(8,128)}, f32[64,128,128]{2,1,0:T(8,128)}) fusion(f32[64,3,128]{2,1,0:T(4,128)S(1)} %get-tuple-element.202, f32[64,3,128]{2,1,0:T(4,128)S(1)} %get-tuple-element.203, f32[64,3,128]{2,1,0:T(4,128)S(1)} %get-tuple-element.204, f32[64,3,128]{2,1,0:T(4,128)S(1)} %get-tuple-element.205), kind=kLoop, calls=%fused_computation.11.clone.1 | loop fusion | flops 15728640 | bytes 12976128 | tf_op jit(solution)/shard_map/while/body/eval_jaxpr/reduce_sum | solution.py:20
  343.4 4.1 fusion.33
  349.3 5.6 %fusion.34 = f32[64,128,128]{2,1,0:T(8,128)S(1)} fusion(f32[64,128,128]{2,1,0:T(8,128)S(1)} %fusion.33, f32[64,128,128]{2,1,0:T(8,128)} %get-tuple-element.206, f32[64,128,128]{2,1,0:T(8,128)} %get-tuple-element.207, f32[64,128,128]{2,1,0:T(8,128)S(1)} %copy-done.1, f32[64]{0:T(128)S(1)} %compare_convert_fusion.2), kind=kLoop, calls=%fused_computation.16.clone.1 | loop fusion | flops 7340032 | bytes 20971776 | tf_op jit(solution)/shard_map/while/body/eval_jaxpr/mul | solution.py:21
  354.9 8.0 %fusion.35 = (f32[64,3,128]{2,1,0:T(4,128)S(1)}, f32[64,3,128]{2,1,0:T(4,128)S(1)}) fusion(f32[64,128,128]{2,1,0:T(8,128)S(1)} %fusion.34, f32[64,3,128]{2,1,0:T(4,128)S(1)} %get-tuple-element.200, f32[64,3,128]{2,1,0:T(4,128)S(1)} %get-tuple-element.201), kind=kLoop, calls=%fused_computation.8.clone.1 | loop fusion | flops 12533760 | bytes 4587520 | tf_op jit(solution)/shard_map/while/body/eval_jaxpr/reduce_sum | solution.py:23
  362.9 6.7 %scatter_fusion.1 = f32[512,3,128]{2,1,0:T(4,128)} fusion(f32[512,3,128]{2,1,0:T(4,128)} %get-tuple-element.224, s32[64]{0:T(128)S(1)} %get-tuple-element.199, f32[64,3,128]{2,1,0:T(4,128)S(1)} %neg.4), kind=kCustom, calls=%fused_computation.4.clone.1 | custom fusion | flops 24576 | bytes 295168 | tf_op jit(solution)/shard_map/while/body/eval_jaxpr/scatter-add | solution.py:74
  376.0 13.1 %multiply_reduce_fusion.6 = (f32[64,128,128]{2,1,0:T(8,128)}, f32[64,128,128]{2,1,0:T(8,128)}, f32[64,128,128]{2,1,0:T(8,128)}) fusion(f32[64,3,128]{2,1,0:T(4,128)S(1)} %get-tuple-element.202, f32[64,3,128]{2,1,0:T(4,128)S(1)} %get-tuple-element.203, f32[64,3,128]{2,1,0:T(4,128)S(1)} %get-tuple-element.204, f32[64,3,128]{2,1,0:T(4,128)S(1)} %get-tuple-element.205), kind=kLoop, calls=%fused_computation.11.clone.1 | loop fusion | flops 15728640 | bytes 12976128 | tf_op jit(solution)/shard_map/while/body/eval_jaxpr/reduce_sum | solution.py:20
  389.1 4.1 fusion.33
  395.1 5.6 %fusion.34 = f32[64,128,128]{2,1,0:T(8,128)S(1)} fusion(f32[64,128,128]{2,1,0:T(8,128)S(1)} %fusion.33, f32[64,128,128]{2,1,0:T(8,128)} %get-tuple-element.206, f32[64,128,128]{2,1,0:T(8,128)} %get-tuple-element.207, f32[64,128,128]{2,1,0:T(8,128)S(1)} %copy-done.1, f32[64]{0:T(128)S(1)} %compare_convert_fusion.2), kind=kLoop, calls=%fused_computation.16.clone.1 | loop fusion | flops 7340032 | bytes 20971776 | tf_op jit(solution)/shard_map/while/body/eval_jaxpr/mul | solution.py:21
  400.6 8.0 %fusion.35 = (f32[64,3,128]{2,1,0:T(4,128)S(1)}, f32[64,3,128]{2,1,0:T(4,128)S(1)}) fusion(f32[64,128,128]{2,1,0:T(8,128)S(1)} %fusion.34, f32[64,3,128]{2,1,0:T(4,128)S(1)} %get-tuple-element.200, f32[64,3,128]{2,1,0:T(4,128)S(1)} %get-tuple-element.201), kind=kLoop, calls=%fused_computation.8.clone.1 | loop fusion | flops 12533760 | bytes 4587520 | tf_op jit(solution)/shard_map/while/body/eval_jaxpr/reduce_sum | solution.py:23
  408.7 6.7 %scatter_fusion.1 = f32[512,3,128]{2,1,0:T(4,128)} fusion(f32[512,3,128]{2,1,0:T(4,128)} %get-tuple-element.224, s32[64]{0:T(128)S(1)} %get-tuple-element.199, f32[64,3,128]{2,1,0:T(4,128)S(1)} %neg.4), kind=kCustom, calls=%fused_computation.4.clone.1 | custom fusion | flops 24576 | bytes 295168 | tf_op jit(solution)/shard_map/while/body/eval_jaxpr/scatter-add | solution.py:74
  421.7 13.1 %multiply_reduce_fusion.6 = (f32[64,128,128]{2,1,0:T(8,128)}, f32[64,128,128]{2,1,0:T(8,128)}, f32[64,128,128]{2,1,0:T(8,128)}) fusion(f32[64,3,128]{2,1,0:T(4,128)S(1)} %get-tuple-element.202, f32[64,3,128]{2,1,0:T(4,128)S(1)} %get-tuple-element.203, f32[64,3,128]{2,1,0:T(4,128)S(1)} %get-tuple-element.204, f32[64,3,128]{2,1,0:T(4,128)S(1)} %get-tuple-element.205), kind=kLoop, calls=%fused_computation.11.clone.1 | loop fusion | flops 15728640 | bytes 12976128 | tf_op jit(solution)/shard_map/while/body/eval_jaxpr/reduce_sum | solution.py:20
  434.8 4.1 fusion.33
  440.8 5.6 %fusion.34 = f32[64,128,128]{2,1,0:T(8,128)S(1)} fusion(f32[64,128,128]{2,1,0:T(8,128)S(1)} %fusion.33, f32[64,128,128]{2,1,0:T(8,128)} %get-tuple-element.206, f32[64,128,128]{2,1,0:T(8,128)} %get-tuple-element.207, f32[64,128,128]{2,1,0:T(8,128)S(1)} %copy-done.1, f32[64]{0:T(128)S(1)} %compare_convert_fusion.2), kind=kLoop, calls=%fused_computation.16.clone.1 | loop fusion | flops 7340032 | bytes 20971776 | tf_op jit(solution)/shard_map/while/body/eval_jaxpr/mul | solution.py:21
  446.4 8.0 %fusion.35 = (f32[64,3,128]{2,1,0:T(4,128)S(1)}, f32[64,3,128]{2,1,0:T(4,128)S(1)}) fusion(f32[64,128,128]{2,1,0:T(8,128)S(1)} %fusion.34, f32[64,3,128]{2,1,0:T(4,128)S(1)} %get-tuple-element.200, f32[64,3,128]{2,1,0:T(4,128)S(1)} %get-tuple-element.201), kind=kLoop, calls=%fused_computation.8.clone.1 | loop fusion | flops 12533760 | bytes 4587520 | tf_op jit(solution)/shard_map/while/body/eval_jaxpr/reduce_sum | solution.py:23
  454.4 6.7 %scatter_fusion.1 = f32[512,3,128]{2,1,0:T(4,128)} fusion(f32[512,3,128]{2,1,0:T(4,128)} %get-tuple-element.224, s32[64]{0:T(128)S(1)} %get-tuple-element.199, f32[64,3,128]{2,1,0:T(4,128)S(1)} %neg.4), kind=kCustom, calls=%fused_computation.4.clone.1 | custom fusion | flops 24576 | bytes 295168 | tf_op jit(solution)/shard_map/while/body/eval_jaxpr/scatter-add | solution.py:74
  466.0 3.8 all-to-all-start.1
  471.2 19.2 %all-to-all-done.1 = f32[32,16,3,128]{3,1,2,0:T(8,128)S(1)} async-done(((f32[32,16,3,128]{3,1,2,0:T(8,128)}), f32[32,16,3,128]{3,1,2,0:T(8,128)S(1)}, u32[]{:S(2)}, u32[]{:S(2)}) %all-to-all-start.1) | async-done | bytes 786464 | tf_op jit(solution)/shard_map/all_to_all | solution.py:84
  491.1 16.7 %scatter_fusion.2 = f32[128,3,128]{2,1,0:T(4,128)S(1)} fusion(f32[128,3,128]{2,1,0:T(4,128)S(1)} %maximum_add_fusion, s32[512]{0:T(512)S(1)} %bitcast.50, f32[512,3,128]{2,1,0:T(4,128)S(1)} %copy.79), kind=kCustom, calls=%fused_computation.5 | custom fusion | flops 196608 | bytes 2361344 | tf_op jit(solution)/shard_map/scatter-add | solution.py:92
  (153 shorter events, 73.5 us)
Async XLA Ops:
  5.5 9.0 %copy-start = (f32[128,9,128]{2,0,1:T(8,128)S(1)}, f32[128,9,128]{2,0,1:T(8,128)}, u32[]{:S(2)}) copy-start(f32[128,9,128]{2,0,1:T(8,128)} %param.8) | copy-start | bytes 1769476
  7.1 8.1 %copy-start.5 = (s32[128]{0:T(128)S(1)}, s32[128]{0:T(128)}, u32[]{:S(2)}) copy-start(s32[128]{0:T(128)} %param.13) | copy-start | bytes 1540
  7.1 83.1 %copy-start.3 = (s32[1,512]{1,0:T(1,128)S(1)}, s32[1,512]{1,0:T(1,128)}, u32[]{:S(2)}) copy-start(s32[1,512]{1,0:T(1,128)} %param.11) | copy-start | bytes 6148
  7.1 83.7 %copy-start.4 = (s32[1,512]{1,0:T(1,128)S(1)}, s32[1,512]{1,0:T(1,128)}, u32[]{:S(2)}) copy-start(s32[1,512]{1,0:T(1,128)} %param.10) | copy-start | bytes 6148
  7.1 84.4 %all-to-all-start = ((f32[32,16,9,128]{3,1,2,0:T(8,128)}), f32[32,16,9,128]{3,1,2,0:T(8,128)}, u32[]{:S(2)}, u32[]{:S(2)}) async-start(f32[32,16,9,128]{3,1,2,0:T(8,128)} %copy.64), calls=%async_computation | async-start | bytes 4718592 | tf_op jit(solution)/shard_map/all_to_all | solution.py:59
  97.9 371.9 %copy-start.2 = (s32[1,32,16]{1,2,0:T(8,128)S(1)}, s32[1,32,16]{1,2,0:T(8,128)}, u32[]{:S(2)}) copy-start(s32[1,32,16]{1,2,0:T(8,128)} %param.9) | copy-start | bytes 6148
  114.6 5.9 %copy-start.1 = (f32[64,128,128]{2,1,0:T(8,128)S(1)}, f32[64,128,128]{2,1,0:T(8,128)}, u32[]{:S(2)}) copy-start(f32[64,128,128]{2,1,0:T(8,128)} %get-tuple-element.208) | copy-start | bytes 12582916 | tf_op jit(solution)/shard_map/while
  160.4 5.9 %copy-start.1 = (f32[64,128,128]{2,1,0:T(8,128)S(1)}, f32[64,128,128]{2,1,0:T(8,128)}, u32[]{:S(2)}) copy-start(f32[64,128,128]{2,1,0:T(8,128)} %get-tuple-element.208) | copy-start | bytes 12582916 | tf_op jit(solution)/shard_map/while
  206.1 5.9 %copy-start.1 = (f32[64,128,128]{2,1,0:T(8,128)S(1)}, f32[64,128,128]{2,1,0:T(8,128)}, u32[]{:S(2)}) copy-start(f32[64,128,128]{2,1,0:T(8,128)} %get-tuple-element.208) | copy-start | bytes 12582916 | tf_op jit(solution)/shard_map/while
  251.8 5.9 %copy-start.1 = (f32[64,128,128]{2,1,0:T(8,128)S(1)}, f32[64,128,128]{2,1,0:T(8,128)}, u32[]{:S(2)}) copy-start(f32[64,128,128]{2,1,0:T(8,128)} %get-tuple-element.208) | copy-start | bytes 12582916 | tf_op jit(solution)/shard_map/while
  297.6 5.9 %copy-start.1 = (f32[64,128,128]{2,1,0:T(8,128)S(1)}, f32[64,128,128]{2,1,0:T(8,128)}, u32[]{:S(2)}) copy-start(f32[64,128,128]{2,1,0:T(8,128)} %get-tuple-element.208) | copy-start | bytes 12582916 | tf_op jit(solution)/shard_map/while
  343.4 5.9 %copy-start.1 = (f32[64,128,128]{2,1,0:T(8,128)S(1)}, f32[64,128,128]{2,1,0:T(8,128)}, u32[]{:S(2)}) copy-start(f32[64,128,128]{2,1,0:T(8,128)} %get-tuple-element.208) | copy-start | bytes 12582916 | tf_op jit(solution)/shard_map/while
  389.1 5.9 %copy-start.1 = (f32[64,128,128]{2,1,0:T(8,128)S(1)}, f32[64,128,128]{2,1,0:T(8,128)}, u32[]{:S(2)}) copy-start(f32[64,128,128]{2,1,0:T(8,128)} %get-tuple-element.208) | copy-start | bytes 12582916 | tf_op jit(solution)/shard_map/while
  434.8 5.9 %copy-start.1 = (f32[64,128,128]{2,1,0:T(8,128)S(1)}, f32[64,128,128]{2,1,0:T(8,128)}, u32[]{:S(2)}) copy-start(f32[64,128,128]{2,1,0:T(8,128)} %get-tuple-element.208) | copy-start | bytes 12582916 | tf_op jit(solution)/shard_map/while
  466.0 24.4 %all-to-all-start.1 = ((f32[32,16,3,128]{3,1,2,0:T(8,128)}), f32[32,16,3,128]{3,1,2,0:T(8,128)S(1)}, u32[]{:S(2)}, u32[]{:S(2)}) async-start(f32[32,16,3,128]{3,1,2,0:T(8,128)} %copy.77), calls=%async_computation.1 | async-start | bytes 1572864 | tf_op jit(solution)/shard_map/all_to_all | solution.py:84
where the time goes:
time: 510 us; the launch traced here: 508 us
  other arithmetic  347 us (68%)
  blocking collectives  74.4 us (15%)
  local copies, waits for them, and re-layouts  50.7 us (10%)
  waiting for transfers between devices  19.2 us (4%)
  starting transfers between devices  11.2 us (2%)
  loops' own time  5.5 us (1%)
    reduce_sum x8, other arithmetic, interact(): jnp.sum(far_block[:, 3:6, None, :] * near_block[:, 6:9, :, None], axis=1)  105 us
    psum x1, blocking collectives, on_device(): moment_sums = lax.psum(local_moments(segments, tile_cell), ('dom', 'sub'))  74.4 us
    reduce_sum x8, other arithmetic, interact(): return (jnp.sum(weighted, axis=3), -jnp.sum(weighted, axis=2))  63.9 us
    scatter-add x8, other arithmetic, advance(): far_forces.at[remote_ids].add(far_part)  53.8 us
    mul x8, other arithmetic, interact(): (burgers_dot + cross_first * cross_second) * inverse  44.6 us
    reduce_sum x8, other arithmetic, interact(): spread = jnp.sum(apart * apart, axis=1) + core_square  32.9 us
    gather x8, local copies, waits for them, and re-layouts, advance(): arrived[remote_ids]  22.3 us
    scatter-add x8, other arithmetic, advance(): near_forces.at[local_ids].add(near_part)  21.9 us
  transfers between devices with their start and end apart: 2, of which 1 were waited for; matrix products, arithmetic and copies ran while one was open for 1% of the time, Pallas kernels for 0%

commit v1 on v0

v1 whole, which is shorter than its diff:
```python
import functools
import jax
import jax.numpy as jnp
from jax import lax
from jax.sharding import PartitionSpec as P
from jax.experimental import pallas as pl
from jax.experimental.pallas import tpu as pltpu

CORE = 0.25
UNROLL = 4


def head(value):
    return value.astype(jnp.bfloat16).astype(jnp.float32)


def pair_terms(near, near_row, far, far_row):
    sub = lax.broadcasted_iota(jnp.int32, (8, 128), 0)
    first = sub < 3
    second = jnp.logical_and(sub >= 3, sub < 6)
    third = sub == 5
    zero = jnp.zeros((8, 128), jnp.float32)

    def thirds(row):
        high = head(row)
        rest = row - high
        middle = head(rest)
        return high, middle, rest - middle

    near_high, near_mid, near_low = thirds(near)
    row_high, row_mid, row_low = thirds(jnp.broadcast_to(near_row, (8, 128)))
    row_part = jnp.where(sub == 0, row_high, jnp.where(sub == 1, row_mid, jnp.where(sub == 2, row_low, jnp.where(second, 1.0, 0.0))))
    left = jnp.concatenate([near_high, near_mid, near_low, near_high, row_part, zero], axis=0)

    far_high = head(far)
    far_mid = far - far_high

    def minus_part(row, others):
        high, middle, low = thirds(jnp.broadcast_to(row, (8, 128)))
        return jnp.where(sub == 3, -high, jnp.where(sub == 4, -middle, jnp.where(third, -low, others)))

    burgers = [jnp.where(first, part, 0.0) for part in (far_high, far_mid)]
    lines_up = [jnp.where(first, pltpu.roll(part, 5, 0), 0.0) for part in (far_high, far_mid)]
    burgers_down = [jnp.where(second, pltpu.roll(part, 3, 0), 0.0) for part in (far_high, far_mid)]
    ones_six = jnp.where(sub == 6, 1.0, 0.0)
    ones_seven = jnp.where(sub == 7, 1.0, 0.0)
    ones_first = jnp.where(first, 1.0, 0.0)
    columns = [
        [pair[0], pair[0], zero, pair[1], zero, zero] for pair in (burgers, lines_up, burgers_down)
    ]
    columns.append([ones_six, ones_six, ones_six, zero, minus_part(far[6:7], zero), zero])
    columns.append([ones_seven, ones_seven, ones_seven, zero, minus_part(far[7:8], zero), zero])
    columns.append([zero, zero, zero, zero, minus_part(far_row, ones_first), zero])
    right = jnp.concatenate([jnp.concatenate(column, axis=0).astype(jnp.bfloat16) for column in columns], axis=1)
    left = left.T.astype(jnp.bfloat16)
    return lax.dot_general(left, right, (((1,), (0,)), ((), ())), preferred_element_type=jnp.float32)


def pair_forces(terms):
    burgers_dot, first, second, x, y, z = [terms[:, 128 * k : 128 * (k + 1)] for k in range(6)]
    spread = x * x + y * y + z * z + CORE
    inverse = lax.rsqrt(spread)
    coupling = (burgers_dot + first * second) * (inverse * inverse * inverse)
    weighted = [coupling * part for part in (x, y, z)]
    far_rows = [-jnp.sum(part, axis=0, keepdims=True) for part in weighted]
    sums = [jnp.sum(part, axis=1, keepdims=True) for part in weighted]
    lane = lax.broadcasted_iota(jnp.int32, (128, 128), 1)
    packed = jnp.where(lane == 0, sums[0], jnp.where(lane == 1, sums[1], sums[2])).T
    return [packed[k : k + 1] for k in range(3)], far_rows


def pair_kernel(near_tiles, far_tiles, count_ref, near_ids, far_ids, near_ref, far_ref, near_out, far_out):
    near_out[...] = jnp.zeros_like(near_out)
    far_out[...] = jnp.zeros_like(far_out)
    count = count_ref[0]
    last = near_ids.shape[0] - 1

    def load(ref, tiles, index):
        group = index // tiles
        tile = index % tiles
        return ref[group, tile], ref[group, tiles + tile // 8, pl.ds(tile % 8, 1), :]

    def step(block, carry):
        picks = []
        for k in range(UNROLL):
            position = block * UNROLL + k
            place = jnp.minimum(position, last)
            live = jnp.where(position < count, 1.0, 0.0)
            near_id = near_ids[place]
            far_id = far_ids[place]
            near, near_row = load(near_ref, near_tiles, near_id)
            far, far_row = load(far_ref, far_tiles, far_id)
            picks.append((near_id, far_id, live, pair_forces(pair_terms(near, near_row, far, far_row))))
        for near_id, far_id, live, (near_rows, far_rows) in picks:
            for axis in range(3):
                near_out[axis, pl.ds(near_id, 1), :] += near_rows[axis] * live
                far_out[axis, pl.ds(far_id, 1), :] += far_rows[axis] * live
        return carry

    lax.fori_loop(0, (count + UNROLL - 1) // UNROLL, step, 0)


def run_pairs(count, near_ids, far_ids, near, far, near_tiles, far_tiles):
    near_total = near.shape[0] * near_tiles
    far_total = far.shape[0] * far_tiles
    smem = pl.BlockSpec(memory_space=pltpu.SMEM)
    vmem = pl.BlockSpec(memory_space=pltpu.VMEM)
    width = near.shape[-1]
    return pl.pallas_call(
        functools.partial(pair_kernel, near_tiles, far_tiles),
        out_shape=(
            jax.ShapeDtypeStruct((3, near_total, width), jnp.float32),
            jax.ShapeDtypeStruct((3, far_total, width), jnp.float32),
        ),
        in_specs=[smem, smem, smem, vmem, vmem],
        out_specs=(vmem, vmem),
        compiler_params=pltpu.CompilerParams(vmem_limit_bytes=48 * 1024 * 1024),
    )(count, near_ids, far_ids, near, far)


def tile_groups(tiles):
    main = jnp.concatenate([tiles[..., 3:9, :], tiles[..., 0:2, :]], axis=-2)
    rows = tiles[..., 2, :]
    short = -rows.shape[-2] % 8
    rows = jnp.pad(rows, [(0, 0)] * (rows.ndim - 2) + [(0, short), (0, 0)])
    rows = rows.reshape(rows.shape[:-2] + (rows.shape[-2] // 8, 8, rows.shape[-1]))
    return jnp.concatenate([main, rows], axis=-3)


NCELL = 64


def far_field(segments, tile_cell, moment_sums, total_segments):
    moments = moment_sums.reshape(NCELL, 3, 3) / jnp.sqrt(jnp.float32(total_segments))
    moments = 0.5 * (moments + jnp.transpose(moments, (0, 2, 1)))
    cells = jnp.arange(NCELL).astype(jnp.float32)
    weights = 8.0 / (8.0 + jnp.abs(cells[:, None] - cells[None, :]))
    stress = jnp.dot(weights, moments.reshape(NCELL, 9), precision=lax.Precision.HIGHEST)
    onehot = (tile_cell[:, None] == jnp.arange(NCELL)[None, :]).astype(jnp.float32)
    tile_stress = jnp.dot(onehot, stress, precision=lax.Precision.HIGHEST).reshape(-1, 3, 3)
    traction = jnp.sum(tile_stress[:, :, :, None] * segments[:, None, 3:6, :], axis=2)
    lines = segments[:, 6:9, :]
    return jnp.stack(
        [
            traction[:, 1] * lines[:, 2] - traction[:, 2] * lines[:, 1],
            traction[:, 2] * lines[:, 0] - traction[:, 0] * lines[:, 2],
            traction[:, 0] * lines[:, 1] - traction[:, 1] * lines[:, 0],
        ],
        axis=1,
    )


def local_moments(segments, tile_cell):
    outer = jnp.sum(segments[:, 3:6, None, :] * segments[:, None, 6:9, :], axis=3).reshape(-1, 9)
    onehot = (jnp.arange(NCELL)[:, None] == tile_cell[None, :]).astype(jnp.float32)
    return jnp.dot(onehot, outer, precision=lax.Precision.HIGHEST)


def on_device(segments, send_tiles, pair_local, pair_remote, pair_count, tile_cell):
    width = segments.shape[2]
    tiles = segments.shape[0]
    peers = send_tiles.shape[1]
    slots = send_tiles.shape[2]
    n_dom = lax.axis_size("dom")
    n_sub = lax.axis_size("sub")
    outgoing = tile_groups(segments[send_tiles[0]])
    arrived = lax.all_to_all(outgoing, ("dom", "sub"), split_axis=0, concat_axis=0, tiled=True)
    moment_sums = lax.psum(local_moments(segments, tile_cell), ("dom", "sub"))
    near_forces, far_forces = run_pairs(
        pair_count, pair_local[0], pair_remote[0], tile_groups(segments)[None], arrived, tiles, slots
    )
    returned = lax.all_to_all(
        far_forces.reshape(3, peers, slots, width),
        ("dom", "sub"),
        split_axis=1,
        concat_axis=1,
        tiled=True,
    )
    returned = returned.reshape(3, peers * slots, width)
    picks = (send_tiles[0].reshape(-1)[None, :] == jnp.arange(tiles)[:, None]).astype(jnp.float32)
    near_forces = near_forces + jnp.einsum("ts,ksw->ktw", picks, returned, precision=lax.Precision.HIGHEST)
    total_segments = tiles * width * n_dom * n_sub
    return near_forces.transpose(1, 0, 2) + far_field(segments, tile_cell, moment_sums, total_segments)


def solution(mesh):
    in_specs = (
        P(("dom", "sub"), None, None),
        P(("dom", "sub"), None, None),
        P(("dom", "sub"), None),
        P(("dom", "sub"), None),
        P(("dom", "sub")),
        P(("dom", "sub")),
    )
    out_specs = P(("dom", "sub"), None, None)
    return jax.shard_map(
        on_device, mesh=mesh, in_specs=in_specs, out_specs=out_specs, check_vma=False
    )
```

time: 510 us -> 215 us (0.42)
  other arithmetic: 347 us -> 4.12 us
  starting transfers between devices: 11.2 us -> 74.9 us
  local copies, waits for them, and re-layouts: 50.7 us -> 9.26 us
  Pallas kernels: 0 us -> 29.1 us
  loops' own time: 5.5 us -> 0 us
    reduce_sum x24 -> x0, other arithmetic: 201 us -> none  [the longest x8 105 us: interact(): jnp.sum(far_block[:, 3:6, None, :] * near_block[:, 6:9, :, None], axis=1)]
    scatter-add x17 -> x0, other arithmetic: 92.5 us -> none  [the longest x8 53.8 us: advance(): far_forces.at[remote_ids].add(far_part)]
    all_to_all x1, starting transfers between devices: 3.78 us -> 67.6 us  [on_device(): lax.all_to_all(far_forces.reshape(3, peers, slots, width), ('dom', 'sub')...]
    mul x8 -> x0, other arithmetic: 44.6 us -> none  [interact(): (burgers_dot + cross_first * cross_second) * inverse]
    pallas_call x0 -> x1, Pallas kernels: none -> 29.1 us  [run_pairs(): pl.pallas_call(functools.partial(pair_kernel, near_tiles, far_tiles), out...]
    gather x18 -> x2, local copies, waits for them, and re-layouts: 33.5 us -> 6.11 us  [on_device(): outgoing = tile_groups(segments[send_tiles[0]])]
    another operation x1 -> x0, loops' own time: 5.5 us -> none  [on_device(): lax.scan(advance, (start_near, start_far), (local_blocks, remote_blocks,...]
    convert_element_type x8 -> x0, other arithmetic: 5.21 us -> none  [advance(): live_mask = (position < live_total).astype(jnp.float32)]
where the time goes in v1:
time: 215 us
  starting transfers between devices  74.9 us (35%)
  blocking collectives  74.2 us (35%)
  Pallas kernels  29.1 us (14%)
  waiting for transfers between devices  20.5 us (10%)
  local copies, waits for them, and re-layouts  9.26 us (4%)
  other arithmetic  4.12 us (2%)
    psum x1, blocking collectives, on_device(): moment_sums = lax.psum(local_moments(segments, tile_cell), ('dom', 'sub'))  74.2 us
    all_to_all x1, starting transfers between devices, on_device(): lax.all_to_all(far_forces.reshape(3, peers, slots, width), ('dom', 'sub')...  67.6 us
    pallas_call x1, Pallas kernels, run_pairs(): pl.pallas_call(functools.partial(pair_kernel, near_tiles, far_tiles), out...  29.1 us
    all_to_all x1, waiting for transfers between devices, on_device(): lax.all_to_all(far_forces.reshape(3, peers, slots, width), ('dom', 'sub')...  20.5 us
    all_to_all x1, starting transfers between devices, on_device(): lax.all_to_all(outgoing, ('dom', 'sub'), split_axis=0, concat_axis=0, til...  7.3 us
    gather x2, local copies, waits for them, and re-layouts, on_device(): outgoing = tile_groups(segments[send_tiles[0]])  6.11 us
  transfers between devices with their start and end apart: 2, of which 1 were waited for; matrix products, arithmetic and copies ran while one was open for 1% of the time, Pallas kernels for 0%

profile of v1, /device:TPU:0, one launch (start us, length us, event | category | flops | bytes accessed | tf_op | source)
XLA Modules:
  0.0 214.6 jit_solution(18123676994341020191)
XLA Ops:
  0.0 0.7 compare_select_fusion
  0.7 0.1 copy.45
  0.8 0.1 reshape.74
  0.9 4.6 %gather_fusion = f32[512,9,128]{2,0,1:T(8,128)S(1)} fusion(f32[128,9,128]{2,0,1:T(8,128)} %param.6, s32[1024]{0:T(1024)S(1)} %pad_clamp_fusion), kind=kCustom, calls=%fused_computation | custom fusion | bytes 4720640 | tf_op jit(solution)/shard_map/gather | solution.py:166
  5.5 1.5 copy.46
  7.0 0.3 slice.69
  7.3 0.2 slice.70
  7.4 0.2 slice.71
  7.7 1.9 pad_maximum_fusion
  9.5 0.0 copy-start.2
  9.5 0.0 copy-start.5
  9.5 7.3 %all-to-all-start = ((f32[32,18,8,128]{3,2,1,0:T(8,128)}), f32[32,18,8,128]{3,2,1,0:T(8,128)S(1)}, u32[]{:S(2)}, u32[]{:S(2)}) async-start(f32[32,18,8,128]{3,2,1,0:T(8,128)} %pad_maximum_fusion), calls=%async_computation | async-start | bytes 4718592 | tf_op jit(solution)/shard_map/all_to_all | solution.py:167
  16.8 0.0 slice-start
  16.9 0.0 slice-start.1
  16.9 0.0 copy-done.2
  16.9 0.0 copy-start.3
  16.9 0.0 copy-start
  16.9 0.0 copy-start.1
  17.0 0.6 copy-done.3
  17.6 0.2 multiply_reduce_fusion.1
  17.9 0.0 copy-done.5
  17.9 0.1 fusion.9
  18.0 74.2 %psum.7 = f32[64,9]{0,1:T(8,128)S(1)} all-reduce(f32[64,9]{0,1:T(8,128)S(1)} %fusion.9), channel_id=1, replica_groups=mesh['dom'=8,'sub'=4] {'dom','sub'}, use_global_device_ids=true, to_apply=%region_1.2 | all-reduce | flops 576 | bytes 4608 | tf_op jit(solution)/shard_map/psum | solution.py:168
  92.2 0.2 fusion.7
  92.4 0.2 fusion.6
  92.7 0.1 slice-done
  92.7 0.2 copy.55
  93.0 0.0 slice-done.1
  93.0 0.1 copy.56
  93.7 1.2 multiply_reduce_fusion
  94.9 0.1 maximum_bitcast_fusion.near_ref
  95.1 0.0 all-to-all-done.far_ref
  95.1 0.0 copy-done
  95.1 0.0 copy-done.1
  95.1 0.0 copy-start.4
  95.1 29.1 %shard_map.64 = (f32[3,128,128]{2,1,0:T(8,128)S(1)}, f32[3,512,128]{2,1,0:T(8,128)S(1)}) custom-call(s32[1]{0:T(128)S(6)} %copy.58.count_ref, s32[512]{0:T(512)S(1)} %bitcast.46, s32[512]{0:T(512)S(1)} %bitcast.47, f32[1,144,8,128]{3,2,1,0:T(8,128)S(1)} %maximum_bitcast_fusion.near_ref, f32[32,18,8,128]{3,2,1,0:T(8,128)S(1)} %all-to-all-done.far_ref), custom_call_target="tpu_custom_call" | custom-call | tf_op jit(solution)/shard_map/pallas_call | solution.py:109
  124.2 0.9 copy.47
  125.1 67.6 %all-to-all-start.1 = ((f32[3,32,16,128]{3,2,0,1:T(8,128)}), f32[3,32,16,128]{3,2,0,1:T(8,128)S(1)}, u32[]{:S(2)}, u32[]{:S(2)}) async-start(f32[3,32,16,128]{3,2,0,1:T(8,128)} %copy.47), calls=%async_computation.1 | async-start | bytes 1572864 | tf_op jit(solution)/shard_map/all_to_all | solution.py:172
  192.8 0.0 copy-done.4
  192.8 0.1 copy.49
  192.9 0.1 eq.20
  192.9 20.5 %all-to-all-done.1 = f32[3,32,16,128]{3,2,0,1:T(8,128)S(1)} async-done(((f32[3,32,16,128]{3,2,0,1:T(8,128)}), f32[3,32,16,128]{3,2,0,1:T(8,128)S(1)}, u32[]{:S(2)}, u32[]{:S(2)}) %all-to-all-start.1) | async-done | bytes 786464 | tf_op jit(solution)/shard_map/all_to_all | solution.py:172
  213.4 0.1 copy.48
  213.5 1.2 fusion.2
  (10 shorter events, 0.1 us)
Async XLA Ops:
  9.5 7.3 %copy-start.2 = (f32[128,9,128]{2,0,1:T(8,128)S(1)}, f32[128,9,128]{2,0,1:T(8,128)}, u32[]{:S(2)}) copy-start(f32[128,9,128]{2,0,1:T(8,128)} %param.6) | copy-start | bytes 1769476
  9.5 8.3 %copy-start.5 = (s32[128]{0:T(128)S(1)}, s32[128]{0:T(128)}, u32[]{:S(2)}) copy-start(s32[128]{0:T(128)} %param.11) | copy-start | bytes 1540
  9.5 85.5 %all-to-all-start = ((f32[32,18,8,128]{3,2,1,0:T(8,128)}), f32[32,18,8,128]{3,2,1,0:T(8,128)S(1)}, u32[]{:S(2)}, u32[]{:S(2)}) async-start(f32[32,18,8,128]{3,2,1,0:T(8,128)} %pad_maximum_fusion), calls=%async_computation | async-start | bytes 4718592 | tf_op jit(solution)/shard_map/all_to_all | solution.py:167
  16.8 75.9 %slice-start = ((f32[128,9,128]{2,0,1:T(8,128)}), f32[128,6,128]{2,0,1:T(8,128)S(1)}, s32[]{:S(2)}) async-start(f32[128,9,128]{2,0,1:T(8,128)} %param.6), calls=%async_computation.2 | async-start | bytes 786432 | tf_op jit(solution)/shard_map/slice | solution.py:122
  16.9 76.1 %slice-start.1 = ((f32[128,9,128]{2,0,1:T(8,128)}), f32[128,2,128]{2,0,1:T(8,128)S(1)}, s32[]{:S(2)}) async-start(f32[128,9,128]{2,0,1:T(8,128)} %param.6), calls=%async_computation.3 | async-start | bytes 262144 | tf_op jit(solution)/shard_map/slice | solution.py:122
  16.9 0.7 copy-start.3
  16.9 78.1 %copy-start = (s32[1,512]{1,0:T(1,128)S(1)}, s32[1,512]{1,0:T(1,128)}, u32[]{:S(2)}) copy-start(s32[1,512]{1,0:T(1,128)} %param.8) | copy-start | bytes 6148
  16.9 78.1 %copy-start.1 = (s32[1,512]{1,0:T(1,128)S(1)}, s32[1,512]{1,0:T(1,128)}, u32[]{:S(2)}) copy-start(s32[1,512]{1,0:T(1,128)} %param.9) | copy-start | bytes 6148
  95.1 97.7 %copy-start.4 = (s32[1,32,16]{1,2,0:T(8,128)S(1)}, s32[1,32,16]{1,2,0:T(8,128)}, u32[]{:S(2)}) copy-start(s32[1,32,16]{1,2,0:T(8,128)} %param.7) | copy-start | bytes 6148
  125.1 88.3 %all-to-all-start.1 = ((f32[3,32,16,128]{3,2,0,1:T(8,128)}), f32[3,32,16,128]{3,2,0,1:T(8,128)S(1)}, u32[]{:S(2)}, u32[]{:S(2)}) async-start(f32[3,32,16,128]{3,2,0,1:T(8,128)} %copy.47), calls=%async_computation.1 | async-start | bytes 1572864 | tf_op jit(solution)/shard_map/all_to_all | solution.py:172

commit v2 on v0

v2 whole, which is shorter than its diff:
```python
import functools
import jax
import jax.numpy as jnp
from jax import lax
from jax.sharding import PartitionSpec as P
from jax.experimental import pallas as pl
from jax.experimental.pallas import tpu as pltpu

CORE = 0.25
GROUP = 4


def head(value):
    return value.astype(jnp.bfloat16).astype(jnp.float32)


def thirds(value):
    high = head(value)
    rest = value - high
    middle = head(rest)
    return high, middle, rest - middle


def halves(value):
    high = value.astype(jnp.bfloat16)
    return high, (value - high.astype(jnp.float32)).astype(jnp.bfloat16)


def tall(groups):
    return jnp.concatenate(groups, axis=0).astype(jnp.bfloat16)


def place(sub, rows, others=0.0):
    filled = others
    for at, row in rows.items():
        filled = jnp.where(sub == at, row, filled)
    return filled


def tile_parts(sub, tile, row):
    row = jnp.broadcast_to(row, tile.shape)
    square = row * row
    for at in (6, 7):
        other = jnp.broadcast_to(tile[at : at + 1], tile.shape)
        square = square + other * other
    main, last = thirds(tile), thirds(row)
    positions = [jnp.where(sub >= 6, m, jnp.where(sub == 5, r, 0.0)) for m, r in zip(main, last)]
    sums = tall([jnp.where(sub == 4, 1.0, positions[0]), positions[1], positions[2], jnp.zeros_like(tile)])
    spot = jnp.where(sub >= 6, tile, jnp.where(sub == 5, row, 0.0))
    return main, last, square, sums, spot


def operands(near, near_row, far, far_row):
    sub = lax.broadcasted_iota(jnp.int32, near.shape, 0)
    first = sub < 3
    second = jnp.logical_and(sub >= 3, sub < 6)
    zero = jnp.zeros_like(near)
    scale = 1.0 / near.shape[1]
    middle = jnp.where(sub >= 6, jnp.sum(near, axis=1, keepdims=True) * scale, 0.0)
    middle_row = jnp.sum(near_row, axis=1, keepdims=True) * scale
    near, far = near - middle, far - middle
    near_row, far_row = near_row - middle_row, far_row - middle_row
    (high, mid, low), (row_high, row_mid, row_low), square, near_sums, near_spot = tile_parts(sub, near, near_row)
    square_parts = thirds(square)
    left = tall(
        [
            high, mid, high, low, high, mid,
            place(sub, {0: row_high, 1: row_mid, 2: row_high, 3: row_low, 4: row_high, 5: row_mid}),
            place(sub, {0: square_parts[0], 1: square_parts[1], 2: square_parts[2]}, jnp.where(second, 1.0, 0.0)),
        ]
    )
    (high, mid, low), (row_high, row_mid, row_low), square, far_sums, far_spot = tile_parts(sub, far, far_row)
    square_parts = thirds(square + CORE)
    twice = [jnp.where(sub >= 6, -2.0 * part, 0.0) for part in (high, mid, low)]
    twice_row = [-2.0 * part for part in (row_high, row_mid, row_low)]
    spread = tall(
        [
            twice[0], twice[0], twice[1], twice[0], twice[2], twice[1],
            place(sub, {0: twice_row[0], 1: twice_row[0], 2: twice_row[1], 3: twice_row[0], 4: twice_row[2], 5: twice_row[1]}, zero),
            place(sub, {3: square_parts[0], 4: square_parts[1], 5: square_parts[2]}, jnp.where(first, 1.0, 0.0)),
        ]
    )
    dots = []
    for part in (
        [jnp.where(first, part, 0.0) for part in (high, mid)],
        [jnp.where(first, pltpu.roll(part, 5, 0), 0.0) for part in (high, mid)],
        [jnp.where(second, pltpu.roll(part, 3, 0), 0.0) for part in (high, mid)],
    ):
        dots.append(tall([part[0], part[0], part[1], zero]))
    return left.T, spread, dots, near_sums, near_spot, far_sums, far_spot


def matmul(left, right, contract=(1, 0)):
    dims = (((contract[0],), (contract[1],)), ((), ()))
    return lax.dot_general(left, right, dims, preferred_element_type=jnp.float32)


def live_list(near_rows, far_rows, ids_ref):
    slots = ids_ref.shape[1]

    def line(rows):
        return jnp.concatenate([rows[k : k + 1] for k in range(rows.shape[0])], axis=1)

    near, far = line(near_rows), line(far_rows)
    alive = near >= 0
    row = lax.broadcasted_iota(jnp.int32, (slots, slots), 0)
    lane = lax.broadcasted_iota(jnp.int32, (slots, slots), 1)
    before = jnp.where(row < lane, 1.0, 0.0).astype(jnp.bfloat16)
    flags = jnp.where(alive, 1.0, 0.0)
    rank = matmul(jnp.broadcast_to(flags, (8, slots)).astype(jnp.bfloat16), before)[0:1]
    rank = jnp.where(alive, rank, -1.0)
    chosen = jnp.where(jnp.broadcast_to(rank, (slots, slots)) == row.astype(jnp.float32), 1.0, 0.0).astype(jnp.bfloat16)
    sub = lax.broadcasted_iota(jnp.int32, (8, slots), 0)
    near, far = jnp.maximum(near, 0).astype(jnp.int32), far.astype(jnp.int32)
    values = [near >> 6, near & 63, far >> 6, far & 63]
    values = place(sub, {k: value.astype(jnp.float32) for k, value in enumerate(values)}, jnp.zeros((8, slots), jnp.float32))
    packed = matmul(values.astype(jnp.bfloat16), chosen, (1, 1)).astype(jnp.int32)
    number = jnp.sum(flags, axis=1, keepdims=True).astype(jnp.int32)
    ids_ref[0:1, :] = packed[0:1] * 64 + packed[1:2]
    ids_ref[1:2, :] = packed[2:3] * 64 + packed[3:4]
    ids_ref[2:3, :] = jnp.broadcast_to(number, (1, slots))


def pair_kernel(plan, refs_in, refs_out, scratch):
    tiles, slots, near_number, far_number, list_group = plan
    (blocks, lists, near_sum, far_sum, ids_vmem, ids, left_ref, wide_ref, cross_ref, part_ref, sums_ref, spots_ref,
     sems, list_sems, out_sems) = scratch
    list_copies = [
        pltpu.make_async_copy(source.at[list_group], lists.at[k], list_sems.at[k]) for k, source in enumerate(refs_in)
    ]
    copies = [pltpu.make_async_copy(source, blocks.at[k], sems.at[k]) for k, source in enumerate(refs_in)]
    for copy in list_copies + copies:
        copy.start()
    near_sum[...] = jnp.zeros_like(near_sum)
    far_sum[...] = jnp.zeros_like(far_sum)
    wide_ref[...] = jnp.zeros_like(wide_ref)
    for copy in list_copies:
        copy.wait()

    width = blocks.shape[-1]
    shape = (4, width)
    position = lax.broadcasted_iota(jnp.int32, shape, 0) * width + lax.broadcasted_iota(jnp.int32, shape, 1)
    near_ids = jnp.full(shape, -1.0)
    for k in range(near_number):
        given = lists[k, 0:4]
        given = jnp.where(given >= 0, given + k * tiles, given)
        near_ids = jnp.where(position // (far_number * slots) == k, given, near_ids)
    far_ids = jnp.zeros(shape)
    for k in range(far_number):
        given = lists[near_number - 1 + k if k else 0, 4:8] + k * tiles
        far_ids = jnp.where(position // slots % far_number == k, given, far_ids)
    live_list(near_ids, far_ids, ids_vmem)
    move = pltpu.make_async_copy(ids_vmem, ids, list_sems.at[0])
    move.start()
    move.wait()
    count = ids[2, 0]
    last = ids.shape[1] - 1
    for copy in copies:
        copy.wait()

    def tile_of(block, tile):
        return blocks[block, tile], blocks[block, tiles + tile // 8, pl.ds(tile % 8, 1), :]

    def pick(group, k):
        at = group * GROUP + k
        held = jnp.clip(at, 0, last)
        near, far = ids[0, held], ids[1, held]
        live = jnp.logical_and(at >= 0, at < count)
        return live, near // tiles, near % tiles, far // tiles, far % tiles

    def step(group, carry):
        for k in range(GROUP):
            live, near_block, near_tile, far_block, far_tile = pick(group - 2, k)
            stash = lax.rem(group + 1, 3)
            near_rows, far_rows = sums_ref[stash, k, 0], sums_ref[stash, k, 1]
            parts = part_ref[k]
            half = parts.shape[1] // 2
            for block, tile, spot, total, out in (
                (near_block, near_tile, 0, matmul(jnp.concatenate([far_rows, far_rows], axis=1), parts, (1, 1)), near_sum),
                (far_block, far_tile, 1, matmul(near_rows, parts), far_sum),
            ):
                total = total[0:8] + total[8:16] + total[16:24]
                if total.shape[1] > half:
                    total = total[:, :half] + total[:, half:]
                force = spots_ref[stash, k, spot] * jnp.broadcast_to(total[4:5], total.shape) - total
                out[block, tile] += jnp.where(live, force, 0.0)
        for k in range(GROUP):
            left = left_ref[k]
            terms = matmul(left, wide_ref[k])
            more = matmul(left[:, : cross_ref.shape[1]], cross_ref[k])
            spread, burgers_dot = terms[:, :width], terms[:, width:]
            inverse = lax.rsqrt(spread)
            coupling = (burgers_dot + more[:, :width] * more[:, width:]) * (inverse * inverse * inverse)
            high, low = halves(coupling)
            part_ref[k, :, :width] = high
            part_ref[k, :, width:] = low
        for k in range(GROUP):
            live, near_block, near_tile, far_block, far_tile = pick(group, k)
            far_place = jnp.where(far_block > 0, far_block + (near_number - 1), 0)
            left, spread, dots, near_rows, near_spot, far_rows, far_spot = operands(
                *tile_of(near_block, near_tile), *tile_of(far_place, far_tile)
            )
            stash = lax.rem(group, 3)
            left_ref[k] = left
            wide_ref[k, :, :width] = spread
            wide_ref[k, : dots[0].shape[0], width:] = dots[0]
            cross_ref[k, :, :width] = dots[1]
            cross_ref[k, :, width:] = dots[2]
            sums_ref[stash, k, 0] = near_rows
            sums_ref[stash, k, 1] = far_rows
            spots_ref[stash, k, 0] = near_spot
            spots_ref[stash, k, 1] = far_spot
        return carry

    lax.fori_loop(0, (count + GROUP - 1) // GROUP + 2, step, 0)

    for total, outs in ((near_sum, refs_out[:near_number]), (far_sum, refs_out[near_number:])):
        for k, out in enumerate(outs):
            for axis, row in enumerate((6, 7, 5)):
                out[axis] = total[k, :, row, :]


def run_pairs(blocks, tiles, slots, near_number, far_number, list_group):
    width = blocks[0].shape[-1]
    number = near_number + far_number
    slot_count = near_number * far_number * slots
    hbm = pl.BlockSpec(memory_space=pl.ANY)
    vmem = pl.BlockSpec(memory_space=pltpu.VMEM)
    forces = (3, tiles, width)
    plan = (tiles, slots, near_number, far_number, list_group)
    depth, dot_depth, sum_rows = 64, 32, 32

    def kernel(*refs):
        given = len(blocks)
        pair_kernel(plan, refs[:given], refs[given : given + number], refs[given + number :])

    return pl.pallas_call(
        kernel,
        out_shape=[jax.ShapeDtypeStruct(forces, jnp.float32)] * number,
        in_specs=[hbm] * len(blocks),
        out_specs=[vmem] * number,
        scratch_shapes=[
            pltpu.VMEM((len(blocks),) + blocks[0].shape, jnp.float32),
            pltpu.VMEM((len(blocks), 8, width), jnp.float32),
            pltpu.VMEM((near_number, tiles, 8, width), jnp.float32),
            pltpu.VMEM((far_number, tiles, 8, width), jnp.float32),
            pltpu.VMEM((8, slot_count), jnp.int32),
            pltpu.SMEM((8, slot_count), jnp.int32),
            pltpu.VMEM((GROUP, width, depth), jnp.bfloat16),
            pltpu.VMEM((GROUP, depth, 2 * width), jnp.bfloat16),
            pltpu.VMEM((GROUP, dot_depth, 2 * width), jnp.bfloat16),
            pltpu.VMEM((GROUP, width, 2 * width), jnp.bfloat16),
            pltpu.VMEM((3, GROUP, 2, sum_rows, width), jnp.bfloat16),
            pltpu.VMEM((3, GROUP, 2, 8, width), jnp.float32),
            pltpu.SemaphoreType.DMA((len(blocks),)),
            pltpu.SemaphoreType.DMA((len(blocks),)),
            pltpu.SemaphoreType.DMA((number,)),
        ],
        compiler_params=pltpu.CompilerParams(vmem_limit_bytes=60 * 1024 * 1024),
        name="pairs",
    )(*blocks)


def tile_groups(tiles):
    main = jnp.concatenate([tiles[..., 3:9, :], tiles[..., 0:2, :]], axis=-2)
    rows = tiles[..., 2, :]
    short = -rows.shape[-2] % 8
    rows = jnp.pad(rows, [(0, 0)] * (rows.ndim - 2) + [(0, short), (0, 0)])
    rows = rows.reshape(rows.shape[:-2] + (rows.shape[-2] // 8, 8, rows.shape[-1]))
    return jnp.concatenate([main, rows], axis=-3)


NCELL = 64


def far_field(segments, tile_cell, moment_sums, total_segments):
    moments = moment_sums.reshape(NCELL, 3, 3) / jnp.sqrt(jnp.float32(total_segments))
    moments = 0.5 * (moments + jnp.transpose(moments, (0, 2, 1)))
    cells = jnp.arange(NCELL).astype(jnp.float32)
    weights = 8.0 / (8.0 + jnp.abs(cells[:, None] - cells[None, :]))
    stress = jnp.dot(weights, moments.reshape(NCELL, 9), precision=lax.Precision.HIGHEST)
    onehot = (tile_cell[:, None] == jnp.arange(NCELL)[None, :]).astype(jnp.float32)
    tile_stress = jnp.dot(onehot, stress, precision=lax.Precision.HIGHEST).reshape(-1, 3, 3)
    traction = jnp.sum(tile_stress[:, :, :, None] * segments[:, None, 3:6, :], axis=2)
    lines = segments[:, 6:9, :]
    return jnp.stack(
        [
            traction[:, 1] * lines[:, 2] - traction[:, 2] * lines[:, 1],
            traction[:, 2] * lines[:, 0] - traction[:, 0] * lines[:, 2],
            traction[:, 0] * lines[:, 1] - traction[:, 1] * lines[:, 0],
        ],
        axis=1,
    )


def local_moments(segments, tile_cell):
    outer = jnp.sum(segments[:, 3:6, None, :] * segments[:, None, 6:9, :], axis=3).reshape(-1, 9)
    onehot = (jnp.arange(NCELL)[:, None] == tile_cell[None, :]).astype(jnp.float32)
    return jnp.dot(onehot, outer, precision=lax.Precision.HIGHEST)


AXES = ("dom", "sub")


def swap(value, mask):
    devices = lax.axis_size(AXES)
    return lax.ppermute(value, AXES, [(k, k ^ mask) for k in range(devices)])


def span(steps):
    masks = [0]
    for step in steps:
        masks += [mask ^ step for mask in masks]
    return masks


def mask_steps(devices):
    bits = devices.bit_length() - 1
    number = bits // 2
    far_steps = [devices >> (k + 2) for k in range(number)]
    near_steps = [devices >> 1] + [devices >> (k + 1) for k in range(number + 1, bits)]
    return near_steps, far_steps


def spread(block, near_steps, far_steps):
    steps = list(near_steps) + list(far_steps)
    allowed = set(span(near_steps)) | set(span(far_steps))
    held = {0: block}
    fresh = {0: -1}
    while fresh:
        arrived = {}
        for mask, last in fresh.items():
            for at in range(last + 1, len(steps)):
                if mask ^ steps[at] in allowed:
                    arrived[mask ^ steps[at]] = (swap(held[mask], steps[at]), at)
        if arrived:
            values = lax.optimization_barrier([value for value, at in arrived.values()])
            held.update(zip(arrived, values))
        fresh = {mask: at for mask, (value, at) in arrived.items()}
    return [held[mask] for mask in span(near_steps)], [held[mask] for mask in span(far_steps)]


def collect(near_parts, near_steps, far_parts, far_steps):
    totals = []
    for parts, steps in ((near_parts, near_steps), (far_parts, far_steps)):
        parts = list(parts)
        for step in reversed(steps):
            half = len(parts) // 2
            received = [swap(part, step) for part in reversed(parts[half:])]
            parts = [part + got for part, got in zip(parts[:half], reversed(received))]
        totals.append(parts[0])
    return totals[0] + totals[1]


def rows_of(values, width):
    flat = values.reshape(-1).astype(jnp.float32)
    groups = -(-flat.shape[0] // (8 * width))
    return jnp.pad(flat, (0, groups * 8 * width - flat.shape[0])).reshape(groups, 8, width)


def on_device(segments, send_tiles, pair_local, pair_remote, pair_count, tile_cell):
    width = segments.shape[2]
    tiles = segments.shape[0]
    devices = send_tiles.shape[1]
    slots = send_tiles.shape[2]
    pairs = pair_local.shape[1]
    near_steps, far_steps = mask_steps(devices)
    near_masks, far_masks = span(near_steps), span(far_steps)

    live = jnp.arange(pairs) < pair_count[0]
    me = lax.axis_index(AXES).astype(jnp.int32)
    peers = jnp.bitwise_xor(me, jnp.array([near ^ far for near in near_masks for far in far_masks], jnp.int32))
    order = (peers[:, None] * slots + jnp.arange(slots)[None, :]).reshape(-1)
    named = jnp.logical_and(pair_remote[0][:, None] == order[None, :], live[:, None])
    table = jnp.sum(jnp.where(named, pair_local[0][:, None] + 1, 0), axis=0) - 1
    chosen = peers[:, None] == jnp.arange(devices)[None, :]
    sent = jnp.sum(jnp.where(chosen[:, :, None], send_tiles[0][None], 0), axis=1)
    lists = jnp.concatenate([table, sent.reshape(-1)])
    moments = local_moments(segments, tile_cell)
    list_rows, moment_rows = rows_of(lists, width), rows_of(moments, width)
    main = tile_groups(segments)
    block = jnp.concatenate([main, list_rows, moment_rows], axis=0)

    near_blocks, far_blocks = spread(block, near_steps, far_steps)
    at_lists = main.shape[0]
    at_moments = at_lists + list_rows.shape[0]
    sums = functools.reduce(jnp.add, [given[at_moments:] for given in near_blocks])
    outs = run_pairs(near_blocks + far_blocks[1:], tiles, slots, len(near_masks), len(far_masks), at_lists)
    outs, sums = lax.optimization_barrier((outs, sums))
    for step in far_steps:
        sums = sums + swap(sums, step)
    moment_sums = sums.reshape(-1)[: NCELL * 9].reshape(NCELL, 9)
    forces = collect(outs[: len(near_masks)], near_steps, outs[len(near_masks) :], far_steps)
    total_segments = tiles * width * devices
    return forces.transpose(1, 0, 2) + far_field(segments, tile_cell, moment_sums, total_segments)


def solution(mesh):
    in_specs = (
        P(("dom", "sub"), None, None),
        P(("dom", "sub"), None, None),
        P(("dom", "sub"), None),
        P(("dom", "sub"), None),
        P(("dom", "sub")),
        P(("dom", "sub")),
    )
    out_specs = P(("dom", "sub"), None, None)
    return jax.shard_map(
        on_device, mesh=mesh, in_specs=in_specs, out_specs=out_specs, check_vma=False
    )
```

time: 510 us -> 115 us (0.23)
  other arithmetic: 347 us -> 2.65 us
  blocking collectives: 74.4 us -> 0 us
  local copies, waits for them, and re-layouts: 50.7 us -> 7.89 us
  waiting for transfers between devices: 19.2 us -> 51.2 us
  Pallas kernels: 0 us -> 23.1 us
  starting transfers between devices: 11.2 us -> 28.6 us
  loops' own time: 5.5 us -> 0 us
    reduce_sum x24 -> x2, other arithmetic: 201 us -> 0.91 us  [the longest x1 0.62 us: on_device(): jnp.sum(jnp.where(chosen[:, :, None], send_tiles[0][None], 0), axis=1)]
    scatter-add x17 -> x0, other arithmetic: 92.5 us -> none  [the longest x8 53.8 us: advance(): far_forces.at[remote_ids].add(far_part)]
    psum x1 -> x0, blocking collectives: 74.4 us -> none  [on_device(): moment_sums = lax.psum(local_moments(segments, tile_cell), ('dom', 'sub'))]
    ppermute x0 -> x22, waiting for transfers between devices: none -> 51.2 us  [swap(): return lax.ppermute(value, AXES, [(k, k ^ mask) for k in range(devices)])]
    mul x8 -> x1, other arithmetic: 44.6 us -> 0.01 us  [on_device(): order = (peers[:, None] * slots + jnp.arange(slots)[None, :]).reshape(-1)]
    gather x18 -> x0, local copies, waits for them, and re-layouts: 33.5 us -> none  [the longest x8 22.3 us: advance(): arrived[remote_ids]]
    ppermute x0 -> x22, starting transfers between devices: none -> 28.6 us  [swap(): return lax.ppermute(value, AXES, [(k, k ^ mask) for k in range(devices)])]
    pallas_call x0 -> x1, Pallas kernels: none -> 23.1 us  [run_pairs(): pl.pallas_call(kernel, out_shape=[jax.ShapeDtypeStruct(forces, jnp.float3...]
  transfers between devices with their start and end apart: 2 -> 22, of which waited for: 1 -> 11; matrix products, arithmetic and copies ran while one was open for 1% -> 1% of each run, Pallas kernels for 0% -> 0%
where the time goes in v2:
time: 115 us
  waiting for transfers between devices  51.2 us (45%)
  starting transfers between devices  28.6 us (25%)
  Pallas kernels  23.1 us (20%)
  local copies, waits for them, and re-layouts  7.89 us (7%)
  other arithmetic  2.65 us (2%)
    ppermute x22, waiting for transfers between devices, swap(): return lax.ppermute(value, AXES, [(k, k ^ mask) for k in range(devices)])  51.2 us
    ppermute x22, starting transfers between devices, swap(): return lax.ppermute(value, AXES, [(k, k ^ mask) for k in range(devices)])  28.6 us
    pallas_call x1, Pallas kernels, run_pairs(): pl.pallas_call(kernel, out_shape=[jax.ShapeDtypeStruct(forces, jnp.float3...  23.1 us
    unnamed x52, local copies, waits for them, and re-layouts  5.01 us
  transfers between devices with their start and end apart: 22, of which 11 were waited for; matrix products, arithmetic and copies ran while one was open for 1% of the time, Pallas kernels for 0%

profile of v2, /device:TPU:0, one launch (start us, length us, event | category | flops | bytes accessed | tf_op | source)
XLA Modules:
  0.0 115.0 jit_solution(7805881802086792649)
XLA Ops:
  0.0 1.0 fusion.10
  1.1 1.0 copy-done.1
  3.0 0.3 select_reduce_fusion
  3.4 0.6 select_reduce_fusion.1
  4.1 0.3 multiply_reduce_fusion.1
  4.3 0.6 copy-done.23
  5.0 0.1 fusion.4
  5.1 0.1 reshape.121
  5.3 0.2 copy.32
  5.5 0.6 slice-done.1
  6.3 0.1 pad_maximum_fusion.refs_0_
  6.4 4.1 %collective-permute-start = (f32[146,8,128]{2,1,0:T(8,128)S(1)}, f32[146,8,128]{2,1,0:T(8,128)S(1)}, u32[]{:S(2)}, u32[]{:S(2)}) collective-permute-start(f32[146,8,128]{2,1,0:T(8,128)S(1)} %pad_maximum_fusion.refs_0_), channel_id=1, source_target_pairs={{0,16},{1,17},{2,18},{3,19},{4,20},{5,21},{6,22},{7,23},{8,24},{9,... | collective-permute-start | bytes 1794056 | tf_op jit(solution)/shard_map/ppermute | solution.py:307
  10.5 1.5 %collective-permute-start.1 = (f32[146,8,128]{2,1,0:T(8,128)S(1)}, f32[146,8,128]{2,1,0:T(8,128)S(1)}, u32[]{:S(2)}, u32[]{:S(2)}) collective-permute-start(f32[146,8,128]{2,1,0:T(8,128)S(1)} %pad_maximum_fusion.refs_0_), channel_id=1, source_target_pairs={{0,2},{1,3},{2,0},{3,1},{4,6},{5,7},{6,4},{7,5},{8,10},{9,11},{10,... | collective-permute-start | bytes 1794056 | tf_op jit(solution)/shard_map/ppermute | solution.py:307
  12.1 1.6 %collective-permute-start.3 = (f32[146,8,128]{2,1,0:T(8,128)S(1)}, f32[146,8,128]{2,1,0:T(8,128)S(1)}, u32[]{:S(2)}, u32[]{:S(2)}) collective-permute-start(f32[146,8,128]{2,1,0:T(8,128)S(1)} %pad_maximum_fusion.refs_0_), channel_id=1, source_target_pairs={{0,8},{1,9},{2,10},{3,11},{4,12},{5,13},{6,14},{7,15},{8,0},{9,1},... | collective-permute-start | bytes 1794056 | tf_op jit(solution)/shard_map/ppermute | solution.py:307
  13.6 1.5 %collective-permute-start.4 = (f32[146,8,128]{2,1,0:T(8,128)S(1)}, f32[146,8,128]{2,1,0:T(8,128)S(1)}, u32[]{:S(2)}, u32[]{:S(2)}) collective-permute-start(f32[146,8,128]{2,1,0:T(8,128)S(1)} %pad_maximum_fusion.refs_0_), channel_id=1, source_target_pairs={{0,4},{1,5},{2,6},{3,7},{4,0},{5,1},{6,2},{7,3},{8,12},{9,13},{10,... | collective-permute-start | bytes 1794056 | tf_op jit(solution)/shard_map/ppermute | solution.py:307
  15.1 21.8 %collective-permute-done.refs_1_ = f32[146,8,128]{2,1,0:T(8,128)S(1)} collective-permute-done((f32[146,8,128]{2,1,0:T(8,128)S(1)}, f32[146,8,128]{2,1,0:T(8,128)S(1)}, u32[]{:S(2)}, u32[]{:S(2)}) %collective-permute-start) | collective-permute-done | bytes 598048 | tf_op jit(solution)/shard_map/ppermute | solution.py:307
  37.0 2.6 %collective-permute-done.3.refs_8_ = f32[146,8,128]{2,1,0:T(8,128)S(1)} collective-permute-done((f32[146,8,128]{2,1,0:T(8,128)S(1)}, f32[146,8,128]{2,1,0:T(8,128)S(1)}, u32[]{:S(2)}, u32[]{:S(2)}) %collective-permute-start.3) | collective-permute-done | bytes 598048 | tf_op jit(solution)/shard_map/ppermute | solution.py:307
  39.6 0.6 collective-permute-start.5
  40.3 0.5 collective-permute-start.7
  40.8 1.5 %collective-permute-start.8 = (f32[146,8,128]{2,1,0:T(8,128)S(1)}, f32[146,8,128]{2,1,0:T(8,128)S(1)}, u32[]{:S(2)}, u32[]{:S(2)}) collective-permute-start(f32[146,8,128]{2,1,0:T(8,128)S(1)} %collective-permute-done.3.refs_8_), channel_id=1, source_target_pairs={{0,4},{1,5},{2,6},{3,7},{4,0},{5,1},{6,2},{7,3},{8,12},{9,13},{10,... | collective-permute-start | bytes 1794056 | tf_op jit(solution)/shard_map/ppermute | solution.py:307
  42.3 12.6 %collective-permute-done.5.refs_3_ = f32[146,8,128]{2,1,0:T(8,128)S(1)} collective-permute-done((f32[146,8,128]{2,1,0:T(8,128)S(1)}, f32[146,8,128]{2,1,0:T(8,128)S(1)}, u32[]{:S(2)}, u32[]{:S(2)}) %collective-permute-start.5) | collective-permute-done | bytes 598048 | tf_op jit(solution)/shard_map/ppermute | solution.py:307
  54.9 1.3 %collective-permute-done.8.refs_10_ = f32[146,8,128]{2,1,0:T(8,128)S(1)} collective-permute-done((f32[146,8,128]{2,1,0:T(8,128)S(1)}, f32[146,8,128]{2,1,0:T(8,128)S(1)}, u32[]{:S(2)}, u32[]{:S(2)}) %collective-permute-start.8) | collective-permute-done | bytes 598048 | tf_op jit(solution)/shard_map/ppermute | solution.py:307
  56.2 0.8 copy-done.12
  57.0 1.2 %collective-permute-done.9.refs_7_ = f32[146,8,128]{2,1,0:T(8,128)S(1)} collective-permute-done((f32[146,8,128]{2,1,0:T(8,128)S(1)}, f32[146,8,128]{2,1,0:T(8,128)S(1)}, u32[]{:S(2)}, u32[]{:S(2)}) %collective-permute-start.9) | collective-permute-done | bytes 598048 | tf_op jit(solution)/shard_map/ppermute | solution.py:307
  58.2 0.8 copy-done.9
  59.1 23.1 %pairs.1 = (f32[3,128,128]{2,1,0:T(8,128)}, f32[3,128,128]{2,1,0:T(8,128)}, f32[3,128,128]{2,1,0:T(8,128)}, f32[3,128,128]{2,1,0:T(8,128)}, f32[3,128,128]{2,1,0...) custom-call(f32[146,8,128]{2,1,0:T(8,128)} %copy-done, ...), custom_call_target="tpu_custom_call" | custom-call | tf_op jit(solution)/shard_map/pairs/pallas_call | solution.py:237
  82.2 4.7 %collective-permute-start.20 = (f32[1,8,128]{2,1,0:T(8,128)S(1)}, f32[1,8,128]{2,1,0:T(8,128)S(1)}, u32[]{:S(2)}, u32[]{:S(2)}) collective-permute-start(f32[1,8,128]{2,1,0:T(8,128)S(1)} %slice_add_fusion), channel_id=1, source_target_pairs={{0,8},{1,9},{2,10},{3,11},{4,12},{5,13},{6,14},{7,15},{8,0},{9,1},... | collective-permute-start | bytes 12296 | tf_op jit(solution)/shard_map/ppermute | solution.py:307
  86.9 1.6 %collective-permute-done.20 = f32[1,8,128]{2,1,0:T(8,128)S(1)} collective-permute-done((f32[1,8,128]{2,1,0:T(8,128)S(1)}, f32[1,8,128]{2,1,0:T(8,128)S(1)}, u32[]{:S(2)}, u32[]{:S(2)}) %collective-permute-start.20) | collective-permute-done | bytes 4128 | tf_op jit(solution)/shard_map/ppermute | solution.py:307
  88.5 1.9 %collective-permute-start.21 = (f32[1,8,128]{2,1,0:T(8,128)S(1)}, f32[1,8,128]{2,1,0:T(8,128)S(1)}, u32[]{:S(2)}, u32[]{:S(2)}) collective-permute-start(f32[1,8,128]{2,1,0:T(8,128)S(1)} %add.142), channel_id=1, source_target_pairs={{0,4},{1,5},{2,6},{3,7},{4,0},{5,1},{6,2},{7,3},{8,12},{9,13},{10,... | collective-permute-start | bytes 12296 | tf_op jit(solution)/shard_map/ppermute | solution.py:307
  90.4 0.5 collective-permute-start.14
  90.9 0.2 collective-permute-start.18
  91.1 1.0 collective-permute-done.21
  92.1 0.2 div.14
  92.4 0.5 copy.29
  93.0 0.2 fusion.2
  93.3 0.5 copy-done.18
  93.9 2.5 %collective-permute-start.15 = (f32[3,128,128]{2,1,0:T(8,128)S(1)}, f32[3,128,128]{2,1,0:T(8,128)S(1)}, u32[]{:S(2)}, u32[]{:S(2)}) collective-permute-start(f32[3,128,128]{2,1,0:T(8,128)S(1)} %add.134), channel_id=1, source_target_pairs={{0,2},{1,3},{2,0},{3,1},{4,6},{5,7},{6,4},{7,5},{8,10},{9,11},{10,... | collective-permute-start | bytes 589832 | tf_op jit(solution)/shard_map/ppermute | solution.py:307
  96.4 0.2 fusion.1
  96.7 0.2 multiply_reduce_fusion
  96.9 0.7 copy-done.24
  97.6 1.9 %collective-permute-start.17 = (f32[3,128,128]{2,1,0:T(8,128)S(1)}, f32[3,128,128]{2,1,0:T(8,128)S(1)}, u32[]{:S(2)}, u32[]{:S(2)}) collective-permute-start(f32[3,128,128]{2,1,0:T(8,128)S(1)} %copy-done.24), channel_id=1, source_target_pairs={{0,4},{1,5},{2,6},{3,7},{4,0},{5,1},{6,2},{7,3},{8,12},{9,13},{10,... | collective-permute-start | bytes 589832 | tf_op jit(solution)/shard_map/ppermute | solution.py:307
  99.6 1.8 %collective-permute-start.12 = (f32[3,128,128]{2,1,0:T(8,128)S(1)}, f32[3,128,128]{2,1,0:T(8,128)S(1)}, u32[]{:S(2)}, u32[]{:S(2)}) collective-permute-start(f32[3,128,128]{2,1,0:T(8,128)S(1)} %add.131), channel_id=1, source_target_pairs={{0,2},{1,3},{2,0},{3,1},{4,6},{5,7},{6,4},{7,5},{8,10},{9,11},{10,... | collective-permute-start | bytes 589832 | tf_op jit(solution)/shard_map/ppermute | solution.py:307
  101.5 0.4 collective-permute-done.15
  101.9 3.7 %collective-permute-start.16 = (f32[3,128,128]{2,1,0:T(8,128)S(1)}, f32[3,128,128]{2,1,0:T(8,128)S(1)}, u32[]{:S(2)}, u32[]{:S(2)}) collective-permute-start(f32[3,128,128]{2,1,0:T(8,128)S(1)} %add_add_fusion), channel_id=1, source_target_pairs={{0,16},{1,17},{2,18},{3,19},{4,20},{5,21},{6,22},{7,23},{8,24},{9,... | collective-permute-start | bytes 589832 | tf_op jit(solution)/shard_map/ppermute | solution.py:307
  105.7 0.6 collective-permute-done.12
  106.2 3.3 %collective-permute-done.19 = f32[3,128,128]{2,1,0:T(8,128)S(1)} collective-permute-done((f32[3,128,128]{2,1,0:T(8,128)S(1)}, f32[3,128,128]{2,1,0:T(8,128)S(1)}, u32[]{:S(2)}, u32[]{:S(2)}) %collective-permute-start.19) | collective-permute-done | bytes 196640 | tf_op jit(solution)/shard_map/ppermute | solution.py:307
  109.5 4.7 %collective-permute-done.16 = f32[3,128,128]{2,1,0:T(8,128)S(1)} collective-permute-done((f32[3,128,128]{2,1,0:T(8,128)S(1)}, f32[3,128,128]{2,1,0:T(8,128)S(1)}, u32[]{:S(2)}, u32[]{:S(2)}) %collective-permute-start.16) | collective-permute-done | bytes 196640 | tf_op jit(solution)/shard_map/ppermute | solution.py:307
  114.3 0.8 maximum_add_fusion
  (92 shorter events, 1.1 us)
Async XLA Ops:
  1.1 1.1 copy-start.1
  1.1 1.1 copy-start.22
  1.1 1.2 %copy-start.21 = (s32[1,512]{1,0:T(1,128)S(1)}, s32[1,512]{1,0:T(1,128)}, u32[]{:S(2)}) copy-start(s32[1,512]{1,0:T(1,128)} %param.9) | copy-start | bytes 6148
  1.1 1.9 %copy-start.20 = (s32[1,512]{1,0:T(1,128)S(1)}, s32[1,512]{1,0:T(1,128)}, u32[]{:S(2)}) copy-start(s32[1,512]{1,0:T(1,128)} %param.10) | copy-start | bytes 6148
  1.1 2.3 %copy-start.19 = (s32[1,32,16]{1,2,0:T(8,128)S(1)}, s32[1,32,16]{1,2,0:T(8,128)}, u32[]{:S(2)}) copy-start(s32[1,32,16]{1,2,0:T(8,128)} %param.8) | copy-start | bytes 6148
  2.1 3.2 %slice-start = ((f32[128,9,128]{2,0,1:T(8,128)}), f32[128,6,128]{2,0,1:T(8,128)S(1)}, s32[]{:S(2)}) async-start(f32[128,9,128]{2,0,1:T(8,128)} %param.7), calls=%async_computation | async-start | bytes 786432 | tf_op jit(solution)/shard_map/slice | solution.py:265
  5.3 0.9 slice-start.1
  6.4 52.6 %copy-start = (f32[146,8,128]{2,1,0:T(8,128)}, f32[146,8,128]{2,1,0:T(8,128)S(1)}, u32[]{:S(2)}) copy-start(f32[146,8,128]{2,1,0:T(8,128)S(1)} %pad_maximum_fusion.refs_0_) | copy-start | bytes 1794052
  6.4 30.5 %collective-permute-start = (f32[146,8,128]{2,1,0:T(8,128)S(1)}, f32[146,8,128]{2,1,0:T(8,128)S(1)}, u32[]{:S(2)}, u32[]{:S(2)}) collective-permute-start(f32[146,8,128]{2,1,0:T(8,128)S(1)} %pad_maximum_fusion.refs_0_), channel_id=1, source_target_pairs={{0,16},{1,17},{2,18},{3,19},{4,20},{5,21},{6,22},{7,23},{8,24},{9,... | collective-permute-start | bytes 1794056 | tf_op jit(solution)/shard_map/ppermute | solution.py:307
  10.5 26.4 %collective-permute-start.1 = (f32[146,8,128]{2,1,0:T(8,128)S(1)}, f32[146,8,128]{2,1,0:T(8,128)S(1)}, u32[]{:S(2)}, u32[]{:S(2)}) collective-permute-start(f32[146,8,128]{2,1,0:T(8,128)S(1)} %pad_maximum_fusion.refs_0_), channel_id=1, source_target_pairs={{0,2},{1,3},{2,0},{3,1},{4,6},{5,7},{6,4},{7,5},{8,10},{9,11},{10,... | collective-permute-start | bytes 1794056 | tf_op jit(solution)/shard_map/ppermute | solution.py:307
  12.1 24.9 %collective-permute-start.2 = (f32[146,8,128]{2,1,0:T(8,128)S(1)}, f32[146,8,128]{2,1,0:T(8,128)S(1)}, u32[]{:S(2)}, u32[]{:S(2)}) collective-permute-start(f32[146,8,128]{2,1,0:T(8,128)S(1)} %pad_maximum_fusion.refs_0_), channel_id=1, source_target_pairs={{0,1},{1,0},{2,3},{3,2},{4,5},{5,4},{6,7},{7,6},{8,9},{9,8},{10,11... | collective-permute-start | bytes 1794056 | tf_op jit(solution)/shard_map/ppermute | solution.py:307
  12.1 27.6 %collective-permute-start.3 = (f32[146,8,128]{2,1,0:T(8,128)S(1)}, f32[146,8,128]{2,1,0:T(8,128)S(1)}, u32[]{:S(2)}, u32[]{:S(2)}) collective-permute-start(f32[146,8,128]{2,1,0:T(8,128)S(1)} %pad_maximum_fusion.refs_0_), channel_id=1, source_target_pairs={{0,8},{1,9},{2,10},{3,11},{4,12},{5,13},{6,14},{7,15},{8,0},{9,1},... | collective-permute-start | bytes 1794056 | tf_op jit(solution)/shard_map/ppermute | solution.py:307
  13.6 26.0 %collective-permute-start.4 = (f32[146,8,128]{2,1,0:T(8,128)S(1)}, f32[146,8,128]{2,1,0:T(8,128)S(1)}, u32[]{:S(2)}, u32[]{:S(2)}) collective-permute-start(f32[146,8,128]{2,1,0:T(8,128)S(1)} %pad_maximum_fusion.refs_0_), channel_id=1, source_target_pairs={{0,4},{1,5},{2,6},{3,7},{4,0},{5,1},{6,2},{7,3},{8,12},{9,13},{10,... | collective-permute-start | bytes 1794056 | tf_op jit(solution)/shard_map/ppermute | solution.py:307
  37.0 22.1 %copy-start.3 = (f32[146,8,128]{2,1,0:T(8,128)}, f32[146,8,128]{2,1,0:T(8,128)S(1)}, u32[]{:S(2)}) copy-start(f32[146,8,128]{2,1,0:T(8,128)S(1)} %collective-permute-done.refs_1_) | copy-start | bytes 1794052
  37.0 22.1 %copy-start.4 = (f32[146,8,128]{2,1,0:T(8,128)}, f32[146,8,128]{2,1,0:T(8,128)S(1)}, u32[]{:S(2)}) copy-start(f32[146,8,128]{2,1,0:T(8,128)S(1)} %collective-permute-done.1.refs_2_) | copy-start | bytes 1794052
  37.0 22.1 %copy-start.5 = (f32[146,8,128]{2,1,0:T(8,128)}, f32[146,8,128]{2,1,0:T(8,128)S(1)}, u32[]{:S(2)}) copy-start(f32[146,8,128]{2,1,0:T(8,128)S(1)} %collective-permute-done.2.refs_4_) | copy-start | bytes 1794052
  39.6 16.5 %copy-start.10 = (f32[146,8,128]{2,1,0:T(8,128)}, f32[146,8,128]{2,1,0:T(8,128)S(1)}, u32[]{:S(2)}) copy-start(f32[146,8,128]{2,1,0:T(8,128)S(1)} %collective-permute-done.3.refs_8_) | copy-start | bytes 1794052
  39.6 16.6 %copy-start.11 = (f32[146,8,128]{2,1,0:T(8,128)}, f32[146,8,128]{2,1,0:T(8,128)S(1)}, u32[]{:S(2)}) copy-start(f32[146,8,128]{2,1,0:T(8,128)S(1)} %collective-permute-done.4.refs_9_) | copy-start | bytes 1794052
  39.6 15.2 %collective-permute-start.5 = (f32[146,8,128]{2,1,0:T(8,128)S(1)}, f32[146,8,128]{2,1,0:T(8,128)S(1)}, u32[]{:S(2)}, u32[]{:S(2)}) collective-permute-start(f32[146,8,128]{2,1,0:T(8,128)S(1)} %collective-permute-done.refs_1_), channel_id=1, source_target_pairs={{0,2},{1,3},{2,0},{3,1},{4,6},{5,7},{6,4},{7,5},{8,10},{9,11},{10,... | collective-permute-start | bytes 1794056 | tf_op jit(solution)/shard_map/ppermute | solution.py:307
  40.3 14.6 %collective-permute-start.6 = (f32[146,8,128]{2,1,0:T(8,128)S(1)}, f32[146,8,128]{2,1,0:T(8,128)S(1)}, u32[]{:S(2)}, u32[]{:S(2)}) collective-permute-start(f32[146,8,128]{2,1,0:T(8,128)S(1)} %collective-permute-done.refs_1_), channel_id=1, source_target_pairs={{0,1},{1,0},{2,3},{3,2},{4,5},{5,4},{6,7},{7,6},{8,9},{9,8},{10,11... | collective-permute-start | bytes 1794056 | tf_op jit(solution)/shard_map/ppermute | solution.py:307
  40.3 14.6 %collective-permute-start.7 = (f32[146,8,128]{2,1,0:T(8,128)S(1)}, f32[146,8,128]{2,1,0:T(8,128)S(1)}, u32[]{:S(2)}, u32[]{:S(2)}) collective-permute-start(f32[146,8,128]{2,1,0:T(8,128)S(1)} %collective-permute-done.1.refs_2_), channel_id=1, source_target_pairs={{0,1},{1,0},{2,3},{3,2},{4,5},{5,4},{6,7},{7,6},{8,9},{9,8},{10,11... | collective-permute-start | bytes 1794056 | tf_op jit(solution)/shard_map/ppermute | solution.py:307
  40.8 15.4 %collective-permute-start.8 = (f32[146,8,128]{2,1,0:T(8,128)S(1)}, f32[146,8,128]{2,1,0:T(8,128)S(1)}, u32[]{:S(2)}, u32[]{:S(2)}) collective-permute-start(f32[146,8,128]{2,1,0:T(8,128)S(1)} %collective-permute-done.3.refs_8_), channel_id=1, source_target_pairs={{0,4},{1,5},{2,6},{3,7},{4,0},{5,1},{6,2},{7,3},{8,12},{9,13},{10,... | collective-permute-start | bytes 1794056 | tf_op jit(solution)/shard_map/ppermute | solution.py:307
  54.8 4.3 %copy-start.6 = (f32[146,8,128]{2,1,0:T(8,128)}, f32[146,8,128]{2,1,0:T(8,128)S(1)}, u32[]{:S(2)}) copy-start(f32[146,8,128]{2,1,0:T(8,128)S(1)} %collective-permute-done.5.refs_3_) | copy-start | bytes 1794052
  54.8 3.4 %copy-start.7 = (f32[146,8,128]{2,1,0:T(8,128)}, f32[146,8,128]{2,1,0:T(8,128)S(1)}, u32[]{:S(2)}) copy-start(f32[146,8,128]{2,1,0:T(8,128)S(1)} %collective-permute-done.6.refs_5_) | copy-start | bytes 1794052
  54.9 3.4 %copy-start.8 = (f32[146,8,128]{2,1,0:T(8,128)}, f32[146,8,128]{2,1,0:T(8,128)S(1)}, u32[]{:S(2)}) copy-start(f32[146,8,128]{2,1,0:T(8,128)S(1)} %collective-permute-done.7.refs_6_) | copy-start | bytes 1794052
  56.2 0.8 copy-start.12
  56.2 2.0 %collective-permute-start.9 = (f32[146,8,128]{2,1,0:T(8,128)S(1)}, f32[146,8,128]{2,1,0:T(8,128)S(1)}, u32[]{:S(2)}, u32[]{:S(2)}) collective-permute-start(f32[146,8,128]{2,1,0:T(8,128)S(1)} %collective-permute-done.5.refs_3_), channel_id=1, source_target_pairs={{0,1},{1,0},{2,3},{3,2},{4,5},{5,4},{6,7},{7,6},{8,9},{9,8},{10,11... | collective-permute-start | bytes 1794056 | tf_op jit(solution)/shard_map/ppermute | solution.py:307
  58.2 0.8 copy-start.9
  82.2 6.3 %collective-permute-start.20 = (f32[1,8,128]{2,1,0:T(8,128)S(1)}, f32[1,8,128]{2,1,0:T(8,128)S(1)}, u32[]{:S(2)}, u32[]{:S(2)}) collective-permute-start(f32[1,8,128]{2,1,0:T(8,128)S(1)} %slice_add_fusion), channel_id=1, source_target_pairs={{0,8},{1,9},{2,10},{3,11},{4,12},{5,13},{6,14},{7,15},{8,0},{9,1},... | collective-permute-start | bytes 12296 | tf_op jit(solution)/shard_map/ppermute | solution.py:307
  88.5 3.6 %collective-permute-start.21 = (f32[1,8,128]{2,1,0:T(8,128)S(1)}, f32[1,8,128]{2,1,0:T(8,128)S(1)}, u32[]{:S(2)}, u32[]{:S(2)}) collective-permute-start(f32[1,8,128]{2,1,0:T(8,128)S(1)} %add.142), channel_id=1, source_target_pairs={{0,4},{1,5},{2,6},{3,7},{4,0},{5,1},{6,2},{7,3},{8,12},{9,13},{10,... | collective-permute-start | bytes 12296 | tf_op jit(solution)/shard_map/ppermute | solution.py:307
  90.4 6.5 %collective-permute-start.11 = (f32[3,128,128]{2,1,0:T(8,128)}, f32[3,128,128]{2,1,0:T(8,128)S(1)}, u32[]{:S(2)}, u32[]{:S(2)}) collective-permute-start(f32[3,128,128]{2,1,0:T(8,128)} %get-tuple-element.63), channel_id=1, source_target_pairs={{0,1},{1,0},{2,3},{3,2},{4,5},{5,4},{6,7},{7,6},{8,9},{9,8},{10,11... | collective-permute-start | bytes 589832 | tf_op jit(solution)/shard_map/ppermute | solution.py:307
  90.4 2.9 %collective-permute-start.14 = (f32[3,128,128]{2,1,0:T(8,128)}, f32[3,128,128]{2,1,0:T(8,128)S(1)}, u32[]{:S(2)}, u32[]{:S(2)}) collective-permute-start(f32[3,128,128]{2,1,0:T(8,128)} %get-tuple-element.67), channel_id=1, source_target_pairs={{0,1},{1,0},{2,3},{3,2},{4,5},{5,4},{6,7},{7,6},{8,9},{9,8},{10,11... | collective-permute-start | bytes 589832 | tf_op jit(solution)/shard_map/ppermute | solution.py:307
  90.9 10.4 %collective-permute-start.13 = (f32[3,128,128]{2,1,0:T(8,128)}, f32[3,128,128]{2,1,0:T(8,128)S(1)}, u32[]{:S(2)}, u32[]{:S(2)}) collective-permute-start(f32[3,128,128]{2,1,0:T(8,128)} %get-tuple-element.65), channel_id=1, source_target_pairs={{0,1},{1,0},{2,3},{3,2},{4,5},{5,4},{6,7},{7,6},{8,9},{9,8},{10,11... | collective-permute-start | bytes 589832 | tf_op jit(solution)/shard_map/ppermute | solution.py:307
  90.9 8.6 %collective-permute-start.18 = (f32[3,128,128]{2,1,0:T(8,128)}, f32[3,128,128]{2,1,0:T(8,128)S(1)}, u32[]{:S(2)}, u32[]{:S(2)}) collective-permute-start(f32[3,128,128]{2,1,0:T(8,128)} %get-tuple-element.71), channel_id=1, source_target_pairs={{0,4},{1,5},{2,6},{3,7},{4,0},{5,1},{6,2},{7,3},{8,12},{9,13},{10,... | collective-permute-start | bytes 589832 | tf_op jit(solution)/shard_map/ppermute | solution.py:307
  92.1 13.5 %collective-permute-start.10 = (f32[3,128,128]{2,1,0:T(8,128)}, f32[3,128,128]{2,1,0:T(8,128)S(1)}, u32[]{:S(2)}, u32[]{:S(2)}) collective-permute-start(f32[3,128,128]{2,1,0:T(8,128)} %get-tuple-element.61), channel_id=1, source_target_pairs={{0,1},{1,0},{2,3},{3,2},{4,5},{5,4},{6,7},{7,6},{8,9},{9,8},{10,11... | collective-permute-start | bytes 589832 | tf_op jit(solution)/shard_map/ppermute | solution.py:307
  92.9 0.9 copy-start.18
  93.9 7.9 %collective-permute-start.15 = (f32[3,128,128]{2,1,0:T(8,128)S(1)}, f32[3,128,128]{2,1,0:T(8,128)S(1)}, u32[]{:S(2)}, u32[]{:S(2)}) collective-permute-start(f32[3,128,128]{2,1,0:T(8,128)S(1)} %add.134), channel_id=1, source_target_pairs={{0,2},{1,3},{2,0},{3,1},{4,6},{5,7},{6,4},{7,5},{8,10},{9,11},{10,... | collective-permute-start | bytes 589832 | tf_op jit(solution)/shard_map/ppermute | solution.py:307
  96.6 1.0 copy-start.24
  96.7 2.9 %copy-start.17 = (f32[3,128,128]{2,1,0:T(8,128)S(1)}, f32[3,128,128]{2,1,0:T(8,128)}, u32[]{:S(2)}) copy-start(f32[3,128,128]{2,1,0:T(8,128)} %get-tuple-element.62) | copy-start | bytes 589828
  96.9 4.4 %copy-start.16 = (f32[3,128,128]{2,1,0:T(8,128)S(1)}, f32[3,128,128]{2,1,0:T(8,128)}, u32[]{:S(2)}) copy-start(f32[3,128,128]{2,1,0:T(8,128)} %get-tuple-element.70) | copy-start | bytes 589828
  97.6 8.1 %collective-permute-start.17 = (f32[3,128,128]{2,1,0:T(8,128)S(1)}, f32[3,128,128]{2,1,0:T(8,128)S(1)}, u32[]{:S(2)}, u32[]{:S(2)}) collective-permute-start(f32[3,128,128]{2,1,0:T(8,128)S(1)} %copy-done.24), channel_id=1, source_target_pairs={{0,4},{1,5},{2,6},{3,7},{4,0},{5,1},{6,2},{7,3},{8,12},{9,13},{10,... | collective-permute-start | bytes 589832 | tf_op jit(solution)/shard_map/ppermute | solution.py:307
  99.5 2.3 %copy-start.15 = (f32[3,128,128]{2,1,0:T(8,128)S(1)}, f32[3,128,128]{2,1,0:T(8,128)}, u32[]{:S(2)}) copy-start(f32[3,128,128]{2,1,0:T(8,128)} %get-tuple-element.64) | copy-start | bytes 589828
  99.5 6.1 %copy-start.2 = (f32[128,9,128]{2,0,1:T(8,128)S(1)}, f32[128,9,128]{2,0,1:T(8,128)}, u32[]{:S(2)}) copy-start(f32[128,9,128]{2,0,1:T(8,128)} %param.7) | copy-start | bytes 1769476
  99.6 6.7 %collective-permute-start.12 = (f32[3,128,128]{2,1,0:T(8,128)S(1)}, f32[3,128,128]{2,1,0:T(8,128)S(1)}, u32[]{:S(2)}, u32[]{:S(2)}) collective-permute-start(f32[3,128,128]{2,1,0:T(8,128)S(1)} %add.131), channel_id=1, source_target_pairs={{0,2},{1,3},{2,0},{3,1},{4,6},{5,7},{6,4},{7,5},{8,10},{9,11},{10,... | collective-permute-start | bytes 589832 | tf_op jit(solution)/shard_map/ppermute | solution.py:307
  101.4 8.2 %collective-permute-start.19 = (f32[3,128,128]{2,1,0:T(8,128)S(1)}, f32[3,128,128]{2,1,0:T(8,128)S(1)}, u32[]{:S(2)}, u32[]{:S(2)}) collective-permute-start(f32[3,128,128]{2,1,0:T(8,128)S(1)} %add.138), channel_id=1, source_target_pairs={{0,8},{1,9},{2,10},{3,11},{4,12},{5,13},{6,14},{7,15},{8,0},{9,1},... | collective-permute-start | bytes 589832 | tf_op jit(solution)/shard_map/ppermute | solution.py:307
  101.9 12.4 %copy-start.13 = (f32[3,128,128]{2,1,0:T(8,128)S(1)}, f32[3,128,128]{2,1,0:T(8,128)}, u32[]{:S(2)}) copy-start(f32[3,128,128]{2,1,0:T(8,128)} %get-tuple-element.60) | copy-start | bytes 589828
  101.9 12.4 %copy-start.14 = (f32[3,128,128]{2,1,0:T(8,128)S(1)}, f32[3,128,128]{2,1,0:T(8,128)}, u32[]{:S(2)}) copy-start(f32[3,128,128]{2,1,0:T(8,128)} %get-tuple-element.68) | copy-start | bytes 589828
  101.9 12.4 %collective-permute-start.16 = (f32[3,128,128]{2,1,0:T(8,128)S(1)}, f32[3,128,128]{2,1,0:T(8,128)S(1)}, u32[]{:S(2)}, u32[]{:S(2)}) collective-permute-start(f32[3,128,128]{2,1,0:T(8,128)S(1)} %add_add_fusion), channel_id=1, source_target_pairs={{0,16},{1,17},{2,18},{3,19},{4,20},{5,21},{6,22},{7,23},{8,24},{9,... | collective-permute-start | bytes 589832 | tf_op jit(solution)/shard_map/ppermute | solution.py:307
  (1 other events, 0.7 us)

commit v3 on v2

--- a/solution.py
+++ b/solution.py
@@ -7,7 +7,7 @@
 from jax.experimental.pallas import tpu as pltpu
 
 CORE = 0.25
-GROUP = 4
+GROUP = 8
 
 
 def head(value):
@@ -44,8 +44,8 @@
         other = jnp.broadcast_to(tile[at : at + 1], tile.shape)
         square = square + other * other
     main, last = thirds(tile), thirds(row)
-    positions = [jnp.where(sub >= 6, m, jnp.where(sub == 5, r, 0.0)) for m, r in zip(main, last)]
-    sums = tall([jnp.where(sub == 4, 1.0, positions[0]), positions[1], positions[2], jnp.zeros_like(tile)])
+    positions = [jnp.where(sub >= 6, m, jnp.where(sub == 5, r, 0.0)) for m, r in zip(main[:2], last[:2])]
+    sums = tall([jnp.where(sub == 4, 1.0, positions[0]), positions[1]])
     spot = jnp.where(sub >= 6, tile, jnp.where(sub == 5, row, 0.0))
     return main, last, square, sums, spot
 
@@ -124,9 +124,9 @@
 def pair_kernel(plan, refs_in, refs_out, scratch):
     tiles, slots, near_number, far_number, list_group = plan
     (blocks, lists, near_sum, far_sum, ids_vmem, ids, left_ref, wide_ref, cross_ref, part_ref, sums_ref, spots_ref,
-     sems, list_sems, out_sems) = scratch
+     sems, list_sems) = scratch
     list_copies = [
-        pltpu.make_async_copy(source.at[list_group], lists.at[k], list_sems.at[k]) for k, source in enumerate(refs_in)
+        pltpu.make_async_copy(source.at[pl.ds(list_group, 2)], lists.at[k], list_sems.at[k]) for k, source in enumerate(refs_in)
     ]
     copies = [pltpu.make_async_copy(source, blocks.at[k], sems.at[k]) for k, source in enumerate(refs_in)]
     for copy in list_copies + copies:
@@ -142,12 +142,12 @@
     position = lax.broadcasted_iota(jnp.int32, shape, 0) * width + lax.broadcasted_iota(jnp.int32, shape, 1)
     near_ids = jnp.full(shape, -1.0)
     for k in range(near_number):
-        given = lists[k, 0:4]
+        given = lists[k, 0, 0:4]
         given = jnp.where(given >= 0, given + k * tiles, given)
         near_ids = jnp.where(position // (far_number * slots) == k, given, near_ids)
     far_ids = jnp.zeros(shape)
     for k in range(far_number):
-        given = lists[near_number - 1 + k if k else 0, 4:8] + k * tiles
+        given = lists[near_number - 1 + k if k else 0, 0, 4:8] + k * tiles
         far_ids = jnp.where(position // slots % far_number == k, given, far_ids)
     live_list(near_ids, far_ids, ids_vmem)
     move = pltpu.make_async_copy(ids_vmem, ids, list_sems.at[0])
@@ -179,7 +179,7 @@
                 (near_block, near_tile, 0, matmul(jnp.concatenate([far_rows, far_rows], axis=1), parts, (1, 1)), near_sum),
                 (far_block, far_tile, 1, matmul(near_rows, parts), far_sum),
             ):
-                total = total[0:8] + total[8:16] + total[16:24]
+                total = total[0:8] + total[8:16]
                 if total.shape[1] > half:
                     total = total[:, :half] + total[:, half:]
                 force = spots_ref[stash, k, spot] * jnp.broadcast_to(total[4:5], total.shape) - total
@@ -214,34 +214,41 @@
 
     lax.fori_loop(0, (count + GROUP - 1) // GROUP + 2, step, 0)
 
-    for total, outs in ((near_sum, refs_out[:near_number]), (far_sum, refs_out[near_number:])):
-        for k, out in enumerate(outs):
+    moments = functools.reduce(jnp.add, [lists[k, 1] for k in range(near_number)])
+    at = 0
+    for out in refs_out:
+        for k in range(out.shape[0]):
+            total, block = (near_sum, at) if at < near_number else (far_sum, at - near_number)
             for axis, row in enumerate((6, 7, 5)):
-                out[axis] = total[k, :, row, :]
-
-
-def run_pairs(blocks, tiles, slots, near_number, far_number, list_group):
+                out[k, axis * tiles : (axis + 1) * tiles, :] = total[block, :, row, :]
+            if at >= near_number:
+                out[k, 3 * tiles :, :] = moments
+            at += 1
+
+
+def run_pairs(blocks, tiles, slots, near_counts, far_counts, list_group):
     width = blocks[0].shape[-1]
-    number = near_number + far_number
+    near_number, far_number = sum(near_counts), sum(far_counts)
     slot_count = near_number * far_number * slots
     hbm = pl.BlockSpec(memory_space=pl.ANY)
     vmem = pl.BlockSpec(memory_space=pltpu.VMEM)
-    forces = (3, tiles, width)
     plan = (tiles, slots, near_number, far_number, list_group)
-    depth, dot_depth, sum_rows = 64, 32, 32
+    shapes = [(count, 3 * tiles, width) for count in near_counts]
+    shapes += [(count, 3 * tiles + 8, width) for count in far_counts]
+    depth, dot_depth, sum_rows = 64, 32, 16
 
     def kernel(*refs):
         given = len(blocks)
-        pair_kernel(plan, refs[:given], refs[given : given + number], refs[given + number :])
+        pair_kernel(plan, refs[:given], refs[given : given + len(shapes)], refs[given + len(shapes) :])
 
     return pl.pallas_call(
         kernel,
-        out_shape=[jax.ShapeDtypeStruct(forces, jnp.float32)] * number,
+        out_shape=[jax.ShapeDtypeStruct(shape, jnp.float32) for shape in shapes],
         in_specs=[hbm] * len(blocks),
-        out_specs=[vmem] * number,
+        out_specs=[vmem] * len(shapes),
         scratch_shapes=[
             pltpu.VMEM((len(blocks),) + blocks[0].shape, jnp.float32),
-            pltpu.VMEM((len(blocks), 8, width), jnp.float32),
+            pltpu.VMEM((len(blocks), 2, 8, width), jnp.float32),
             pltpu.VMEM((near_number, tiles, 8, width), jnp.float32),
             pltpu.VMEM((far_number, tiles, 8, width), jnp.float32),
             pltpu.VMEM((8, slot_count), jnp.int32),
@@ -254,7 +261,6 @@
             pltpu.VMEM((3, GROUP, 2, 8, width), jnp.float32),
             pltpu.SemaphoreType.DMA((len(blocks),)),
             pltpu.SemaphoreType.DMA((len(blocks),)),
-            pltpu.SemaphoreType.DMA((number,)),
         ],
         compiler_params=pltpu.CompilerParams(vmem_limit_bytes=60 * 1024 * 1024),
         name="pairs",
@@ -340,16 +346,32 @@
     return [held[mask] for mask in span(near_steps)], [held[mask] for mask in span(far_steps)]
 
 
-def collect(near_parts, near_steps, far_parts, far_steps):
-    totals = []
-    for parts, steps in ((near_parts, near_steps), (far_parts, far_steps)):
-        parts = list(parts)
-        for step in reversed(steps):
-            half = len(parts) // 2
-            received = [swap(part, step) for part in reversed(parts[half:])]
-            parts = [part + got for part, got in zip(parts[:half], reversed(received))]
-        totals.append(parts[0])
-    return totals[0] + totals[1]
+def message_counts(steps):
+    counts = [1] * min(len(steps) and 2, 1 << len(steps))
+    while sum(counts) < 1 << len(steps):
+        counts.append(2 if sum(counts) >= 4 or len(steps) < 3 else 1)
+    return counts
+
+
+def collect(outs, counts, steps):
+    groups = list(zip(outs, counts))
+    for step in reversed(steps):
+        half = sum(count for value, count in groups) // 2
+        kept, sent, seen = [], [], 0
+        for value, count in groups:
+            (kept if seen < half else sent).append((value, count))
+            seen += count
+        arrived = []
+        for value, count in reversed(sent):
+            got = swap(value, step)
+            arrived = [got[k : k + 1] for k in range(count)] + arrived
+        merged, at = [], 0
+        for value, count in kept:
+            more = arrived[at : at + count]
+            merged.append((value + (jnp.concatenate(more) if count > 1 else more[0]), count))
+            at += count
+        groups = merged
+    return groups[0][0][0]
 
 
 def rows_of(values, width):
@@ -383,14 +405,12 @@
 
     near_blocks, far_blocks = spread(block, near_steps, far_steps)
     at_lists = main.shape[0]
-    at_moments = at_lists + list_rows.shape[0]
-    sums = functools.reduce(jnp.add, [given[at_moments:] for given in near_blocks])
-    outs = run_pairs(near_blocks + far_blocks[1:], tiles, slots, len(near_masks), len(far_masks), at_lists)
-    outs, sums = lax.optimization_barrier((outs, sums))
-    for step in far_steps:
-        sums = sums + swap(sums, step)
-    moment_sums = sums.reshape(-1)[: NCELL * 9].reshape(NCELL, 9)
-    forces = collect(outs[: len(near_masks)], near_steps, outs[len(near_masks) :], far_steps)
+    near_counts, far_counts = message_counts(near_steps), message_counts(far_steps)
+    outs = run_pairs(near_blocks + far_blocks[1:], tiles, slots, near_counts, far_counts, at_lists)
+    near_total = collect(outs[: len(near_counts)], near_counts, near_steps)
+    far_total = collect(outs[len(near_counts) :], far_counts, far_steps)
+    forces = (near_total + far_total[: 3 * tiles]).reshape(3, tiles, width)
+    moment_sums = far_total[3 * tiles :].reshape(-1)[: NCELL * 9].reshape(NCELL, 9)
     total_segments = tiles * width * devices
     return forces.transpose(1, 0, 2) + far_field(segments, tile_cell, moment_sums, total_segments)
 

time: 115 us -> 111 us (0.965); the launches traced: 115 us -> 113 us
  Pallas kernels: 23.1 us -> 20 us
  local copies, waits for them, and re-layouts: 7.89 us -> 5.89 us
  other arithmetic: 2.65 us -> 3.85 us
    pallas_call x1, Pallas kernels: 23.1 us -> 20 us  [run_pairs(): pl.pallas_call(kernel, out_shape=[jax.ShapeDtypeStruct(shape, jnp.float32...]
    unnamed x52 -> x44, local copies, waits for them, and re-layouts: 5.01 us -> 3.01 us
    add x6 -> x5, other arithmetic: 0.14 us -> 1.31 us  [the longest x4 1.24 us: collect(): value + (jnp.concatenate(more) if count > 1 else more[0])]
    ppermute x22 -> x17, waiting for transfers between devices: 51.2 us -> 52.1 us  [swap(): return lax.ppermute(value, AXES, [(k, k ^ mask) for k in range(devices)])]
    ppermute x22 -> x17, starting transfers between devices: 28.6 us -> 29.4 us  [swap(): return lax.ppermute(value, AXES, [(k, k ^ mask) for k in range(devices)])]
  transfers between devices with their start and end apart: 22 -> 17, of which waited for: 11 -> 8; matrix products, arithmetic and copies ran while one was open for 1% -> 3% of each run, Pallas kernels for 0% -> 0%
where the time goes in v3:
time: 111 us; the launch traced here: 113 us
  waiting for transfers between devices  52.1 us (47%)
  starting transfers between devices  29.4 us (26%)
  Pallas kernels  20 us (18%)
  local copies, waits for them, and re-layouts  5.89 us (5%)
  other arithmetic  3.85 us (3%)
    ppermute x17, waiting for transfers between devices, swap(): return lax.ppermute(value, AXES, [(k, k ^ mask) for k in range(devices)])  52.1 us
    ppermute x17, starting transfers between devices, swap(): return lax.ppermute(value, AXES, [(k, k ^ mask) for k in range(devices)])  29.4 us
    pallas_call x1, Pallas kernels, run_pairs(): pl.pallas_call(kernel, out_shape=[jax.ShapeDtypeStruct(shape, jnp.float32...  20 us
    unnamed x44, local copies, waits for them, and re-layouts  3.01 us
  transfers between devices with their start and end apart: 17, of which 8 were waited for; matrix products, arithmetic and copies ran while one was open for 3% of the time, Pallas kernels for 0%

profile of v3, /device:TPU:0, one launch (start us, length us, event | category | flops | bytes accessed | tf_op | source)
XLA Modules:
  0.0 112.8 jit_solution(10157913703417291751)
XLA Ops:
  0.0 1.0 fusion.14
  1.1 1.0 copy-done.1
  2.2 0.1 add.96
  3.0 0.3 select_reduce_fusion
  3.4 0.6 select_reduce_fusion.1
  4.0 0.1 concatenate.21
  4.1 0.3 multiply_reduce_fusion.1
  4.3 0.6 copy-done.20
  5.0 0.1 fusion.8
  5.1 0.1 reshape.128
  5.3 0.2 copy.32
  5.5 0.6 slice-done.1
  6.2 0.1 copy.33
  6.3 0.1 pad_maximum_fusion.refs_0_
  6.4 4.1 %collective-permute-start = (f32[146,8,128]{2,1,0:T(8,128)S(1)}, f32[146,8,128]{2,1,0:T(8,128)S(1)}, u32[]{:S(2)}, u32[]{:S(2)}) collective-permute-start(f32[146,8,128]{2,1,0:T(8,128)S(1)} %pad_maximum_fusion.refs_0_), channel_id=1, source_target_pairs={{0,16},{1,17},{2,18},{3,19},{4,20},{5,21},{6,22},{7,23},{8,24},{9,... | collective-permute-start | bytes 1794056 | tf_op jit(solution)/shard_map/ppermute | solution.py:313
  10.5 1.5 %collective-permute-start.1 = (f32[146,8,128]{2,1,0:T(8,128)S(1)}, f32[146,8,128]{2,1,0:T(8,128)S(1)}, u32[]{:S(2)}, u32[]{:S(2)}) collective-permute-start(f32[146,8,128]{2,1,0:T(8,128)S(1)} %pad_maximum_fusion.refs_0_), channel_id=1, source_target_pairs={{0,2},{1,3},{2,0},{3,1},{4,6},{5,7},{6,4},{7,5},{8,10},{9,11},{10,... | collective-permute-start | bytes 1794056 | tf_op jit(solution)/shard_map/ppermute | solution.py:313
  12.1 1.6 %collective-permute-start.3 = (f32[146,8,128]{2,1,0:T(8,128)S(1)}, f32[146,8,128]{2,1,0:T(8,128)S(1)}, u32[]{:S(2)}, u32[]{:S(2)}) collective-permute-start(f32[146,8,128]{2,1,0:T(8,128)S(1)} %pad_maximum_fusion.refs_0_), channel_id=1, source_target_pairs={{0,8},{1,9},{2,10},{3,11},{4,12},{5,13},{6,14},{7,15},{8,0},{9,1},... | collective-permute-start | bytes 1794056 | tf_op jit(solution)/shard_map/ppermute | solution.py:313
  13.6 1.5 %collective-permute-start.4 = (f32[146,8,128]{2,1,0:T(8,128)S(1)}, f32[146,8,128]{2,1,0:T(8,128)S(1)}, u32[]{:S(2)}, u32[]{:S(2)}) collective-permute-start(f32[146,8,128]{2,1,0:T(8,128)S(1)} %pad_maximum_fusion.refs_0_), channel_id=1, source_target_pairs={{0,4},{1,5},{2,6},{3,7},{4,0},{5,1},{6,2},{7,3},{8,12},{9,13},{10,... | collective-permute-start | bytes 1794056 | tf_op jit(solution)/shard_map/ppermute | solution.py:313
  15.1 21.8 %collective-permute-done.refs_1_ = f32[146,8,128]{2,1,0:T(8,128)S(1)} collective-permute-done((f32[146,8,128]{2,1,0:T(8,128)S(1)}, f32[146,8,128]{2,1,0:T(8,128)S(1)}, u32[]{:S(2)}, u32[]{:S(2)}) %collective-permute-start) | collective-permute-done | bytes 598048 | tf_op jit(solution)/shard_map/ppermute | solution.py:313
  37.0 2.6 %collective-permute-done.3.refs_8_ = f32[146,8,128]{2,1,0:T(8,128)S(1)} collective-permute-done((f32[146,8,128]{2,1,0:T(8,128)S(1)}, f32[146,8,128]{2,1,0:T(8,128)S(1)}, u32[]{:S(2)}, u32[]{:S(2)}) %collective-permute-start.3) | collective-permute-done | bytes 598048 | tf_op jit(solution)/shard_map/ppermute | solution.py:313
  39.6 0.6 collective-permute-start.5
  40.3 0.5 collective-permute-start.7
  40.8 1.5 %collective-permute-start.8 = (f32[146,8,128]{2,1,0:T(8,128)S(1)}, f32[146,8,128]{2,1,0:T(8,128)S(1)}, u32[]{:S(2)}, u32[]{:S(2)}) collective-permute-start(f32[146,8,128]{2,1,0:T(8,128)S(1)} %collective-permute-done.3.refs_8_), channel_id=1, source_target_pairs={{0,4},{1,5},{2,6},{3,7},{4,0},{5,1},{6,2},{7,3},{8,12},{9,13},{10,... | collective-permute-start | bytes 1794056 | tf_op jit(solution)/shard_map/ppermute | solution.py:313
  42.3 12.6 %collective-permute-done.5.refs_3_ = f32[146,8,128]{2,1,0:T(8,128)S(1)} collective-permute-done((f32[146,8,128]{2,1,0:T(8,128)S(1)}, f32[146,8,128]{2,1,0:T(8,128)S(1)}, u32[]{:S(2)}, u32[]{:S(2)}) %collective-permute-start.5) | collective-permute-done | bytes 598048 | tf_op jit(solution)/shard_map/ppermute | solution.py:313
  54.9 1.3 %collective-permute-done.8.refs_10_ = f32[146,8,128]{2,1,0:T(8,128)S(1)} collective-permute-done((f32[146,8,128]{2,1,0:T(8,128)S(1)}, f32[146,8,128]{2,1,0:T(8,128)S(1)}, u32[]{:S(2)}, u32[]{:S(2)}) %collective-permute-start.8) | collective-permute-done | bytes 598048 | tf_op jit(solution)/shard_map/ppermute | solution.py:313
  56.2 0.8 copy-done.11
  57.0 1.3 %collective-permute-done.9.refs_7_ = f32[146,8,128]{2,1,0:T(8,128)} collective-permute-done((f32[146,8,128]{2,1,0:T(8,128)S(1)}, f32[146,8,128]{2,1,0:T(8,128)}, u32[]{:S(2)}, u32[]{:S(2)}) %collective-permute-start.9) | collective-permute-done | bytes 598048 | tf_op jit(solution)/shard_map/ppermute | solution.py:313
  58.4 20.0 %pairs.1 = (f32[1,384,128]{2,1,0:T(8,128)}, f32[1,384,128]{2,1,0:T(8,128)}, f32[1,384,128]{2,1,0:T(8,128)}, f32[1,384,128]{2,1,0:T(8,128)}, f32[2,384,128]{2,1,0...) custom-call(f32[146,8,128]{2,1,0:T(8,128)} %copy-done, ...), custom_call_target="tpu_custom_call" | custom-call | tf_op jit(solution)/shard_map/pairs/pallas_call | solution.py:244
  78.4 1.7 %collective-permute-start.11 = (f32[2,384,128]{2,1,0:T(8,128)}, f32[2,384,128]{2,1,0:T(8,128)S(1)}, u32[]{:S(2)}, u32[]{:S(2)}) collective-permute-start(f32[2,384,128]{2,1,0:T(8,128)} %get-tuple-element.35), channel_id=1, source_target_pairs={{0,1},{1,0},{2,3},{3,2},{4,5},{5,4},{6,7},{7,6},{8,9},{9,8},{10,11... | collective-permute-start | bytes 1179656 | tf_op jit(solution)/shard_map/ppermute | solution.py:313
  80.1 3.0 %collective-permute-start.15 = (f32[2,392,128]{2,1,0:T(8,128)}, f32[2,392,128]{2,1,0:T(8,128)S(1)}, u32[]{:S(2)}, u32[]{:S(2)}) collective-permute-start(f32[2,392,128]{2,1,0:T(8,128)} %get-tuple-element.39), channel_id=1, source_target_pairs={{0,4},{1,5},{2,6},{3,7},{4,0},{5,1},{6,2},{7,3},{8,12},{9,13},{10,... | collective-permute-start | bytes 1204232 | tf_op jit(solution)/shard_map/ppermute | solution.py:313
  83.1 0.1 collective-permute-start.10
  83.2 1.1 slice_add_fusion.5
  84.3 3.0 %collective-permute-start.13 = (f32[1,384,128]{2,1,0:T(8,128)S(1)}, f32[1,384,128]{2,1,0:T(8,128)S(1)}, u32[]{:S(2)}, u32[]{:S(2)}) collective-permute-start(f32[1,384,128]{2,1,0:T(8,128)S(1)} %get-tuple-element.47), channel_id=1, source_target_pairs={{0,2},{1,3},{2,0},{3,1},{4,6},{5,7},{6,4},{7,5},{8,10},{9,11},{10,... | collective-permute-start | bytes 589832 | tf_op jit(solution)/shard_map/ppermute | solution.py:313
  87.3 0.1 collective-permute-start.12
  87.4 5.7 %collective-permute-done.15 = f32[2,392,128]{2,1,0:T(8,128)S(1)} collective-permute-done((f32[2,392,128]{2,1,0:T(8,128)}, f32[2,392,128]{2,1,0:T(8,128)S(1)}, u32[]{:S(2)}, u32[]{:S(2)}) %collective-permute-start.15) | collective-permute-done | bytes 401440 | tf_op jit(solution)/shard_map/ppermute | solution.py:313
  93.1 6.0 %collective-permute-start.16 = (f32[1,392,128]{2,1,0:T(8,128)S(1)}, f32[1,392,128]{2,1,0:T(8,128)S(1)}, u32[]{:S(2)}, u32[]{:S(2)}) collective-permute-start(f32[1,392,128]{2,1,0:T(8,128)S(1)} %slice_add_fusion), channel_id=1, source_target_pairs={{0,8},{1,9},{2,10},{3,11},{4,12},{5,13},{6,14},{7,15},{8,0},{9,1},... | collective-permute-start | bytes 602120 | tf_op jit(solution)/shard_map/ppermute | solution.py:313
  99.2 4.2 %collective-permute-start.14 = (f32[1,384,128]{2,1,0:T(8,128)S(1)}, f32[1,384,128]{2,1,0:T(8,128)S(1)}, u32[]{:S(2)}, u32[]{:S(2)}) collective-permute-start(f32[1,384,128]{2,1,0:T(8,128)S(1)} %fusion.1), channel_id=1, source_target_pairs={{0,16},{1,17},{2,18},{3,19},{4,20},{5,21},{6,22},{7,23},{8,24},{9,... | collective-permute-start | bytes 589832 | tf_op jit(solution)/shard_map/ppermute | solution.py:313
  103.4 3.8 %collective-permute-done.16 = f32[1,392,128]{2,1,0:T(8,128)S(1)} collective-permute-done((f32[1,392,128]{2,1,0:T(8,128)S(1)}, f32[1,392,128]{2,1,0:T(8,128)S(1)}, u32[]{:S(2)}, u32[]{:S(2)}) %collective-permute-start.16) | collective-permute-done | bytes 200736 | tf_op jit(solution)/shard_map/ppermute | solution.py:313
  107.3 0.2 div.14
  107.6 0.5 copy.29
  108.1 0.1 copy.30
  108.2 0.2 fusion.6
  108.5 0.2 fusion.5
  108.7 0.3 multiply_reduce_fusion
  109.0 0.1 copy-done.2
  109.2 2.9 %collective-permute-done.14 = f32[1,384,128]{2,1,0:T(8,128)S(1)} collective-permute-done((f32[1,384,128]{2,1,0:T(8,128)S(1)}, f32[1,384,128]{2,1,0:T(8,128)S(1)}, u32[]{:S(2)}, u32[]{:S(2)}) %collective-permute-start.14) | collective-permute-done | bytes 196640 | tf_op jit(solution)/shard_map/ppermute | solution.py:313
  112.0 0.1 slice_add_fusion.2
  112.1 0.7 maximum_add_fusion
  (73 shorter events, 0.5 us)
Async XLA Ops:
  1.1 1.1 copy-start.1
  1.1 1.1 copy-start.19
  1.1 1.2 %copy-start.18 = (s32[1,512]{1,0:T(1,128)S(1)}, s32[1,512]{1,0:T(1,128)}, u32[]{:S(2)}) copy-start(s32[1,512]{1,0:T(1,128)} %param.9) | copy-start | bytes 6148
  1.1 1.9 %copy-start.17 = (s32[1,512]{1,0:T(1,128)S(1)}, s32[1,512]{1,0:T(1,128)}, u32[]{:S(2)}) copy-start(s32[1,512]{1,0:T(1,128)} %param.10) | copy-start | bytes 6148
  1.1 2.3 %copy-start.16 = (s32[1,32,16]{1,2,0:T(8,128)S(1)}, s32[1,32,16]{1,2,0:T(8,128)}, u32[]{:S(2)}) copy-start(s32[1,32,16]{1,2,0:T(8,128)} %param.8) | copy-start | bytes 6148
  2.1 3.2 %slice-start = ((f32[128,9,128]{2,0,1:T(8,128)}), f32[128,6,128]{2,0,1:T(8,128)S(1)}, s32[]{:S(2)}) async-start(f32[128,9,128]{2,0,1:T(8,128)} %param.7), calls=%async_computation | async-start | bytes 786432 | tf_op jit(solution)/shard_map/slice | solution.py:271
  4.3 0.7 copy-start.20
  5.3 0.9 slice-start.1
  6.4 51.9 %copy-start = (f32[146,8,128]{2,1,0:T(8,128)}, f32[146,8,128]{2,1,0:T(8,128)S(1)}, u32[]{:S(2)}) copy-start(f32[146,8,128]{2,1,0:T(8,128)S(1)} %pad_maximum_fusion.refs_0_) | copy-start | bytes 1794052
  6.4 30.5 %collective-permute-start = (f32[146,8,128]{2,1,0:T(8,128)S(1)}, f32[146,8,128]{2,1,0:T(8,128)S(1)}, u32[]{:S(2)}, u32[]{:S(2)}) collective-permute-start(f32[146,8,128]{2,1,0:T(8,128)S(1)} %pad_maximum_fusion.refs_0_), channel_id=1, source_target_pairs={{0,16},{1,17},{2,18},{3,19},{4,20},{5,21},{6,22},{7,23},{8,24},{9,... | collective-permute-start | bytes 1794056 | tf_op jit(solution)/shard_map/ppermute | solution.py:313
  10.5 26.4 %collective-permute-start.1 = (f32[146,8,128]{2,1,0:T(8,128)S(1)}, f32[146,8,128]{2,1,0:T(8,128)S(1)}, u32[]{:S(2)}, u32[]{:S(2)}) collective-permute-start(f32[146,8,128]{2,1,0:T(8,128)S(1)} %pad_maximum_fusion.refs_0_), channel_id=1, source_target_pairs={{0,2},{1,3},{2,0},{3,1},{4,6},{5,7},{6,4},{7,5},{8,10},{9,11},{10,... | collective-permute-start | bytes 1794056 | tf_op jit(solution)/shard_map/ppermute | solution.py:313
  12.1 24.9 %collective-permute-start.2 = (f32[146,8,128]{2,1,0:T(8,128)S(1)}, f32[146,8,128]{2,1,0:T(8,128)S(1)}, u32[]{:S(2)}, u32[]{:S(2)}) collective-permute-start(f32[146,8,128]{2,1,0:T(8,128)S(1)} %pad_maximum_fusion.refs_0_), channel_id=1, source_target_pairs={{0,1},{1,0},{2,3},{3,2},{4,5},{5,4},{6,7},{7,6},{8,9},{9,8},{10,11... | collective-permute-start | bytes 1794056 | tf_op jit(solution)/shard_map/ppermute | solution.py:313
  12.1 27.6 %collective-permute-start.3 = (f32[146,8,128]{2,1,0:T(8,128)S(1)}, f32[146,8,128]{2,1,0:T(8,128)S(1)}, u32[]{:S(2)}, u32[]{:S(2)}) collective-permute-start(f32[146,8,128]{2,1,0:T(8,128)S(1)} %pad_maximum_fusion.refs_0_), channel_id=1, source_target_pairs={{0,8},{1,9},{2,10},{3,11},{4,12},{5,13},{6,14},{7,15},{8,0},{9,1},... | collective-permute-start | bytes 1794056 | tf_op jit(solution)/shard_map/ppermute | solution.py:313
  13.6 26.0 %collective-permute-start.4 = (f32[146,8,128]{2,1,0:T(8,128)S(1)}, f32[146,8,128]{2,1,0:T(8,128)S(1)}, u32[]{:S(2)}, u32[]{:S(2)}) collective-permute-start(f32[146,8,128]{2,1,0:T(8,128)S(1)} %pad_maximum_fusion.refs_0_), channel_id=1, source_target_pairs={{0,4},{1,5},{2,6},{3,7},{4,0},{5,1},{6,2},{7,3},{8,12},{9,13},{10,... | collective-permute-start | bytes 1794056 | tf_op jit(solution)/shard_map/ppermute | solution.py:313
  37.0 21.4 %copy-start.3 = (f32[146,8,128]{2,1,0:T(8,128)}, f32[146,8,128]{2,1,0:T(8,128)S(1)}, u32[]{:S(2)}) copy-start(f32[146,8,128]{2,1,0:T(8,128)S(1)} %collective-permute-done.refs_1_) | copy-start | bytes 1794052
  37.0 21.4 %copy-start.4 = (f32[146,8,128]{2,1,0:T(8,128)}, f32[146,8,128]{2,1,0:T(8,128)S(1)}, u32[]{:S(2)}) copy-start(f32[146,8,128]{2,1,0:T(8,128)S(1)} %collective-permute-done.1.refs_2_) | copy-start | bytes 1794052
  37.0 21.4 %copy-start.5 = (f32[146,8,128]{2,1,0:T(8,128)}, f32[146,8,128]{2,1,0:T(8,128)S(1)}, u32[]{:S(2)}) copy-start(f32[146,8,128]{2,1,0:T(8,128)S(1)} %collective-permute-done.2.refs_4_) | copy-start | bytes 1794052
  39.6 18.7 %copy-start.6 = (f32[146,8,128]{2,1,0:T(8,128)}, f32[146,8,128]{2,1,0:T(8,128)S(1)}, u32[]{:S(2)}) copy-start(f32[146,8,128]{2,1,0:T(8,128)S(1)} %collective-permute-done.3.refs_8_) | copy-start | bytes 1794052
  39.6 16.5 %copy-start.7 = (f32[146,8,128]{2,1,0:T(8,128)}, f32[146,8,128]{2,1,0:T(8,128)S(1)}, u32[]{:S(2)}) copy-start(f32[146,8,128]{2,1,0:T(8,128)S(1)} %collective-permute-done.4.refs_9_) | copy-start | bytes 1794052
  39.6 15.2 %collective-permute-start.5 = (f32[146,8,128]{2,1,0:T(8,128)S(1)}, f32[146,8,128]{2,1,0:T(8,128)S(1)}, u32[]{:S(2)}, u32[]{:S(2)}) collective-permute-start(f32[146,8,128]{2,1,0:T(8,128)S(1)} %collective-permute-done.refs_1_), channel_id=1, source_target_pairs={{0,2},{1,3},{2,0},{3,1},{4,6},{5,7},{6,4},{7,5},{8,10},{9,11},{10,... | collective-permute-start | bytes 1794056 | tf_op jit(solution)/shard_map/ppermute | solution.py:313
  40.3 14.6 %collective-permute-start.6 = (f32[146,8,128]{2,1,0:T(8,128)S(1)}, f32[146,8,128]{2,1,0:T(8,128)S(1)}, u32[]{:S(2)}, u32[]{:S(2)}) collective-permute-start(f32[146,8,128]{2,1,0:T(8,128)S(1)} %collective-permute-done.refs_1_), channel_id=1, source_target_pairs={{0,1},{1,0},{2,3},{3,2},{4,5},{5,4},{6,7},{7,6},{8,9},{9,8},{10,11... | collective-permute-start | bytes 1794056 | tf_op jit(solution)/shard_map/ppermute | solution.py:313
  40.3 14.6 %collective-permute-start.7 = (f32[146,8,128]{2,1,0:T(8,128)S(1)}, f32[146,8,128]{2,1,0:T(8,128)S(1)}, u32[]{:S(2)}, u32[]{:S(2)}) collective-permute-start(f32[146,8,128]{2,1,0:T(8,128)S(1)} %collective-permute-done.1.refs_2_), channel_id=1, source_target_pairs={{0,1},{1,0},{2,3},{3,2},{4,5},{5,4},{6,7},{7,6},{8,9},{9,8},{10,11... | collective-permute-start | bytes 1794056 | tf_op jit(solution)/shard_map/ppermute | solution.py:313
  40.8 15.4 %collective-permute-start.8 = (f32[146,8,128]{2,1,0:T(8,128)S(1)}, f32[146,8,128]{2,1,0:T(8,128)S(1)}, u32[]{:S(2)}, u32[]{:S(2)}) collective-permute-start(f32[146,8,128]{2,1,0:T(8,128)S(1)} %collective-permute-done.3.refs_8_), channel_id=1, source_target_pairs={{0,4},{1,5},{2,6},{3,7},{4,0},{5,1},{6,2},{7,3},{8,12},{9,13},{10,... | collective-permute-start | bytes 1794056 | tf_op jit(solution)/shard_map/ppermute | solution.py:313
  54.8 1.4 %copy-start.8 = (f32[146,8,128]{2,1,0:T(8,128)}, f32[146,8,128]{2,1,0:T(8,128)S(1)}, u32[]{:S(2)}) copy-start(f32[146,8,128]{2,1,0:T(8,128)S(1)} %collective-permute-done.5.refs_3_) | copy-start | bytes 1794052
  54.8 1.4 %copy-start.9 = (f32[146,8,128]{2,1,0:T(8,128)}, f32[146,8,128]{2,1,0:T(8,128)S(1)}, u32[]{:S(2)}) copy-start(f32[146,8,128]{2,1,0:T(8,128)S(1)} %collective-permute-done.6.refs_5_) | copy-start | bytes 1794052
  54.9 1.4 %copy-start.10 = (f32[146,8,128]{2,1,0:T(8,128)}, f32[146,8,128]{2,1,0:T(8,128)S(1)}, u32[]{:S(2)}) copy-start(f32[146,8,128]{2,1,0:T(8,128)S(1)} %collective-permute-done.7.refs_6_) | copy-start | bytes 1794052
  56.2 0.8 copy-start.11
  56.2 2.1 %collective-permute-start.9 = (f32[146,8,128]{2,1,0:T(8,128)S(1)}, f32[146,8,128]{2,1,0:T(8,128)}, u32[]{:S(2)}, u32[]{:S(2)}) collective-permute-start(f32[146,8,128]{2,1,0:T(8,128)S(1)} %collective-permute-done.5.refs_3_), channel_id=1, source_target_pairs={{0,1},{1,0},{2,3},{3,2},{4,5},{5,4},{6,7},{7,6},{8,9},{9,8},{10,11... | collective-permute-start | bytes 1794056 | tf_op jit(solution)/shard_map/ppermute | solution.py:313
  78.4 4.8 %collective-permute-start.11 = (f32[2,384,128]{2,1,0:T(8,128)}, f32[2,384,128]{2,1,0:T(8,128)S(1)}, u32[]{:S(2)}, u32[]{:S(2)}) collective-permute-start(f32[2,384,128]{2,1,0:T(8,128)} %get-tuple-element.35), channel_id=1, source_target_pairs={{0,1},{1,0},{2,3},{3,2},{4,5},{5,4},{6,7},{7,6},{8,9},{9,8},{10,11... | collective-permute-start | bytes 1179656 | tf_op jit(solution)/shard_map/ppermute | solution.py:313
  80.1 13.0 %collective-permute-start.15 = (f32[2,392,128]{2,1,0:T(8,128)}, f32[2,392,128]{2,1,0:T(8,128)S(1)}, u32[]{:S(2)}, u32[]{:S(2)}) collective-permute-start(f32[2,392,128]{2,1,0:T(8,128)} %get-tuple-element.39), channel_id=1, source_target_pairs={{0,4},{1,5},{2,6},{3,7},{4,0},{5,1},{6,2},{7,3},{8,12},{9,13},{10,... | collective-permute-start | bytes 1204232 | tf_op jit(solution)/shard_map/ppermute | solution.py:313
  83.1 16.0 %collective-permute-start.10 = (f32[2,384,128]{2,1,0:T(8,128)}, f32[2,384,128]{2,1,0:T(8,128)S(1)}, u32[]{:S(2)}, u32[]{:S(2)}) collective-permute-start(f32[2,384,128]{2,1,0:T(8,128)} %get-tuple-element.33), channel_id=1, source_target_pairs={{0,1},{1,0},{2,3},{3,2},{4,5},{5,4},{6,7},{7,6},{8,9},{9,8},{10,11... | collective-permute-start | bytes 1179656 | tf_op jit(solution)/shard_map/ppermute | solution.py:313
  83.2 9.9 %copy-start.13 = (f32[1,392,128]{2,1,0:T(8,128)S(1)}, f32[1,392,128]{2,1,0:T(8,128)}, u32[]{:S(2)}) copy-start(f32[1,392,128]{2,1,0:T(8,128)} %get-tuple-element.40) | copy-start | bytes 602116
  84.3 14.8 %collective-permute-start.13 = (f32[1,384,128]{2,1,0:T(8,128)S(1)}, f32[1,384,128]{2,1,0:T(8,128)S(1)}, u32[]{:S(2)}, u32[]{:S(2)}) collective-permute-start(f32[1,384,128]{2,1,0:T(8,128)S(1)} %get-tuple-element.47), channel_id=1, source_target_pairs={{0,2},{1,3},{2,0},{3,1},{4,6},{5,7},{6,4},{7,5},{8,10},{9,11},{10,... | collective-permute-start | bytes 589832 | tf_op jit(solution)/shard_map/ppermute | solution.py:313
  87.3 21.9 %collective-permute-start.12 = (f32[1,384,128]{2,1,0:T(8,128)S(1)}, f32[1,384,128]{2,1,0:T(8,128)S(1)}, u32[]{:S(2)}, u32[]{:S(2)}) collective-permute-start(f32[1,384,128]{2,1,0:T(8,128)S(1)} %get-tuple-element.46), channel_id=1, source_target_pairs={{0,2},{1,3},{2,0},{3,1},{4,6},{5,7},{6,4},{7,5},{8,10},{9,11},{10,... | collective-permute-start | bytes 589832 | tf_op jit(solution)/shard_map/ppermute | solution.py:313
  93.1 6.0 %copy-start.15 = (f32[1,384,128]{2,1,0:T(8,128)S(1)}, f32[1,384,128]{2,1,0:T(8,128)}, u32[]{:S(2)}) copy-start(f32[1,384,128]{2,1,0:T(8,128)} %get-tuple-element.36) | copy-start | bytes 589828
  93.1 14.1 %collective-permute-start.16 = (f32[1,392,128]{2,1,0:T(8,128)S(1)}, f32[1,392,128]{2,1,0:T(8,128)S(1)}, u32[]{:S(2)}, u32[]{:S(2)}) collective-permute-start(f32[1,392,128]{2,1,0:T(8,128)S(1)} %slice_add_fusion), channel_id=1, source_target_pairs={{0,8},{1,9},{2,10},{3,11},{4,12},{5,13},{6,14},{7,15},{8,0},{9,1},... | collective-permute-start | bytes 602120 | tf_op jit(solution)/shard_map/ppermute | solution.py:313
  99.1 8.1 %copy-start.12 = (f32[1,392,128]{2,1,0:T(8,128)S(1)}, f32[1,392,128]{2,1,0:T(8,128)}, u32[]{:S(2)}) copy-start(f32[1,392,128]{2,1,0:T(8,128)} %get-tuple-element.38) | copy-start | bytes 602116
  99.2 12.8 %collective-permute-start.14 = (f32[1,384,128]{2,1,0:T(8,128)S(1)}, f32[1,384,128]{2,1,0:T(8,128)S(1)}, u32[]{:S(2)}, u32[]{:S(2)}) collective-permute-start(f32[1,384,128]{2,1,0:T(8,128)S(1)} %fusion.1), channel_id=1, source_target_pairs={{0,16},{1,17},{2,18},{3,19},{4,20},{5,21},{6,22},{7,23},{8,24},{9,... | collective-permute-start | bytes 589832 | tf_op jit(solution)/shard_map/ppermute | solution.py:313
  108.1 1.1 copy-start.2
  109.1 2.9 %copy-start.14 = (f32[1,384,128]{2,1,0:T(8,128)S(1)}, f32[1,384,128]{2,1,0:T(8,128)}, u32[]{:S(2)}) copy-start(f32[1,384,128]{2,1,0:T(8,128)} %get-tuple-element.32) | copy-start | bytes 589828

commit v4 on v3

--- a/solution.py
+++ b/solution.py
@@ -111,7 +111,7 @@
     rank = jnp.where(alive, rank, -1.0)
     chosen = jnp.where(jnp.broadcast_to(rank, (slots, slots)) == row.astype(jnp.float32), 1.0, 0.0).astype(jnp.bfloat16)
     sub = lax.broadcasted_iota(jnp.int32, (8, slots), 0)
-    near, far = jnp.maximum(near, 0).astype(jnp.int32), far.astype(jnp.int32)
+    near, far = jnp.maximum(near, 0).astype(jnp.int32), jnp.maximum(far, 0).astype(jnp.int32)
     values = [near >> 6, near & 63, far >> 6, far & 63]
     values = place(sub, {k: value.astype(jnp.float32) for k, value in enumerate(values)}, jnp.zeros((8, slots), jnp.float32))
     packed = matmul(values.astype(jnp.bfloat16), chosen, (1, 1)).astype(jnp.int32)
@@ -121,14 +121,16 @@
     ids_ref[2:3, :] = jnp.broadcast_to(number, (1, slots))
 
 
-def pair_kernel(plan, refs_in, refs_out, scratch):
-    tiles, slots, near_number, far_number, list_group = plan
+def pair_kernel(plan, sources, earlier, refs_out, scratch):
+    tiles, slots, list_group, near_total, far_total, near, far, done, final = plan
+    near_number, far_number = len(near), len(far)
     (blocks, lists, near_sum, far_sum, ids_vmem, ids, left_ref, wide_ref, cross_ref, part_ref, sums_ref, spots_ref,
      sems, list_sems) = scratch
     list_copies = [
-        pltpu.make_async_copy(source.at[pl.ds(list_group, 2)], lists.at[k], list_sems.at[k]) for k, source in enumerate(refs_in)
+        pltpu.make_async_copy(source.at[pl.ds(list_group, 2)], lists.at[k], list_sems.at[k])
+        for k, source in enumerate(sources)
     ]
-    copies = [pltpu.make_async_copy(source, blocks.at[k], sems.at[k]) for k, source in enumerate(refs_in)]
+    copies = [pltpu.make_async_copy(source, blocks.at[k], sems.at[k]) for k, source in enumerate(sources)]
     for copy in list_copies + copies:
         copy.start()
     near_sum[...] = jnp.zeros_like(near_sum)
@@ -141,14 +143,21 @@
     shape = (4, width)
     position = lax.broadcasted_iota(jnp.int32, shape, 0) * width + lax.broadcasted_iota(jnp.int32, shape, 1)
     near_ids = jnp.full(shape, -1.0)
-    for k in range(near_number):
+    near_at = position // (far_total * slots)
+    far_at = position // slots % far_total
+    for k, block in enumerate(near):
         given = lists[k, 0, 0:4]
         given = jnp.where(given >= 0, given + k * tiles, given)
-        near_ids = jnp.where(position // (far_number * slots) == k, given, near_ids)
-    far_ids = jnp.zeros(shape)
-    for k in range(far_number):
+        near_ids = jnp.where(near_at == block, given, near_ids)
+    far_ids = jnp.full(shape, -1.0)
+    for k, block in enumerate(far):
         given = lists[near_number - 1 + k if k else 0, 0, 4:8] + k * tiles
-        far_ids = jnp.where(position // slots % far_number == k, given, far_ids)
+        far_ids = jnp.where(far_at == block, given, far_ids)
+    near_ids = jnp.where(far_ids >= 0, near_ids, -1.0)
+    if done:
+        old_near = functools.reduce(jnp.logical_or, [near_at == block for block in done[0]])
+        old_far = functools.reduce(jnp.logical_or, [far_at == block for block in done[1]])
+        near_ids = jnp.where(jnp.logical_and(old_near, old_far), -1.0, near_ids)
     live_list(near_ids, far_ids, ids_vmem)
     move = pltpu.make_async_copy(ids_vmem, ids, list_sems.at[0])
     move.start()
@@ -214,37 +223,55 @@
 
     lax.fori_loop(0, (count + GROUP - 1) // GROUP + 2, step, 0)
 
-    moments = functools.reduce(jnp.add, [lists[k, 1] for k in range(near_number)])
     at = 0
+    if final:
+        moments = functools.reduce(jnp.add, [lists[k, 1] for k in range(near_number)])
+        old = [list(blocks) for blocks in done]
     for out in refs_out:
         for k in range(out.shape[0]):
-            total, block = (near_sum, at) if at < near_number else (far_sum, at - near_number)
+            is_near = at < near_number
+            total, block = (near_sum, at) if is_near else (far_sum, at - near_number)
+            known = None
+            if final:
+                row = old[0 if is_near else 1]
+                if block in row:
+                    known = earlier[row.index(block) + (0 if is_near else len(old[0]))]
             for axis, row in enumerate((6, 7, 5)):
-                out[k, axis * tiles : (axis + 1) * tiles, :] = total[block, :, row, :]
-            if at >= near_number:
+                rows = slice(axis * tiles, (axis + 1) * tiles)
+                value = total[block, :, row, :]
+                out[k, rows, :] = value if known is None else value + known[0, rows, :]
+            if final and not is_near:
                 out[k, 3 * tiles :, :] = moments
             at += 1
 
 
-def run_pairs(blocks, tiles, slots, near_counts, far_counts, list_group):
+def run_pairs(blocks, tiles, slots, list_group, totals, near, far, counts=None, done=None, earlier=()):
     width = blocks[0].shape[-1]
-    near_number, far_number = sum(near_counts), sum(far_counts)
-    slot_count = near_number * far_number * slots
+    final = counts is not None
+    near_number, far_number = len(near), len(far)
+    slot_count = totals[0] * totals[1] * slots
     hbm = pl.BlockSpec(memory_space=pl.ANY)
     vmem = pl.BlockSpec(memory_space=pltpu.VMEM)
-    plan = (tiles, slots, near_number, far_number, list_group)
-    shapes = [(count, 3 * tiles, width) for count in near_counts]
-    shapes += [(count, 3 * tiles + 8, width) for count in far_counts]
+    plan = (tiles, slots, list_group) + tuple(totals) + (near, far, done, final)
+    if final:
+        shapes = [(count, 3 * tiles, width) for count in counts[0]]
+        shapes += [(count, 3 * tiles + 8, width) for count in counts[1]]
+    else:
+        shapes = [(1, 3 * tiles, width)] * (near_number + far_number)
     depth, dot_depth, sum_rows = 64, 32, 16
+    share = len(near) * len(far) / (totals[0] * totals[1])
+    elements = int(share * slot_count / 3) * width * width
 
     def kernel(*refs):
         given = len(blocks)
-        pair_kernel(plan, refs[:given], refs[given : given + len(shapes)], refs[given + len(shapes) :])
+        known = given + len(earlier)
+        made = known + len(shapes)
+        pair_kernel(plan, refs[:given], refs[given:known], refs[known:made], refs[made:])
 
     return pl.pallas_call(
         kernel,
         out_shape=[jax.ShapeDtypeStruct(shape, jnp.float32) for shape in shapes],
-        in_specs=[hbm] * len(blocks),
+        in_specs=[hbm] * len(blocks) + [vmem] * len(earlier),
         out_specs=[vmem] * len(shapes),
         scratch_shapes=[
             pltpu.VMEM((len(blocks),) + blocks[0].shape, jnp.float32),
@@ -263,8 +290,9 @@
             pltpu.SemaphoreType.DMA((len(blocks),)),
         ],
         compiler_params=pltpu.CompilerParams(vmem_limit_bytes=60 * 1024 * 1024),
-        name="pairs",
-    )(*blocks)
+        cost_estimate=pl.CostEstimate(flops=1000 * elements, bytes_accessed=1 << 22, transcendentals=elements),
+        name="pairs" if final else "early_pairs",
+    )(*blocks, *earlier)
 
 
 def tile_groups(tiles):
@@ -328,11 +356,12 @@
     return near_steps, far_steps
 
 
-def spread(block, near_steps, far_steps):
+def spread(block, near_steps, far_steps, work):
     steps = list(near_steps) + list(far_steps)
     allowed = set(span(near_steps)) | set(span(far_steps))
     held = {0: block}
     fresh = {0: -1}
+    sums = None
     while fresh:
         arrived = {}
         for mask, last in fresh.items():
@@ -340,10 +369,15 @@
                 if mask ^ steps[at] in allowed:
                     arrived[mask ^ steps[at]] = (swap(held[mask], steps[at]), at)
         if arrived:
-            values = lax.optimization_barrier([value for value, at in arrived.values()])
+            values = [value for value, at in arrived.values()]
+            if len(held) > 1 and sums is None:
+                sums = work([held[step] for step in near_steps], [held[step] for step in far_steps])
+                values, sums = lax.optimization_barrier((values, sums))
+            else:
+                values = lax.optimization_barrier(values)
             held.update(zip(arrived, values))
         fresh = {mask: at for mask, (value, at) in arrived.items()}
-    return [held[mask] for mask in span(near_steps)], [held[mask] for mask in span(far_steps)]
+    return [held[mask] for mask in span(near_steps)], [held[mask] for mask in span(far_steps)], sums
 
 
 def message_counts(steps):
@@ -403,10 +437,18 @@
     main = tile_groups(segments)
     block = jnp.concatenate([main, list_rows, moment_rows], axis=0)
 
-    near_blocks, far_blocks = spread(block, near_steps, far_steps)
-    at_lists = main.shape[0]
+    totals = (len(near_masks), len(far_masks))
+    early = [[0] + [masks.index(step) for step in steps] for masks, steps in ((near_masks, near_steps), (far_masks, far_steps))]
+
+    def early_pairs(near, far):
+        return run_pairs([block] + near + far, tiles, slots, main.shape[0], totals, early[0], early[1])
+
+    near_blocks, far_blocks, sums = spread(block, near_steps, far_steps, early_pairs)
     near_counts, far_counts = message_counts(near_steps), message_counts(far_steps)
-    outs = run_pairs(near_blocks + far_blocks[1:], tiles, slots, near_counts, far_counts, at_lists)
+    outs = run_pairs(
+        near_blocks + far_blocks[1:], tiles, slots, main.shape[0], totals, list(range(totals[0])), list(range(totals[1])),
+        (near_counts, far_counts), early, sums,
+    )
     near_total = collect(outs[: len(near_counts)], near_counts, near_steps)
     far_total = collect(outs[len(near_counts) :], far_counts, far_steps)
     forces = (near_total + far_total[: 3 * tiles]).reshape(3, tiles, width)

time: 111 us -> 109 us (0.982); the launches traced: 113 us -> 108 us
  Pallas kernels: 20 us -> 30 us
  waiting for transfers between devices: 52.1 us -> 43.9 us
  starting transfers between devices: 29.4 us -> 22.5 us
    pallas_call x1 -> x2, Pallas kernels: 20 us -> 30 us  [run_pairs(): pl.pallas_call(kernel, out_shape=[jax.ShapeDtypeStruct(shape, jnp.float32...]
    ppermute x17, waiting for transfers between devices: 52.1 us -> 43.9 us  [swap(): return lax.ppermute(value, AXES, [(k, k ^ mask) for k in range(devices)])]
    ppermute x17, starting transfers between devices: 29.4 us -> 22.5 us  [swap(): return lax.ppermute(value, AXES, [(k, k ^ mask) for k in range(devices)])]
    unnamed x44 -> x38, local copies, waits for them, and re-layouts: 3.01 us -> 3.29 us
  transfers between devices with their start and end apart: 17 -> 17, of which waited for: 8 -> 7; matrix products, arithmetic and copies ran while one was open for 3% -> 3% of each run, Pallas kernels for 0% -> 12%
where the time goes in v4:
time: 109 us; the launch traced here: 108 us
  waiting for transfers between devices  43.9 us (40%)
  Pallas kernels  30 us (28%)
  starting transfers between devices  22.5 us (21%)
  local copies, waits for them, and re-layouts  6.17 us (6%)
  other arithmetic  3.81 us (3%)
    ppermute x17, waiting for transfers between devices, swap(): return lax.ppermute(value, AXES, [(k, k ^ mask) for k in range(devices)])  43.9 us
    pallas_call x2, Pallas kernels, run_pairs(): pl.pallas_call(kernel, out_shape=[jax.ShapeDtypeStruct(shape, jnp.float32...  30 us
    ppermute x17, starting transfers between devices, swap(): return lax.ppermute(value, AXES, [(k, k ^ mask) for k in range(devices)])  22.5 us
    unnamed x38, local copies, waits for them, and re-layouts  3.29 us
  transfers between devices with their start and end apart: 17, of which 7 were waited for; matrix products, arithmetic and copies ran while one was open for 3% of the time, Pallas kernels for 12%

profile of v4, /device:TPU:0, one launch (start us, length us, event | category | flops | bytes accessed | tf_op | source)
XLA Modules:
  0.0 108.0 jit_solution(11074565454460197990)
XLA Ops:
  0.0 1.0 fusion.14
  1.1 1.0 copy-done
  2.1 0.1 iota_add_fusion
  2.2 0.1 add.96
  3.0 0.3 select_reduce_fusion
  3.3 0.1 iota_compare_fusion.4
  3.4 0.6 select_reduce_fusion.1
  4.0 0.1 concatenate.21
  4.1 0.3 multiply_reduce_fusion.1
  4.3 0.6 copy-done.11
  5.0 0.1 fusion.8
  5.1 0.1 reshape.128
  5.3 0.2 copy.32
  5.5 0.6 slice-done.1
  6.2 0.1 copy.33
  6.3 0.1 pad_maximum_fusion.refs_0_
  6.4 4.1 %collective-permute-start = (f32[146,8,128]{2,1,0:T(8,128)S(1)}, f32[146,8,128]{2,1,0:T(8,128)S(1)}, u32[]{:S(2)}, u32[]{:S(2)}) collective-permute-start(f32[146,8,128]{2,1,0:T(8,128)S(1)} %pad_maximum_fusion.refs_0_), channel_id=1, source_target_pairs={{0,16},{1,17},{2,18},{3,19},{4,20},{5,21},{6,22},{7,23},{8,24},{9,... | collective-permute-start | bytes 1794056 | tf_op jit(solution)/shard_map/ppermute | solution.py:341
  10.5 1.5 %collective-permute-start.1 = (f32[146,8,128]{2,1,0:T(8,128)S(1)}, f32[146,8,128]{2,1,0:T(8,128)S(1)}, u32[]{:S(2)}, u32[]{:S(2)}) collective-permute-start(f32[146,8,128]{2,1,0:T(8,128)S(1)} %pad_maximum_fusion.refs_0_), channel_id=1, source_target_pairs={{0,2},{1,3},{2,0},{3,1},{4,6},{5,7},{6,4},{7,5},{8,10},{9,11},{10,... | collective-permute-start | bytes 1794056 | tf_op jit(solution)/shard_map/ppermute | solution.py:341
  12.1 1.6 %collective-permute-start.3 = (f32[146,8,128]{2,1,0:T(8,128)S(1)}, f32[146,8,128]{2,1,0:T(8,128)S(1)}, u32[]{:S(2)}, u32[]{:S(2)}) collective-permute-start(f32[146,8,128]{2,1,0:T(8,128)S(1)} %pad_maximum_fusion.refs_0_), channel_id=1, source_target_pairs={{0,8},{1,9},{2,10},{3,11},{4,12},{5,13},{6,14},{7,15},{8,0},{9,1},... | collective-permute-start | bytes 1794056 | tf_op jit(solution)/shard_map/ppermute | solution.py:341
  13.6 1.5 %collective-permute-start.4 = (f32[146,8,128]{2,1,0:T(8,128)S(1)}, f32[146,8,128]{2,1,0:T(8,128)S(1)}, u32[]{:S(2)}, u32[]{:S(2)}) collective-permute-start(f32[146,8,128]{2,1,0:T(8,128)S(1)} %pad_maximum_fusion.refs_0_), channel_id=1, source_target_pairs={{0,4},{1,5},{2,6},{3,7},{4,0},{5,1},{6,2},{7,3},{8,12},{9,13},{10,... | collective-permute-start | bytes 1794056 | tf_op jit(solution)/shard_map/ppermute | solution.py:341
  15.1 21.8 %collective-permute-done.refs_1_ = f32[146,8,128]{2,1,0:T(8,128)S(1)} collective-permute-done((f32[146,8,128]{2,1,0:T(8,128)S(1)}, f32[146,8,128]{2,1,0:T(8,128)S(1)}, u32[]{:S(2)}, u32[]{:S(2)}) %collective-permute-start) | collective-permute-done | bytes 598048 | tf_op jit(solution)/shard_map/ppermute | solution.py:341
  37.0 2.6 %collective-permute-done.3.refs_4_.refs_8_ = f32[146,8,128]{2,1,0:T(8,128)S(1)} collective-permute-done((f32[146,8,128]{2,1,0:T(8,128)S(1)}, f32[146,8,128]{2,1,0:T(8,128)S(1)}, u32[]{:S(2)}, u32[]{:S(2)}) %collective-permute-start.3) | collective-permute-done | bytes 598048 | tf_op jit(solution)/shard_map/ppermute | solution.py:341
  39.6 0.6 collective-permute-start.5
  40.3 0.3 copy-done.16
  40.5 0.2 collective-permute-start.7
  40.8 1.5 %collective-permute-start.8 = (f32[146,8,128]{2,1,0:T(8,128)S(1)}, f32[146,8,128]{2,1,0:T(8,128)}, u32[]{:S(2)}, u32[]{:S(2)}) collective-permute-start(f32[146,8,128]{2,1,0:T(8,128)S(1)} %collective-permute-done.3.refs_4_.refs_8_), channel_id=1, source_target_pairs={{0,4},{1,5},{2,6},{3,7},{4,0},{5,1},{6,2},{7,3},{8,12},{9,13},{10,... | collective-permute-start | bytes 1794056 | tf_op jit(solution)/shard_map/ppermute | solution.py:341
  42.3 13.0 %early_pairs.1 = (f32[1,384,128]{2,1,0:T(8,128)}, f32[1,384,128]{2,1,0:T(8,128)}, f32[1,384,128]{2,1,0:T(8,128)}, f32[1,384,128]{2,1,0:T(8,128)}, f32[1,384,128]...) custom-call(f32[146,8,128]{2,1,0:T(8,128)} %copy-done.2, f32[146,8,128]{2,1,0:T(8,128)} %copy-done.12, ...), custom_call_target="tpu_custom_call" | custom-call | flops 1048576000 | bytes 4194304 | tf_op jit(solution)/shard_map/early_pairs/pallas_call | solution.py:271
  55.3 1.2 %collective-permute-done.8.refs_10_ = f32[146,8,128]{2,1,0:T(8,128)} collective-permute-done((f32[146,8,128]{2,1,0:T(8,128)S(1)}, f32[146,8,128]{2,1,0:T(8,128)}, u32[]{:S(2)}, u32[]{:S(2)}) %collective-permute-start.8) | collective-permute-done | bytes 598048 | tf_op jit(solution)/shard_map/ppermute | solution.py:341
  56.6 2.2 %collective-permute-done.9.refs_7_ = f32[146,8,128]{2,1,0:T(8,128)S(1)} collective-permute-done((f32[146,8,128]{2,1,0:T(8,128)}, f32[146,8,128]{2,1,0:T(8,128)S(1)}, u32[]{:S(2)}, u32[]{:S(2)}) %collective-permute-start.9) | collective-permute-done | bytes 598048 | tf_op jit(solution)/shard_map/ppermute | solution.py:341
  58.8 0.8 copy-done.17
  59.6 17.0 %pairs.1 = (f32[1,384,128]{2,1,0:T(8,128)}, f32[1,384,128]{2,1,0:T(8,128)}, f32[1,384,128]{2,1,0:T(8,128)}, f32[1,384,128]{2,1,0:T(8,128)}, f32[2,384,128]{2,1,0...) custom-call(f32[146,8,128]{2,1,0:T(8,128)} %copy-done.2, ...), custom_call_target="tpu_custom_call" | custom-call | flops 2785280000 | bytes 4194304 | tf_op jit(solution)/shard_map/pairs/pallas_call | solution.py:271
  76.6 2.4 %collective-permute-start.11 = (f32[2,384,128]{2,1,0:T(8,128)}, f32[2,384,128]{2,1,0:T(8,128)S(1)}, u32[]{:S(2)}, u32[]{:S(2)}) collective-permute-start(f32[2,384,128]{2,1,0:T(8,128)} %get-tuple-element.63), channel_id=1, source_target_pairs={{0,1},{1,0},{2,3},{3,2},{4,5},{5,4},{6,7},{7,6},{8,9},{9,8},{10,11... | collective-permute-start | bytes 1179656 | tf_op jit(solution)/shard_map/ppermute | solution.py:341
  79.1 4.5 %collective-permute-start.15 = (f32[2,392,128]{2,1,0:T(8,128)}, f32[2,392,128]{2,1,0:T(8,128)S(1)}, u32[]{:S(2)}, u32[]{:S(2)}) collective-permute-start(f32[2,392,128]{2,1,0:T(8,128)} %get-tuple-element.67), channel_id=1, source_target_pairs={{0,4},{1,5},{2,6},{3,7},{4,0},{5,1},{6,2},{7,3},{8,12},{9,13},{10,... | collective-permute-start | bytes 1204232 | tf_op jit(solution)/shard_map/ppermute | solution.py:341
  83.6 1.1 %slice_add_fusion.5 = (f32[1,384,128]{2,1,0:T(8,128)S(1)}, f32[1,384,128]{2,1,0:T(8,128)S(1)}) fusion(f32[1,384,128]{2,1,0:T(8,128)} %get-tuple-element.62, f32[2,384,128]{2,1,0:T(8,128)S(1)} %collective-permute-done.11, f32[1,384,128]{2,1,0:T(8,128)} %get-tuple-element.65), kind=kLoop, calls=%fused_computation.12 | loop fusion | flops 98304 | bytes 1179648 | tf_op jit(solution)/shard_map/add | solution.py:405
  84.7 2.1 %collective-permute-start.13 = (f32[1,384,128]{2,1,0:T(8,128)S(1)}, f32[1,384,128]{2,1,0:T(8,128)S(1)}, u32[]{:S(2)}, u32[]{:S(2)}) collective-permute-start(f32[1,384,128]{2,1,0:T(8,128)S(1)} %get-tuple-element.75), channel_id=1, source_target_pairs={{0,2},{1,3},{2,0},{3,1},{4,6},{5,7},{6,4},{7,5},{8,10},{9,11},{10,... | collective-permute-start | bytes 589832 | tf_op jit(solution)/shard_map/ppermute | solution.py:341
  86.8 0.1 collective-permute-start.12
  86.9 6.4 %collective-permute-done.15 = f32[2,392,128]{2,1,0:T(8,128)S(1)} collective-permute-done((f32[2,392,128]{2,1,0:T(8,128)}, f32[2,392,128]{2,1,0:T(8,128)S(1)}, u32[]{:S(2)}, u32[]{:S(2)}) %collective-permute-start.15) | collective-permute-done | bytes 401440 | tf_op jit(solution)/shard_map/ppermute | solution.py:341
  93.4 2.3 %collective-permute-start.16 = (f32[1,392,128]{2,1,0:T(8,128)S(1)}, f32[1,392,128]{2,1,0:T(8,128)S(1)}, u32[]{:S(2)}, u32[]{:S(2)}) collective-permute-start(f32[1,392,128]{2,1,0:T(8,128)S(1)} %slice_add_fusion), channel_id=1, source_target_pairs={{0,8},{1,9},{2,10},{3,11},{4,12},{5,13},{6,14},{7,15},{8,0},{9,1},... | collective-permute-start | bytes 602120 | tf_op jit(solution)/shard_map/ppermute | solution.py:341
  95.8 6.5 %collective-permute-done.16 = f32[1,392,128]{2,1,0:T(8,128)S(1)} collective-permute-done((f32[1,392,128]{2,1,0:T(8,128)S(1)}, f32[1,392,128]{2,1,0:T(8,128)S(1)}, u32[]{:S(2)}, u32[]{:S(2)}) %collective-permute-start.16) | collective-permute-done | bytes 200736 | tf_op jit(solution)/shard_map/ppermute | solution.py:341
  102.3 0.2 div.14
  102.6 0.5 copy.29
  103.1 0.1 copy.30
  103.2 0.2 fusion.6
  103.5 0.2 fusion.5
  103.7 0.3 multiply_reduce_fusion
  104.0 0.1 copy-done.1
  104.2 3.1 %collective-permute-done.14 = f32[1,384,128]{2,1,0:T(8,128)S(1)} collective-permute-done((f32[1,384,128]{2,1,0:T(8,128)S(1)}, f32[1,384,128]{2,1,0:T(8,128)S(1)}, u32[]{:S(2)}, u32[]{:S(2)}) %collective-permute-start.14) | collective-permute-done | bytes 196640 | tf_op jit(solution)/shard_map/ppermute | solution.py:341
  107.3 0.7 maximum_add_fusion
  (68 shorter events, 0.5 us)
Async XLA Ops:
  1.1 1.1 copy-start
  1.1 1.1 copy-start.10
  1.1 1.2 %copy-start.9 = (s32[1,512]{1,0:T(1,128)S(1)}, s32[1,512]{1,0:T(1,128)}, u32[]{:S(2)}) copy-start(s32[1,512]{1,0:T(1,128)} %param.9) | copy-start | bytes 6148
  1.1 1.9 %copy-start.8 = (s32[1,512]{1,0:T(1,128)S(1)}, s32[1,512]{1,0:T(1,128)}, u32[]{:S(2)}) copy-start(s32[1,512]{1,0:T(1,128)} %param.10) | copy-start | bytes 6148
  1.1 2.3 %copy-start.7 = (s32[1,32,16]{1,2,0:T(8,128)S(1)}, s32[1,32,16]{1,2,0:T(8,128)}, u32[]{:S(2)}) copy-start(s32[1,32,16]{1,2,0:T(8,128)} %param.8) | copy-start | bytes 6148
  2.1 3.2 %slice-start = ((f32[128,9,128]{2,0,1:T(8,128)}), f32[128,6,128]{2,0,1:T(8,128)S(1)}, s32[]{:S(2)}) async-start(f32[128,9,128]{2,0,1:T(8,128)} %param.7), calls=%async_computation | async-start | bytes 786432 | tf_op jit(solution)/shard_map/slice | solution.py:299
  4.3 0.7 copy-start.11
  5.3 0.9 slice-start.1
  6.4 35.8 %copy-start.2 = (f32[146,8,128]{2,1,0:T(8,128)}, f32[146,8,128]{2,1,0:T(8,128)S(1)}, u32[]{:S(2)}) copy-start(f32[146,8,128]{2,1,0:T(8,128)S(1)} %pad_maximum_fusion.refs_0_) | copy-start | bytes 1794052
  6.4 30.5 %collective-permute-start = (f32[146,8,128]{2,1,0:T(8,128)S(1)}, f32[146,8,128]{2,1,0:T(8,128)S(1)}, u32[]{:S(2)}, u32[]{:S(2)}) collective-permute-start(f32[146,8,128]{2,1,0:T(8,128)S(1)} %pad_maximum_fusion.refs_0_), channel_id=1, source_target_pairs={{0,16},{1,17},{2,18},{3,19},{4,20},{5,21},{6,22},{7,23},{8,24},{9,... | collective-permute-start | bytes 1794056 | tf_op jit(solution)/shard_map/ppermute | solution.py:341
  10.5 26.4 %collective-permute-start.1 = (f32[146,8,128]{2,1,0:T(8,128)S(1)}, f32[146,8,128]{2,1,0:T(8,128)S(1)}, u32[]{:S(2)}, u32[]{:S(2)}) collective-permute-start(f32[146,8,128]{2,1,0:T(8,128)S(1)} %pad_maximum_fusion.refs_0_), channel_id=1, source_target_pairs={{0,2},{1,3},{2,0},{3,1},{4,6},{5,7},{6,4},{7,5},{8,10},{9,11},{10,... | collective-permute-start | bytes 1794056 | tf_op jit(solution)/shard_map/ppermute | solution.py:341
  12.1 24.9 %collective-permute-start.2 = (f32[146,8,128]{2,1,0:T(8,128)S(1)}, f32[146,8,128]{2,1,0:T(8,128)S(1)}, u32[]{:S(2)}, u32[]{:S(2)}) collective-permute-start(f32[146,8,128]{2,1,0:T(8,128)S(1)} %pad_maximum_fusion.refs_0_), channel_id=1, source_target_pairs={{0,1},{1,0},{2,3},{3,2},{4,5},{5,4},{6,7},{7,6},{8,9},{9,8},{10,11... | collective-permute-start | bytes 1794056 | tf_op jit(solution)/shard_map/ppermute | solution.py:341
  12.1 27.6 %collective-permute-start.3 = (f32[146,8,128]{2,1,0:T(8,128)S(1)}, f32[146,8,128]{2,1,0:T(8,128)S(1)}, u32[]{:S(2)}, u32[]{:S(2)}) collective-permute-start(f32[146,8,128]{2,1,0:T(8,128)S(1)} %pad_maximum_fusion.refs_0_), channel_id=1, source_target_pairs={{0,8},{1,9},{2,10},{3,11},{4,12},{5,13},{6,14},{7,15},{8,0},{9,1},... | collective-permute-start | bytes 1794056 | tf_op jit(solution)/shard_map/ppermute | solution.py:341
  13.6 26.0 %collective-permute-start.4 = (f32[146,8,128]{2,1,0:T(8,128)S(1)}, f32[146,8,128]{2,1,0:T(8,128)S(1)}, u32[]{:S(2)}, u32[]{:S(2)}) collective-permute-start(f32[146,8,128]{2,1,0:T(8,128)S(1)} %pad_maximum_fusion.refs_0_), channel_id=1, source_target_pairs={{0,4},{1,5},{2,6},{3,7},{4,0},{5,1},{6,2},{7,3},{8,12},{9,13},{10,... | collective-permute-start | bytes 1794056 | tf_op jit(solution)/shard_map/ppermute | solution.py:341
  37.0 5.3 %copy-start.12 = (f32[146,8,128]{2,1,0:T(8,128)}, f32[146,8,128]{2,1,0:T(8,128)S(1)}, u32[]{:S(2)}) copy-start(f32[146,8,128]{2,1,0:T(8,128)S(1)} %collective-permute-done.refs_1_) | copy-start | bytes 1794052
  37.0 5.3 %copy-start.13 = (f32[146,8,128]{2,1,0:T(8,128)}, f32[146,8,128]{2,1,0:T(8,128)S(1)}, u32[]{:S(2)}) copy-start(f32[146,8,128]{2,1,0:T(8,128)S(1)} %collective-permute-done.1.refs_2_) | copy-start | bytes 1794052
  37.0 5.3 %copy-start.14 = (f32[146,8,128]{2,1,0:T(8,128)}, f32[146,8,128]{2,1,0:T(8,128)S(1)}, u32[]{:S(2)}) copy-start(f32[146,8,128]{2,1,0:T(8,128)S(1)} %collective-permute-done.2.refs_3_.refs_4_) | copy-start | bytes 1794052
  39.6 2.6 %copy-start.15 = (f32[146,8,128]{2,1,0:T(8,128)}, f32[146,8,128]{2,1,0:T(8,128)S(1)}, u32[]{:S(2)}) copy-start(f32[146,8,128]{2,1,0:T(8,128)S(1)} %collective-permute-done.3.refs_4_.refs_8_) | copy-start | bytes 1794052
  39.6 0.9 copy-start.16
  39.6 15.7 %collective-permute-start.5 = (f32[146,8,128]{2,1,0:T(8,128)S(1)}, f32[146,8,128]{2,1,0:T(8,128)}, u32[]{:S(2)}, u32[]{:S(2)}) collective-permute-start(f32[146,8,128]{2,1,0:T(8,128)S(1)} %collective-permute-done.refs_1_), channel_id=1, source_target_pairs={{0,2},{1,3},{2,0},{3,1},{4,6},{5,7},{6,4},{7,5},{8,10},{9,11},{10,... | collective-permute-start | bytes 1794056 | tf_op jit(solution)/shard_map/ppermute | solution.py:341
  40.3 15.1 %collective-permute-start.6 = (f32[146,8,128]{2,1,0:T(8,128)S(1)}, f32[146,8,128]{2,1,0:T(8,128)}, u32[]{:S(2)}, u32[]{:S(2)}) collective-permute-start(f32[146,8,128]{2,1,0:T(8,128)S(1)} %collective-permute-done.refs_1_), channel_id=1, source_target_pairs={{0,1},{1,0},{2,3},{3,2},{4,5},{5,4},{6,7},{7,6},{8,9},{9,8},{10,11... | collective-permute-start | bytes 1794056 | tf_op jit(solution)/shard_map/ppermute | solution.py:341
  40.5 14.8 %collective-permute-start.7 = (f32[146,8,128]{2,1,0:T(8,128)S(1)}, f32[146,8,128]{2,1,0:T(8,128)}, u32[]{:S(2)}, u32[]{:S(2)}) collective-permute-start(f32[146,8,128]{2,1,0:T(8,128)S(1)} %collective-permute-done.1.refs_2_), channel_id=1, source_target_pairs={{0,1},{1,0},{2,3},{3,2},{4,5},{5,4},{6,7},{7,6},{8,9},{9,8},{10,11... | collective-permute-start | bytes 1794056 | tf_op jit(solution)/shard_map/ppermute | solution.py:341
  40.8 15.8 %collective-permute-start.8 = (f32[146,8,128]{2,1,0:T(8,128)S(1)}, f32[146,8,128]{2,1,0:T(8,128)}, u32[]{:S(2)}, u32[]{:S(2)}) collective-permute-start(f32[146,8,128]{2,1,0:T(8,128)S(1)} %collective-permute-done.3.refs_4_.refs_8_), channel_id=1, source_target_pairs={{0,4},{1,5},{2,6},{3,7},{4,0},{5,1},{6,2},{7,3},{8,12},{9,13},{10,... | collective-permute-start | bytes 1794056 | tf_op jit(solution)/shard_map/ppermute | solution.py:341
  56.5 2.2 %collective-permute-start.9 = (f32[146,8,128]{2,1,0:T(8,128)}, f32[146,8,128]{2,1,0:T(8,128)S(1)}, u32[]{:S(2)}, u32[]{:S(2)}) collective-permute-start(f32[146,8,128]{2,1,0:T(8,128)} %collective-permute-done.5.refs_3_), channel_id=1, source_target_pairs={{0,1},{1,0},{2,3},{3,2},{4,5},{5,4},{6,7},{7,6},{8,9},{9,8},{10,11... | collective-permute-start | bytes 1794056 | tf_op jit(solution)/shard_map/ppermute | solution.py:341
  58.8 0.8 copy-start.17
  76.6 7.0 %collective-permute-start.11 = (f32[2,384,128]{2,1,0:T(8,128)}, f32[2,384,128]{2,1,0:T(8,128)S(1)}, u32[]{:S(2)}, u32[]{:S(2)}) collective-permute-start(f32[2,384,128]{2,1,0:T(8,128)} %get-tuple-element.63), channel_id=1, source_target_pairs={{0,1},{1,0},{2,3},{3,2},{4,5},{5,4},{6,7},{7,6},{8,9},{9,8},{10,11... | collective-permute-start | bytes 1179656 | tf_op jit(solution)/shard_map/ppermute | solution.py:341
  79.1 14.3 %collective-permute-start.15 = (f32[2,392,128]{2,1,0:T(8,128)}, f32[2,392,128]{2,1,0:T(8,128)S(1)}, u32[]{:S(2)}, u32[]{:S(2)}) collective-permute-start(f32[2,392,128]{2,1,0:T(8,128)} %get-tuple-element.67), channel_id=1, source_target_pairs={{0,4},{1,5},{2,6},{3,7},{4,0},{5,1},{6,2},{7,3},{8,12},{9,13},{10,... | collective-permute-start | bytes 1204232 | tf_op jit(solution)/shard_map/ppermute | solution.py:341
  83.6 12.0 %collective-permute-start.10 = (f32[2,384,128]{2,1,0:T(8,128)}, f32[2,384,128]{2,1,0:T(8,128)S(1)}, u32[]{:S(2)}, u32[]{:S(2)}) collective-permute-start(f32[2,384,128]{2,1,0:T(8,128)} %get-tuple-element.61), channel_id=1, source_target_pairs={{0,1},{1,0},{2,3},{3,2},{4,5},{5,4},{6,7},{7,6},{8,9},{9,8},{10,11... | collective-permute-start | bytes 1179656 | tf_op jit(solution)/shard_map/ppermute | solution.py:341
  83.6 9.7 %copy-start.4 = (f32[1,392,128]{2,1,0:T(8,128)S(1)}, f32[1,392,128]{2,1,0:T(8,128)}, u32[]{:S(2)}) copy-start(f32[1,392,128]{2,1,0:T(8,128)} %get-tuple-element.68) | copy-start | bytes 602116
  84.7 10.9 %collective-permute-start.13 = (f32[1,384,128]{2,1,0:T(8,128)S(1)}, f32[1,384,128]{2,1,0:T(8,128)S(1)}, u32[]{:S(2)}, u32[]{:S(2)}) collective-permute-start(f32[1,384,128]{2,1,0:T(8,128)S(1)} %get-tuple-element.75), channel_id=1, source_target_pairs={{0,2},{1,3},{2,0},{3,1},{4,6},{5,7},{6,4},{7,5},{8,10},{9,11},{10,... | collective-permute-start | bytes 589832 | tf_op jit(solution)/shard_map/ppermute | solution.py:341
  86.8 17.3 %collective-permute-start.12 = (f32[1,384,128]{2,1,0:T(8,128)S(1)}, f32[1,384,128]{2,1,0:T(8,128)S(1)}, u32[]{:S(2)}, u32[]{:S(2)}) collective-permute-start(f32[1,384,128]{2,1,0:T(8,128)S(1)} %get-tuple-element.74), channel_id=1, source_target_pairs={{0,2},{1,3},{2,0},{3,1},{4,6},{5,7},{6,4},{7,5},{8,10},{9,11},{10,... | collective-permute-start | bytes 589832 | tf_op jit(solution)/shard_map/ppermute | solution.py:341
  93.3 2.3 %copy-start.6 = (f32[1,384,128]{2,1,0:T(8,128)S(1)}, f32[1,384,128]{2,1,0:T(8,128)}, u32[]{:S(2)}) copy-start(f32[1,384,128]{2,1,0:T(8,128)} %get-tuple-element.64) | copy-start | bytes 589828
  93.4 8.9 %collective-permute-start.16 = (f32[1,392,128]{2,1,0:T(8,128)S(1)}, f32[1,392,128]{2,1,0:T(8,128)S(1)}, u32[]{:S(2)}, u32[]{:S(2)}) collective-permute-start(f32[1,392,128]{2,1,0:T(8,128)S(1)} %slice_add_fusion), channel_id=1, source_target_pairs={{0,8},{1,9},{2,10},{3,11},{4,12},{5,13},{6,14},{7,15},{8,0},{9,1},... | collective-permute-start | bytes 602120 | tf_op jit(solution)/shard_map/ppermute | solution.py:341
  95.6 6.6 %copy-start.3 = (f32[1,392,128]{2,1,0:T(8,128)S(1)}, f32[1,392,128]{2,1,0:T(8,128)}, u32[]{:S(2)}) copy-start(f32[1,392,128]{2,1,0:T(8,128)} %get-tuple-element.66) | copy-start | bytes 602116
  95.7 11.6 %collective-permute-start.14 = (f32[1,384,128]{2,1,0:T(8,128)S(1)}, f32[1,384,128]{2,1,0:T(8,128)S(1)}, u32[]{:S(2)}, u32[]{:S(2)}) collective-permute-start(f32[1,384,128]{2,1,0:T(8,128)S(1)} %fusion.1), channel_id=1, source_target_pairs={{0,16},{1,17},{2,18},{3,19},{4,20},{5,21},{6,22},{7,23},{8,24},{9,... | collective-permute-start | bytes 589832 | tf_op jit(solution)/shard_map/ppermute | solution.py:341
  103.1 1.1 copy-start.1
  104.1 3.1 %copy-start.5 = (f32[1,384,128]{2,1,0:T(8,128)S(1)}, f32[1,384,128]{2,1,0:T(8,128)}, u32[]{:S(2)}) copy-start(f32[1,384,128]{2,1,0:T(8,128)} %get-tuple-element.60) | copy-start | bytes 589828

commit v5 on v4

--- a/solution.py
+++ b/solution.py
@@ -37,57 +37,49 @@
     return filled
 
 
-def tile_parts(sub, tile, row):
-    row = jnp.broadcast_to(row, tile.shape)
-    square = row * row
-    for at in (6, 7):
-        other = jnp.broadcast_to(tile[at : at + 1], tile.shape)
-        square = square + other * other
-    main, last = thirds(tile), thirds(row)
-    positions = [jnp.where(sub >= 6, m, jnp.where(sub == 5, r, 0.0)) for m, r in zip(main[:2], last[:2])]
-    sums = tall([jnp.where(sub == 4, 1.0, positions[0]), positions[1]])
-    spot = jnp.where(sub >= 6, tile, jnp.where(sub == 5, row, 0.0))
-    return main, last, square, sums, spot
-
-
-def operands(near, near_row, far, far_row):
-    sub = lax.broadcasted_iota(jnp.int32, near.shape, 0)
-    first = sub < 3
-    second = jnp.logical_and(sub >= 3, sub < 6)
-    zero = jnp.zeros_like(near)
-    scale = 1.0 / near.shape[1]
-    middle = jnp.where(sub >= 6, jnp.sum(near, axis=1, keepdims=True) * scale, 0.0)
-    middle_row = jnp.sum(near_row, axis=1, keepdims=True) * scale
-    near, far = near - middle, far - middle
-    near_row, far_row = near_row - middle_row, far_row - middle_row
-    (high, mid, low), (row_high, row_mid, row_low), square, near_sums, near_spot = tile_parts(sub, near, near_row)
-    square_parts = thirds(square)
-    left = tall(
-        [
-            high, mid, high, low, high, mid,
-            place(sub, {0: row_high, 1: row_mid, 2: row_high, 3: row_low, 4: row_high, 5: row_mid}),
-            place(sub, {0: square_parts[0], 1: square_parts[1], 2: square_parts[2]}, jnp.where(second, 1.0, 0.0)),
-        ]
-    )
-    (high, mid, low), (row_high, row_mid, row_low), square, far_sums, far_spot = tile_parts(sub, far, far_row)
-    square_parts = thirds(square + CORE)
-    twice = [jnp.where(sub >= 6, -2.0 * part, 0.0) for part in (high, mid, low)]
-    twice_row = [-2.0 * part for part in (row_high, row_mid, row_low)]
-    spread = tall(
-        [
-            twice[0], twice[0], twice[1], twice[0], twice[2], twice[1],
-            place(sub, {0: twice_row[0], 1: twice_row[0], 2: twice_row[1], 3: twice_row[0], 4: twice_row[2], 5: twice_row[1]}, zero),
-            place(sub, {3: square_parts[0], 4: square_parts[1], 5: square_parts[2]}, jnp.where(first, 1.0, 0.0)),
-        ]
-    )
-    dots = []
-    for part in (
-        [jnp.where(first, part, 0.0) for part in (high, mid)],
-        [jnp.where(first, pltpu.roll(part, 5, 0), 0.0) for part in (high, mid)],
-        [jnp.where(second, pltpu.roll(part, 3, 0), 0.0) for part in (high, mid)],
-    ):
-        dots.append(tall([part[0], part[0], part[1], zero]))
-    return left.T, spread, dots, near_sums, near_spot, far_sums, far_spot
+def tile_parts(sub, rows):
+    parts = [thirds(rows[k]) for k in range(3)]
+    square = rows[0] * rows[0] + rows[1] * rows[1] + rows[2] * rows[2]
+    ones = jnp.where(sub == 3, 1.0, 0.0)
+    high, middle = [place(sub, {k: parts[k][at] for k in range(3)}, 0.0) for at in range(2)]
+    sums = tall([high + ones, middle])
+    return parts, square, sums, place(sub, {k: rows[k] for k in range(3)}, 0.0)
+
+
+def products(sub, first, second, burgers):
+    major = jnp.where(sub < 3, first[0], jnp.where(sub < 6, first[1], first[2]))
+    minor = jnp.where(sub % 3 == 0, second[0], jnp.where(sub % 3 == 1, second[1], second[2]))
+    rest = place(sub, {0: first[2] * second[2], 1: burgers[0], 2: burgers[1], 3: burgers[2]}, 0.0)
+    return [head(major * minor), head(rest)], [major * minor - head(major * minor), rest - head(rest)]
+
+
+def operands(near, far):
+    sub = lax.broadcasted_iota(jnp.int32, (8, near[0].shape[1]), 0)
+    near = [jnp.broadcast_to(row, sub.shape) for row in near]
+    far = [jnp.broadcast_to(row, sub.shape) for row in far]
+    scale = 1.0 / near[0].shape[1]
+    for k in range(3):
+        middle = jnp.sum(near[k], axis=1, keepdims=True) * scale
+        near[k], far[k] = near[k] - middle, far[k] - middle
+    zero = jnp.zeros(sub.shape, jnp.float32)
+    parts, square, near_sums, near_spot = tile_parts(sub, near)
+    square = thirds(square)
+    ends = [{6: square[0], 7: square[1]}, {6: square[2], 7: 1.0}, {6: 1.0, 7: 1.0}]
+    left = [
+        place(sub, {1: middle, 5: middle, 3: low, **end}, high) for (high, middle, low), end in zip(parts, ends)
+    ]
+    high, low = products(sub, near[3:6], near[6:9], near[3:6])
+    left = tall(left + [zero] + high + low + high)
+
+    parts, square, far_sums, far_spot = tile_parts(sub, far)
+    square = thirds(square + CORE)
+    ends = [{6: 1.0, 7: 1.0}, {6: 1.0, 7: square[0]}, {6: square[1], 7: square[2]}]
+    spread = [
+        place(sub, {2: -2.0 * middle, 5: -2.0 * middle, 4: -2.0 * low, **end}, -2.0 * high)
+        for (high, middle, low), end in zip(parts, ends)
+    ]
+    high, low = products(sub, far[6:9], far[3:6], far[3:6])
+    return left.T, tall(spread + [zero]), tall(high + high + low), near_sums, near_spot, far_sums, far_spot
 
 
 def matmul(left, right, contract=(1, 0)):
@@ -124,7 +116,7 @@
 def pair_kernel(plan, sources, earlier, refs_out, scratch):
     tiles, slots, list_group, near_total, far_total, near, far, done, final = plan
     near_number, far_number = len(near), len(far)
-    (blocks, lists, near_sum, far_sum, ids_vmem, ids, left_ref, wide_ref, cross_ref, part_ref, sums_ref, spots_ref,
+    (blocks, lists, near_sum, far_sum, ids_vmem, ids, left_ref, right_ref, part_ref, sums_ref, spots_ref,
      sems, list_sems) = scratch
     list_copies = [
         pltpu.make_async_copy(source.at[pl.ds(list_group, 2)], lists.at[k], list_sems.at[k])
@@ -135,7 +127,7 @@
         copy.start()
     near_sum[...] = jnp.zeros_like(near_sum)
     far_sum[...] = jnp.zeros_like(far_sum)
-    wide_ref[...] = jnp.zeros_like(wide_ref)
+    right_ref[...] = jnp.zeros_like(right_ref)
     for copy in list_copies:
         copy.wait()
 
@@ -168,7 +160,8 @@
         copy.wait()
 
     def tile_of(block, tile):
-        return blocks[block, tile], blocks[block, tiles + tile // 8, pl.ds(tile % 8, 1), :]
+        rows = [blocks[block, tile, pl.ds(k, 1), :] for k in range(8)]
+        return rows[6:8] + [blocks[block, tiles + tile // 8, pl.ds(tile % 8, 1), :]] + rows[0:6]
 
     def pick(group, k):
         at = group * GROUP + k
@@ -191,30 +184,25 @@
                 total = total[0:8] + total[8:16]
                 if total.shape[1] > half:
                     total = total[:, :half] + total[:, half:]
-                force = spots_ref[stash, k, spot] * jnp.broadcast_to(total[4:5], total.shape) - total
-                out[block, tile] += jnp.where(live, force, 0.0)
+                force = spots_ref[stash, k, spot] * jnp.broadcast_to(total[3:4], total.shape) - total
+                out[block, pl.ds(pl.multiple_of(tile * 8, 8), 8), :] += jnp.where(live, force, 0.0)
         for k in range(GROUP):
-            left = left_ref[k]
-            terms = matmul(left, wide_ref[k])
-            more = matmul(left[:, : cross_ref.shape[1]], cross_ref[k])
-            spread, burgers_dot = terms[:, :width], terms[:, width:]
-            inverse = lax.rsqrt(spread)
-            coupling = (burgers_dot + more[:, :width] * more[:, width:]) * (inverse * inverse * inverse)
+            terms = matmul(left_ref[k], right_ref[k])
+            inverse = lax.rsqrt(terms[:, :width])
+            coupling = terms[:, width:] * (inverse * inverse * inverse)
             high, low = halves(coupling)
             part_ref[k, :, :width] = high
             part_ref[k, :, width:] = low
         for k in range(GROUP):
             live, near_block, near_tile, far_block, far_tile = pick(group, k)
             far_place = jnp.where(far_block > 0, far_block + (near_number - 1), 0)
-            left, spread, dots, near_rows, near_spot, far_rows, far_spot = operands(
-                *tile_of(near_block, near_tile), *tile_of(far_place, far_tile)
+            left, spread, numerator, near_rows, near_spot, far_rows, far_spot = operands(
+                tile_of(near_block, near_tile), tile_of(far_place, far_tile)
             )
             stash = lax.rem(group, 3)
             left_ref[k] = left
-            wide_ref[k, :, :width] = spread
-            wide_ref[k, : dots[0].shape[0], width:] = dots[0]
-            cross_ref[k, :, :width] = dots[1]
-            cross_ref[k, :, width:] = dots[2]
+            right_ref[k, : spread.shape[0], :width] = spread
+            right_ref[k, spread.shape[0] :, width:] = numerator
             sums_ref[stash, k, 0] = near_rows
             sums_ref[stash, k, 1] = far_rows
             spots_ref[stash, k, 0] = near_spot
@@ -236,9 +224,9 @@
                 row = old[0 if is_near else 1]
                 if block in row:
                     known = earlier[row.index(block) + (0 if is_near else len(old[0]))]
-            for axis, row in enumerate((6, 7, 5)):
+            for axis in range(3):
                 rows = slice(axis * tiles, (axis + 1) * tiles)
-                value = total[block, :, row, :]
+                value = total[block, pl.ds(axis, tiles, stride=8), :]
                 out[k, rows, :] = value if known is None else value + known[0, rows, :]
             if final and not is_near:
                 out[k, 3 * tiles :, :] = moments
@@ -258,7 +246,7 @@
         shapes += [(count, 3 * tiles + 8, width) for count in counts[1]]
     else:
         shapes = [(1, 3 * tiles, width)] * (near_number + far_number)
-    depth, dot_depth, sum_rows = 64, 32, 16
+    depth, sum_rows = 80, 16
     share = len(near) * len(far) / (totals[0] * totals[1])
     elements = int(share * slot_count / 3) * width * width
 
@@ -276,13 +264,12 @@
         scratch_shapes=[
             pltpu.VMEM((len(blocks),) + blocks[0].shape, jnp.float32),
             pltpu.VMEM((len(blocks), 2, 8, width), jnp.float32),
-            pltpu.VMEM((near_number, tiles, 8, width), jnp.float32),
-            pltpu.VMEM((far_number, tiles, 8, width), jnp.float32),
+            pltpu.VMEM((near_number, 8 * tiles, width), jnp.float32),
+            pltpu.VMEM((far_number, 8 * tiles, width), jnp.float32),
             pltpu.VMEM((8, slot_count), jnp.int32),
             pltpu.SMEM((8, slot_count), jnp.int32),
             pltpu.VMEM((GROUP, width, depth), jnp.bfloat16),
             pltpu.VMEM((GROUP, depth, 2 * width), jnp.bfloat16),
-            pltpu.VMEM((GROUP, dot_depth, 2 * width), jnp.bfloat16),
             pltpu.VMEM((GROUP, width, 2 * width), jnp.bfloat16),
             pltpu.VMEM((3, GROUP, 2, sum_rows, width), jnp.bfloat16),
             pltpu.VMEM((3, GROUP, 2, 8, width), jnp.float32),

time: 109 us -> 107 us (0.982); the launches traced: 108 us -> 108 us
  Pallas kernels: 30 us -> 27.2 us
  starting transfers between devices: 22.5 us -> 24.2 us
    pallas_call x2, Pallas kernels: 30 us -> 27.2 us  [run_pairs(): pl.pallas_call(kernel, out_shape=[jax.ShapeDtypeStruct(shape, jnp.float32...]
    ppermute x17, starting transfers between devices: 22.5 us -> 24.2 us  [swap(): return lax.ppermute(value, AXES, [(k, k ^ mask) for k in range(devices)])]
  transfers between devices with their start and end apart: 17 -> 17, of which waited for: 7 -> 7; matrix products, arithmetic and copies ran while one was open for 3% -> 3% of each run, Pallas kernels for 12% -> 9%
where the time goes in v5:
time: 107 us; the launch traced here: 108 us
  waiting for transfers between devices  44 us (41%)
  Pallas kernels  27.2 us (25%)
  starting transfers between devices  24.2 us (23%)
  local copies, waits for them, and re-layouts  6.84 us (6%)
  other arithmetic  3.81 us (4%)
    ppermute x17, waiting for transfers between devices, swap(): return lax.ppermute(value, AXES, [(k, k ^ mask) for k in range(devices)])  44 us
    pallas_call x2, Pallas kernels, run_pairs(): pl.pallas_call(kernel, out_shape=[jax.ShapeDtypeStruct(shape, jnp.float32...  27.2 us
    ppermute x17, starting transfers between devices, swap(): return lax.ppermute(value, AXES, [(k, k ^ mask) for k in range(devices)])  24.2 us
    unnamed x38, local copies, waits for them, and re-layouts  3.96 us
  transfers between devices with their start and end apart: 17, of which 7 were waited for; matrix products, arithmetic and copies ran while one was open for 3% of the time, Pallas kernels for 9%

profile of v5, /device:TPU:0, one launch (start us, length us, event | category | flops | bytes accessed | tf_op | source)
XLA Modules:
  0.0 107.6 jit_solution(17697197039424732557)
XLA Ops:
  0.0 1.0 fusion.14
  1.1 1.0 copy-done
  2.2 0.1 add.96
  3.0 0.3 select_reduce_fusion
  3.4 0.6 select_reduce_fusion.1
  4.0 0.1 concatenate.21
  4.1 0.3 multiply_reduce_fusion.1
  4.3 0.6 copy-done.11
  5.0 0.1 fusion.8
  5.1 0.1 reshape.128
  5.3 0.2 copy.32
  5.5 0.6 slice-done.1
  6.2 0.1 copy.33
  6.3 0.1 pad_maximum_fusion.refs_0_
  6.4 4.1 %collective-permute-start = (f32[146,8,128]{2,1,0:T(8,128)S(1)}, f32[146,8,128]{2,1,0:T(8,128)S(1)}, u32[]{:S(2)}, u32[]{:S(2)}) collective-permute-start(f32[146,8,128]{2,1,0:T(8,128)S(1)} %pad_maximum_fusion.refs_0_), channel_id=1, source_target_pairs={{0,16},{1,17},{2,18},{3,19},{4,20},{5,21},{6,22},{7,23},{8,24},{9,... | collective-permute-start | bytes 1794056 | tf_op jit(solution)/shard_map/ppermute | solution.py:328
  10.5 1.5 %collective-permute-start.1 = (f32[146,8,128]{2,1,0:T(8,128)S(1)}, f32[146,8,128]{2,1,0:T(8,128)S(1)}, u32[]{:S(2)}, u32[]{:S(2)}) collective-permute-start(f32[146,8,128]{2,1,0:T(8,128)S(1)} %pad_maximum_fusion.refs_0_), channel_id=1, source_target_pairs={{0,2},{1,3},{2,0},{3,1},{4,6},{5,7},{6,4},{7,5},{8,10},{9,11},{10,... | collective-permute-start | bytes 1794056 | tf_op jit(solution)/shard_map/ppermute | solution.py:328
  12.1 1.6 %collective-permute-start.3 = (f32[146,8,128]{2,1,0:T(8,128)S(1)}, f32[146,8,128]{2,1,0:T(8,128)S(1)}, u32[]{:S(2)}, u32[]{:S(2)}) collective-permute-start(f32[146,8,128]{2,1,0:T(8,128)S(1)} %pad_maximum_fusion.refs_0_), channel_id=1, source_target_pairs={{0,8},{1,9},{2,10},{3,11},{4,12},{5,13},{6,14},{7,15},{8,0},{9,1},... | collective-permute-start | bytes 1794056 | tf_op jit(solution)/shard_map/ppermute | solution.py:328
  13.6 1.5 %collective-permute-start.4 = (f32[146,8,128]{2,1,0:T(8,128)S(1)}, f32[146,8,128]{2,1,0:T(8,128)S(1)}, u32[]{:S(2)}, u32[]{:S(2)}) collective-permute-start(f32[146,8,128]{2,1,0:T(8,128)S(1)} %pad_maximum_fusion.refs_0_), channel_id=1, source_target_pairs={{0,4},{1,5},{2,6},{3,7},{4,0},{5,1},{6,2},{7,3},{8,12},{9,13},{10,... | collective-permute-start | bytes 1794056 | tf_op jit(solution)/shard_map/ppermute | solution.py:328
  15.1 21.8 %collective-permute-done.refs_1_ = f32[146,8,128]{2,1,0:T(8,128)S(1)} collective-permute-done((f32[146,8,128]{2,1,0:T(8,128)S(1)}, f32[146,8,128]{2,1,0:T(8,128)S(1)}, u32[]{:S(2)}, u32[]{:S(2)}) %collective-permute-start) | collective-permute-done | bytes 598048 | tf_op jit(solution)/shard_map/ppermute | solution.py:328
  37.0 2.6 %collective-permute-done.3.refs_4_.refs_8_ = f32[146,8,128]{2,1,0:T(8,128)S(1)} collective-permute-done((f32[146,8,128]{2,1,0:T(8,128)S(1)}, f32[146,8,128]{2,1,0:T(8,128)S(1)}, u32[]{:S(2)}, u32[]{:S(2)}) %collective-permute-start.3) | collective-permute-done | bytes 598048 | tf_op jit(solution)/shard_map/ppermute | solution.py:328
  39.6 0.6 collective-permute-start.5
  40.3 0.3 copy-done.16
  40.5 0.2 collective-permute-start.7
  40.8 1.5 %collective-permute-start.8 = (f32[146,8,128]{2,1,0:T(8,128)S(1)}, f32[146,8,128]{2,1,0:T(8,128)}, u32[]{:S(2)}, u32[]{:S(2)}) collective-permute-start(f32[146,8,128]{2,1,0:T(8,128)S(1)} %collective-permute-done.3.refs_4_.refs_8_), channel_id=1, source_target_pairs={{0,4},{1,5},{2,6},{3,7},{4,0},{5,1},{6,2},{7,3},{8,12},{9,13},{10,... | collective-permute-start | bytes 1794056 | tf_op jit(solution)/shard_map/ppermute | solution.py:328
  42.3 10.0 %early_pairs.1 = (f32[1,384,128]{2,1,0:T(8,128)}, f32[1,384,128]{2,1,0:T(8,128)}, f32[1,384,128]{2,1,0:T(8,128)}, f32[1,384,128]{2,1,0:T(8,128)}, f32[1,384,128]...) custom-call(f32[146,8,128]{2,1,0:T(8,128)} %copy-done.2, f32[146,8,128]{2,1,0:T(8,128)} %copy-done.12, ...), custom_call_target="tpu_custom_call" | custom-call | flops 1048576000 | bytes 4194304 | tf_op jit(solution)/shard_map/early_pairs/pallas_call | solution.py:259
  52.3 2.7 %collective-permute-done.5.refs_3_ = f32[146,8,128]{2,1,0:T(8,128)} collective-permute-done((f32[146,8,128]{2,1,0:T(8,128)S(1)}, f32[146,8,128]{2,1,0:T(8,128)}, u32[]{:S(2)}, u32[]{:S(2)}) %collective-permute-start.5) | collective-permute-done | bytes 598048 | tf_op jit(solution)/shard_map/ppermute | solution.py:328
  55.0 1.6 %collective-permute-done.8.refs_10_ = f32[146,8,128]{2,1,0:T(8,128)} collective-permute-done((f32[146,8,128]{2,1,0:T(8,128)S(1)}, f32[146,8,128]{2,1,0:T(8,128)}, u32[]{:S(2)}, u32[]{:S(2)}) %collective-permute-start.8) | collective-permute-done | bytes 598048 | tf_op jit(solution)/shard_map/ppermute | solution.py:328
  56.6 2.2 %collective-permute-done.9.refs_7_ = f32[146,8,128]{2,1,0:T(8,128)S(1)} collective-permute-done((f32[146,8,128]{2,1,0:T(8,128)}, f32[146,8,128]{2,1,0:T(8,128)S(1)}, u32[]{:S(2)}, u32[]{:S(2)}) %collective-permute-start.9) | collective-permute-done | bytes 598048 | tf_op jit(solution)/shard_map/ppermute | solution.py:328
  58.8 0.8 copy-done.17
  59.6 17.2 %pairs.1 = (f32[1,384,128]{2,1,0:T(8,128)}, f32[1,384,128]{2,1,0:T(8,128)}, f32[1,384,128]{2,1,0:T(8,128)}, f32[1,384,128]{2,1,0:T(8,128)}, f32[2,384,128]{2,1,0...) custom-call(f32[146,8,128]{2,1,0:T(8,128)} %copy-done.2, ...), custom_call_target="tpu_custom_call" | custom-call | flops 2785280000 | bytes 4194304 | tf_op jit(solution)/shard_map/pairs/pallas_call | solution.py:259
  76.9 3.8 %collective-permute-start.15 = (f32[2,392,128]{2,1,0:T(8,128)}, f32[2,392,128]{2,1,0:T(8,128)S(1)}, u32[]{:S(2)}, u32[]{:S(2)}) collective-permute-start(f32[2,392,128]{2,1,0:T(8,128)} %get-tuple-element.67), channel_id=1, source_target_pairs={{0,4},{1,5},{2,6},{3,7},{4,0},{5,1},{6,2},{7,3},{8,12},{9,13},{10,... | collective-permute-start | bytes 1204232 | tf_op jit(solution)/shard_map/ppermute | solution.py:328
  80.7 0.2 collective-permute-start.10
  80.9 1.1 %slice_add_fusion.5 = (f32[1,384,128]{2,1,0:T(8,128)S(1)}, f32[1,384,128]{2,1,0:T(8,128)S(1)}) fusion(f32[1,384,128]{2,1,0:T(8,128)} %get-tuple-element.62, f32[2,384,128]{2,1,0:T(8,128)S(1)} %collective-permute-done.11, f32[1,384,128]{2,1,0:T(8,128)} %get-tuple-element.65), kind=kLoop, calls=%fused_computation.12 | loop fusion | flops 98304 | bytes 1179648 | tf_op jit(solution)/shard_map/add | solution.py:392
  82.0 1.2 %collective-permute-start.13 = (f32[1,384,128]{2,1,0:T(8,128)S(1)}, f32[1,384,128]{2,1,0:T(8,128)S(1)}, u32[]{:S(2)}, u32[]{:S(2)}) collective-permute-start(f32[1,384,128]{2,1,0:T(8,128)S(1)} %get-tuple-element.75), channel_id=1, source_target_pairs={{0,2},{1,3},{2,0},{3,1},{4,6},{5,7},{6,4},{7,5},{8,10},{9,11},{10,... | collective-permute-start | bytes 589832 | tf_op jit(solution)/shard_map/ppermute | solution.py:328
  83.2 0.9 collective-permute-start.12
  84.1 6.7 %collective-permute-done.15 = f32[2,392,128]{2,1,0:T(8,128)S(1)} collective-permute-done((f32[2,392,128]{2,1,0:T(8,128)}, f32[2,392,128]{2,1,0:T(8,128)S(1)}, u32[]{:S(2)}, u32[]{:S(2)}) %collective-permute-start.15) | collective-permute-done | bytes 401440 | tf_op jit(solution)/shard_map/ppermute | solution.py:328
  90.8 0.2 collective-permute-start.16
  91.0 0.7 copy-done.6
  91.8 6.8 %collective-permute-start.14 = (f32[1,384,128]{2,1,0:T(8,128)S(1)}, f32[1,384,128]{2,1,0:T(8,128)S(1)}, u32[]{:S(2)}, u32[]{:S(2)}) collective-permute-start(f32[1,384,128]{2,1,0:T(8,128)S(1)} %fusion.1), channel_id=1, source_target_pairs={{0,16},{1,17},{2,18},{3,19},{4,20},{5,21},{6,22},{7,23},{8,24},{9,... | collective-permute-start | bytes 589832 | tf_op jit(solution)/shard_map/ppermute | solution.py:328
  98.7 0.2 div.14
  98.9 0.5 copy.29
  99.5 0.1 copy.30
  99.6 0.2 fusion.6
  99.8 0.2 fusion.5
  100.1 0.3 multiply_reduce_fusion
  100.4 0.1 copy-done.1
  100.5 6.3 %collective-permute-done.14 = f32[1,384,128]{2,1,0:T(8,128)S(1)} collective-permute-done((f32[1,384,128]{2,1,0:T(8,128)S(1)}, f32[1,384,128]{2,1,0:T(8,128)S(1)}, u32[]{:S(2)}, u32[]{:S(2)}) %collective-permute-start.14) | collective-permute-done | bytes 196640 | tf_op jit(solution)/shard_map/ppermute | solution.py:328
  106.9 0.7 maximum_add_fusion
  (68 shorter events, 0.6 us)
Async XLA Ops:
  1.1 1.1 copy-start
  1.1 1.1 copy-start.10
  1.1 1.2 %copy-start.9 = (s32[1,512]{1,0:T(1,128)S(1)}, s32[1,512]{1,0:T(1,128)}, u32[]{:S(2)}) copy-start(s32[1,512]{1,0:T(1,128)} %param.9) | copy-start | bytes 6148
  1.1 1.9 %copy-start.8 = (s32[1,512]{1,0:T(1,128)S(1)}, s32[1,512]{1,0:T(1,128)}, u32[]{:S(2)}) copy-start(s32[1,512]{1,0:T(1,128)} %param.10) | copy-start | bytes 6148
  1.1 2.3 %copy-start.7 = (s32[1,32,16]{1,2,0:T(8,128)S(1)}, s32[1,32,16]{1,2,0:T(8,128)}, u32[]{:S(2)}) copy-start(s32[1,32,16]{1,2,0:T(8,128)} %param.8) | copy-start | bytes 6148
  2.1 3.2 %slice-start = ((f32[128,9,128]{2,0,1:T(8,128)}), f32[128,6,128]{2,0,1:T(8,128)S(1)}, s32[]{:S(2)}) async-start(f32[128,9,128]{2,0,1:T(8,128)} %param.7), calls=%async_computation | async-start | bytes 786432 | tf_op jit(solution)/shard_map/slice | solution.py:286
  4.3 0.7 copy-start.11
  5.3 0.9 slice-start.1
  6.4 35.8 %copy-start.2 = (f32[146,8,128]{2,1,0:T(8,128)}, f32[146,8,128]{2,1,0:T(8,128)S(1)}, u32[]{:S(2)}) copy-start(f32[146,8,128]{2,1,0:T(8,128)S(1)} %pad_maximum_fusion.refs_0_) | copy-start | bytes 1794052
  6.4 30.5 %collective-permute-start = (f32[146,8,128]{2,1,0:T(8,128)S(1)}, f32[146,8,128]{2,1,0:T(8,128)S(1)}, u32[]{:S(2)}, u32[]{:S(2)}) collective-permute-start(f32[146,8,128]{2,1,0:T(8,128)S(1)} %pad_maximum_fusion.refs_0_), channel_id=1, source_target_pairs={{0,16},{1,17},{2,18},{3,19},{4,20},{5,21},{6,22},{7,23},{8,24},{9,... | collective-permute-start | bytes 1794056 | tf_op jit(solution)/shard_map/ppermute | solution.py:328
  10.5 26.4 %collective-permute-start.1 = (f32[146,8,128]{2,1,0:T(8,128)S(1)}, f32[146,8,128]{2,1,0:T(8,128)S(1)}, u32[]{:S(2)}, u32[]{:S(2)}) collective-permute-start(f32[146,8,128]{2,1,0:T(8,128)S(1)} %pad_maximum_fusion.refs_0_), channel_id=1, source_target_pairs={{0,2},{1,3},{2,0},{3,1},{4,6},{5,7},{6,4},{7,5},{8,10},{9,11},{10,... | collective-permute-start | bytes 1794056 | tf_op jit(solution)/shard_map/ppermute | solution.py:328
  12.1 24.9 %collective-permute-start.2 = (f32[146,8,128]{2,1,0:T(8,128)S(1)}, f32[146,8,128]{2,1,0:T(8,128)S(1)}, u32[]{:S(2)}, u32[]{:S(2)}) collective-permute-start(f32[146,8,128]{2,1,0:T(8,128)S(1)} %pad_maximum_fusion.refs_0_), channel_id=1, source_target_pairs={{0,1},{1,0},{2,3},{3,2},{4,5},{5,4},{6,7},{7,6},{8,9},{9,8},{10,11... | collective-permute-start | bytes 1794056 | tf_op jit(solution)/shard_map/ppermute | solution.py:328
  12.1 27.6 %collective-permute-start.3 = (f32[146,8,128]{2,1,0:T(8,128)S(1)}, f32[146,8,128]{2,1,0:T(8,128)S(1)}, u32[]{:S(2)}, u32[]{:S(2)}) collective-permute-start(f32[146,8,128]{2,1,0:T(8,128)S(1)} %pad_maximum_fusion.refs_0_), channel_id=1, source_target_pairs={{0,8},{1,9},{2,10},{3,11},{4,12},{5,13},{6,14},{7,15},{8,0},{9,1},... | collective-permute-start | bytes 1794056 | tf_op jit(solution)/shard_map/ppermute | solution.py:328
  13.6 26.0 %collective-permute-start.4 = (f32[146,8,128]{2,1,0:T(8,128)S(1)}, f32[146,8,128]{2,1,0:T(8,128)S(1)}, u32[]{:S(2)}, u32[]{:S(2)}) collective-permute-start(f32[146,8,128]{2,1,0:T(8,128)S(1)} %pad_maximum_fusion.refs_0_), channel_id=1, source_target_pairs={{0,4},{1,5},{2,6},{3,7},{4,0},{5,1},{6,2},{7,3},{8,12},{9,13},{10,... | collective-permute-start | bytes 1794056 | tf_op jit(solution)/shard_map/ppermute | solution.py:328
  37.0 5.3 %copy-start.12 = (f32[146,8,128]{2,1,0:T(8,128)}, f32[146,8,128]{2,1,0:T(8,128)S(1)}, u32[]{:S(2)}) copy-start(f32[146,8,128]{2,1,0:T(8,128)S(1)} %collective-permute-done.refs_1_) | copy-start | bytes 1794052
  37.0 5.3 %copy-start.13 = (f32[146,8,128]{2,1,0:T(8,128)}, f32[146,8,128]{2,1,0:T(8,128)S(1)}, u32[]{:S(2)}) copy-start(f32[146,8,128]{2,1,0:T(8,128)S(1)} %collective-permute-done.1.refs_2_) | copy-start | bytes 1794052
  37.0 5.3 %copy-start.14 = (f32[146,8,128]{2,1,0:T(8,128)}, f32[146,8,128]{2,1,0:T(8,128)S(1)}, u32[]{:S(2)}) copy-start(f32[146,8,128]{2,1,0:T(8,128)S(1)} %collective-permute-done.2.refs_3_.refs_4_) | copy-start | bytes 1794052
  39.6 2.6 %copy-start.15 = (f32[146,8,128]{2,1,0:T(8,128)}, f32[146,8,128]{2,1,0:T(8,128)S(1)}, u32[]{:S(2)}) copy-start(f32[146,8,128]{2,1,0:T(8,128)S(1)} %collective-permute-done.3.refs_4_.refs_8_) | copy-start | bytes 1794052
  39.6 0.9 copy-start.16
  39.6 15.3 %collective-permute-start.5 = (f32[146,8,128]{2,1,0:T(8,128)S(1)}, f32[146,8,128]{2,1,0:T(8,128)}, u32[]{:S(2)}, u32[]{:S(2)}) collective-permute-start(f32[146,8,128]{2,1,0:T(8,128)S(1)} %collective-permute-done.refs_1_), channel_id=1, source_target_pairs={{0,2},{1,3},{2,0},{3,1},{4,6},{5,7},{6,4},{7,5},{8,10},{9,11},{10,... | collective-permute-start | bytes 1794056 | tf_op jit(solution)/shard_map/ppermute | solution.py:328
  40.3 14.7 %collective-permute-start.6 = (f32[146,8,128]{2,1,0:T(8,128)S(1)}, f32[146,8,128]{2,1,0:T(8,128)}, u32[]{:S(2)}, u32[]{:S(2)}) collective-permute-start(f32[146,8,128]{2,1,0:T(8,128)S(1)} %collective-permute-done.refs_1_), channel_id=1, source_target_pairs={{0,1},{1,0},{2,3},{3,2},{4,5},{5,4},{6,7},{7,6},{8,9},{9,8},{10,11... | collective-permute-start | bytes 1794056 | tf_op jit(solution)/shard_map/ppermute | solution.py:328
  40.5 14.4 %collective-permute-start.7 = (f32[146,8,128]{2,1,0:T(8,128)S(1)}, f32[146,8,128]{2,1,0:T(8,128)}, u32[]{:S(2)}, u32[]{:S(2)}) collective-permute-start(f32[146,8,128]{2,1,0:T(8,128)S(1)} %collective-permute-done.1.refs_2_), channel_id=1, source_target_pairs={{0,1},{1,0},{2,3},{3,2},{4,5},{5,4},{6,7},{7,6},{8,9},{9,8},{10,11... | collective-permute-start | bytes 1794056 | tf_op jit(solution)/shard_map/ppermute | solution.py:328
  40.8 15.8 %collective-permute-start.8 = (f32[146,8,128]{2,1,0:T(8,128)S(1)}, f32[146,8,128]{2,1,0:T(8,128)}, u32[]{:S(2)}, u32[]{:S(2)}) collective-permute-start(f32[146,8,128]{2,1,0:T(8,128)S(1)} %collective-permute-done.3.refs_4_.refs_8_), channel_id=1, source_target_pairs={{0,4},{1,5},{2,6},{3,7},{4,0},{5,1},{6,2},{7,3},{8,12},{9,13},{10,... | collective-permute-start | bytes 1794056 | tf_op jit(solution)/shard_map/ppermute | solution.py:328
  56.5 2.2 %collective-permute-start.9 = (f32[146,8,128]{2,1,0:T(8,128)}, f32[146,8,128]{2,1,0:T(8,128)S(1)}, u32[]{:S(2)}, u32[]{:S(2)}) collective-permute-start(f32[146,8,128]{2,1,0:T(8,128)} %collective-permute-done.5.refs_3_), channel_id=1, source_target_pairs={{0,1},{1,0},{2,3},{3,2},{4,5},{5,4},{6,7},{7,6},{8,9},{9,8},{10,11... | collective-permute-start | bytes 1794056 | tf_op jit(solution)/shard_map/ppermute | solution.py:328
  58.8 0.8 copy-start.17
  76.8 4.1 %collective-permute-start.11 = (f32[2,384,128]{2,1,0:T(8,128)}, f32[2,384,128]{2,1,0:T(8,128)S(1)}, u32[]{:S(2)}, u32[]{:S(2)}) collective-permute-start(f32[2,384,128]{2,1,0:T(8,128)} %get-tuple-element.63), channel_id=1, source_target_pairs={{0,1},{1,0},{2,3},{3,2},{4,5},{5,4},{6,7},{7,6},{8,9},{9,8},{10,11... | collective-permute-start | bytes 1179656 | tf_op jit(solution)/shard_map/ppermute | solution.py:328
  76.9 13.9 %collective-permute-start.15 = (f32[2,392,128]{2,1,0:T(8,128)}, f32[2,392,128]{2,1,0:T(8,128)S(1)}, u32[]{:S(2)}, u32[]{:S(2)}) collective-permute-start(f32[2,392,128]{2,1,0:T(8,128)} %get-tuple-element.67), channel_id=1, source_target_pairs={{0,4},{1,5},{2,6},{3,7},{4,0},{5,1},{6,2},{7,3},{8,12},{9,13},{10,... | collective-permute-start | bytes 1204232 | tf_op jit(solution)/shard_map/ppermute | solution.py:328
  80.7 10.3 %collective-permute-start.10 = (f32[2,384,128]{2,1,0:T(8,128)}, f32[2,384,128]{2,1,0:T(8,128)S(1)}, u32[]{:S(2)}, u32[]{:S(2)}) collective-permute-start(f32[2,384,128]{2,1,0:T(8,128)} %get-tuple-element.61), channel_id=1, source_target_pairs={{0,1},{1,0},{2,3},{3,2},{4,5},{5,4},{6,7},{7,6},{8,9},{9,8},{10,11... | collective-permute-start | bytes 1179656 | tf_op jit(solution)/shard_map/ppermute | solution.py:328
  80.9 9.9 %copy-start.4 = (f32[1,392,128]{2,1,0:T(8,128)S(1)}, f32[1,392,128]{2,1,0:T(8,128)}, u32[]{:S(2)}) copy-start(f32[1,392,128]{2,1,0:T(8,128)} %get-tuple-element.68) | copy-start | bytes 602116
  82.0 9.0 %collective-permute-start.13 = (f32[1,384,128]{2,1,0:T(8,128)S(1)}, f32[1,384,128]{2,1,0:T(8,128)S(1)}, u32[]{:S(2)}, u32[]{:S(2)}) collective-permute-start(f32[1,384,128]{2,1,0:T(8,128)S(1)} %get-tuple-element.75), channel_id=1, source_target_pairs={{0,2},{1,3},{2,0},{3,1},{4,6},{5,7},{6,4},{7,5},{8,10},{9,11},{10,... | collective-permute-start | bytes 589832 | tf_op jit(solution)/shard_map/ppermute | solution.py:328
  83.2 17.3 %collective-permute-start.12 = (f32[1,384,128]{2,1,0:T(8,128)S(1)}, f32[1,384,128]{2,1,0:T(8,128)S(1)}, u32[]{:S(2)}, u32[]{:S(2)}) collective-permute-start(f32[1,384,128]{2,1,0:T(8,128)S(1)} %get-tuple-element.74), channel_id=1, source_target_pairs={{0,2},{1,3},{2,0},{3,1},{4,6},{5,7},{6,4},{7,5},{8,10},{9,11},{10,... | collective-permute-start | bytes 589832 | tf_op jit(solution)/shard_map/ppermute | solution.py:328
  90.8 0.9 copy-start.6
  90.8 7.8 %collective-permute-start.16 = (f32[1,392,128]{2,1,0:T(8,128)S(1)}, f32[1,392,128]{2,1,0:T(8,128)S(1)}, u32[]{:S(2)}, u32[]{:S(2)}) collective-permute-start(f32[1,392,128]{2,1,0:T(8,128)S(1)} %slice_add_fusion), channel_id=1, source_target_pairs={{0,8},{1,9},{2,10},{3,11},{4,12},{5,13},{6,14},{7,15},{8,0},{9,1},... | collective-permute-start | bytes 602120 | tf_op jit(solution)/shard_map/ppermute | solution.py:328
  91.7 6.9 %copy-start.3 = (f32[1,392,128]{2,1,0:T(8,128)S(1)}, f32[1,392,128]{2,1,0:T(8,128)}, u32[]{:S(2)}) copy-start(f32[1,392,128]{2,1,0:T(8,128)} %get-tuple-element.66) | copy-start | bytes 602116
  91.8 15.1 %collective-permute-start.14 = (f32[1,384,128]{2,1,0:T(8,128)S(1)}, f32[1,384,128]{2,1,0:T(8,128)S(1)}, u32[]{:S(2)}, u32[]{:S(2)}) collective-permute-start(f32[1,384,128]{2,1,0:T(8,128)S(1)} %fusion.1), channel_id=1, source_target_pairs={{0,16},{1,17},{2,18},{3,19},{4,20},{5,21},{6,22},{7,23},{8,24},{9,... | collective-permute-start | bytes 589832 | tf_op jit(solution)/shard_map/ppermute | solution.py:328
  99.4 1.1 copy-start.1
  100.5 6.4 %copy-start.5 = (f32[1,384,128]{2,1,0:T(8,128)S(1)}, f32[1,384,128]{2,1,0:T(8,128)}, u32[]{:S(2)}) copy-start(f32[1,384,128]{2,1,0:T(8,128)} %get-tuple-element.60) | copy-start | bytes 589828

commit v6 on v5

--- a/solution.py
+++ b/solution.py
@@ -114,15 +114,16 @@
 
 
 def pair_kernel(plan, sources, earlier, refs_out, scratch):
-    tiles, slots, list_group, near_total, far_total, near, far, done, final = plan
+    tiles, slots, list_group, near_total, far_total, near, far, combos, done, final, layout = plan
     near_number, far_number = len(near), len(far)
     (blocks, lists, near_sum, far_sum, ids_vmem, ids, left_ref, right_ref, part_ref, sums_ref, spots_ref,
      sems, list_sems) = scratch
-    list_copies = [
-        pltpu.make_async_copy(source.at[pl.ds(list_group, 2)], lists.at[k], list_sems.at[k])
-        for k, source in enumerate(sources)
-    ]
-    copies = [pltpu.make_async_copy(source, blocks.at[k], sems.at[k]) for k, source in enumerate(sources)]
+    list_copies, copies = [], []
+    for at, (k, offset, size) in enumerate(layout):
+        copies.append(pltpu.make_async_copy(sources[at], blocks.at[k, pl.ds(offset, size)], sems.at[at]))
+        if offset <= list_group < offset + size:
+            rows = sources[at].at[pl.ds(list_group - offset, 2)]
+            list_copies.append(pltpu.make_async_copy(rows, lists.at[k], list_sems.at[k]))
     for copy in list_copies + copies:
         copy.start()
     near_sum[...] = jnp.zeros_like(near_sum)
@@ -140,16 +141,14 @@
     for k, block in enumerate(near):
         given = lists[k, 0, 0:4]
         given = jnp.where(given >= 0, given + k * tiles, given)
-        near_ids = jnp.where(near_at == block, given, near_ids)
+        wanted = [far_at == other for first, other in combos if first == block]
+        if wanted:
+            wanted = functools.reduce(jnp.logical_or, wanted)
+            near_ids = jnp.where(jnp.logical_and(near_at == block, wanted), given, near_ids)
     far_ids = jnp.full(shape, -1.0)
     for k, block in enumerate(far):
         given = lists[near_number - 1 + k if k else 0, 0, 4:8] + k * tiles
         far_ids = jnp.where(far_at == block, given, far_ids)
-    near_ids = jnp.where(far_ids >= 0, near_ids, -1.0)
-    if done:
-        old_near = functools.reduce(jnp.logical_or, [near_at == block for block in done[0]])
-        old_far = functools.reduce(jnp.logical_or, [far_at == block for block in done[1]])
-        near_ids = jnp.where(jnp.logical_and(old_near, old_far), -1.0, near_ids)
     live_list(near_ids, far_ids, ids_vmem)
     move = pltpu.make_async_copy(ids_vmem, ids, list_sems.at[0])
     move.start()
@@ -214,16 +213,12 @@
     at = 0
     if final:
         moments = functools.reduce(jnp.add, [lists[k, 1] for k in range(near_number)])
-        old = [list(blocks) for blocks in done]
     for out in refs_out:
         for k in range(out.shape[0]):
             is_near = at < near_number
             total, block = (near_sum, at) if is_near else (far_sum, at - near_number)
-            known = None
-            if final:
-                row = old[0 if is_near else 1]
-                if block in row:
-                    known = earlier[row.index(block) + (0 if is_near else len(old[0]))]
+            old, name = (done[0], near[block]) if is_near else (done[1], far[block])
+            known = earlier[old.index(name) + (0 if is_near else len(done[0]))] if name in old else None
             for axis in range(3):
                 rows = slice(axis * tiles, (axis + 1) * tiles)
                 value = total[block, pl.ds(axis, tiles, stride=8), :]
@@ -233,22 +228,30 @@
             at += 1
 
 
-def run_pairs(blocks, tiles, slots, list_group, totals, near, far, counts=None, done=None, earlier=()):
-    width = blocks[0].shape[-1]
+def run_pairs(held, sizes, near, far, combos, done=((), ()), earlier=(), counts=None):
+    tiles, slots, list_group, near_total, far_total = sizes
+    given_blocks = [held[0][k] for k in near] + [held[1][k] for k in far if k]
+    layout, blocks = [], []
+    for k, pieces in enumerate(given_blocks):
+        offset = 0
+        for piece in pieces:
+            layout.append((k, offset, piece.shape[0]))
+            blocks.append(piece)
+            offset += piece.shape[0]
+    groups, width = offset, blocks[0].shape[-1]
     final = counts is not None
     near_number, far_number = len(near), len(far)
-    slot_count = totals[0] * totals[1] * slots
+    slot_count = near_total * far_total * slots
     hbm = pl.BlockSpec(memory_space=pl.ANY)
     vmem = pl.BlockSpec(memory_space=pltpu.VMEM)
-    plan = (tiles, slots, list_group) + tuple(totals) + (near, far, done, final)
+    plan = tuple(sizes) + (near, far, combos, done, final, layout)
     if final:
         shapes = [(count, 3 * tiles, width) for count in counts[0]]
         shapes += [(count, 3 * tiles + 8, width) for count in counts[1]]
     else:
         shapes = [(1, 3 * tiles, width)] * (near_number + far_number)
     depth, sum_rows = 80, 16
-    share = len(near) * len(far) / (totals[0] * totals[1])
-    elements = int(share * slot_count / 3) * width * width
+    elements = len(combos) * slots // 3 * width * width
 
     def kernel(*refs):
         given = len(blocks)
@@ -262,8 +265,8 @@
         in_specs=[hbm] * len(blocks) + [vmem] * len(earlier),
         out_specs=[vmem] * len(shapes),
         scratch_shapes=[
-            pltpu.VMEM((len(blocks),) + blocks[0].shape, jnp.float32),
-            pltpu.VMEM((len(blocks), 2, 8, width), jnp.float32),
+            pltpu.VMEM((len(given_blocks), groups, 8, width), jnp.float32),
+            pltpu.VMEM((len(given_blocks), 2, 8, width), jnp.float32),
             pltpu.VMEM((near_number, 8 * tiles, width), jnp.float32),
             pltpu.VMEM((far_number, 8 * tiles, width), jnp.float32),
             pltpu.VMEM((8, slot_count), jnp.int32),
@@ -343,28 +346,38 @@
     return near_steps, far_steps
 
 
-def spread(block, near_steps, far_steps, work):
-    steps = list(near_steps) + list(far_steps)
-    allowed = set(span(near_steps)) | set(span(far_steps))
-    held = {0: block}
-    fresh = {0: -1}
-    sums = None
+def spread(block, pieces, steps, allowed, work):
+    held = {0: [block]}
+
+    def onward(items):
+        made = []
+        for mask, at, last, value in items:
+            for step in range(last + 1, len(steps)):
+                if mask ^ steps[step] in allowed:
+                    made.append((mask ^ steps[step], at, step, swap(value, steps[step])))
+        return made
+
+    def settle(items, sums):
+        values, sums = lax.optimization_barrier(([item[3] for item in items], sums))
+        fresh = [item[:3] + (value,) for item, value in zip(items, values)]
+        for mask, at, last, value in fresh:
+            held.setdefault(mask, []).insert(at, value)
+        return fresh, sums
+
+    first = [(steps[0], at, 0, swap(piece, steps[0])) for at, piece in enumerate(pieces)]
+    fresh, sums = settle(first[:1] + onward([(0, 0, 0, block)]), ())
+    late = first[1:]
+    stage = 0
     while fresh:
-        arrived = {}
-        for mask, last in fresh.items():
-            for at in range(last + 1, len(steps)):
-                if mask ^ steps[at] in allowed:
-                    arrived[mask ^ steps[at]] = (swap(held[mask], steps[at]), at)
-        if arrived:
-            values = [value for value, at in arrived.values()]
-            if len(held) > 1 and sums is None:
-                sums = work([held[step] for step in near_steps], [held[step] for step in far_steps])
-                values, sums = lax.optimization_barrier((values, sums))
-            else:
-                values = lax.optimization_barrier(values)
-            held.update(zip(arrived, values))
-        fresh = {mask: at for mask, (value, at) in arrived.items()}
-    return [held[mask] for mask in span(near_steps)], [held[mask] for mask in span(far_steps)], sums
+        made = onward(fresh) + late
+        late = []
+        if not made:
+            break
+        if stage < 2:
+            sums = work(stage, held, sums)
+        fresh, sums = settle(made, sums)
+        stage += 1
+    return held, sums
 
 
 def message_counts(steps):
@@ -408,7 +421,7 @@
     slots = send_tiles.shape[2]
     pairs = pair_local.shape[1]
     near_steps, far_steps = mask_steps(devices)
-    near_masks, far_masks = span(near_steps), span(far_steps)
+    near_masks, far_masks = span(near_steps), span(far_steps[::-1])
 
     live = jnp.arange(pairs) < pair_count[0]
     me = lax.axis_index(AXES).astype(jnp.int32)
@@ -422,22 +435,39 @@
     moments = local_moments(segments, tile_cell)
     list_rows, moment_rows = rows_of(lists, width), rows_of(moments, width)
     main = tile_groups(segments)
-    block = jnp.concatenate([main, list_rows, moment_rows], axis=0)
-
-    totals = (len(near_masks), len(far_masks))
-    early = [[0] + [masks.index(step) for step in steps] for masks, steps in ((near_masks, near_steps), (far_masks, far_steps))]
-
-    def early_pairs(near, far):
-        return run_pairs([block] + near + far, tiles, slots, main.shape[0], totals, early[0], early[1])
-
-    near_blocks, far_blocks, sums = spread(block, near_steps, far_steps, early_pairs)
+    cut = main.shape[0] // 2
+    pieces = [main[:cut], jnp.concatenate([main[cut:], list_rows, moment_rows], axis=0)]
+    block = jnp.concatenate(pieces, axis=0)
+
+    sizes = (tiles, slots, main.shape[0], len(near_masks), len(far_masks))
+    near_all, far_all = list(range(len(near_masks))), list(range(len(far_masks)))
+    state = {"near": (), "far": (), "combos": []}
+
+    def chosen_blocks(held):
+        return {k: held[mask] for k, mask in enumerate(near_masks) if mask in held}, {
+            k: held[mask] for k, mask in enumerate(far_masks) if mask in held
+        }
+
+    def work(stage, held, sums):
+        split = near_steps[0]
+        ready = [
+            [k for k in every if masks[k] in held and len(held[masks[k]]) == (2 if masks[k] & split else 1)]
+            for every, masks in ((near_all, near_masks), (far_all, far_masks))
+        ]
+        combos = [(i, j) for i in ready[0] for j in ready[1] if (i, j) not in state["combos"]]
+        done = (state["near"], state["far"])
+        state.update(near=ready[0], far=ready[1], combos=state["combos"] + combos)
+        return run_pairs(chosen_blocks(held), sizes, ready[0], ready[1], combos, done, sums)
+
+    held, sums = spread(block, pieces, near_steps + far_steps, set(near_masks) | set(far_masks), work)
     near_counts, far_counts = message_counts(near_steps), message_counts(far_steps)
+    combos = [(i, j) for i in near_all for j in far_all if (i, j) not in state["combos"]]
     outs = run_pairs(
-        near_blocks + far_blocks[1:], tiles, slots, main.shape[0], totals, list(range(totals[0])), list(range(totals[1])),
-        (near_counts, far_counts), early, sums,
+        chosen_blocks(held), sizes, near_all, far_all, combos, (state["near"], state["far"]), sums,
+        (near_counts, far_counts),
     )
     near_total = collect(outs[: len(near_counts)], near_counts, near_steps)
-    far_total = collect(outs[len(near_counts) :], far_counts, far_steps)
+    far_total = collect(outs[len(near_counts) :], far_counts, far_steps[::-1])
     forces = (near_total + far_total[: 3 * tiles]).reshape(3, tiles, width)
     moment_sums = far_total[3 * tiles :].reshape(-1)[: NCELL * 9].reshape(NCELL, 9)
     total_segments = tiles * width * devices

time: 107 us -> 113 us (1.056); the launches traced: 108 us -> 112 us
  Pallas kernels: 27.2 us -> 39.7 us
  waiting for transfers between devices: 44 us -> 38 us
  starting transfers between devices: 24.2 us -> 21.9 us
    pallas_call x2 -> x3, Pallas kernels: 27.2 us -> 39.7 us  [run_pairs(): pl.pallas_call(kernel, out_shape=[jax.ShapeDtypeStruct(shape, jnp.float32...]
    ppermute x17 -> x21, waiting for transfers between devices: 44 us -> 38 us  [swap(): return lax.ppermute(value, AXES, [(k, k ^ mask) for k in range(devices)])]
    ppermute x17 -> x21, starting transfers between devices: 24.2 us -> 21.9 us  [swap(): return lax.ppermute(value, AXES, [(k, k ^ mask) for k in range(devices)])]
    unnamed x38 -> x50, local copies, waits for them, and re-layouts: 3.96 us -> 3.1 us
  transfers between devices with their start and end apart: 17 -> 21, of which waited for: 7 -> 9; matrix products, arithmetic and copies ran while one was open for 3% -> 3% of each run, Pallas kernels for 9% -> 20%
where the time goes in v6:
time: 113 us; the launch traced here: 112 us
  Pallas kernels  39.7 us (35%)
  waiting for transfers between devices  38 us (34%)
  starting transfers between devices  21.9 us (19%)
  local copies, waits for them, and re-layouts  5.98 us (5%)
  other arithmetic  4.53 us (4%)
    pallas_call x3, Pallas kernels, run_pairs(): pl.pallas_call(kernel, out_shape=[jax.ShapeDtypeStruct(shape, jnp.float32...  39.7 us
    ppermute x21, waiting for transfers between devices, swap(): return lax.ppermute(value, AXES, [(k, k ^ mask) for k in range(devices)])  38 us
    ppermute x21, starting transfers between devices, swap(): return lax.ppermute(value, AXES, [(k, k ^ mask) for k in range(devices)])  21.9 us
    unnamed x50, local copies, waits for them, and re-layouts  3.1 us
  transfers between devices with their start and end apart: 21, of which 9 were waited for; matrix products, arithmetic and copies ran while one was open for 3% of the time, Pallas kernels for 20%

profile of v6, /device:TPU:0, one launch (start us, length us, event | category | flops | bytes accessed | tf_op | source)
XLA Modules:
  0.0 111.8 jit_solution(2969068460589332405)
XLA Ops:
  0.0 1.0 fusion.14
  1.1 1.1 copy-done.6
  2.3 0.1 add.96
  3.1 0.3 select_reduce_fusion
  3.4 0.6 select_reduce_fusion.1
  4.1 0.3 multiply_reduce_fusion.1
  4.4 0.6 copy-done.23
  5.1 0.1 fusion.8
  5.2 0.1 reshape.128
  5.4 0.2 copy.32
  5.6 0.6 slice-done.1
  6.3 0.1 copy.33
  6.4 0.1 pad_maximum_fusion.4
  6.6 3.0 %collective-permute-start.1 = (f32[146,8,128]{2,1,0:T(8,128)S(1)}, f32[146,8,128]{2,1,0:T(8,128)S(1)}, u32[]{:S(2)}, u32[]{:S(2)}) collective-permute-start(f32[146,8,128]{2,1,0:T(8,128)S(1)} %pad_maximum_fusion.refs_0_), channel_id=1, source_target_pairs={{0,2},{1,3},{2,0},{3,1},{4,6},{5,7},{6,4},{7,5},{8,10},{9,11},{10,... | collective-permute-start | bytes 1794056 | tf_op jit(solution)/shard_map/ppermute | solution.py:331
  9.6 1.6 %collective-permute-start.3 = (f32[146,8,128]{2,1,0:T(8,128)S(1)}, f32[146,8,128]{2,1,0:T(8,128)S(1)}, u32[]{:S(2)}, u32[]{:S(2)}) collective-permute-start(f32[146,8,128]{2,1,0:T(8,128)S(1)} %pad_maximum_fusion.refs_0_), channel_id=1, source_target_pairs={{0,8},{1,9},{2,10},{3,11},{4,12},{5,13},{6,14},{7,15},{8,0},{9,1},... | collective-permute-start | bytes 1794056 | tf_op jit(solution)/shard_map/ppermute | solution.py:331
  11.2 1.5 %collective-permute-start.4 = (f32[146,8,128]{2,1,0:T(8,128)S(1)}, f32[146,8,128]{2,1,0:T(8,128)S(1)}, u32[]{:S(2)}, u32[]{:S(2)}) collective-permute-start(f32[146,8,128]{2,1,0:T(8,128)S(1)} %pad_maximum_fusion.refs_0_), channel_id=1, source_target_pairs={{0,4},{1,5},{2,6},{3,7},{4,0},{5,1},{6,2},{7,3},{8,12},{9,13},{10,... | collective-permute-start | bytes 1794056 | tf_op jit(solution)/shard_map/ppermute | solution.py:331
  12.7 2.6 %collective-permute-start = (f32[72,8,128]{2,1,0:T(8,128)S(1)}, f32[72,8,128]{2,1,0:T(8,128)}, u32[]{:S(2)}, u32[]{:S(2)}) collective-permute-start(f32[72,8,128]{2,1,0:T(8,128)S(1)} %get-tuple-element.132), channel_id=1, source_target_pairs={{0,16},{1,17},{2,18},{3,19},{4,20},{5,21},{6,22},{7,23},{8,24},{9,... | collective-permute-start | bytes 884744 | tf_op jit(solution)/shard_map/ppermute | solution.py:331
  15.3 15.7 %collective-permute-done.refs_1_ = f32[72,8,128]{2,1,0:T(8,128)} collective-permute-done((f32[72,8,128]{2,1,0:T(8,128)S(1)}, f32[72,8,128]{2,1,0:T(8,128)}, u32[]{:S(2)}, u32[]{:S(2)}) %collective-permute-start) | collective-permute-done | bytes 294944 | tf_op jit(solution)/shard_map/ppermute | solution.py:331
  31.0 0.9 collective-permute-done.3.refs_4_.refs_7_.refs_13_
  31.9 1.6 %collective-permute-start.8 = (f32[146,8,128]{2,1,0:T(8,128)S(1)}, f32[146,8,128]{2,1,0:T(8,128)}, u32[]{:S(2)}, u32[]{:S(2)}) collective-permute-start(f32[146,8,128]{2,1,0:T(8,128)S(1)} %collective-permute-done.3.refs_4_.refs_7_.refs_13_), channel_id=1, source_target_pairs={{0,4},{1,5},{2,6},{3,7},{4,0},{5,1},{6,2},{7,3},{8,12},{9,13},{10,... | collective-permute-start | bytes 1794056 | tf_op jit(solution)/shard_map/ppermute | solution.py:331
  33.5 0.7 pad_maximum_fusion.1
  34.2 2.6 %collective-permute-start.9 = (f32[74,8,128]{2,1,0:T(8,128)}, f32[74,8,128]{2,1,0:T(8,128)S(1)}, u32[]{:S(2)}, u32[]{:S(2)}) collective-permute-start(f32[74,8,128]{2,1,0:T(8,128)} %pad_maximum_fusion.1), channel_id=1, source_target_pairs={{0,16},{1,17},{2,18},{3,19},{4,20},{5,21},{6,22},{7,23},{8,24},{9,... | collective-permute-start | bytes 909320 | tf_op jit(solution)/shard_map/ppermute | solution.py:331
  36.9 0.5 collective-permute-start.5
  37.4 9.8 %early_pairs.2 = (f32[1,384,128]{2,1,0:T(8,128)}, f32[1,384,128]{2,1,0:T(8,128)}, f32[1,384,128]{2,1,0:T(8,128)}, f32[1,384,128]{2,1,0:T(8,128)}, f32[1,384,128]{2,1,0:T(8,128)}, /*index=5*/f32[1,384,128]{2,1,0:T(8,128)}) custom-call(f32[146,8,128]{2,1,0:T(8,128)} %copy-done, f32[146,8,128]{2,1,0:T(8,128)} %copy-done.1, f32[146,8,128]{2,1,0:T(8,128)} %copy-done.2, ...), custom_call_target="tpu_custom_call" | custom-call | flops 786432000 | bytes 4194304 | tf_op jit(solution)/shard_map/early_pairs/pallas_call | solution.py:262
  47.2 3.9 %collective-permute-done.9.refs_2_ = f32[74,8,128]{2,1,0:T(8,128)S(1)} collective-permute-done((f32[74,8,128]{2,1,0:T(8,128)}, f32[74,8,128]{2,1,0:T(8,128)S(1)}, u32[]{:S(2)}, u32[]{:S(2)}) %collective-permute-start.9) | collective-permute-done | bytes 303136 | tf_op jit(solution)/shard_map/ppermute | solution.py:331
  51.1 0.6 collective-permute-start.11
  51.7 0.5 collective-permute-start.10
  52.2 12.7 %early_pairs.3 = (f32[1,384,128]{2,1,0:T(8,128)}, f32[1,384,128]{2,1,0:T(8,128)}, f32[1,384,128]{2,1,0:T(8,128)}, f32[1,384,128]{2,1,0:T(8,128)}, f32[1,384,128]...) custom-call(f32[146,8,128]{2,1,0:T(8,128)} %copy-done, ...), custom_call_target="tpu_custom_call" | custom-call | flops 950272000 | bytes 4194304 | tf_op jit(solution)/shard_map/early_pairs/pallas_call | solution.py:262
  65.0 1.6 %collective-permute-done.13.refs_11_ = f32[74,8,128]{2,1,0:T(8,128)S(1)} collective-permute-done((f32[74,8,128]{2,1,0:T(8,128)S(1)}, f32[74,8,128]{2,1,0:T(8,128)S(1)}, u32[]{:S(2)}, u32[]{:S(2)}) %collective-permute-start.13) | collective-permute-done | bytes 303136 | tf_op jit(solution)/shard_map/ppermute | solution.py:331
  66.6 0.7 copy-done.13
  67.3 17.3 %pairs.1 = (f32[1,384,128]{2,1,0:T(8,128)}, f32[1,384,128]{2,1,0:T(8,128)}, f32[1,384,128]{2,1,0:T(8,128)}, f32[1,384,128]{2,1,0:T(8,128)}, f32[2,384,128]{2,1,0...) custom-call(f32[146,8,128]{2,1,0:T(8,128)} %copy-done, ...), custom_call_target="tpu_custom_call" | custom-call | flops 1048576000 | bytes 4194304 | tf_op jit(solution)/shard_map/pairs/pallas_call | solution.py:262
  84.7 1.7 %collective-permute-start.15 = (f32[2,384,128]{2,1,0:T(8,128)}, f32[2,384,128]{2,1,0:T(8,128)S(1)}, u32[]{:S(2)}, u32[]{:S(2)}) collective-permute-start(f32[2,384,128]{2,1,0:T(8,128)} %get-tuple-element.123), channel_id=1, source_target_pairs={{0,1},{1,0},{2,3},{3,2},{4,5},{5,4},{6,7},{7,6},{8,9},{9,8},{10,11... | collective-permute-start | bytes 1179656 | tf_op jit(solution)/shard_map/ppermute | solution.py:331
  86.4 0.2 collective-permute-start.14
  86.5 1.4 %collective-permute-done.15 = f32[2,384,128]{2,1,0:T(8,128)S(1)} collective-permute-done((f32[2,384,128]{2,1,0:T(8,128)}, f32[2,384,128]{2,1,0:T(8,128)S(1)}, u32[]{:S(2)}, u32[]{:S(2)}) %collective-permute-start.15) | collective-permute-done | bytes 393248 | tf_op jit(solution)/shard_map/ppermute | solution.py:331
  87.9 1.1 %slice_add_fusion.5 = (f32[1,384,128]{2,1,0:T(8,128)S(1)}, f32[1,384,128]{2,1,0:T(8,128)S(1)}) fusion(f32[1,384,128]{2,1,0:T(8,128)} %get-tuple-element.122, f32[2,384,128]{2,1,0:T(8,128)S(1)} %collective-permute-done.15, f32[1,384,128]{2,1,0:T(8,128)} %get-tuple-element.125), kind=kLoop, calls=%fused_computation.16 | loop fusion | flops 98304 | bytes 1179648 | tf_op jit(solution)/shard_map/add | solution.py:405
  89.0 5.2 %collective-permute-start.17 = (f32[1,384,128]{2,1,0:T(8,128)S(1)}, f32[1,384,128]{2,1,0:T(8,128)S(1)}, u32[]{:S(2)}, u32[]{:S(2)}) collective-permute-start(f32[1,384,128]{2,1,0:T(8,128)S(1)} %get-tuple-element.137), channel_id=1, source_target_pairs={{0,2},{1,3},{2,0},{3,1},{4,6},{5,7},{6,4},{7,5},{8,10},{9,11},{10,... | collective-permute-start | bytes 589832 | tf_op jit(solution)/shard_map/ppermute | solution.py:331
  94.3 3.6 %collective-permute-done.19 = f32[2,392,128]{2,1,0:T(8,128)S(1)} collective-permute-done((f32[2,392,128]{2,1,0:T(8,128)}, f32[2,392,128]{2,1,0:T(8,128)S(1)}, u32[]{:S(2)}, u32[]{:S(2)}) %collective-permute-start.19) | collective-permute-done | bytes 401440 | tf_op jit(solution)/shard_map/ppermute | solution.py:331
  98.0 1.9 %collective-permute-done.17 = f32[1,384,128]{2,1,0:T(8,128)S(1)} collective-permute-done((f32[1,384,128]{2,1,0:T(8,128)S(1)}, f32[1,384,128]{2,1,0:T(8,128)S(1)}, u32[]{:S(2)}, u32[]{:S(2)}) %collective-permute-start.17) | collective-permute-done | bytes 196640 | tf_op jit(solution)/shard_map/ppermute | solution.py:331
  100.0 4.1 %collective-permute-done.20 = f32[1,392,128]{2,1,0:T(8,128)S(1)} collective-permute-done((f32[1,392,128]{2,1,0:T(8,128)S(1)}, f32[1,392,128]{2,1,0:T(8,128)S(1)}, u32[]{:S(2)}, u32[]{:S(2)}) %collective-permute-start.20) | collective-permute-done | bytes 200736 | tf_op jit(solution)/shard_map/ppermute | solution.py:331
  104.1 0.2 div.14
  104.4 0.5 copy.29
  105.0 0.1 copy.30
  105.1 0.2 fusion.6
  105.3 0.2 fusion.5
  105.6 0.2 multiply_reduce_fusion
  105.8 0.2 copy-done.7
  106.0 5.0 %collective-permute-done.18 = f32[1,384,128]{2,1,0:T(8,128)S(1)} collective-permute-done((f32[1,384,128]{2,1,0:T(8,128)S(1)}, f32[1,384,128]{2,1,0:T(8,128)S(1)}, u32[]{:S(2)}, u32[]{:S(2)}) %collective-permute-start.18) | collective-permute-done | bytes 196640 | tf_op jit(solution)/shard_map/ppermute | solution.py:331
  111.1 0.7 maximum_add_fusion
  (91 shorter events, 1.2 us)
Async XLA Ops:
  1.1 3.1 %copy-start.8 = (f32[128,3,128]{2,0,1:T(8,128)}, f32[128,3,128]{2,0,1:T(8,128)S(1)}, u32[]{:S(2)}) copy-start(f32[128,3,128]{2,0,1:T(8,128)S(1)} %get-tuple-element.134) | copy-start | bytes 589828
  1.1 1.1 %copy-start.6 = (f32[128,9,128]{2,0,1:T(8,128)S(1)}, f32[128,9,128]{2,0,1:T(8,128)}, u32[]{:S(2)}) copy-start(f32[128,9,128]{2,0,1:T(8,128)} %param.7) | copy-start | bytes 1769476
  1.1 1.1 %copy-start.22 = (s32[32]{0:T(128)S(1)}, s32[32]{0:T(128)}, u32[]{:S(2)}) copy-start(s32[32]{0:T(128)} %constant.32.clone) | copy-start | bytes 388
  1.1 1.3 %copy-start.21 = (s32[1,512]{1,0:T(1,128)S(1)}, s32[1,512]{1,0:T(1,128)}, u32[]{:S(2)}) copy-start(s32[1,512]{1,0:T(1,128)} %param.9) | copy-start | bytes 6148
  1.1 2.0 %copy-start.20 = (s32[1,512]{1,0:T(1,128)S(1)}, s32[1,512]{1,0:T(1,128)}, u32[]{:S(2)}) copy-start(s32[1,512]{1,0:T(1,128)} %param.10) | copy-start | bytes 6148
  1.1 2.3 %copy-start.19 = (s32[1,32,16]{1,2,0:T(8,128)S(1)}, s32[1,32,16]{1,2,0:T(8,128)}, u32[]{:S(2)}) copy-start(s32[1,32,16]{1,2,0:T(8,128)} %param.8) | copy-start | bytes 6148
  2.2 3.2 %slice-start = ((f32[128,9,128]{2,0,1:T(8,128)}), f32[128,6,128]{2,0,1:T(8,128)S(1)}, s32[]{:S(2)}) async-start(f32[128,9,128]{2,0,1:T(8,128)} %param.7), calls=%async_computation | async-start | bytes 786432 | tf_op jit(solution)/shard_map/slice | solution.py:289
  4.4 0.7 copy-start.23
  5.4 0.9 slice-start.1
  6.6 30.8 %copy-start = (f32[146,8,128]{2,1,0:T(8,128)}, f32[146,8,128]{2,1,0:T(8,128)S(1)}, u32[]{:S(2)}) copy-start(f32[146,8,128]{2,1,0:T(8,128)S(1)} %pad_maximum_fusion.refs_0_) | copy-start | bytes 1794052
  6.6 24.4 %collective-permute-start.1 = (f32[146,8,128]{2,1,0:T(8,128)S(1)}, f32[146,8,128]{2,1,0:T(8,128)S(1)}, u32[]{:S(2)}, u32[]{:S(2)}) collective-permute-start(f32[146,8,128]{2,1,0:T(8,128)S(1)} %pad_maximum_fusion.refs_0_), channel_id=1, source_target_pairs={{0,2},{1,3},{2,0},{3,1},{4,6},{5,7},{6,4},{7,5},{8,10},{9,11},{10,... | collective-permute-start | bytes 1794056 | tf_op jit(solution)/shard_map/ppermute | solution.py:331
  9.6 21.3 %collective-permute-start.2 = (f32[146,8,128]{2,1,0:T(8,128)S(1)}, f32[146,8,128]{2,1,0:T(8,128)S(1)}, u32[]{:S(2)}, u32[]{:S(2)}) collective-permute-start(f32[146,8,128]{2,1,0:T(8,128)S(1)} %pad_maximum_fusion.refs_0_), channel_id=1, source_target_pairs={{0,1},{1,0},{2,3},{3,2},{4,5},{5,4},{6,7},{7,6},{8,9},{9,8},{10,11... | collective-permute-start | bytes 1794056 | tf_op jit(solution)/shard_map/ppermute | solution.py:331
  9.6 22.2 %collective-permute-start.3 = (f32[146,8,128]{2,1,0:T(8,128)S(1)}, f32[146,8,128]{2,1,0:T(8,128)S(1)}, u32[]{:S(2)}, u32[]{:S(2)}) collective-permute-start(f32[146,8,128]{2,1,0:T(8,128)S(1)} %pad_maximum_fusion.refs_0_), channel_id=1, source_target_pairs={{0,8},{1,9},{2,10},{3,11},{4,12},{5,13},{6,14},{7,15},{8,0},{9,1},... | collective-permute-start | bytes 1794056 | tf_op jit(solution)/shard_map/ppermute | solution.py:331
  11.2 20.7 %collective-permute-start.4 = (f32[146,8,128]{2,1,0:T(8,128)S(1)}, f32[146,8,128]{2,1,0:T(8,128)S(1)}, u32[]{:S(2)}, u32[]{:S(2)}) collective-permute-start(f32[146,8,128]{2,1,0:T(8,128)S(1)} %pad_maximum_fusion.refs_0_), channel_id=1, source_target_pairs={{0,4},{1,5},{2,6},{3,7},{4,0},{5,1},{6,2},{7,3},{8,12},{9,13},{10,... | collective-permute-start | bytes 1794056 | tf_op jit(solution)/shard_map/ppermute | solution.py:331
  12.7 18.3 %collective-permute-start = (f32[72,8,128]{2,1,0:T(8,128)S(1)}, f32[72,8,128]{2,1,0:T(8,128)}, u32[]{:S(2)}, u32[]{:S(2)}) collective-permute-start(f32[72,8,128]{2,1,0:T(8,128)S(1)} %get-tuple-element.132), channel_id=1, source_target_pairs={{0,16},{1,17},{2,18},{3,19},{4,20},{5,21},{6,22},{7,23},{8,24},{9,... | collective-permute-start | bytes 884744 | tf_op jit(solution)/shard_map/ppermute | solution.py:331
  30.9 6.4 %copy-start.1 = (f32[146,8,128]{2,1,0:T(8,128)}, f32[146,8,128]{2,1,0:T(8,128)S(1)}, u32[]{:S(2)}) copy-start(f32[146,8,128]{2,1,0:T(8,128)S(1)} %collective-permute-done.1.refs_1_.refs_3_) | copy-start | bytes 1794052
  30.9 6.4 %copy-start.2 = (f32[146,8,128]{2,1,0:T(8,128)}, f32[146,8,128]{2,1,0:T(8,128)S(1)}, u32[]{:S(2)}) copy-start(f32[146,8,128]{2,1,0:T(8,128)S(1)} %collective-permute-done.2.refs_2_.refs_4_.refs_6_) | copy-start | bytes 1794052
  31.8 5.5 %copy-start.3 = (f32[146,8,128]{2,1,0:T(8,128)}, f32[146,8,128]{2,1,0:T(8,128)S(1)}, u32[]{:S(2)}) copy-start(f32[146,8,128]{2,1,0:T(8,128)S(1)} %collective-permute-done.3.refs_4_.refs_7_.refs_13_) | copy-start | bytes 1794052
  31.9 5.5 %copy-start.4 = (f32[146,8,128]{2,1,0:T(8,128)}, f32[146,8,128]{2,1,0:T(8,128)S(1)}, u32[]{:S(2)}) copy-start(f32[146,8,128]{2,1,0:T(8,128)S(1)} %collective-permute-done.4.refs_3_.refs_6_.refs_12_) | copy-start | bytes 1794052
  31.9 19.2 %collective-permute-start.7 = (f32[146,8,128]{2,1,0:T(8,128)S(1)}, f32[146,8,128]{2,1,0:T(8,128)S(1)}, u32[]{:S(2)}, u32[]{:S(2)}) collective-permute-start(f32[146,8,128]{2,1,0:T(8,128)S(1)} %collective-permute-done.1.refs_1_.refs_3_), channel_id=1, source_target_pairs={{0,1},{1,0},{2,3},{3,2},{4,5},{5,4},{6,7},{7,6},{8,9},{9,8},{10,11... | collective-permute-start | bytes 1794056 | tf_op jit(solution)/shard_map/ppermute | solution.py:331
  31.9 19.2 %collective-permute-start.8 = (f32[146,8,128]{2,1,0:T(8,128)S(1)}, f32[146,8,128]{2,1,0:T(8,128)}, u32[]{:S(2)}, u32[]{:S(2)}) collective-permute-start(f32[146,8,128]{2,1,0:T(8,128)S(1)} %collective-permute-done.3.refs_4_.refs_7_.refs_13_), channel_id=1, source_target_pairs={{0,4},{1,5},{2,6},{3,7},{4,0},{5,1},{6,2},{7,3},{8,12},{9,13},{10,... | collective-permute-start | bytes 1794056 | tf_op jit(solution)/shard_map/ppermute | solution.py:331
  34.2 16.9 %collective-permute-start.9 = (f32[74,8,128]{2,1,0:T(8,128)}, f32[74,8,128]{2,1,0:T(8,128)S(1)}, u32[]{:S(2)}, u32[]{:S(2)}) collective-permute-start(f32[74,8,128]{2,1,0:T(8,128)} %pad_maximum_fusion.1), channel_id=1, source_target_pairs={{0,16},{1,17},{2,18},{3,19},{4,20},{5,21},{6,22},{7,23},{8,24},{9,... | collective-permute-start | bytes 909320 | tf_op jit(solution)/shard_map/ppermute | solution.py:331
  36.9 14.2 %collective-permute-start.5 = (f32[72,8,128]{2,1,0:T(8,128)}, f32[72,8,128]{2,1,0:T(8,128)}, u32[]{:S(2)}, u32[]{:S(2)}) collective-permute-start(f32[72,8,128]{2,1,0:T(8,128)} %collective-permute-done.refs_1_), channel_id=1, source_target_pairs={{0,2},{1,3},{2,0},{3,1},{4,6},{5,7},{6,4},{7,5},{8,10},{9,11},{10,... | collective-permute-start | bytes 884744 | tf_op jit(solution)/shard_map/ppermute | solution.py:331
  37.4 13.7 %collective-permute-start.6 = (f32[72,8,128]{2,1,0:T(8,128)}, f32[72,8,128]{2,1,0:T(8,128)}, u32[]{:S(2)}, u32[]{:S(2)}) collective-permute-start(f32[72,8,128]{2,1,0:T(8,128)} %collective-permute-done.refs_1_), channel_id=1, source_target_pairs={{0,1},{1,0},{2,3},{3,2},{4,5},{5,4},{6,7},{7,6},{8,9},{9,8},{10,11... | collective-permute-start | bytes 884744 | tf_op jit(solution)/shard_map/ppermute | solution.py:331
  51.1 1.1 %copy-start.10 = (f32[74,8,128]{2,1,0:T(8,128)}, f32[74,8,128]{2,1,0:T(8,128)S(1)}, u32[]{:S(2)}) copy-start(f32[74,8,128]{2,1,0:T(8,128)S(1)} %collective-permute-done.9.refs_2_) | copy-start | bytes 909316
  51.1 1.1 copy-start.5
  51.1 13.8 %collective-permute-start.11 = (f32[74,8,128]{2,1,0:T(8,128)S(1)}, f32[74,8,128]{2,1,0:T(8,128)S(1)}, u32[]{:S(2)}, u32[]{:S(2)}) collective-permute-start(f32[74,8,128]{2,1,0:T(8,128)S(1)} %collective-permute-done.9.refs_2_), channel_id=1, source_target_pairs={{0,2},{1,3},{2,0},{3,1},{4,6},{5,7},{6,4},{7,5},{8,10},{9,11},{10,... | collective-permute-start | bytes 909320 | tf_op jit(solution)/shard_map/ppermute | solution.py:331
  51.7 13.2 %collective-permute-start.12 = (f32[74,8,128]{2,1,0:T(8,128)S(1)}, f32[74,8,128]{2,1,0:T(8,128)S(1)}, u32[]{:S(2)}, u32[]{:S(2)}) collective-permute-start(f32[74,8,128]{2,1,0:T(8,128)S(1)} %collective-permute-done.9.refs_2_), channel_id=1, source_target_pairs={{0,1},{1,0},{2,3},{3,2},{4,5},{5,4},{6,7},{7,6},{8,9},{9,8},{10,11... | collective-permute-start | bytes 909320 | tf_op jit(solution)/shard_map/ppermute | solution.py:331
  51.7 13.2 %collective-permute-start.10 = (f32[72,8,128]{2,1,0:T(8,128)}, f32[72,8,128]{2,1,0:T(8,128)S(1)}, u32[]{:S(2)}, u32[]{:S(2)}) collective-permute-start(f32[72,8,128]{2,1,0:T(8,128)} %collective-permute-done.5.refs_4_), channel_id=1, source_target_pairs={{0,1},{1,0},{2,3},{3,2},{4,5},{5,4},{6,7},{7,6},{8,9},{9,8},{10,11... | collective-permute-start | bytes 884744 | tf_op jit(solution)/shard_map/ppermute | solution.py:331
  64.9 1.7 %copy-start.14 = (f32[72,8,128]{2,1,0:T(8,128)}, f32[72,8,128]{2,1,0:T(8,128)S(1)}, u32[]{:S(2)}) copy-start(f32[72,8,128]{2,1,0:T(8,128)S(1)} %collective-permute-done.10.refs_10_) | copy-start | bytes 884740
  64.9 1.7 %copy-start.11 = (f32[74,8,128]{2,1,0:T(8,128)}, f32[74,8,128]{2,1,0:T(8,128)S(1)}, u32[]{:S(2)}) copy-start(f32[74,8,128]{2,1,0:T(8,128)S(1)} %collective-permute-done.11.refs_5_) | copy-start | bytes 909316
  64.9 1.7 %copy-start.12 = (f32[74,8,128]{2,1,0:T(8,128)}, f32[74,8,128]{2,1,0:T(8,128)S(1)}, u32[]{:S(2)}) copy-start(f32[74,8,128]{2,1,0:T(8,128)S(1)} %collective-permute-done.12.refs_8_) | copy-start | bytes 909316
  64.9 1.7 %collective-permute-start.13 = (f32[74,8,128]{2,1,0:T(8,128)S(1)}, f32[74,8,128]{2,1,0:T(8,128)S(1)}, u32[]{:S(2)}, u32[]{:S(2)}) collective-permute-start(f32[74,8,128]{2,1,0:T(8,128)S(1)} %collective-permute-done.11.refs_5_), channel_id=1, source_target_pairs={{0,1},{1,0},{2,3},{3,2},{4,5},{5,4},{6,7},{7,6},{8,9},{9,8},{10,11... | collective-permute-start | bytes 909320 | tf_op jit(solution)/shard_map/ppermute | solution.py:331
  66.6 0.7 copy-start.13
  84.7 3.3 %collective-permute-start.15 = (f32[2,384,128]{2,1,0:T(8,128)}, f32[2,384,128]{2,1,0:T(8,128)S(1)}, u32[]{:S(2)}, u32[]{:S(2)}) collective-permute-start(f32[2,384,128]{2,1,0:T(8,128)} %get-tuple-element.123), channel_id=1, source_target_pairs={{0,1},{1,0},{2,3},{3,2},{4,5},{5,4},{6,7},{7,6},{8,9},{9,8},{10,11... | collective-permute-start | bytes 1179656 | tf_op jit(solution)/shard_map/ppermute | solution.py:331
  86.4 11.5 %collective-permute-start.19 = (f32[2,392,128]{2,1,0:T(8,128)}, f32[2,392,128]{2,1,0:T(8,128)S(1)}, u32[]{:S(2)}, u32[]{:S(2)}) collective-permute-start(f32[2,392,128]{2,1,0:T(8,128)} %get-tuple-element.127), channel_id=1, source_target_pairs={{0,8},{1,9},{2,10},{3,11},{4,12},{5,13},{6,14},{7,15},{8,0},{9,1},... | collective-permute-start | bytes 1204232 | tf_op jit(solution)/shard_map/ppermute | solution.py:331
  86.4 11.6 %collective-permute-start.14 = (f32[2,384,128]{2,1,0:T(8,128)}, f32[2,384,128]{2,1,0:T(8,128)S(1)}, u32[]{:S(2)}, u32[]{:S(2)}) collective-permute-start(f32[2,384,128]{2,1,0:T(8,128)} %get-tuple-element.121), channel_id=1, source_target_pairs={{0,1},{1,0},{2,3},{3,2},{4,5},{5,4},{6,7},{7,6},{8,9},{9,8},{10,11... | collective-permute-start | bytes 1179656 | tf_op jit(solution)/shard_map/ppermute | solution.py:331
  87.9 9.9 %copy-start.16 = (f32[1,392,128]{2,1,0:T(8,128)S(1)}, f32[1,392,128]{2,1,0:T(8,128)}, u32[]{:S(2)}) copy-start(f32[1,392,128]{2,1,0:T(8,128)} %get-tuple-element.128) | copy-start | bytes 602116
  89.0 10.9 %collective-permute-start.17 = (f32[1,384,128]{2,1,0:T(8,128)S(1)}, f32[1,384,128]{2,1,0:T(8,128)S(1)}, u32[]{:S(2)}, u32[]{:S(2)}) collective-permute-start(f32[1,384,128]{2,1,0:T(8,128)S(1)} %get-tuple-element.137), channel_id=1, source_target_pairs={{0,2},{1,3},{2,0},{3,1},{4,6},{5,7},{6,4},{7,5},{8,10},{9,11},{10,... | collective-permute-start | bytes 589832 | tf_op jit(solution)/shard_map/ppermute | solution.py:331
  94.2 11.8 %collective-permute-start.16 = (f32[1,384,128]{2,1,0:T(8,128)S(1)}, f32[1,384,128]{2,1,0:T(8,128)S(1)}, u32[]{:S(2)}, u32[]{:S(2)}) collective-permute-start(f32[1,384,128]{2,1,0:T(8,128)S(1)} %get-tuple-element.136), channel_id=1, source_target_pairs={{0,2},{1,3},{2,0},{3,1},{4,6},{5,7},{6,4},{7,5},{8,10},{9,11},{10,... | collective-permute-start | bytes 589832 | tf_op jit(solution)/shard_map/ppermute | solution.py:331
  97.8 2.1 %copy-start.18 = (f32[1,384,128]{2,1,0:T(8,128)S(1)}, f32[1,384,128]{2,1,0:T(8,128)}, u32[]{:S(2)}) copy-start(f32[1,384,128]{2,1,0:T(8,128)} %get-tuple-element.124) | copy-start | bytes 589828
  97.9 6.2 %collective-permute-start.20 = (f32[1,392,128]{2,1,0:T(8,128)S(1)}, f32[1,392,128]{2,1,0:T(8,128)S(1)}, u32[]{:S(2)}, u32[]{:S(2)}) collective-permute-start(f32[1,392,128]{2,1,0:T(8,128)S(1)} %slice_add_fusion), channel_id=1, source_target_pairs={{0,4},{1,5},{2,6},{3,7},{4,0},{5,1},{6,2},{7,3},{8,12},{9,13},{10,... | collective-permute-start | bytes 602120 | tf_op jit(solution)/shard_map/ppermute | solution.py:331
  99.9 4.2 %copy-start.15 = (f32[1,392,128]{2,1,0:T(8,128)S(1)}, f32[1,392,128]{2,1,0:T(8,128)}, u32[]{:S(2)}) copy-start(f32[1,392,128]{2,1,0:T(8,128)} %get-tuple-element.126) | copy-start | bytes 602116
  99.9 11.1 %collective-permute-start.18 = (f32[1,384,128]{2,1,0:T(8,128)S(1)}, f32[1,384,128]{2,1,0:T(8,128)S(1)}, u32[]{:S(2)}, u32[]{:S(2)}) collective-permute-start(f32[1,384,128]{2,1,0:T(8,128)S(1)} %fusion.1), channel_id=1, source_target_pairs={{0,16},{1,17},{2,18},{3,19},{4,20},{5,21},{6,22},{7,23},{8,24},{9,... | collective-permute-start | bytes 589832 | tf_op jit(solution)/shard_map/ppermute | solution.py:331
  104.4 1.2 %copy-start.9 = (f32[128,3,128]{2,0,1:T(8,128)S(1)}, f32[128,3,128]{2,0,1:T(8,128)}, u32[]{:S(2)}) copy-start(f32[128,3,128]{2,0,1:T(8,128)} %copy-done.8) | copy-start | bytes 589828
  104.9 1.1 copy-start.7
  106.0 5.1 %copy-start.17 = (f32[1,384,128]{2,1,0:T(8,128)S(1)}, f32[1,384,128]{2,1,0:T(8,128)}, u32[]{:S(2)}) copy-start(f32[1,384,128]{2,1,0:T(8,128)} %get-tuple-element.120) | copy-start | bytes 589828

commit v7 on v5

--- a/solution.py
+++ b/solution.py
@@ -116,14 +116,15 @@
 def pair_kernel(plan, sources, earlier, refs_out, scratch):
     tiles, slots, list_group, near_total, far_total, near, far, done, final = plan
     near_number, far_number = len(near), len(far)
-    (blocks, lists, near_sum, far_sum, ids_vmem, ids, left_ref, right_ref, part_ref, sums_ref, spots_ref,
-     sems, list_sems) = scratch
+    (blocks, lists, near_sum, far_sum, ids_vmem, ids, left_ref, right_ref, part_ref, sums_ref, spots_ref, earlier_sums,
+     sems, list_sems, sum_sems) = scratch
     list_copies = [
         pltpu.make_async_copy(source.at[pl.ds(list_group, 2)], lists.at[k], list_sems.at[k])
         for k, source in enumerate(sources)
     ]
     copies = [pltpu.make_async_copy(source, blocks.at[k], sems.at[k]) for k, source in enumerate(sources)]
-    for copy in list_copies + copies:
+    sum_copies = [pltpu.make_async_copy(given.at[0], earlier_sums.at[k], sum_sems.at[k]) for k, given in enumerate(earlier)]
+    for copy in list_copies + copies + sum_copies:
         copy.start()
     near_sum[...] = jnp.zeros_like(near_sum)
     far_sum[...] = jnp.zeros_like(far_sum)
@@ -170,10 +171,10 @@
         live = jnp.logical_and(at >= 0, at < count)
         return live, near // tiles, near % tiles, far // tiles, far % tiles
 
-    def step(group, carry):
+    def add_sums(group):
         for k in range(GROUP):
-            live, near_block, near_tile, far_block, far_tile = pick(group - 2, k)
-            stash = lax.rem(group + 1, 3)
+            live, near_block, near_tile, far_block, far_tile = pick(group, k)
+            stash = lax.rem(group, 3)
             near_rows, far_rows = sums_ref[stash, k, 0], sums_ref[stash, k, 1]
             parts = part_ref[k]
             half = parts.shape[1] // 2
@@ -186,6 +187,8 @@
                     total = total[:, :half] + total[:, half:]
                 force = spots_ref[stash, k, spot] * jnp.broadcast_to(total[3:4], total.shape) - total
                 out[block, pl.ds(pl.multiple_of(tile * 8, 8), 8), :] += jnp.where(live, force, 0.0)
+
+    def couple():
         for k in range(GROUP):
             terms = matmul(left_ref[k], right_ref[k])
             inverse = lax.rsqrt(terms[:, :width])
@@ -193,6 +196,8 @@
             high, low = halves(coupling)
             part_ref[k, :, :width] = high
             part_ref[k, :, width:] = low
+
+    def build(group):
         for k in range(GROUP):
             live, near_block, near_tile, far_block, far_tile = pick(group, k)
             far_place = jnp.where(far_block > 0, far_block + (near_number - 1), 0)
@@ -207,10 +212,24 @@
             sums_ref[stash, k, 1] = far_rows
             spots_ref[stash, k, 0] = near_spot
             spots_ref[stash, k, 1] = far_spot
+
+    def step(group, carry):
+        add_sums(group - 2)
+        couple()
+        build(group)
         return carry
 
-    lax.fori_loop(0, (count + GROUP - 1) // GROUP + 2, step, 0)
-
+    groups = jnp.maximum((count + GROUP - 1) // GROUP, 2)
+    build(jnp.int32(0))
+    couple()
+    build(jnp.int32(1))
+    lax.fori_loop(2, groups, step, 0)
+    add_sums(groups - 2)
+    couple()
+    add_sums(groups - 1)
+
+    for copy in sum_copies:
+        copy.wait()
     at = 0
     if final:
         moments = functools.reduce(jnp.add, [lists[k, 1] for k in range(near_number)])
@@ -223,11 +242,11 @@
             if final:
                 row = old[0 if is_near else 1]
                 if block in row:
-                    known = earlier[row.index(block) + (0 if is_near else len(old[0]))]
+                    known = earlier_sums.at[row.index(block) + (0 if is_near else len(old[0]))]
             for axis in range(3):
                 rows = slice(axis * tiles, (axis + 1) * tiles)
                 value = total[block, pl.ds(axis, tiles, stride=8), :]
-                out[k, rows, :] = value if known is None else value + known[0, rows, :]
+                out[k, rows, :] = value if known is None else value + known[rows, :]
             if final and not is_near:
                 out[k, 3 * tiles :, :] = moments
             at += 1
@@ -250,6 +269,26 @@
     share = len(near) * len(far) / (totals[0] * totals[1])
     elements = int(share * slot_count / 3) * width * width
 
+    scratch = [
+        pltpu.VMEM((len(blocks),) + blocks[0].shape, jnp.float32),
+        pltpu.VMEM((len(blocks), 2, 8, width), jnp.float32),
+        pltpu.VMEM((near_number, 8 * tiles, width), jnp.float32),
+        pltpu.VMEM((far_number, 8 * tiles, width), jnp.float32),
+        pltpu.VMEM((8, slot_count), jnp.int32),
+        pltpu.SMEM((8, slot_count), jnp.int32),
+        pltpu.VMEM((GROUP, width, depth), jnp.bfloat16),
+        pltpu.VMEM((GROUP, depth, 2 * width), jnp.bfloat16),
+        pltpu.VMEM((GROUP, width, 2 * width), jnp.bfloat16),
+        pltpu.VMEM((3, GROUP, 2, sum_rows, width), jnp.bfloat16),
+        pltpu.VMEM((3, GROUP, 2, 8, width), jnp.float32),
+        pltpu.VMEM((max(len(earlier), 1), 3 * tiles, width), jnp.float32),
+        pltpu.SemaphoreType.DMA((len(blocks),)),
+        pltpu.SemaphoreType.DMA((len(blocks),)),
+        pltpu.SemaphoreType.DMA((max(len(earlier), 1),)),
+    ]
+    rows = 8 * blocks[0].shape[0] * len(blocks) + (11 * (near_number + far_number) + 3 * len(earlier)) * tiles
+    limit = 4 * width * rows + 8 * 1024 * 1024
+
     def kernel(*refs):
         given = len(blocks)
         known = given + len(earlier)
@@ -259,24 +298,10 @@
     return pl.pallas_call(
         kernel,
         out_shape=[jax.ShapeDtypeStruct(shape, jnp.float32) for shape in shapes],
-        in_specs=[hbm] * len(blocks) + [vmem] * len(earlier),
+        in_specs=[hbm] * (len(blocks) + len(earlier)),
         out_specs=[vmem] * len(shapes),
-        scratch_shapes=[
-            pltpu.VMEM((len(blocks),) + blocks[0].shape, jnp.float32),
-            pltpu.VMEM((len(blocks), 2, 8, width), jnp.float32),
-            pltpu.VMEM((near_number, 8 * tiles, width), jnp.float32),
-            pltpu.VMEM((far_number, 8 * tiles, width), jnp.float32),
-            pltpu.VMEM((8, slot_count), jnp.int32),
-            pltpu.SMEM((8, slot_count), jnp.int32),
-            pltpu.VMEM((GROUP, width, depth), jnp.bfloat16),
-            pltpu.VMEM((GROUP, depth, 2 * width), jnp.bfloat16),
-            pltpu.VMEM((GROUP, width, 2 * width), jnp.bfloat16),
-            pltpu.VMEM((3, GROUP, 2, sum_rows, width), jnp.bfloat16),
-            pltpu.VMEM((3, GROUP, 2, 8, width), jnp.float32),
-            pltpu.SemaphoreType.DMA((len(blocks),)),
-            pltpu.SemaphoreType.DMA((len(blocks),)),
-        ],
-        compiler_params=pltpu.CompilerParams(vmem_limit_bytes=60 * 1024 * 1024),
+        scratch_shapes=scratch,
+        compiler_params=pltpu.CompilerParams(vmem_limit_bytes=limit),
         cost_estimate=pl.CostEstimate(flops=1000 * elements, bytes_accessed=1 << 22, transcendentals=elements),
         name="pairs" if final else "early_pairs",
     )(*blocks, *earlier)

time: 107 us -> 102 us (0.953)
  starting transfers between devices: 24.2 us -> 17 us
  waiting for transfers between devices: 44 us -> 48.6 us
  local copies, waits for them, and re-layouts: 6.84 us -> 5.04 us
  other arithmetic: 3.81 us -> 2.73 us
    ppermute x17, starting transfers between devices: 24.2 us -> 17 us  [swap(): return lax.ppermute(value, AXES, [(k, k ^ mask) for k in range(devices)])]
    ppermute x17, waiting for transfers between devices: 44 us -> 48.6 us  [swap(): return lax.ppermute(value, AXES, [(k, k ^ mask) for k in range(devices)])]
    unnamed x38 -> x16, local copies, waits for them, and re-layouts: 3.96 us -> 2.16 us
  transfers between devices with their start and end apart: 17 -> 17, of which waited for: 7 -> 8; matrix products, arithmetic and copies ran while one was open for 3% -> 2% of each run, Pallas kernels for 9% -> 8%
where the time goes in v7:
time: 102 us; the launch traced here: 103 us
  waiting for transfers between devices  48.6 us (48%)
  Pallas kernels  27.8 us (27%)
  starting transfers between devices  17 us (17%)
  local copies, waits for them, and re-layouts  5.04 us (5%)
  other arithmetic  2.73 us (3%)
    ppermute x17, waiting for transfers between devices, swap(): return lax.ppermute(value, AXES, [(k, k ^ mask) for k in range(devices)])  48.6 us
    pallas_call x2, Pallas kernels, run_pairs(): pl.pallas_call(kernel, out_shape=[jax.ShapeDtypeStruct(shape, jnp.float32...  27.8 us
    ppermute x17, starting transfers between devices, swap(): return lax.ppermute(value, AXES, [(k, k ^ mask) for k in range(devices)])  17 us
    unnamed x16, local copies, waits for them, and re-layouts  2.16 us
  transfers between devices with their start and end apart: 17, of which 8 were waited for; matrix products, arithmetic and copies ran while one was open for 2% of the time, Pallas kernels for 8%

profile of v7, /device:TPU:0, one launch (start us, length us, event | category | flops | bytes accessed | tf_op | source)
XLA Modules:
  0.0 102.7 jit_solution(14079203485977146262)
XLA Ops:
  0.0 1.0 %fusion.14 = (f32[128,3,128]{2,0,1:T(8,128)S(1)}, f32[128,3,128]{2,0,1:T(8,128)S(1)}) fusion(f32[128,9,128]{2,0,1:T(8,128)} %param.7), kind=kLoop, calls=%fused_computation.47 | loop fusion | bytes 786432 | tf_op jit(solution)/shard_map/slice | solution.py:343
  1.1 1.0 copy-done
  2.1 0.1 iota_add_fusion
  2.2 0.1 add.96
  3.0 0.3 select_reduce_fusion
  3.3 0.1 iota_compare_fusion.4
  3.4 0.6 select_reduce_fusion.1
  4.0 0.1 concatenate.21
  4.1 0.3 multiply_reduce_fusion.1
  4.3 0.6 copy-done.6
  5.0 0.1 fusion.8
  5.1 0.1 reshape.128
  5.3 0.2 copy.32
  5.5 0.6 slice-done.1
  6.2 0.1 copy.33
  6.3 0.1 pad_maximum_fusion.refs_0_
  6.4 4.1 %collective-permute-start = (f32[146,8,128]{2,1,0:T(8,128)S(1)}, f32[146,8,128]{2,1,0:T(8,128)S(1)}, u32[]{:S(2)}, u32[]{:S(2)}) collective-permute-start(f32[146,8,128]{2,1,0:T(8,128)S(1)} %pad_maximum_fusion.refs_0_), channel_id=1, source_target_pairs={{0,16},{1,17},{2,18},{3,19},{4,20},{5,21},{6,22},{7,23},{8,24},{9,... | collective-permute-start | bytes 1794056 | tf_op jit(solution)/shard_map/ppermute | solution.py:353
  10.5 1.5 %collective-permute-start.1 = (f32[146,8,128]{2,1,0:T(8,128)S(1)}, f32[146,8,128]{2,1,0:T(8,128)S(1)}, u32[]{:S(2)}, u32[]{:S(2)}) collective-permute-start(f32[146,8,128]{2,1,0:T(8,128)S(1)} %pad_maximum_fusion.refs_0_), channel_id=1, source_target_pairs={{0,2},{1,3},{2,0},{3,1},{4,6},{5,7},{6,4},{7,5},{8,10},{9,11},{10,... | collective-permute-start | bytes 1794056 | tf_op jit(solution)/shard_map/ppermute | solution.py:353
  12.1 1.6 %collective-permute-start.3 = (f32[146,8,128]{2,1,0:T(8,128)S(1)}, f32[146,8,128]{2,1,0:T(8,128)S(1)}, u32[]{:S(2)}, u32[]{:S(2)}) collective-permute-start(f32[146,8,128]{2,1,0:T(8,128)S(1)} %pad_maximum_fusion.refs_0_), channel_id=1, source_target_pairs={{0,8},{1,9},{2,10},{3,11},{4,12},{5,13},{6,14},{7,15},{8,0},{9,1},... | collective-permute-start | bytes 1794056 | tf_op jit(solution)/shard_map/ppermute | solution.py:353
  13.6 1.5 %collective-permute-start.4 = (f32[146,8,128]{2,1,0:T(8,128)S(1)}, f32[146,8,128]{2,1,0:T(8,128)S(1)}, u32[]{:S(2)}, u32[]{:S(2)}) collective-permute-start(f32[146,8,128]{2,1,0:T(8,128)S(1)} %pad_maximum_fusion.refs_0_), channel_id=1, source_target_pairs={{0,4},{1,5},{2,6},{3,7},{4,0},{5,1},{6,2},{7,3},{8,12},{9,13},{10,... | collective-permute-start | bytes 1794056 | tf_op jit(solution)/shard_map/ppermute | solution.py:353
  15.1 21.8 %collective-permute-done.refs_1_ = f32[146,8,128]{2,1,0:T(8,128)S(1)} collective-permute-done((f32[146,8,128]{2,1,0:T(8,128)S(1)}, f32[146,8,128]{2,1,0:T(8,128)S(1)}, u32[]{:S(2)}, u32[]{:S(2)}) %collective-permute-start) | collective-permute-done | bytes 598048 | tf_op jit(solution)/shard_map/ppermute | solution.py:353
  37.0 2.7 %collective-permute-done.3.refs_4_.refs_8_ = f32[146,8,128]{2,1,0:T(8,128)S(1)} collective-permute-done((f32[146,8,128]{2,1,0:T(8,128)S(1)}, f32[146,8,128]{2,1,0:T(8,128)S(1)}, u32[]{:S(2)}, u32[]{:S(2)}) %collective-permute-start.3) | collective-permute-done | bytes 598048 | tf_op jit(solution)/shard_map/ppermute | solution.py:353
  39.6 0.6 collective-permute-start.5
  40.2 0.5 collective-permute-start.7
  40.7 1.5 %collective-permute-start.8 = (f32[146,8,128]{2,1,0:T(8,128)S(1)}, f32[146,8,128]{2,1,0:T(8,128)S(1)}, u32[]{:S(2)}, u32[]{:S(2)}) collective-permute-start(f32[146,8,128]{2,1,0:T(8,128)S(1)} %collective-permute-done.3.refs_4_.refs_8_), channel_id=1, source_target_pairs={{0,4},{1,5},{2,6},{3,7},{4,0},{5,1},{6,2},{7,3},{8,12},{9,13},{10,... | collective-permute-start | bytes 1794056 | tf_op jit(solution)/shard_map/ppermute | solution.py:353
  42.2 8.6 %early_pairs.1 = (f32[1,384,128]{2,1,0:T(8,128)S(1)}, f32[1,384,128]{2,1,0:T(8,128)S(1)}, f32[1,384,128]{2,1,0:T(8,128)S(1)}, f32[1,384,128]{2,1,0:T(8,128)S(1)}...) custom-call(f32[146,8,128]{2,1,0:T(8,128)S(1)} %pad_maximum_fusion.refs_0_, ...), custom_call_target="tpu_custom_call" | custom-call | flops 1048576000 | bytes 4194304 | tf_op jit(solution)/shard_map/early_pairs/pallas_call | solution.py:298
  50.8 4.0 %collective-permute-done.5.refs_3_ = f32[146,8,128]{2,1,0:T(8,128)S(1)} collective-permute-done((f32[146,8,128]{2,1,0:T(8,128)S(1)}, f32[146,8,128]{2,1,0:T(8,128)S(1)}, u32[]{:S(2)}, u32[]{:S(2)}) %collective-permute-start.5) | collective-permute-done | bytes 598048 | tf_op jit(solution)/shard_map/ppermute | solution.py:353
  54.8 1.3 %collective-permute-done.8.refs_10_ = f32[146,8,128]{2,1,0:T(8,128)S(1)} collective-permute-done((f32[146,8,128]{2,1,0:T(8,128)S(1)}, f32[146,8,128]{2,1,0:T(8,128)S(1)}, u32[]{:S(2)}, u32[]{:S(2)}) %collective-permute-start.8) | collective-permute-done | bytes 598048 | tf_op jit(solution)/shard_map/ppermute | solution.py:353
  56.1 2.0 %collective-permute-done.9.refs_7_ = f32[146,8,128]{2,1,0:T(8,128)S(1)} collective-permute-done((f32[146,8,128]{2,1,0:T(8,128)S(1)}, f32[146,8,128]{2,1,0:T(8,128)S(1)}, u32[]{:S(2)}, u32[]{:S(2)}) %collective-permute-start.9) | collective-permute-done | bytes 598048 | tf_op jit(solution)/shard_map/ppermute | solution.py:353
  58.1 19.2 %pairs.1 = (f32[1,384,128]{2,1,0:T(8,128)S(1)}, f32[1,384,128]{2,1,0:T(8,128)S(1)}, f32[1,384,128]{2,1,0:T(8,128)S(1)}, f32[1,384,128]{2,1,0:T(8,128)S(1)}, f32[...) custom-call(f32[146,8,128]{2,1,0:T(8,128)S(1)} %pad_maximum_fusion.r, ...), custom_call_target="tpu_custom_call" | custom-call | flops 2785280000 | bytes 4194304 | tf_op jit(solution)/shard_map/pairs/pallas_call | solution.py:298
  77.3 0.2 collective-permute-start.11
  77.5 0.4 collective-permute-start.10
  77.9 1.2 %collective-permute-done.11 = f32[2,384,128]{2,1,0:T(8,128)S(1)} collective-permute-done((f32[2,384,128]{2,1,0:T(8,128)S(1)}, f32[2,384,128]{2,1,0:T(8,128)S(1)}, u32[]{:S(2)}, u32[]{:S(2)}) %collective-permute-start.11) | collective-permute-done | bytes 393248 | tf_op jit(solution)/shard_map/ppermute | solution.py:353
  79.1 0.1 slice_add_fusion.5
  79.2 2.2 %collective-permute-start.13 = (f32[1,384,128]{2,1,0:T(8,128)S(1)}, f32[1,384,128]{2,1,0:T(8,128)S(1)}, u32[]{:S(2)}, u32[]{:S(2)}) collective-permute-start(f32[1,384,128]{2,1,0:T(8,128)S(1)} %get-tuple-element.75), channel_id=1, source_target_pairs={{0,2},{1,3},{2,0},{3,1},{4,6},{5,7},{6,4},{7,5},{8,10},{9,11},{10,... | collective-permute-start | bytes 589832 | tf_op jit(solution)/shard_map/ppermute | solution.py:353
  81.4 0.1 collective-permute-start.12
  81.5 7.6 %collective-permute-done.15 = f32[2,392,128]{2,1,0:T(8,128)S(1)} collective-permute-done((f32[2,392,128]{2,1,0:T(8,128)S(1)}, f32[2,392,128]{2,1,0:T(8,128)S(1)}, u32[]{:S(2)}, u32[]{:S(2)}) %collective-permute-start.15) | collective-permute-done | bytes 401440 | tf_op jit(solution)/shard_map/ppermute | solution.py:353
  89.2 0.1 collective-permute-start.16
  89.3 2.7 %collective-permute-start.14 = (f32[1,384,128]{2,1,0:T(8,128)S(1)}, f32[1,384,128]{2,1,0:T(8,128)S(1)}, u32[]{:S(2)}, u32[]{:S(2)}) collective-permute-start(f32[1,384,128]{2,1,0:T(8,128)S(1)} %fusion.1), channel_id=1, source_target_pairs={{0,16},{1,17},{2,18},{3,19},{4,20},{5,21},{6,22},{7,23},{8,24},{9,... | collective-permute-start | bytes 589832 | tf_op jit(solution)/shard_map/ppermute | solution.py:353
  92.0 7.9 %collective-permute-done.16 = f32[1,392,128]{2,1,0:T(8,128)S(1)} collective-permute-done((f32[1,392,128]{2,1,0:T(8,128)S(1)}, f32[1,392,128]{2,1,0:T(8,128)S(1)}, u32[]{:S(2)}, u32[]{:S(2)}) %collective-permute-start.16) | collective-permute-done | bytes 200736 | tf_op jit(solution)/shard_map/ppermute | solution.py:353
  100.0 0.2 div.14
  100.3 0.5 copy.29
  100.8 0.1 copy.30
  100.9 0.2 fusion.6
  101.2 0.2 fusion.5
  101.4 0.3 multiply_reduce_fusion
  101.7 0.1 copy-done.1
  102.0 0.7 maximum_add_fusion
  (46 shorter events, 0.4 us)
Async XLA Ops:
  1.1 1.1 %copy-start = (f32[128,9,128]{2,0,1:T(8,128)S(1)}, f32[128,9,128]{2,0,1:T(8,128)}, u32[]{:S(2)}) copy-start(f32[128,9,128]{2,0,1:T(8,128)} %param.7) | copy-start | bytes 1769476
  1.1 1.1 %copy-start.5 = (s32[32]{0:T(128)S(1)}, s32[32]{0:T(128)}, u32[]{:S(2)}) copy-start(s32[32]{0:T(128)} %constant.32.clone) | copy-start | bytes 388
  1.1 1.2 %copy-start.4 = (s32[1,512]{1,0:T(1,128)S(1)}, s32[1,512]{1,0:T(1,128)}, u32[]{:S(2)}) copy-start(s32[1,512]{1,0:T(1,128)} %param.9) | copy-start | bytes 6148
  1.1 1.9 %copy-start.3 = (s32[1,512]{1,0:T(1,128)S(1)}, s32[1,512]{1,0:T(1,128)}, u32[]{:S(2)}) copy-start(s32[1,512]{1,0:T(1,128)} %param.10) | copy-start | bytes 6148
  1.1 2.3 %copy-start.2 = (s32[1,32,16]{1,2,0:T(8,128)S(1)}, s32[1,32,16]{1,2,0:T(8,128)}, u32[]{:S(2)}) copy-start(s32[1,32,16]{1,2,0:T(8,128)} %param.8) | copy-start | bytes 6148
  2.1 3.2 %slice-start = ((f32[128,9,128]{2,0,1:T(8,128)}), f32[128,6,128]{2,0,1:T(8,128)S(1)}, s32[]{:S(2)}) async-start(f32[128,9,128]{2,0,1:T(8,128)} %param.7), calls=%async_computation | async-start | bytes 786432 | tf_op jit(solution)/shard_map/slice | solution.py:311
  4.3 0.7 copy-start.6
  5.3 0.9 slice-start.1
  6.4 30.5 %collective-permute-start = (f32[146,8,128]{2,1,0:T(8,128)S(1)}, f32[146,8,128]{2,1,0:T(8,128)S(1)}, u32[]{:S(2)}, u32[]{:S(2)}) collective-permute-start(f32[146,8,128]{2,1,0:T(8,128)S(1)} %pad_maximum_fusion.refs_0_), channel_id=1, source_target_pairs={{0,16},{1,17},{2,18},{3,19},{4,20},{5,21},{6,22},{7,23},{8,24},{9,... | collective-permute-start | bytes 1794056 | tf_op jit(solution)/shard_map/ppermute | solution.py:353
  10.5 26.4 %collective-permute-start.1 = (f32[146,8,128]{2,1,0:T(8,128)S(1)}, f32[146,8,128]{2,1,0:T(8,128)S(1)}, u32[]{:S(2)}, u32[]{:S(2)}) collective-permute-start(f32[146,8,128]{2,1,0:T(8,128)S(1)} %pad_maximum_fusion.refs_0_), channel_id=1, source_target_pairs={{0,2},{1,3},{2,0},{3,1},{4,6},{5,7},{6,4},{7,5},{8,10},{9,11},{10,... | collective-permute-start | bytes 1794056 | tf_op jit(solution)/shard_map/ppermute | solution.py:353
  12.1 24.9 %collective-permute-start.2 = (f32[146,8,128]{2,1,0:T(8,128)S(1)}, f32[146,8,128]{2,1,0:T(8,128)S(1)}, u32[]{:S(2)}, u32[]{:S(2)}) collective-permute-start(f32[146,8,128]{2,1,0:T(8,128)S(1)} %pad_maximum_fusion.refs_0_), channel_id=1, source_target_pairs={{0,1},{1,0},{2,3},{3,2},{4,5},{5,4},{6,7},{7,6},{8,9},{9,8},{10,11... | collective-permute-start | bytes 1794056 | tf_op jit(solution)/shard_map/ppermute | solution.py:353
  12.1 27.6 %collective-permute-start.3 = (f32[146,8,128]{2,1,0:T(8,128)S(1)}, f32[146,8,128]{2,1,0:T(8,128)S(1)}, u32[]{:S(2)}, u32[]{:S(2)}) collective-permute-start(f32[146,8,128]{2,1,0:T(8,128)S(1)} %pad_maximum_fusion.refs_0_), channel_id=1, source_target_pairs={{0,8},{1,9},{2,10},{3,11},{4,12},{5,13},{6,14},{7,15},{8,0},{9,1},... | collective-permute-start | bytes 1794056 | tf_op jit(solution)/shard_map/ppermute | solution.py:353
  13.6 26.0 %collective-permute-start.4 = (f32[146,8,128]{2,1,0:T(8,128)S(1)}, f32[146,8,128]{2,1,0:T(8,128)S(1)}, u32[]{:S(2)}, u32[]{:S(2)}) collective-permute-start(f32[146,8,128]{2,1,0:T(8,128)S(1)} %pad_maximum_fusion.refs_0_), channel_id=1, source_target_pairs={{0,4},{1,5},{2,6},{3,7},{4,0},{5,1},{6,2},{7,3},{8,12},{9,13},{10,... | collective-permute-start | bytes 1794056 | tf_op jit(solution)/shard_map/ppermute | solution.py:353
  39.6 15.1 %collective-permute-start.5 = (f32[146,8,128]{2,1,0:T(8,128)S(1)}, f32[146,8,128]{2,1,0:T(8,128)S(1)}, u32[]{:S(2)}, u32[]{:S(2)}) collective-permute-start(f32[146,8,128]{2,1,0:T(8,128)S(1)} %collective-permute-done.refs_1_), channel_id=1, source_target_pairs={{0,2},{1,3},{2,0},{3,1},{4,6},{5,7},{6,4},{7,5},{8,10},{9,11},{10,... | collective-permute-start | bytes 1794056 | tf_op jit(solution)/shard_map/ppermute | solution.py:353
  40.2 14.6 %collective-permute-start.6 = (f32[146,8,128]{2,1,0:T(8,128)S(1)}, f32[146,8,128]{2,1,0:T(8,128)S(1)}, u32[]{:S(2)}, u32[]{:S(2)}) collective-permute-start(f32[146,8,128]{2,1,0:T(8,128)S(1)} %collective-permute-done.refs_1_), channel_id=1, source_target_pairs={{0,1},{1,0},{2,3},{3,2},{4,5},{5,4},{6,7},{7,6},{8,9},{9,8},{10,11... | collective-permute-start | bytes 1794056 | tf_op jit(solution)/shard_map/ppermute | solution.py:353
  40.2 14.6 %collective-permute-start.7 = (f32[146,8,128]{2,1,0:T(8,128)S(1)}, f32[146,8,128]{2,1,0:T(8,128)S(1)}, u32[]{:S(2)}, u32[]{:S(2)}) collective-permute-start(f32[146,8,128]{2,1,0:T(8,128)S(1)} %collective-permute-done.1.refs_2_), channel_id=1, source_target_pairs={{0,1},{1,0},{2,3},{3,2},{4,5},{5,4},{6,7},{7,6},{8,9},{9,8},{10,11... | collective-permute-start | bytes 1794056 | tf_op jit(solution)/shard_map/ppermute | solution.py:353
  40.7 15.4 %collective-permute-start.8 = (f32[146,8,128]{2,1,0:T(8,128)S(1)}, f32[146,8,128]{2,1,0:T(8,128)S(1)}, u32[]{:S(2)}, u32[]{:S(2)}) collective-permute-start(f32[146,8,128]{2,1,0:T(8,128)S(1)} %collective-permute-done.3.refs_4_.refs_8_), channel_id=1, source_target_pairs={{0,4},{1,5},{2,6},{3,7},{4,0},{5,1},{6,2},{7,3},{8,12},{9,13},{10,... | collective-permute-start | bytes 1794056 | tf_op jit(solution)/shard_map/ppermute | solution.py:353
  56.1 2.0 %collective-permute-start.9 = (f32[146,8,128]{2,1,0:T(8,128)S(1)}, f32[146,8,128]{2,1,0:T(8,128)S(1)}, u32[]{:S(2)}, u32[]{:S(2)}) collective-permute-start(f32[146,8,128]{2,1,0:T(8,128)S(1)} %collective-permute-done.5.refs_3_), channel_id=1, source_target_pairs={{0,1},{1,0},{2,3},{3,2},{4,5},{5,4},{6,7},{7,6},{8,9},{9,8},{10,11... | collective-permute-start | bytes 1794056 | tf_op jit(solution)/shard_map/ppermute | solution.py:353
  77.3 1.8 %collective-permute-start.11 = (f32[2,384,128]{2,1,0:T(8,128)S(1)}, f32[2,384,128]{2,1,0:T(8,128)S(1)}, u32[]{:S(2)}, u32[]{:S(2)}) collective-permute-start(f32[2,384,128]{2,1,0:T(8,128)S(1)} %get-tuple-element.63), channel_id=1, source_target_pairs={{0,1},{1,0},{2,3},{3,2},{4,5},{5,4},{6,7},{7,6},{8,9},{9,8},{10,11... | collective-permute-start | bytes 1179656 | tf_op jit(solution)/shard_map/ppermute | solution.py:353
  77.5 11.6 %collective-permute-start.15 = (f32[2,392,128]{2,1,0:T(8,128)S(1)}, f32[2,392,128]{2,1,0:T(8,128)S(1)}, u32[]{:S(2)}, u32[]{:S(2)}) collective-permute-start(f32[2,392,128]{2,1,0:T(8,128)S(1)} %get-tuple-element.67), channel_id=1, source_target_pairs={{0,4},{1,5},{2,6},{3,7},{4,0},{5,1},{6,2},{7,3},{8,12},{9,13},{10,... | collective-permute-start | bytes 1204232 | tf_op jit(solution)/shard_map/ppermute | solution.py:353
  77.5 11.7 %collective-permute-start.10 = (f32[2,384,128]{2,1,0:T(8,128)S(1)}, f32[2,384,128]{2,1,0:T(8,128)S(1)}, u32[]{:S(2)}, u32[]{:S(2)}) collective-permute-start(f32[2,384,128]{2,1,0:T(8,128)S(1)} %get-tuple-element.61), channel_id=1, source_target_pairs={{0,1},{1,0},{2,3},{3,2},{4,5},{5,4},{6,7},{7,6},{8,9},{9,8},{10,11... | collective-permute-start | bytes 1179656 | tf_op jit(solution)/shard_map/ppermute | solution.py:353
  79.2 10.1 %collective-permute-start.13 = (f32[1,384,128]{2,1,0:T(8,128)S(1)}, f32[1,384,128]{2,1,0:T(8,128)S(1)}, u32[]{:S(2)}, u32[]{:S(2)}) collective-permute-start(f32[1,384,128]{2,1,0:T(8,128)S(1)} %get-tuple-element.75), channel_id=1, source_target_pairs={{0,2},{1,3},{2,0},{3,1},{4,6},{5,7},{6,4},{7,5},{8,10},{9,11},{10,... | collective-permute-start | bytes 589832 | tf_op jit(solution)/shard_map/ppermute | solution.py:353
  81.4 20.5 %collective-permute-start.12 = (f32[1,384,128]{2,1,0:T(8,128)S(1)}, f32[1,384,128]{2,1,0:T(8,128)S(1)}, u32[]{:S(2)}, u32[]{:S(2)}) collective-permute-start(f32[1,384,128]{2,1,0:T(8,128)S(1)} %get-tuple-element.74), channel_id=1, source_target_pairs={{0,2},{1,3},{2,0},{3,1},{4,6},{5,7},{6,4},{7,5},{8,10},{9,11},{10,... | collective-permute-start | bytes 589832 | tf_op jit(solution)/shard_map/ppermute | solution.py:353
  89.2 10.8 %collective-permute-start.16 = (f32[1,392,128]{2,1,0:T(8,128)S(1)}, f32[1,392,128]{2,1,0:T(8,128)S(1)}, u32[]{:S(2)}, u32[]{:S(2)}) collective-permute-start(f32[1,392,128]{2,1,0:T(8,128)S(1)} %slice_add_fusion), channel_id=1, source_target_pairs={{0,8},{1,9},{2,10},{3,11},{4,12},{5,13},{6,14},{7,15},{8,0},{9,1},... | collective-permute-start | bytes 602120 | tf_op jit(solution)/shard_map/ppermute | solution.py:353
  89.3 12.6 %collective-permute-start.14 = (f32[1,384,128]{2,1,0:T(8,128)S(1)}, f32[1,384,128]{2,1,0:T(8,128)S(1)}, u32[]{:S(2)}, u32[]{:S(2)}) collective-permute-start(f32[1,384,128]{2,1,0:T(8,128)S(1)} %fusion.1), channel_id=1, source_target_pairs={{0,16},{1,17},{2,18},{3,19},{4,20},{5,21},{6,22},{7,23},{8,24},{9,... | collective-permute-start | bytes 589832 | tf_op jit(solution)/shard_map/ppermute | solution.py:353
  100.8 1.1 %copy-start.1 = (f32[128,9,128]{2,0,1:T(8,128)S(1)}, f32[128,9,128]{2,0,1:T(8,128)}, u32[]{:S(2)}) copy-start(f32[128,9,128]{2,0,1:T(8,128)} %param.7) | copy-start | bytes 1769476

commit v8 on v7

--- a/solution.py
+++ b/solution.py
@@ -302,7 +302,7 @@
         out_specs=[vmem] * len(shapes),
         scratch_shapes=scratch,
         compiler_params=pltpu.CompilerParams(vmem_limit_bytes=limit),
-        cost_estimate=pl.CostEstimate(flops=1000 * elements, bytes_accessed=1 << 22, transcendentals=elements),
+        cost_estimate=pl.CostEstimate(flops=(1000 if final else 1) * elements, bytes_accessed=1 << 16, transcendentals=0),
         name="pairs" if final else "early_pairs",
     )(*blocks, *earlier)
 
@@ -381,13 +381,14 @@
                 if mask ^ steps[at] in allowed:
                     arrived[mask ^ steps[at]] = (swap(held[mask], steps[at]), at)
         if arrived:
-            values = [value for value, at in arrived.values()]
+            quick, slow = [], list(arrived)
             if len(held) > 1 and sums is None:
-                sums = work([held[step] for step in near_steps], [held[step] for step in far_steps])
-                values, sums = lax.optimization_barrier((values, sums))
-            else:
-                values = lax.optimization_barrier(values)
-            held.update(zip(arrived, values))
+                quick = [mask for mask in arrived if arrived[mask][1] == len(near_steps) - 1]
+                slow = [mask for mask in arrived if mask not in quick]
+                held.update(zip(quick, lax.optimization_barrier([arrived[mask][0] for mask in quick])))
+                sums = work(held)
+            values, sums = lax.optimization_barrier(([arrived[mask][0] for mask in slow], sums))
+            held.update(zip(slow, values))
         fresh = {mask: at for mask, (value, at) in arrived.items()}
     return [held[mask] for mask in span(near_steps)], [held[mask] for mask in span(far_steps)], sums
 
@@ -450,10 +451,12 @@
     block = jnp.concatenate([main, list_rows, moment_rows], axis=0)
 
     totals = (len(near_masks), len(far_masks))
-    early = [[0] + [masks.index(step) for step in steps] for masks, steps in ((near_masks, near_steps), (far_masks, far_steps))]
-
-    def early_pairs(near, far):
-        return run_pairs([block] + near + far, tiles, slots, main.shape[0], totals, early[0], early[1])
+    early = []
+
+    def early_pairs(held):
+        early.extend([k for k, mask in enumerate(masks) if mask in held] for masks in (near_masks, far_masks))
+        blocks = [held[near_masks[k]] for k in early[0]] + [held[far_masks[k]] for k in early[1][1:]]
+        return run_pairs(blocks, tiles, slots, main.shape[0], totals, early[0], early[1])
 
     near_blocks, far_blocks, sums = spread(block, near_steps, far_steps, early_pairs)
     near_counts, far_counts = message_counts(near_steps), message_counts(far_steps)

time: 102 us -> 101 us (level); the launches traced: 103 us -> 99.6 us
  waiting for transfers between devices: 48.6 us -> 43.3 us
  starting transfers between devices: 17 us -> 20.3 us
  Pallas kernels: 27.8 us -> 26.7 us
    ppermute x17, waiting for transfers between devices: 48.6 us -> 43.3 us  [swap(): return lax.ppermute(value, AXES, [(k, k ^ mask) for k in range(devices)])]
    ppermute x17, starting transfers between devices: 17 us -> 20.3 us  [swap(): return lax.ppermute(value, AXES, [(k, k ^ mask) for k in range(devices)])]
    pallas_call x2, Pallas kernels: 27.8 us -> 26.7 us  [run_pairs(): pl.pallas_call(kernel, out_shape=[jax.ShapeDtypeStruct(shape, jnp.float32...]
  transfers between devices with their start and end apart: 17 -> 17, of which waited for: 8 -> 10; matrix products, arithmetic and copies ran while one was open for 2% -> 2% of each run, Pallas kernels for 8% -> 13%
where the time goes in v8:
time: 101 us; the launch traced here: 99.6 us
  waiting for transfers between devices  43.3 us (43%)
  Pallas kernels  26.7 us (26%)
  starting transfers between devices  20.3 us (20%)
  local copies, waits for them, and re-layouts  5.04 us (5%)
  other arithmetic  2.72 us (3%)
    ppermute x17, waiting for transfers between devices, swap(): return lax.ppermute(value, AXES, [(k, k ^ mask) for k in range(devices)])  43.3 us
    pallas_call x2, Pallas kernels, run_pairs(): pl.pallas_call(kernel, out_shape=[jax.ShapeDtypeStruct(shape, jnp.float32...  26.7 us
    ppermute x17, starting transfers between devices, swap(): return lax.ppermute(value, AXES, [(k, k ^ mask) for k in range(devices)])  20.3 us
    unnamed x16, local copies, waits for them, and re-layouts  2.16 us
  transfers between devices with their start and end apart: 17, of which 10 were waited for; matrix products, arithmetic and copies ran while one was open for 2% of the time, Pallas kernels for 13%

profile of v8, /device:TPU:0, one launch (start us, length us, event | category | flops | bytes accessed | tf_op | source)
XLA Modules:
  0.0 99.6 jit_solution(15923500281484615361)
XLA Ops:
  0.0 1.0 %fusion.14 = (f32[128,3,128]{2,0,1:T(8,128)S(1)}, f32[128,3,128]{2,0,1:T(8,128)S(1)}) fusion(f32[128,9,128]{2,0,1:T(8,128)} %param.7), kind=kLoop, calls=%fused_computation.47 | loop fusion | bytes 786432 | tf_op jit(solution)/shard_map/slice | solution.py:343
  1.1 1.0 %copy-done = f32[128,9,128]{2,0,1:T(8,128)S(1)} copy-done((f32[128,9,128]{2,0,1:T(8,128)S(1)}, f32[128,9,128]{2,0,1:T(8,128)}, u32[]{:S(2)}) %copy-start) | copy-done | bytes 589848
  2.2 0.1 add.96
  3.0 0.3 select_reduce_fusion
  3.3 0.1 iota_compare_fusion.4
  3.4 0.6 select_reduce_fusion.1
  4.0 0.1 concatenate.21
  4.1 0.3 multiply_reduce_fusion.1
  4.3 0.6 copy-done.6
  5.0 0.1 fusion.8
  5.1 0.1 reshape.128
  5.3 0.2 copy.32
  5.5 0.6 slice-done.1
  6.2 0.1 copy.33
  6.3 0.1 pad_maximum_fusion.refs_0_
  6.4 4.1 %collective-permute-start = (f32[146,8,128]{2,1,0:T(8,128)S(1)}, f32[146,8,128]{2,1,0:T(8,128)S(1)}, u32[]{:S(2)}, u32[]{:S(2)}) collective-permute-start(f32[146,8,128]{2,1,0:T(8,128)S(1)} %pad_maximum_fusion.refs_0_), channel_id=1, source_target_pairs={{0,16},{1,17},{2,18},{3,19},{4,20},{5,21},{6,22},{7,23},{8,24},{9,... | collective-permute-start | bytes 1794056 | tf_op jit(solution)/shard_map/ppermute | solution.py:353
  10.5 1.5 %collective-permute-start.1 = (f32[146,8,128]{2,1,0:T(8,128)S(1)}, f32[146,8,128]{2,1,0:T(8,128)S(1)}, u32[]{:S(2)}, u32[]{:S(2)}) collective-permute-start(f32[146,8,128]{2,1,0:T(8,128)S(1)} %pad_maximum_fusion.refs_0_), channel_id=1, source_target_pairs={{0,2},{1,3},{2,0},{3,1},{4,6},{5,7},{6,4},{7,5},{8,10},{9,11},{10,... | collective-permute-start | bytes 1794056 | tf_op jit(solution)/shard_map/ppermute | solution.py:353
  12.1 1.6 %collective-permute-start.3 = (f32[146,8,128]{2,1,0:T(8,128)S(1)}, f32[146,8,128]{2,1,0:T(8,128)S(1)}, u32[]{:S(2)}, u32[]{:S(2)}) collective-permute-start(f32[146,8,128]{2,1,0:T(8,128)S(1)} %pad_maximum_fusion.refs_0_), channel_id=1, source_target_pairs={{0,8},{1,9},{2,10},{3,11},{4,12},{5,13},{6,14},{7,15},{8,0},{9,1},... | collective-permute-start | bytes 1794056 | tf_op jit(solution)/shard_map/ppermute | solution.py:353
  13.6 1.5 %collective-permute-start.4 = (f32[146,8,128]{2,1,0:T(8,128)S(1)}, f32[146,8,128]{2,1,0:T(8,128)S(1)}, u32[]{:S(2)}, u32[]{:S(2)}) collective-permute-start(f32[146,8,128]{2,1,0:T(8,128)S(1)} %pad_maximum_fusion.refs_0_), channel_id=1, source_target_pairs={{0,4},{1,5},{2,6},{3,7},{4,0},{5,1},{6,2},{7,3},{8,12},{9,13},{10,... | collective-permute-start | bytes 1794056 | tf_op jit(solution)/shard_map/ppermute | solution.py:353
  15.1 21.8 %collective-permute-done.refs_1_ = f32[146,8,128]{2,1,0:T(8,128)S(1)} collective-permute-done((f32[146,8,128]{2,1,0:T(8,128)S(1)}, f32[146,8,128]{2,1,0:T(8,128)S(1)}, u32[]{:S(2)}, u32[]{:S(2)}) %collective-permute-start) | collective-permute-done | bytes 598048 | tf_op jit(solution)/shard_map/ppermute | solution.py:353
  37.0 2.7 %collective-permute-done.3.refs_6_.refs_8_ = f32[146,8,128]{2,1,0:T(8,128)S(1)} collective-permute-done((f32[146,8,128]{2,1,0:T(8,128)S(1)}, f32[146,8,128]{2,1,0:T(8,128)S(1)}, u32[]{:S(2)}, u32[]{:S(2)}) %collective-permute-start.3) | collective-permute-done | bytes 598048 | tf_op jit(solution)/shard_map/ppermute | solution.py:353
  39.6 0.5 collective-permute-start.8
  40.1 0.6 collective-permute-start.5
  40.7 1.5 %collective-permute-start.6 = (f32[146,8,128]{2,1,0:T(8,128)S(1)}, f32[146,8,128]{2,1,0:T(8,128)S(1)}, u32[]{:S(2)}, u32[]{:S(2)}) collective-permute-start(f32[146,8,128]{2,1,0:T(8,128)S(1)} %collective-permute-done.3.refs_6_.refs_8_), channel_id=1, source_target_pairs={{0,4},{1,5},{2,6},{3,7},{4,0},{5,1},{6,2},{7,3},{8,12},{9,13},{10,... | collective-permute-start | bytes 1794056 | tf_op jit(solution)/shard_map/ppermute | solution.py:353
  42.2 0.3 collective-permute-done.8.refs_5_.refs_6_
  42.5 12.7 %early_pairs.1 = (f32[1,384,128]{2,1,0:T(8,128)S(1)}, f32[1,384,128]{2,1,0:T(8,128)S(1)}, f32[1,384,128]{2,1,0:T(8,128)S(1)}, f32[1,384,128]{2,1,0:T(8,128)S(1)}...) custom-call(f32[146,8,128]{2,1,0:T(8,128)S(1)} %pad_maximum_fusion.r, ...), custom_call_target="tpu_custom_call" | custom-call | flops 1572864 | bytes 65536 | tf_op jit(solution)/shard_map/early_pairs/pallas_call | solution.py:298
  55.3 0.3 collective-permute-done.5.refs_3_
  55.6 0.3 collective-permute-done.6.refs_10_
  55.8 2.0 %collective-permute-done.9.refs_7_ = f32[146,8,128]{2,1,0:T(8,128)S(1)} collective-permute-done((f32[146,8,128]{2,1,0:T(8,128)S(1)}, f32[146,8,128]{2,1,0:T(8,128)S(1)}, u32[]{:S(2)}, u32[]{:S(2)}) %collective-permute-start.9) | collective-permute-done | bytes 598048 | tf_op jit(solution)/shard_map/ppermute | solution.py:353
  57.8 14.0 %pairs.1 = (f32[1,384,128]{2,1,0:T(8,128)S(1)}, f32[1,384,128]{2,1,0:T(8,128)S(1)}, f32[1,384,128]{2,1,0:T(8,128)S(1)}, f32[1,384,128]{2,1,0:T(8,128)S(1)}, f32[...) custom-call(f32[146,8,128]{2,1,0:T(8,128)S(1)} %pad_maximum_fusion.r, ...), custom_call_target="tpu_custom_call" | custom-call | flops 2785280000 | bytes 65536 | tf_op jit(solution)/shard_map/pairs/pallas_call | solution.py:298
  71.8 1.7 %collective-permute-start.11 = (f32[2,384,128]{2,1,0:T(8,128)S(1)}, f32[2,384,128]{2,1,0:T(8,128)S(1)}, u32[]{:S(2)}, u32[]{:S(2)}) collective-permute-start(f32[2,384,128]{2,1,0:T(8,128)S(1)} %get-tuple-element.91), channel_id=1, source_target_pairs={{0,1},{1,0},{2,3},{3,2},{4,5},{5,4},{6,7},{7,6},{8,9},{9,8},{10,11... | collective-permute-start | bytes 1179656 | tf_op jit(solution)/shard_map/ppermute | solution.py:353
  73.5 0.2 collective-permute-start.10
  73.7 1.2 %collective-permute-done.11 = f32[2,384,128]{2,1,0:T(8,128)S(1)} collective-permute-done((f32[2,384,128]{2,1,0:T(8,128)S(1)}, f32[2,384,128]{2,1,0:T(8,128)S(1)}, u32[]{:S(2)}, u32[]{:S(2)}) %collective-permute-start.11) | collective-permute-done | bytes 393248 | tf_op jit(solution)/shard_map/ppermute | solution.py:353
  74.9 1.8 %collective-permute-start.13 = (f32[1,384,128]{2,1,0:T(8,128)S(1)}, f32[1,384,128]{2,1,0:T(8,128)S(1)}, u32[]{:S(2)}, u32[]{:S(2)}) collective-permute-start(f32[1,384,128]{2,1,0:T(8,128)S(1)} %get-tuple-element.103), channel_id=1, source_target_pairs={{0,2},{1,3},{2,0},{3,1},{4,6},{5,7},{6,4},{7,5},{8,10},{9,11},{10,... | collective-permute-start | bytes 589832 | tf_op jit(solution)/shard_map/ppermute | solution.py:353
  76.7 0.3 collective-permute-start.12
  77.0 7.8 %collective-permute-done.15 = f32[2,392,128]{2,1,0:T(8,128)S(1)} collective-permute-done((f32[2,392,128]{2,1,0:T(8,128)S(1)}, f32[2,392,128]{2,1,0:T(8,128)S(1)}, u32[]{:S(2)}, u32[]{:S(2)}) %collective-permute-start.15) | collective-permute-done | bytes 401440 | tf_op jit(solution)/shard_map/ppermute | solution.py:353
  84.8 3.0 %collective-permute-start.16 = (f32[1,392,128]{2,1,0:T(8,128)S(1)}, f32[1,392,128]{2,1,0:T(8,128)S(1)}, u32[]{:S(2)}, u32[]{:S(2)}) collective-permute-start(f32[1,392,128]{2,1,0:T(8,128)S(1)} %slice_add_fusion), channel_id=1, source_target_pairs={{0,8},{1,9},{2,10},{3,11},{4,12},{5,13},{6,14},{7,15},{8,0},{9,1},... | collective-permute-start | bytes 602120 | tf_op jit(solution)/shard_map/ppermute | solution.py:353
  87.8 2.1 %collective-permute-start.14 = (f32[1,384,128]{2,1,0:T(8,128)S(1)}, f32[1,384,128]{2,1,0:T(8,128)S(1)}, u32[]{:S(2)}, u32[]{:S(2)}) collective-permute-start(f32[1,384,128]{2,1,0:T(8,128)S(1)} %fusion.1), channel_id=1, source_target_pairs={{0,16},{1,17},{2,18},{3,19},{4,20},{5,21},{6,22},{7,23},{8,24},{9,... | collective-permute-start | bytes 589832 | tf_op jit(solution)/shard_map/ppermute | solution.py:353
  90.0 6.0 %collective-permute-done.16 = f32[1,392,128]{2,1,0:T(8,128)S(1)} collective-permute-done((f32[1,392,128]{2,1,0:T(8,128)S(1)}, f32[1,392,128]{2,1,0:T(8,128)S(1)}, u32[]{:S(2)}, u32[]{:S(2)}) %collective-permute-start.16) | collective-permute-done | bytes 200736 | tf_op jit(solution)/shard_map/ppermute | solution.py:353
  96.1 0.2 div.14
  96.3 0.5 copy.29
  96.9 0.1 copy.30
  97.0 0.2 fusion.6
  97.2 0.2 fusion.5
  97.4 0.3 multiply_reduce_fusion
  97.7 0.1 copy-done.1
  97.9 0.9 collective-permute-done.14
  98.9 0.7 maximum_add_fusion
  (46 shorter events, 0.5 us)
Async XLA Ops:
  1.1 1.1 %copy-start = (f32[128,9,128]{2,0,1:T(8,128)S(1)}, f32[128,9,128]{2,0,1:T(8,128)}, u32[]{:S(2)}) copy-start(f32[128,9,128]{2,0,1:T(8,128)} %param.7) | copy-start | bytes 1769476
  1.1 1.1 %copy-start.5 = (s32[32]{0:T(128)S(1)}, s32[32]{0:T(128)}, u32[]{:S(2)}) copy-start(s32[32]{0:T(128)} %constant.32.clone) | copy-start | bytes 388
  1.1 1.2 %copy-start.4 = (s32[1,512]{1,0:T(1,128)S(1)}, s32[1,512]{1,0:T(1,128)}, u32[]{:S(2)}) copy-start(s32[1,512]{1,0:T(1,128)} %param.9) | copy-start | bytes 6148
  1.1 1.9 %copy-start.3 = (s32[1,512]{1,0:T(1,128)S(1)}, s32[1,512]{1,0:T(1,128)}, u32[]{:S(2)}) copy-start(s32[1,512]{1,0:T(1,128)} %param.10) | copy-start | bytes 6148
  1.1 2.3 %copy-start.2 = (s32[1,32,16]{1,2,0:T(8,128)S(1)}, s32[1,32,16]{1,2,0:T(8,128)}, u32[]{:S(2)}) copy-start(s32[1,32,16]{1,2,0:T(8,128)} %param.8) | copy-start | bytes 6148
  2.1 3.2 %slice-start = ((f32[128,9,128]{2,0,1:T(8,128)}), f32[128,6,128]{2,0,1:T(8,128)S(1)}, s32[]{:S(2)}) async-start(f32[128,9,128]{2,0,1:T(8,128)} %param.7), calls=%async_computation | async-start | bytes 786432 | tf_op jit(solution)/shard_map/slice | solution.py:311
  4.3 0.7 copy-start.6
  5.3 0.9 slice-start.1
  6.4 30.5 %collective-permute-start = (f32[146,8,128]{2,1,0:T(8,128)S(1)}, f32[146,8,128]{2,1,0:T(8,128)S(1)}, u32[]{:S(2)}, u32[]{:S(2)}) collective-permute-start(f32[146,8,128]{2,1,0:T(8,128)S(1)} %pad_maximum_fusion.refs_0_), channel_id=1, source_target_pairs={{0,16},{1,17},{2,18},{3,19},{4,20},{5,21},{6,22},{7,23},{8,24},{9,... | collective-permute-start | bytes 1794056 | tf_op jit(solution)/shard_map/ppermute | solution.py:353
  10.5 26.4 %collective-permute-start.1 = (f32[146,8,128]{2,1,0:T(8,128)S(1)}, f32[146,8,128]{2,1,0:T(8,128)S(1)}, u32[]{:S(2)}, u32[]{:S(2)}) collective-permute-start(f32[146,8,128]{2,1,0:T(8,128)S(1)} %pad_maximum_fusion.refs_0_), channel_id=1, source_target_pairs={{0,2},{1,3},{2,0},{3,1},{4,6},{5,7},{6,4},{7,5},{8,10},{9,11},{10,... | collective-permute-start | bytes 1794056 | tf_op jit(solution)/shard_map/ppermute | solution.py:353
  12.1 24.9 %collective-permute-start.2 = (f32[146,8,128]{2,1,0:T(8,128)S(1)}, f32[146,8,128]{2,1,0:T(8,128)S(1)}, u32[]{:S(2)}, u32[]{:S(2)}) collective-permute-start(f32[146,8,128]{2,1,0:T(8,128)S(1)} %pad_maximum_fusion.refs_0_), channel_id=1, source_target_pairs={{0,1},{1,0},{2,3},{3,2},{4,5},{5,4},{6,7},{7,6},{8,9},{9,8},{10,11... | collective-permute-start | bytes 1794056 | tf_op jit(solution)/shard_map/ppermute | solution.py:353
  12.1 27.6 %collective-permute-start.3 = (f32[146,8,128]{2,1,0:T(8,128)S(1)}, f32[146,8,128]{2,1,0:T(8,128)S(1)}, u32[]{:S(2)}, u32[]{:S(2)}) collective-permute-start(f32[146,8,128]{2,1,0:T(8,128)S(1)} %pad_maximum_fusion.refs_0_), channel_id=1, source_target_pairs={{0,8},{1,9},{2,10},{3,11},{4,12},{5,13},{6,14},{7,15},{8,0},{9,1},... | collective-permute-start | bytes 1794056 | tf_op jit(solution)/shard_map/ppermute | solution.py:353
  13.6 26.0 %collective-permute-start.4 = (f32[146,8,128]{2,1,0:T(8,128)S(1)}, f32[146,8,128]{2,1,0:T(8,128)S(1)}, u32[]{:S(2)}, u32[]{:S(2)}) collective-permute-start(f32[146,8,128]{2,1,0:T(8,128)S(1)} %pad_maximum_fusion.refs_0_), channel_id=1, source_target_pairs={{0,4},{1,5},{2,6},{3,7},{4,0},{5,1},{6,2},{7,3},{8,12},{9,13},{10,... | collective-permute-start | bytes 1794056 | tf_op jit(solution)/shard_map/ppermute | solution.py:353
  39.6 2.6 %collective-permute-start.7 = (f32[146,8,128]{2,1,0:T(8,128)S(1)}, f32[146,8,128]{2,1,0:T(8,128)S(1)}, u32[]{:S(2)}, u32[]{:S(2)}) collective-permute-start(f32[146,8,128]{2,1,0:T(8,128)S(1)} %collective-permute-done.refs_1_), channel_id=1, source_target_pairs={{0,1},{1,0},{2,3},{3,2},{4,5},{5,4},{6,7},{7,6},{8,9},{9,8},{10,11... | collective-permute-start | bytes 1794056 | tf_op jit(solution)/shard_map/ppermute | solution.py:353
  39.6 2.9 %collective-permute-start.8 = (f32[146,8,128]{2,1,0:T(8,128)S(1)}, f32[146,8,128]{2,1,0:T(8,128)S(1)}, u32[]{:S(2)}, u32[]{:S(2)}) collective-permute-start(f32[146,8,128]{2,1,0:T(8,128)S(1)} %collective-permute-done.1.refs_2_), channel_id=1, source_target_pairs={{0,1},{1,0},{2,3},{3,2},{4,5},{5,4},{6,7},{7,6},{8,9},{9,8},{10,11... | collective-permute-start | bytes 1794056 | tf_op jit(solution)/shard_map/ppermute | solution.py:353
  40.1 15.4 %collective-permute-start.5 = (f32[146,8,128]{2,1,0:T(8,128)S(1)}, f32[146,8,128]{2,1,0:T(8,128)S(1)}, u32[]{:S(2)}, u32[]{:S(2)}) collective-permute-start(f32[146,8,128]{2,1,0:T(8,128)S(1)} %collective-permute-done.refs_1_), channel_id=1, source_target_pairs={{0,2},{1,3},{2,0},{3,1},{4,6},{5,7},{6,4},{7,5},{8,10},{9,11},{10,... | collective-permute-start | bytes 1794056 | tf_op jit(solution)/shard_map/ppermute | solution.py:353
  40.7 15.1 %collective-permute-start.6 = (f32[146,8,128]{2,1,0:T(8,128)S(1)}, f32[146,8,128]{2,1,0:T(8,128)S(1)}, u32[]{:S(2)}, u32[]{:S(2)}) collective-permute-start(f32[146,8,128]{2,1,0:T(8,128)S(1)} %collective-permute-done.3.refs_6_.refs_8_), channel_id=1, source_target_pairs={{0,4},{1,5},{2,6},{3,7},{4,0},{5,1},{6,2},{7,3},{8,12},{9,13},{10,... | collective-permute-start | bytes 1794056 | tf_op jit(solution)/shard_map/ppermute | solution.py:353
  55.8 2.0 %collective-permute-start.9 = (f32[146,8,128]{2,1,0:T(8,128)S(1)}, f32[146,8,128]{2,1,0:T(8,128)S(1)}, u32[]{:S(2)}, u32[]{:S(2)}) collective-permute-start(f32[146,8,128]{2,1,0:T(8,128)S(1)} %collective-permute-done.5.refs_3_), channel_id=1, source_target_pairs={{0,1},{1,0},{2,3},{3,2},{4,5},{5,4},{6,7},{7,6},{8,9},{9,8},{10,11... | collective-permute-start | bytes 1794056 | tf_op jit(solution)/shard_map/ppermute | solution.py:353
  71.8 3.0 %collective-permute-start.11 = (f32[2,384,128]{2,1,0:T(8,128)S(1)}, f32[2,384,128]{2,1,0:T(8,128)S(1)}, u32[]{:S(2)}, u32[]{:S(2)}) collective-permute-start(f32[2,384,128]{2,1,0:T(8,128)S(1)} %get-tuple-element.91), channel_id=1, source_target_pairs={{0,1},{1,0},{2,3},{3,2},{4,5},{5,4},{6,7},{7,6},{8,9},{9,8},{10,11... | collective-permute-start | bytes 1179656 | tf_op jit(solution)/shard_map/ppermute | solution.py:353
  73.5 11.3 %collective-permute-start.15 = (f32[2,392,128]{2,1,0:T(8,128)S(1)}, f32[2,392,128]{2,1,0:T(8,128)S(1)}, u32[]{:S(2)}, u32[]{:S(2)}) collective-permute-start(f32[2,392,128]{2,1,0:T(8,128)S(1)} %get-tuple-element.95), channel_id=1, source_target_pairs={{0,4},{1,5},{2,6},{3,7},{4,0},{5,1},{6,2},{7,3},{8,12},{9,13},{10,... | collective-permute-start | bytes 1204232 | tf_op jit(solution)/shard_map/ppermute | solution.py:353
  73.5 14.3 %collective-permute-start.10 = (f32[2,384,128]{2,1,0:T(8,128)S(1)}, f32[2,384,128]{2,1,0:T(8,128)S(1)}, u32[]{:S(2)}, u32[]{:S(2)}) collective-permute-start(f32[2,384,128]{2,1,0:T(8,128)S(1)} %get-tuple-element.89), channel_id=1, source_target_pairs={{0,1},{1,0},{2,3},{3,2},{4,5},{5,4},{6,7},{7,6},{8,9},{9,8},{10,11... | collective-permute-start | bytes 1179656 | tf_op jit(solution)/shard_map/ppermute | solution.py:353
  74.9 12.9 %collective-permute-start.13 = (f32[1,384,128]{2,1,0:T(8,128)S(1)}, f32[1,384,128]{2,1,0:T(8,128)S(1)}, u32[]{:S(2)}, u32[]{:S(2)}) collective-permute-start(f32[1,384,128]{2,1,0:T(8,128)S(1)} %get-tuple-element.103), channel_id=1, source_target_pairs={{0,2},{1,3},{2,0},{3,1},{4,6},{5,7},{6,4},{7,5},{8,10},{9,11},{10,... | collective-permute-start | bytes 589832 | tf_op jit(solution)/shard_map/ppermute | solution.py:353
  76.7 21.2 %collective-permute-start.12 = (f32[1,384,128]{2,1,0:T(8,128)S(1)}, f32[1,384,128]{2,1,0:T(8,128)S(1)}, u32[]{:S(2)}, u32[]{:S(2)}) collective-permute-start(f32[1,384,128]{2,1,0:T(8,128)S(1)} %get-tuple-element.102), channel_id=1, source_target_pairs={{0,2},{1,3},{2,0},{3,1},{4,6},{5,7},{6,4},{7,5},{8,10},{9,11},{10,... | collective-permute-start | bytes 589832 | tf_op jit(solution)/shard_map/ppermute | solution.py:353
  84.8 11.2 %collective-permute-start.16 = (f32[1,392,128]{2,1,0:T(8,128)S(1)}, f32[1,392,128]{2,1,0:T(8,128)S(1)}, u32[]{:S(2)}, u32[]{:S(2)}) collective-permute-start(f32[1,392,128]{2,1,0:T(8,128)S(1)} %slice_add_fusion), channel_id=1, source_target_pairs={{0,8},{1,9},{2,10},{3,11},{4,12},{5,13},{6,14},{7,15},{8,0},{9,1},... | collective-permute-start | bytes 602120 | tf_op jit(solution)/shard_map/ppermute | solution.py:353
  87.8 11.0 %collective-permute-start.14 = (f32[1,384,128]{2,1,0:T(8,128)S(1)}, f32[1,384,128]{2,1,0:T(8,128)S(1)}, u32[]{:S(2)}, u32[]{:S(2)}) collective-permute-start(f32[1,384,128]{2,1,0:T(8,128)S(1)} %fusion.1), channel_id=1, source_target_pairs={{0,16},{1,17},{2,18},{3,19},{4,20},{5,21},{6,22},{7,23},{8,24},{9,... | collective-permute-start | bytes 589832 | tf_op jit(solution)/shard_map/ppermute | solution.py:353
  96.8 1.1 %copy-start.1 = (f32[128,9,128]{2,0,1:T(8,128)S(1)}, f32[128,9,128]{2,0,1:T(8,128)}, u32[]{:S(2)}) copy-start(f32[128,9,128]{2,0,1:T(8,128)} %param.7) | copy-start | bytes 1769476

commit v9 on v8

--- a/solution.py
+++ b/solution.py
@@ -307,16 +307,72 @@
     )(*blocks, *earlier)
 
 
-def tile_groups(tiles):
-    main = jnp.concatenate([tiles[..., 3:9, :], tiles[..., 0:2, :]], axis=-2)
-    rows = tiles[..., 2, :]
-    short = -rows.shape[-2] % 8
-    rows = jnp.pad(rows, [(0, 0)] * (rows.ndim - 2) + [(0, short), (0, 0)])
-    rows = rows.reshape(rows.shape[:-2] + (rows.shape[-2] // 8, 8, rows.shape[-1]))
-    return jnp.concatenate([main, rows], axis=-3)
-
-
 NCELL = 64
+
+
+def pack_kernel(steps, me_ref, count_ref, segment_ref, local_ref, remote_ref, sent_ref, cell_ref, out_ref):
+    tiles, width = segment_ref.shape[1:]
+    slots, devices = sent_ref.shape
+    pairs = local_ref.shape[1]
+    for row, axis in enumerate((3, 4, 5, 6, 7, 8, 0, 1)):
+        out_ref[pl.ds(row, tiles, stride=8), :] = segment_ref[axis]
+    out_ref[8 * tiles : 9 * tiles, :] = segment_ref[2]
+
+    def order(shape, dim):
+        slot = lax.broadcasted_iota(jnp.int32, shape, dim)
+        part = slot // slots
+        peer = jnp.full(shape, me_ref[0])
+        for k, step in enumerate(steps):
+            peer = jnp.bitwise_xor(peer, step * jnp.bitwise_and(part >> k, 1))
+        return peer, slot % slots
+
+    peer, column = order((pairs, width), 0)
+    wanted = peer * slots + column
+    table = jnp.zeros((8, pairs), jnp.float32)
+    for k in range(pairs // width):
+        lanes = slice(k * width, (k + 1) * width)
+        position = lax.broadcasted_iota(jnp.int32, (8, width), 1) + k * width
+        near = jnp.where(position < count_ref[0], local_ref[:, lanes] + 1, 0).astype(jnp.float32)
+        named = jnp.where(wanted == remote_ref[:, lanes], 1.0, 0.0)
+        table += matmul(near.astype(jnp.bfloat16), named.astype(jnp.bfloat16), (1, 1))
+    peer = order((pairs, devices), 0)[0]
+    named = jnp.where(peer == lax.broadcasted_iota(jnp.int32, (pairs, devices), 1), 1.0, 0.0)
+    sent = matmul(sent_ref[...].astype(jnp.float32).astype(jnp.bfloat16), named.astype(jnp.bfloat16), (1, 1))
+    column = lax.broadcasted_iota(jnp.int32, (slots, pairs), 1) % slots
+    sent = jnp.where(lax.broadcasted_iota(jnp.int32, (slots, pairs), 0) == column, sent, 0.0)
+    sent = jnp.sum(sent, axis=0, keepdims=True)
+    for k in range(pairs // width):
+        lanes = slice(k * width, (k + 1) * width)
+        out_ref[9 * tiles + k : 9 * tiles + k + 1, :] = table[0:1, lanes] - 1.0
+        out_ref[9 * tiles + 4 + k : 9 * tiles + 5 + k, :] = sent[:, lanes]
+
+    lane = lax.broadcasted_iota(jnp.int32, (tiles, width), 1)
+    outer = jnp.zeros((tiles, width), jnp.float32)
+    for k in range(9):
+        product = segment_ref[3 + k // 3] * segment_ref[6 + k % 3]
+        outer = jnp.where(lane == k, jnp.sum(product, axis=1, keepdims=True), outer)
+    cells = lax.broadcasted_iota(jnp.int32, (NCELL, tiles), 0)
+    held = jnp.where(cells == cell_ref[...], 1.0, 0.0).astype(jnp.bfloat16)
+    moments = sum(matmul(part.astype(jnp.bfloat16), held, (1, 1)) for part in thirds(outer.T[0:16]))
+    last = jnp.where(lax.broadcasted_iota(jnp.int32, (8, NCELL), 0) == 0, moments[8:16], 0.0)
+    out_ref[9 * tiles + 8 : 9 * tiles + 16, :] = jnp.concatenate([moments[0:8], last], axis=1)
+
+
+def pack(me, segments, send_tiles, pair_local, pair_remote, pair_count, tile_cell, steps):
+    tiles, rows, width = segments.shape
+    smem = pl.BlockSpec(memory_space=pltpu.SMEM)
+    vmem = pl.BlockSpec(memory_space=pltpu.VMEM)
+    block = pl.pallas_call(
+        functools.partial(pack_kernel, steps),
+        out_shape=jax.ShapeDtypeStruct((rows * tiles + 16, width), jnp.float32),
+        in_specs=[smem, smem] + [vmem] * 5,
+        out_specs=vmem,
+        compiler_params=pltpu.CompilerParams(vmem_limit_bytes=16 * 1024 * 1024),
+        name="pack",
+    )(
+        me, pair_count, segments.transpose(1, 0, 2), pair_local, pair_remote, send_tiles[0].T, tile_cell.reshape(1, -1)
+    )
+    return block.reshape(-1, 8, width)
 
 
 def far_field(segments, tile_cell, moment_sums, total_segments):
@@ -337,12 +393,6 @@
         ],
         axis=1,
     )
-
-
-def local_moments(segments, tile_cell):
-    outer = jnp.sum(segments[:, 3:6, None, :] * segments[:, None, 6:9, :], axis=3).reshape(-1, 9)
-    onehot = (jnp.arange(NCELL)[:, None] == tile_cell[None, :]).astype(jnp.float32)
-    return jnp.dot(onehot, outer, precision=lax.Precision.HIGHEST)
 
 
 AXES = ("dom", "sub")
@@ -421,53 +471,38 @@
     return groups[0][0][0]
 
 
-def rows_of(values, width):
-    flat = values.reshape(-1).astype(jnp.float32)
-    groups = -(-flat.shape[0] // (8 * width))
-    return jnp.pad(flat, (0, groups * 8 * width - flat.shape[0])).reshape(groups, 8, width)
-
-
 def on_device(segments, send_tiles, pair_local, pair_remote, pair_count, tile_cell):
     width = segments.shape[2]
     tiles = segments.shape[0]
     devices = send_tiles.shape[1]
     slots = send_tiles.shape[2]
-    pairs = pair_local.shape[1]
     near_steps, far_steps = mask_steps(devices)
     near_masks, far_masks = span(near_steps), span(far_steps)
 
-    live = jnp.arange(pairs) < pair_count[0]
-    me = lax.axis_index(AXES).astype(jnp.int32)
-    peers = jnp.bitwise_xor(me, jnp.array([near ^ far for near in near_masks for far in far_masks], jnp.int32))
-    order = (peers[:, None] * slots + jnp.arange(slots)[None, :]).reshape(-1)
-    named = jnp.logical_and(pair_remote[0][:, None] == order[None, :], live[:, None])
-    table = jnp.sum(jnp.where(named, pair_local[0][:, None] + 1, 0), axis=0) - 1
-    chosen = peers[:, None] == jnp.arange(devices)[None, :]
-    sent = jnp.sum(jnp.where(chosen[:, :, None], send_tiles[0][None], 0), axis=1)
-    lists = jnp.concatenate([table, sent.reshape(-1)])
-    moments = local_moments(segments, tile_cell)
-    list_rows, moment_rows = rows_of(lists, width), rows_of(moments, width)
-    main = tile_groups(segments)
-    block = jnp.concatenate([main, list_rows, moment_rows], axis=0)
-
+    me = lax.axis_index(AXES).astype(jnp.int32).reshape(1)
+    block = pack(
+        me, segments, send_tiles, pair_local, pair_remote, pair_count, tile_cell, far_steps + near_steps
+    )
+    list_group = block.shape[0] - 2
     totals = (len(near_masks), len(far_masks))
     early = []
 
     def early_pairs(held):
         early.extend([k for k, mask in enumerate(masks) if mask in held] for masks in (near_masks, far_masks))
         blocks = [held[near_masks[k]] for k in early[0]] + [held[far_masks[k]] for k in early[1][1:]]
-        return run_pairs(blocks, tiles, slots, main.shape[0], totals, early[0], early[1])
+        return run_pairs(blocks, tiles, slots, list_group, totals, early[0], early[1])
 
     near_blocks, far_blocks, sums = spread(block, near_steps, far_steps, early_pairs)
     near_counts, far_counts = message_counts(near_steps), message_counts(far_steps)
     outs = run_pairs(
-        near_blocks + far_blocks[1:], tiles, slots, main.shape[0], totals, list(range(totals[0])), list(range(totals[1])),
+        near_blocks + far_blocks[1:], tiles, slots, list_group, totals, list(range(totals[0])), list(range(totals[1])),
         (near_counts, far_counts), early, sums,
     )
     near_total = collect(outs[: len(near_counts)], near_counts, near_steps)
     far_total = collect(outs[len(near_counts) :], far_counts, far_steps)
     forces = (near_total + far_total[: 3 * tiles]).reshape(3, tiles, width)
-    moment_sums = far_total[3 * tiles :].reshape(-1)[: NCELL * 9].reshape(NCELL, 9)
+    rows = far_total[3 * tiles :]
+    moment_sums = jnp.concatenate([rows[:, :NCELL], rows[:1, NCELL : 2 * NCELL]]).T
     total_segments = tiles * width * devices
     return forces.transpose(1, 0, 2) + far_field(segments, tile_cell, moment_sums, total_segments)
 

time: 101 us -> 96 us (0.950); the launches traced: 99.6 us -> 96.1 us
  starting transfers between devices: 20.3 us -> 15.4 us
  Pallas kernels: 26.7 us -> 31.1 us
  local copies, waits for them, and re-layouts: 5.04 us -> 1.86 us
  waiting for transfers between devices: 43.3 us -> 45.2 us
  other arithmetic: 2.72 us -> 1.22 us
    ppermute x17, starting transfers between devices: 20.3 us -> 15.4 us  [swap(): return lax.ppermute(value, AXES, [(k, k ^ mask) for k in range(devices)])]
    pallas_call x2, Pallas kernels: 26.7 us -> 30.4 us  [run_pairs(): pl.pallas_call(kernel, out_shape=[jax.ShapeDtypeStruct(shape, jnp.float32...]
    ppermute x17, waiting for transfers between devices: 43.3 us -> 45.2 us  [swap(): return lax.ppermute(value, AXES, [(k, k ^ mask) for k in range(devices)])]
    slice x5 -> x3, local copies, waits for them, and re-layouts: 1.7 us -> 0.09 us  [the longest x1 0.07 us: on_device(): rows[:1, NCELL:2 * NCELL]]
    reduce_sum x3 -> x0, other arithmetic: 1.17 us -> none  [the longest x1 0.62 us: on_device(): jnp.sum(jnp.where(chosen[:, :, None], send_tiles[0][None], 0), axis=1)]
    unnamed x16 -> x12, local copies, waits for them, and re-layouts: 2.16 us -> 1.74 us
  transfers between devices with their start and end apart: 17 -> 17, of which waited for: 10 -> 8; matrix products, arithmetic and copies ran while one was open for 2% -> 1% of each run, Pallas kernels for 13% -> 17%
where the time goes in v9:
time: 96 us; the launch traced here: 96.1 us
  waiting for transfers between devices  45.2 us (47%)
  Pallas kernels  31.1 us (32%)
  starting transfers between devices  15.4 us (16%)
  local copies, waits for them, and re-layouts  1.86 us (2%)
  other arithmetic  1.22 us (1%)
    ppermute x17, waiting for transfers between devices, swap(): return lax.ppermute(value, AXES, [(k, k ^ mask) for k in range(devices)])  45.2 us
    pallas_call x2, Pallas kernels, run_pairs(): pl.pallas_call(kernel, out_shape=[jax.ShapeDtypeStruct(shape, jnp.float32...  30.4 us
    ppermute x17, starting transfers between devices, swap(): return lax.ppermute(value, AXES, [(k, k ^ mask) for k in range(devices)])  15.4 us
  transfers between devices with their start and end apart: 17, of which 8 were waited for; matrix products, arithmetic and copies ran while one was open for 1% of the time, Pallas kernels for 17%

profile of v9, /device:TPU:0, one launch (start us, length us, event | category | flops | bytes accessed | tf_op | source)
XLA Modules:
  0.0 96.1 jit_solution(2182403374028968663)
XLA Ops:
  0.7 0.6 copy-done.4
  1.4 0.0 copy-done.3
  1.4 1.1 %copy-done = f32[128,9,128]{2,0,1:T(8,128)S(1)} copy-done((f32[128,9,128]{2,0,1:T(8,128)S(1)}, f32[128,9,128]{2,0,1:T(8,128)}, u32[]{:S(2)}) %copy-start) | copy-done | bytes 589848
  2.4 0.7 pack.1
  3.2 4.0 %collective-permute-start = (f32[146,8,128]{2,1,0:T(8,128)S(1)}, f32[146,8,128]{2,1,0:T(8,128)S(1)}, u32[]{:S(2)}, u32[]{:S(2)}) collective-permute-start(f32[146,8,128]{2,1,0:T(8,128)S(1)} %bitcast.27), channel_id=1, source_target_pairs={{0,16},{1,17},{2,18},{3,19},{4,20},{5,21},{6,22},{7,23},{8,24},{9,... | collective-permute-start | bytes 1794056 | tf_op jit(solution)/shard_map/ppermute | solution.py:403
  7.2 1.5 %collective-permute-start.1 = (f32[146,8,128]{2,1,0:T(8,128)S(1)}, f32[146,8,128]{2,1,0:T(8,128)S(1)}, u32[]{:S(2)}, u32[]{:S(2)}) collective-permute-start(f32[146,8,128]{2,1,0:T(8,128)S(1)} %bitcast.28), channel_id=1, source_target_pairs={{0,2},{1,3},{2,0},{3,1},{4,6},{5,7},{6,4},{7,5},{8,10},{9,11},{10,... | collective-permute-start | bytes 1794056 | tf_op jit(solution)/shard_map/ppermute | solution.py:403
  8.7 0.0 collective-permute-start.2
  8.7 1.6 %collective-permute-start.3 = (f32[146,8,128]{2,1,0:T(8,128)S(1)}, f32[146,8,128]{2,1,0:T(8,128)S(1)}, u32[]{:S(2)}, u32[]{:S(2)}) collective-permute-start(f32[146,8,128]{2,1,0:T(8,128)S(1)} %bitcast.30), channel_id=1, source_target_pairs={{0,8},{1,9},{2,10},{3,11},{4,12},{5,13},{6,14},{7,15},{8,0},{9,1},... | collective-permute-start | bytes 1794056 | tf_op jit(solution)/shard_map/ppermute | solution.py:403
  10.3 1.5 %collective-permute-start.4 = (f32[146,8,128]{2,1,0:T(8,128)S(1)}, f32[146,8,128]{2,1,0:T(8,128)S(1)}, u32[]{:S(2)}, u32[]{:S(2)}) collective-permute-start(f32[146,8,128]{2,1,0:T(8,128)S(1)} %bitcast.31), channel_id=1, source_target_pairs={{0,4},{1,5},{2,6},{3,7},{4,0},{5,1},{6,2},{7,3},{8,12},{9,13},{10,... | collective-permute-start | bytes 1794056 | tf_op jit(solution)/shard_map/ppermute | solution.py:403
  11.8 21.8 %collective-permute-done.refs_1_ = f32[146,8,128]{2,1,0:T(8,128)S(1)} collective-permute-done((f32[146,8,128]{2,1,0:T(8,128)S(1)}, f32[146,8,128]{2,1,0:T(8,128)S(1)}, u32[]{:S(2)}, u32[]{:S(2)}) %collective-permute-start) | collective-permute-done | bytes 598048 | tf_op jit(solution)/shard_map/ppermute | solution.py:403
  33.6 0.0 collective-permute-done.1.refs_2_
  33.6 0.0 collective-permute-done.2.refs_3_.refs_4_
  33.6 2.7 %collective-permute-done.3.refs_6_.refs_8_ = f32[146,8,128]{2,1,0:T(8,128)S(1)} collective-permute-done((f32[146,8,128]{2,1,0:T(8,128)S(1)}, f32[146,8,128]{2,1,0:T(8,128)S(1)}, u32[]{:S(2)}, u32[]{:S(2)}) %collective-permute-start.3) | collective-permute-done | bytes 598048 | tf_op jit(solution)/shard_map/ppermute | solution.py:403
  36.3 0.0 collective-permute-done.4.refs_7_.refs_9_
  36.3 0.0 collective-permute-start.7
  36.3 0.5 collective-permute-start.8
  36.8 0.6 collective-permute-start.5
  37.4 1.5 %collective-permute-start.6 = (f32[146,8,128]{2,1,0:T(8,128)S(1)}, f32[146,8,128]{2,1,0:T(8,128)S(1)}, u32[]{:S(2)}, u32[]{:S(2)}) collective-permute-start(f32[146,8,128]{2,1,0:T(8,128)S(1)} %collective-permute-done.3.refs_6_.refs_8_), channel_id=1, source_target_pairs={{0,4},{1,5},{2,6},{3,7},{4,0},{5,1},{6,2},{7,3},{8,12},{9,13},{10,... | collective-permute-start | bytes 1794056 | tf_op jit(solution)/shard_map/ppermute | solution.py:403
  38.9 0.0 collective-permute-done.7.refs_4_.refs_5_
  38.9 0.3 collective-permute-done.8.refs_5_.refs_6_
  39.2 16.4 %early_pairs.1 = (f32[1,384,128]{2,1,0:T(8,128)S(1)}, f32[1,384,128]{2,1,0:T(8,128)S(1)}, f32[1,384,128]{2,1,0:T(8,128)S(1)}, f32[1,384,128]{2,1,0:T(8,128)S(1)}...) custom-call(f32[146,8,128]{2,1,0:T(8,128)S(1)} %bitcast.32, ...), custom_call_target="tpu_custom_call" | custom-call | flops 1572864 | bytes 65536 | tf_op jit(solution)/shard_map/early_pairs/pallas_call | solution.py:298
  55.6 0.0 collective-permute-done.5.refs_3_
  55.6 0.0 collective-permute-done.6.refs_10_
  55.6 0.0 copy-start.1
  55.6 0.1 collective-permute-start.9
  55.7 2.0 %collective-permute-done.9.refs_7_ = f32[146,8,128]{2,1,0:T(8,128)S(1)} collective-permute-done((f32[146,8,128]{2,1,0:T(8,128)S(1)}, f32[146,8,128]{2,1,0:T(8,128)S(1)}, u32[]{:S(2)}, u32[]{:S(2)}) %collective-permute-start.9) | collective-permute-done | bytes 598048 | tf_op jit(solution)/shard_map/ppermute | solution.py:403
  57.7 14.0 %pairs.1 = (f32[1,384,128]{2,1,0:T(8,128)S(1)}, f32[1,384,128]{2,1,0:T(8,128)S(1)}, f32[1,384,128]{2,1,0:T(8,128)S(1)}, f32[1,384,128]{2,1,0:T(8,128)S(1)}, f32[...) custom-call(f32[146,8,128]{2,1,0:T(8,128)S(1)} %bitcast.33, ...), custom_call_target="tpu_custom_call" | custom-call | flops 2785280000 | bytes 65536 | tf_op jit(solution)/shard_map/pairs/pallas_call | solution.py:298
  71.7 0.9 collective-permute-start.11
  72.6 0.0 collective-permute-start.15
  72.6 0.2 collective-permute-start.10
  72.8 1.1 %collective-permute-done.11 = f32[2,384,128]{2,1,0:T(8,128)S(1)} collective-permute-done((f32[2,384,128]{2,1,0:T(8,128)S(1)}, f32[2,384,128]{2,1,0:T(8,128)S(1)}, u32[]{:S(2)}, u32[]{:S(2)}) %collective-permute-start.11) | collective-permute-done | bytes 393248 | tf_op jit(solution)/shard_map/ppermute | solution.py:403
  74.0 0.1 slice_add_fusion.5
  74.0 2.3 %collective-permute-start.13 = (f32[1,384,128]{2,1,0:T(8,128)S(1)}, f32[1,384,128]{2,1,0:T(8,128)S(1)}, u32[]{:S(2)}, u32[]{:S(2)}) collective-permute-start(f32[1,384,128]{2,1,0:T(8,128)S(1)} %get-tuple-element.101), channel_id=1, source_target_pairs={{0,2},{1,3},{2,0},{3,1},{4,6},{5,7},{6,4},{7,5},{8,10},{9,11},{10,... | collective-permute-start | bytes 589832 | tf_op jit(solution)/shard_map/ppermute | solution.py:403
  76.3 0.1 collective-permute-start.12
  76.4 7.5 %collective-permute-done.15 = f32[2,392,128]{2,1,0:T(8,128)S(1)} collective-permute-done((f32[2,392,128]{2,1,0:T(8,128)S(1)}, f32[2,392,128]{2,1,0:T(8,128)S(1)}, u32[]{:S(2)}, u32[]{:S(2)}) %collective-permute-start.15) | collective-permute-done | bytes 401440 | tf_op jit(solution)/shard_map/ppermute | solution.py:403
  83.9 0.1 collective-permute-start.16
  84.0 0.0 collective-permute-done.10
  84.0 0.0 collective-permute-done.13
  84.0 0.6 collective-permute-start.14
  84.7 9.2 %collective-permute-done.16 = f32[1,392,128]{2,1,0:T(8,128)S(1)} collective-permute-done((f32[1,392,128]{2,1,0:T(8,128)S(1)}, f32[1,392,128]{2,1,0:T(8,128)S(1)}, u32[]{:S(2)}, u32[]{:S(2)}) %collective-permute-start.16) | collective-permute-done | bytes 200736 | tf_op jit(solution)/shard_map/ppermute | solution.py:403
  93.9 0.1 slice.75
  94.0 0.2 fusion.5
  94.3 0.2 fusion.4
  94.5 0.3 multiply_reduce_fusion
  94.8 0.0 collective-permute-done.12
  94.8 0.5 collective-permute-done.14
  95.3 0.1 slice_add_fusion.2
  95.4 0.7 maximum_add_fusion
  (20 shorter events, 0.2 us)
Async XLA Ops:
  0.0 0.7 copy-start.2
  0.7 0.7 copy-start.4
  0.7 0.7 copy-start.3
  0.7 0.7 copy-start.5
  1.4 1.1 %copy-start = (f32[128,9,128]{2,0,1:T(8,128)S(1)}, f32[128,9,128]{2,0,1:T(8,128)}, u32[]{:S(2)}) copy-start(f32[128,9,128]{2,0,1:T(8,128)} %param.6) | copy-start | bytes 1769476
  3.2 30.5 %collective-permute-start = (f32[146,8,128]{2,1,0:T(8,128)S(1)}, f32[146,8,128]{2,1,0:T(8,128)S(1)}, u32[]{:S(2)}, u32[]{:S(2)}) collective-permute-start(f32[146,8,128]{2,1,0:T(8,128)S(1)} %bitcast.27), channel_id=1, source_target_pairs={{0,16},{1,17},{2,18},{3,19},{4,20},{5,21},{6,22},{7,23},{8,24},{9,... | collective-permute-start | bytes 1794056 | tf_op jit(solution)/shard_map/ppermute | solution.py:403
  7.2 26.4 %collective-permute-start.1 = (f32[146,8,128]{2,1,0:T(8,128)S(1)}, f32[146,8,128]{2,1,0:T(8,128)S(1)}, u32[]{:S(2)}, u32[]{:S(2)}) collective-permute-start(f32[146,8,128]{2,1,0:T(8,128)S(1)} %bitcast.28), channel_id=1, source_target_pairs={{0,2},{1,3},{2,0},{3,1},{4,6},{5,7},{6,4},{7,5},{8,10},{9,11},{10,... | collective-permute-start | bytes 1794056 | tf_op jit(solution)/shard_map/ppermute | solution.py:403
  8.7 24.9 %collective-permute-start.2 = (f32[146,8,128]{2,1,0:T(8,128)S(1)}, f32[146,8,128]{2,1,0:T(8,128)S(1)}, u32[]{:S(2)}, u32[]{:S(2)}) collective-permute-start(f32[146,8,128]{2,1,0:T(8,128)S(1)} %bitcast.29), channel_id=1, source_target_pairs={{0,1},{1,0},{2,3},{3,2},{4,5},{5,4},{6,7},{7,6},{8,9},{9,8},{10,11... | collective-permute-start | bytes 1794056 | tf_op jit(solution)/shard_map/ppermute | solution.py:403
  8.7 27.6 %collective-permute-start.3 = (f32[146,8,128]{2,1,0:T(8,128)S(1)}, f32[146,8,128]{2,1,0:T(8,128)S(1)}, u32[]{:S(2)}, u32[]{:S(2)}) collective-permute-start(f32[146,8,128]{2,1,0:T(8,128)S(1)} %bitcast.30), channel_id=1, source_target_pairs={{0,8},{1,9},{2,10},{3,11},{4,12},{5,13},{6,14},{7,15},{8,0},{9,1},... | collective-permute-start | bytes 1794056 | tf_op jit(solution)/shard_map/ppermute | solution.py:403
  10.3 26.0 %collective-permute-start.4 = (f32[146,8,128]{2,1,0:T(8,128)S(1)}, f32[146,8,128]{2,1,0:T(8,128)S(1)}, u32[]{:S(2)}, u32[]{:S(2)}) collective-permute-start(f32[146,8,128]{2,1,0:T(8,128)S(1)} %bitcast.31), channel_id=1, source_target_pairs={{0,4},{1,5},{2,6},{3,7},{4,0},{5,1},{6,2},{7,3},{8,12},{9,13},{10,... | collective-permute-start | bytes 1794056 | tf_op jit(solution)/shard_map/ppermute | solution.py:403
  36.3 2.6 %collective-permute-start.7 = (f32[146,8,128]{2,1,0:T(8,128)S(1)}, f32[146,8,128]{2,1,0:T(8,128)S(1)}, u32[]{:S(2)}, u32[]{:S(2)}) collective-permute-start(f32[146,8,128]{2,1,0:T(8,128)S(1)} %collective-permute-done.refs_1_), channel_id=1, source_target_pairs={{0,1},{1,0},{2,3},{3,2},{4,5},{5,4},{6,7},{7,6},{8,9},{9,8},{10,11... | collective-permute-start | bytes 1794056 | tf_op jit(solution)/shard_map/ppermute | solution.py:403
  36.3 2.9 %collective-permute-start.8 = (f32[146,8,128]{2,1,0:T(8,128)S(1)}, f32[146,8,128]{2,1,0:T(8,128)S(1)}, u32[]{:S(2)}, u32[]{:S(2)}) collective-permute-start(f32[146,8,128]{2,1,0:T(8,128)S(1)} %collective-permute-done.1.refs_2_), channel_id=1, source_target_pairs={{0,1},{1,0},{2,3},{3,2},{4,5},{5,4},{6,7},{7,6},{8,9},{9,8},{10,11... | collective-permute-start | bytes 1794056 | tf_op jit(solution)/shard_map/ppermute | solution.py:403
  36.8 18.8 %collective-permute-start.5 = (f32[146,8,128]{2,1,0:T(8,128)S(1)}, f32[146,8,128]{2,1,0:T(8,128)S(1)}, u32[]{:S(2)}, u32[]{:S(2)}) collective-permute-start(f32[146,8,128]{2,1,0:T(8,128)S(1)} %collective-permute-done.refs_1_), channel_id=1, source_target_pairs={{0,2},{1,3},{2,0},{3,1},{4,6},{5,7},{6,4},{7,5},{8,10},{9,11},{10,... | collective-permute-start | bytes 1794056 | tf_op jit(solution)/shard_map/ppermute | solution.py:403
  37.4 18.2 %collective-permute-start.6 = (f32[146,8,128]{2,1,0:T(8,128)S(1)}, f32[146,8,128]{2,1,0:T(8,128)S(1)}, u32[]{:S(2)}, u32[]{:S(2)}) collective-permute-start(f32[146,8,128]{2,1,0:T(8,128)S(1)} %collective-permute-done.3.refs_6_.refs_8_), channel_id=1, source_target_pairs={{0,4},{1,5},{2,6},{3,7},{4,0},{5,1},{6,2},{7,3},{8,12},{9,13},{10,... | collective-permute-start | bytes 1794056 | tf_op jit(solution)/shard_map/ppermute | solution.py:403
  55.6 17.0 %copy-start.1 = (f32[128,9,128]{2,0,1:T(8,128)S(1)}, f32[128,9,128]{2,0,1:T(8,128)}, u32[]{:S(2)}) copy-start(f32[128,9,128]{2,0,1:T(8,128)} %param.6) | copy-start | bytes 1769476
  55.6 2.1 %collective-permute-start.9 = (f32[146,8,128]{2,1,0:T(8,128)S(1)}, f32[146,8,128]{2,1,0:T(8,128)S(1)}, u32[]{:S(2)}, u32[]{:S(2)}) collective-permute-start(f32[146,8,128]{2,1,0:T(8,128)S(1)} %collective-permute-done.5.refs_3_), channel_id=1, source_target_pairs={{0,1},{1,0},{2,3},{3,2},{4,5},{5,4},{6,7},{7,6},{8,9},{9,8},{10,11... | collective-permute-start | bytes 1794056 | tf_op jit(solution)/shard_map/ppermute | solution.py:403
  71.7 2.3 %collective-permute-start.11 = (f32[2,384,128]{2,1,0:T(8,128)S(1)}, f32[2,384,128]{2,1,0:T(8,128)S(1)}, u32[]{:S(2)}, u32[]{:S(2)}) collective-permute-start(f32[2,384,128]{2,1,0:T(8,128)S(1)} %get-tuple-element.91), channel_id=1, source_target_pairs={{0,1},{1,0},{2,3},{3,2},{4,5},{5,4},{6,7},{7,6},{8,9},{9,8},{10,11... | collective-permute-start | bytes 1179656 | tf_op jit(solution)/shard_map/ppermute | solution.py:403
  72.6 11.3 %collective-permute-start.15 = (f32[2,392,128]{2,1,0:T(8,128)S(1)}, f32[2,392,128]{2,1,0:T(8,128)S(1)}, u32[]{:S(2)}, u32[]{:S(2)}) collective-permute-start(f32[2,392,128]{2,1,0:T(8,128)S(1)} %get-tuple-element.95), channel_id=1, source_target_pairs={{0,4},{1,5},{2,6},{3,7},{4,0},{5,1},{6,2},{7,3},{8,12},{9,13},{10,... | collective-permute-start | bytes 1204232 | tf_op jit(solution)/shard_map/ppermute | solution.py:403
  72.6 11.3 %collective-permute-start.10 = (f32[2,384,128]{2,1,0:T(8,128)S(1)}, f32[2,384,128]{2,1,0:T(8,128)S(1)}, u32[]{:S(2)}, u32[]{:S(2)}) collective-permute-start(f32[2,384,128]{2,1,0:T(8,128)S(1)} %get-tuple-element.89), channel_id=1, source_target_pairs={{0,1},{1,0},{2,3},{3,2},{4,5},{5,4},{6,7},{7,6},{8,9},{9,8},{10,11... | collective-permute-start | bytes 1179656 | tf_op jit(solution)/shard_map/ppermute | solution.py:403
  74.0 10.0 %collective-permute-start.13 = (f32[1,384,128]{2,1,0:T(8,128)S(1)}, f32[1,384,128]{2,1,0:T(8,128)S(1)}, u32[]{:S(2)}, u32[]{:S(2)}) collective-permute-start(f32[1,384,128]{2,1,0:T(8,128)S(1)} %get-tuple-element.101), channel_id=1, source_target_pairs={{0,2},{1,3},{2,0},{3,1},{4,6},{5,7},{6,4},{7,5},{8,10},{9,11},{10,... | collective-permute-start | bytes 589832 | tf_op jit(solution)/shard_map/ppermute | solution.py:403
  76.3 18.5 %collective-permute-start.12 = (f32[1,384,128]{2,1,0:T(8,128)S(1)}, f32[1,384,128]{2,1,0:T(8,128)S(1)}, u32[]{:S(2)}, u32[]{:S(2)}) collective-permute-start(f32[1,384,128]{2,1,0:T(8,128)S(1)} %get-tuple-element.100), channel_id=1, source_target_pairs={{0,2},{1,3},{2,0},{3,1},{4,6},{5,7},{6,4},{7,5},{8,10},{9,11},{10,... | collective-permute-start | bytes 589832 | tf_op jit(solution)/shard_map/ppermute | solution.py:403
  83.9 9.9 %collective-permute-start.16 = (f32[1,392,128]{2,1,0:T(8,128)S(1)}, f32[1,392,128]{2,1,0:T(8,128)S(1)}, u32[]{:S(2)}, u32[]{:S(2)}) collective-permute-start(f32[1,392,128]{2,1,0:T(8,128)S(1)} %slice_add_fusion), channel_id=1, source_target_pairs={{0,8},{1,9},{2,10},{3,11},{4,12},{5,13},{6,14},{7,15},{8,0},{9,1},... | collective-permute-start | bytes 602120 | tf_op jit(solution)/shard_map/ppermute | solution.py:403
  84.0 11.3 %collective-permute-start.14 = (f32[1,384,128]{2,1,0:T(8,128)S(1)}, f32[1,384,128]{2,1,0:T(8,128)S(1)}, u32[]{:S(2)}, u32[]{:S(2)}) collective-permute-start(f32[1,384,128]{2,1,0:T(8,128)S(1)} %fusion.1), channel_id=1, source_target_pairs={{0,16},{1,17},{2,18},{3,19},{4,20},{5,21},{6,22},{7,23},{8,24},{9,... | collective-permute-start | bytes 589832 | tf_op jit(solution)/shard_map/ppermute | solution.py:403

commit v10 on v9

--- a/solution.py
+++ b/solution.py
@@ -493,13 +493,14 @@
         return run_pairs(blocks, tiles, slots, list_group, totals, early[0], early[1])
 
     near_blocks, far_blocks, sums = spread(block, near_steps, far_steps, early_pairs)
-    near_counts, far_counts = message_counts(near_steps), message_counts(far_steps)
+    near_counts, far_counts = message_counts(near_steps), [1] * len(far_masks)
     outs = run_pairs(
         near_blocks + far_blocks[1:], tiles, slots, list_group, totals, list(range(totals[0])), list(range(totals[1])),
         (near_counts, far_counts), early, sums,
     )
     near_total = collect(outs[: len(near_counts)], near_counts, near_steps)
     far_total = collect(outs[len(near_counts) :], far_counts, far_steps)
+    near_total, far_total = lax.optimization_barrier((near_total, far_total))
     forces = (near_total + far_total[: 3 * tiles]).reshape(3, tiles, width)
     rows = far_total[3 * tiles :]
     moment_sums = jnp.concatenate([rows[:, :NCELL], rows[:1, NCELL : 2 * NCELL]]).T

time: 96 us -> 94.3 us (0.982); the launches traced: 96.1 us -> 93.1 us
  starting transfers between devices: 15.4 us -> 21.5 us
  waiting for transfers between devices: 45.2 us -> 39.4 us
  Pallas kernels: 31.1 us -> 27.5 us
    ppermute x17 -> x18, starting transfers between devices: 15.4 us -> 21.5 us  [swap(): return lax.ppermute(value, AXES, [(k, k ^ mask) for k in range(devices)])]
    ppermute x17 -> x18, waiting for transfers between devices: 45.2 us -> 39.4 us  [swap(): return lax.ppermute(value, AXES, [(k, k ^ mask) for k in range(devices)])]
    pallas_call x2, Pallas kernels: 30.4 us -> 26.8 us  [run_pairs(): pl.pallas_call(kernel, out_shape=[jax.ShapeDtypeStruct(shape, jnp.float32...]
  transfers between devices with their start and end apart: 17 -> 18, of which waited for: 8 -> 9; matrix products, arithmetic and copies ran while one was open for 1% -> 0% of each run, Pallas kernels for 17% -> 14%
where the time goes in v10:
time: 94.3 us; the launch traced here: 93.1 us
  waiting for transfers between devices  39.4 us (42%)
  Pallas kernels  27.5 us (29%)
  starting transfers between devices  21.5 us (23%)
  local copies, waits for them, and re-layouts  2.17 us (2%)
  other arithmetic  1.25 us (1%)
    ppermute x18, waiting for transfers between devices, swap(): return lax.ppermute(value, AXES, [(k, k ^ mask) for k in range(devices)])  39.4 us
    pallas_call x2, Pallas kernels, run_pairs(): pl.pallas_call(kernel, out_shape=[jax.ShapeDtypeStruct(shape, jnp.float32...  26.8 us
    ppermute x18, starting transfers between devices, swap(): return lax.ppermute(value, AXES, [(k, k ^ mask) for k in range(devices)])  21.5 us
    unnamed x12, local copies, waits for them, and re-layouts  2.05 us
  transfers between devices with their start and end apart: 18, of which 9 were waited for; matrix products, arithmetic and copies ran while one was open for 0% of the time, Pallas kernels for 14%

profile of v10, /device:TPU:0, one launch (start us, length us, event | category | flops | bytes accessed | tf_op | source)
XLA Modules:
  0.0 93.1 jit_solution(13381225185846125495)
XLA Ops:
  0.7 0.6 copy-done.4
  1.4 0.0 copy-done.3
  1.4 1.1 %copy-done = f32[128,9,128]{2,0,1:T(8,128)S(1)} copy-done((f32[128,9,128]{2,0,1:T(8,128)S(1)}, f32[128,9,128]{2,0,1:T(8,128)}, u32[]{:S(2)}) %copy-start) | copy-done | bytes 589848
  2.4 0.7 pack.1
  3.2 4.0 %collective-permute-start = (f32[146,8,128]{2,1,0:T(8,128)S(1)}, f32[146,8,128]{2,1,0:T(8,128)S(1)}, u32[]{:S(2)}, u32[]{:S(2)}) collective-permute-start(f32[146,8,128]{2,1,0:T(8,128)S(1)} %bitcast.28), channel_id=1, source_target_pairs={{0,16},{1,17},{2,18},{3,19},{4,20},{5,21},{6,22},{7,23},{8,24},{9,... | collective-permute-start | bytes 1794056 | tf_op jit(solution)/shard_map/ppermute | solution.py:403
  7.2 1.5 %collective-permute-start.1 = (f32[146,8,128]{2,1,0:T(8,128)S(1)}, f32[146,8,128]{2,1,0:T(8,128)S(1)}, u32[]{:S(2)}, u32[]{:S(2)}) collective-permute-start(f32[146,8,128]{2,1,0:T(8,128)S(1)} %bitcast.29), channel_id=1, source_target_pairs={{0,2},{1,3},{2,0},{3,1},{4,6},{5,7},{6,4},{7,5},{8,10},{9,11},{10,... | collective-permute-start | bytes 1794056 | tf_op jit(solution)/shard_map/ppermute | solution.py:403
  8.7 0.0 collective-permute-start.2
  8.7 1.6 %collective-permute-start.3 = (f32[146,8,128]{2,1,0:T(8,128)S(1)}, f32[146,8,128]{2,1,0:T(8,128)S(1)}, u32[]{:S(2)}, u32[]{:S(2)}) collective-permute-start(f32[146,8,128]{2,1,0:T(8,128)S(1)} %bitcast.31), channel_id=1, source_target_pairs={{0,8},{1,9},{2,10},{3,11},{4,12},{5,13},{6,14},{7,15},{8,0},{9,1},... | collective-permute-start | bytes 1794056 | tf_op jit(solution)/shard_map/ppermute | solution.py:403
  10.3 1.5 %collective-permute-start.4 = (f32[146,8,128]{2,1,0:T(8,128)S(1)}, f32[146,8,128]{2,1,0:T(8,128)S(1)}, u32[]{:S(2)}, u32[]{:S(2)}) collective-permute-start(f32[146,8,128]{2,1,0:T(8,128)S(1)} %bitcast.32), channel_id=1, source_target_pairs={{0,4},{1,5},{2,6},{3,7},{4,0},{5,1},{6,2},{7,3},{8,12},{9,13},{10,... | collective-permute-start | bytes 1794056 | tf_op jit(solution)/shard_map/ppermute | solution.py:403
  11.8 21.8 %collective-permute-done.refs_1_ = f32[146,8,128]{2,1,0:T(8,128)S(1)} collective-permute-done((f32[146,8,128]{2,1,0:T(8,128)S(1)}, f32[146,8,128]{2,1,0:T(8,128)S(1)}, u32[]{:S(2)}, u32[]{:S(2)}) %collective-permute-start) | collective-permute-done | bytes 598048 | tf_op jit(solution)/shard_map/ppermute | solution.py:403
  33.6 0.0 collective-permute-done.1.refs_2_
  33.6 0.0 collective-permute-done.2.refs_3_.refs_4_
  33.6 2.7 %collective-permute-done.3.refs_6_.refs_8_ = f32[146,8,128]{2,1,0:T(8,128)S(1)} collective-permute-done((f32[146,8,128]{2,1,0:T(8,128)S(1)}, f32[146,8,128]{2,1,0:T(8,128)S(1)}, u32[]{:S(2)}, u32[]{:S(2)}) %collective-permute-start.3) | collective-permute-done | bytes 598048 | tf_op jit(solution)/shard_map/ppermute | solution.py:403
  36.3 0.0 collective-permute-done.4.refs_7_.refs_9_
  36.3 0.0 collective-permute-start.7
  36.3 0.5 collective-permute-start.8
  36.8 0.6 collective-permute-start.5
  37.4 1.5 %collective-permute-start.6 = (f32[146,8,128]{2,1,0:T(8,128)S(1)}, f32[146,8,128]{2,1,0:T(8,128)S(1)}, u32[]{:S(2)}, u32[]{:S(2)}) collective-permute-start(f32[146,8,128]{2,1,0:T(8,128)S(1)} %collective-permute-done.3.refs_6_.refs_8_), channel_id=1, source_target_pairs={{0,4},{1,5},{2,6},{3,7},{4,0},{5,1},{6,2},{7,3},{8,12},{9,13},{10,... | collective-permute-start | bytes 1794056 | tf_op jit(solution)/shard_map/ppermute | solution.py:403
  38.9 0.0 collective-permute-done.7.refs_4_.refs_5_
  38.9 0.3 collective-permute-done.8.refs_5_.refs_6_
  39.2 13.5 %early_pairs.1 = (f32[1,384,128]{2,1,0:T(8,128)S(1)}, f32[1,384,128]{2,1,0:T(8,128)S(1)}, f32[1,384,128]{2,1,0:T(8,128)S(1)}, f32[1,384,128]{2,1,0:T(8,128)S(1)}...) custom-call(f32[146,8,128]{2,1,0:T(8,128)S(1)} %bitcast.33, ...), custom_call_target="tpu_custom_call" | custom-call | flops 1572864 | bytes 65536 | tf_op jit(solution)/shard_map/early_pairs/pallas_call | solution.py:298
  52.7 0.0 collective-permute-done.5.refs_3_
  52.7 0.0 collective-permute-done.6.refs_10_
  52.7 0.2 collective-permute-start.9
  52.9 1.9 %collective-permute-done.9.refs_7_ = f32[146,8,128]{2,1,0:T(8,128)S(1)} collective-permute-done((f32[146,8,128]{2,1,0:T(8,128)S(1)}, f32[146,8,128]{2,1,0:T(8,128)S(1)}, u32[]{:S(2)}, u32[]{:S(2)}) %collective-permute-start.9) | collective-permute-done | bytes 598048 | tf_op jit(solution)/shard_map/ppermute | solution.py:403
  54.8 13.3 %pairs.1 = (f32[1,384,128]{2,1,0:T(8,128)S(1)}, f32[1,384,128]{2,1,0:T(8,128)S(1)}, f32[1,384,128]{2,1,0:T(8,128)S(1)}, f32[1,384,128]{2,1,0:T(8,128)S(1)}, f32[...) custom-call(f32[146,8,128]{2,1,0:T(8,128)S(1)} %bitcast.34, ...), custom_call_target="tpu_custom_call" | custom-call | flops 2785280000 | bytes 65536 | tf_op jit(solution)/shard_map/pairs/pallas_call | solution.py:298
  68.1 0.1 collective-permute-start.11
  68.2 4.3 %collective-permute-start.16 = (f32[1,392,128]{2,1,0:T(8,128)S(1)}, f32[1,392,128]{2,1,0:T(8,128)S(1)}, u32[]{:S(2)}, u32[]{:S(2)}) collective-permute-start(f32[1,392,128]{2,1,0:T(8,128)S(1)} %get-tuple-element.100), channel_id=1, source_target_pairs={{0,4},{1,5},{2,6},{3,7},{4,0},{5,1},{6,2},{7,3},{8,12},{9,13},{10,... | collective-permute-start | bytes 602120 | tf_op jit(solution)/shard_map/ppermute | solution.py:403
  72.4 0.2 collective-permute-start.10
  72.6 0.0 collective-permute-done.11
  72.7 0.7 collective-permute-start.13
  73.4 0.3 copy-done.1
  73.7 1.5 %collective-permute-start.15 = (f32[1,392,128]{2,1,0:T(8,128)S(1)}, f32[1,392,128]{2,1,0:T(8,128)S(1)}, u32[]{:S(2)}, u32[]{:S(2)}) collective-permute-start(f32[1,392,128]{2,1,0:T(8,128)S(1)} %get-tuple-element.98), channel_id=1, source_target_pairs={{0,4},{1,5},{2,6},{3,7},{4,0},{5,1},{6,2},{7,3},{8,12},{9,13},{10,... | collective-permute-start | bytes 602120 | tf_op jit(solution)/shard_map/ppermute | solution.py:403
  75.2 3.0 %collective-permute-done.16 = f32[1,392,128]{2,1,0:T(8,128)S(1)} collective-permute-done((f32[1,392,128]{2,1,0:T(8,128)S(1)}, f32[1,392,128]{2,1,0:T(8,128)S(1)}, u32[]{:S(2)}, u32[]{:S(2)}) %collective-permute-start.16) | collective-permute-done | bytes 200736 | tf_op jit(solution)/shard_map/ppermute | solution.py:403
  78.3 0.1 collective-permute-start.17
  78.4 1.3 %collective-permute-start.12 = (f32[1,384,128]{2,1,0:T(8,128)S(1)}, f32[1,384,128]{2,1,0:T(8,128)S(1)}, u32[]{:S(2)}, u32[]{:S(2)}) collective-permute-start(f32[1,384,128]{2,1,0:T(8,128)S(1)} %get-tuple-element.106), channel_id=1, source_target_pairs={{0,2},{1,3},{2,0},{3,1},{4,6},{5,7},{6,4},{7,5},{8,10},{9,11},{10,... | collective-permute-start | bytes 589832 | tf_op jit(solution)/shard_map/ppermute | solution.py:403
  79.7 0.0 collective-permute-done.10
  79.7 0.2 collective-permute-done.13
  79.9 2.0 %collective-permute-start.14 = (f32[1,384,128]{2,1,0:T(8,128)S(1)}, f32[1,384,128]{2,1,0:T(8,128)S(1)}, u32[]{:S(2)}, u32[]{:S(2)}) collective-permute-start(f32[1,384,128]{2,1,0:T(8,128)S(1)} %fusion), channel_id=1, source_target_pairs={{0,16},{1,17},{2,18},{3,19},{4,20},{5,21},{6,22},{7,23},{8,24},{9,... | collective-permute-start | bytes 589832 | tf_op jit(solution)/shard_map/ppermute | solution.py:403
  81.9 0.4 collective-permute-done.15
  82.3 5.0 %collective-permute-done.17 = f32[1,392,128]{2,1,0:T(8,128)S(1)} collective-permute-done((f32[1,392,128]{2,1,0:T(8,128)S(1)}, f32[1,392,128]{2,1,0:T(8,128)S(1)}, u32[]{:S(2)}, u32[]{:S(2)}) %collective-permute-start.17) | collective-permute-done | bytes 200736 | tf_op jit(solution)/shard_map/ppermute | solution.py:403
  87.3 4.1 %collective-permute-done.14 = f32[1,384,128]{2,1,0:T(8,128)S(1)} collective-permute-done((f32[1,384,128]{2,1,0:T(8,128)S(1)}, f32[1,384,128]{2,1,0:T(8,128)S(1)}, u32[]{:S(2)}, u32[]{:S(2)}) %collective-permute-start.14) | collective-permute-done | bytes 196640 | tf_op jit(solution)/shard_map/ppermute | solution.py:403
  91.4 0.1 fusion.3
  91.5 0.1 slice.61
  91.6 0.2 fusion.5
  91.9 0.2 fusion.4
  92.1 0.3 multiply_reduce_fusion
  92.4 0.7 maximum_add_fusion
  (23 shorter events, 0.3 us)
Async XLA Ops:
  0.0 0.7 copy-start.2
  0.7 0.7 copy-start.4
  0.7 0.7 copy-start.3
  0.7 0.7 copy-start.5
  1.4 1.1 %copy-start = (f32[128,9,128]{2,0,1:T(8,128)S(1)}, f32[128,9,128]{2,0,1:T(8,128)}, u32[]{:S(2)}) copy-start(f32[128,9,128]{2,0,1:T(8,128)} %param.6) | copy-start | bytes 1769476
  3.2 30.5 %collective-permute-start = (f32[146,8,128]{2,1,0:T(8,128)S(1)}, f32[146,8,128]{2,1,0:T(8,128)S(1)}, u32[]{:S(2)}, u32[]{:S(2)}) collective-permute-start(f32[146,8,128]{2,1,0:T(8,128)S(1)} %bitcast.28), channel_id=1, source_target_pairs={{0,16},{1,17},{2,18},{3,19},{4,20},{5,21},{6,22},{7,23},{8,24},{9,... | collective-permute-start | bytes 1794056 | tf_op jit(solution)/shard_map/ppermute | solution.py:403
  7.2 26.4 %collective-permute-start.1 = (f32[146,8,128]{2,1,0:T(8,128)S(1)}, f32[146,8,128]{2,1,0:T(8,128)S(1)}, u32[]{:S(2)}, u32[]{:S(2)}) collective-permute-start(f32[146,8,128]{2,1,0:T(8,128)S(1)} %bitcast.29), channel_id=1, source_target_pairs={{0,2},{1,3},{2,0},{3,1},{4,6},{5,7},{6,4},{7,5},{8,10},{9,11},{10,... | collective-permute-start | bytes 1794056 | tf_op jit(solution)/shard_map/ppermute | solution.py:403
  8.7 24.9 %collective-permute-start.2 = (f32[146,8,128]{2,1,0:T(8,128)S(1)}, f32[146,8,128]{2,1,0:T(8,128)S(1)}, u32[]{:S(2)}, u32[]{:S(2)}) collective-permute-start(f32[146,8,128]{2,1,0:T(8,128)S(1)} %bitcast.30), channel_id=1, source_target_pairs={{0,1},{1,0},{2,3},{3,2},{4,5},{5,4},{6,7},{7,6},{8,9},{9,8},{10,11... | collective-permute-start | bytes 1794056 | tf_op jit(solution)/shard_map/ppermute | solution.py:403
  8.7 27.6 %collective-permute-start.3 = (f32[146,8,128]{2,1,0:T(8,128)S(1)}, f32[146,8,128]{2,1,0:T(8,128)S(1)}, u32[]{:S(2)}, u32[]{:S(2)}) collective-permute-start(f32[146,8,128]{2,1,0:T(8,128)S(1)} %bitcast.31), channel_id=1, source_target_pairs={{0,8},{1,9},{2,10},{3,11},{4,12},{5,13},{6,14},{7,15},{8,0},{9,1},... | collective-permute-start | bytes 1794056 | tf_op jit(solution)/shard_map/ppermute | solution.py:403
  10.3 26.0 %collective-permute-start.4 = (f32[146,8,128]{2,1,0:T(8,128)S(1)}, f32[146,8,128]{2,1,0:T(8,128)S(1)}, u32[]{:S(2)}, u32[]{:S(2)}) collective-permute-start(f32[146,8,128]{2,1,0:T(8,128)S(1)} %bitcast.32), channel_id=1, source_target_pairs={{0,4},{1,5},{2,6},{3,7},{4,0},{5,1},{6,2},{7,3},{8,12},{9,13},{10,... | collective-permute-start | bytes 1794056 | tf_op jit(solution)/shard_map/ppermute | solution.py:403
  36.3 2.6 %collective-permute-start.7 = (f32[146,8,128]{2,1,0:T(8,128)S(1)}, f32[146,8,128]{2,1,0:T(8,128)S(1)}, u32[]{:S(2)}, u32[]{:S(2)}) collective-permute-start(f32[146,8,128]{2,1,0:T(8,128)S(1)} %collective-permute-done.refs_1_), channel_id=1, source_target_pairs={{0,1},{1,0},{2,3},{3,2},{4,5},{5,4},{6,7},{7,6},{8,9},{9,8},{10,11... | collective-permute-start | bytes 1794056 | tf_op jit(solution)/shard_map/ppermute | solution.py:403
  36.3 2.9 %collective-permute-start.8 = (f32[146,8,128]{2,1,0:T(8,128)S(1)}, f32[146,8,128]{2,1,0:T(8,128)S(1)}, u32[]{:S(2)}, u32[]{:S(2)}) collective-permute-start(f32[146,8,128]{2,1,0:T(8,128)S(1)} %collective-permute-done.1.refs_2_), channel_id=1, source_target_pairs={{0,1},{1,0},{2,3},{3,2},{4,5},{5,4},{6,7},{7,6},{8,9},{9,8},{10,11... | collective-permute-start | bytes 1794056 | tf_op jit(solution)/shard_map/ppermute | solution.py:403
  36.8 15.9 %collective-permute-start.5 = (f32[146,8,128]{2,1,0:T(8,128)S(1)}, f32[146,8,128]{2,1,0:T(8,128)S(1)}, u32[]{:S(2)}, u32[]{:S(2)}) collective-permute-start(f32[146,8,128]{2,1,0:T(8,128)S(1)} %collective-permute-done.refs_1_), channel_id=1, source_target_pairs={{0,2},{1,3},{2,0},{3,1},{4,6},{5,7},{6,4},{7,5},{8,10},{9,11},{10,... | collective-permute-start | bytes 1794056 | tf_op jit(solution)/shard_map/ppermute | solution.py:403
  37.4 15.3 %collective-permute-start.6 = (f32[146,8,128]{2,1,0:T(8,128)S(1)}, f32[146,8,128]{2,1,0:T(8,128)S(1)}, u32[]{:S(2)}, u32[]{:S(2)}) collective-permute-start(f32[146,8,128]{2,1,0:T(8,128)S(1)} %collective-permute-done.3.refs_6_.refs_8_), channel_id=1, source_target_pairs={{0,4},{1,5},{2,6},{3,7},{4,0},{5,1},{6,2},{7,3},{8,12},{9,13},{10,... | collective-permute-start | bytes 1794056 | tf_op jit(solution)/shard_map/ppermute | solution.py:403
  52.7 2.1 %collective-permute-start.9 = (f32[146,8,128]{2,1,0:T(8,128)S(1)}, f32[146,8,128]{2,1,0:T(8,128)S(1)}, u32[]{:S(2)}, u32[]{:S(2)}) collective-permute-start(f32[146,8,128]{2,1,0:T(8,128)S(1)} %collective-permute-done.5.refs_3_), channel_id=1, source_target_pairs={{0,1},{1,0},{2,3},{3,2},{4,5},{5,4},{6,7},{7,6},{8,9},{9,8},{10,11... | collective-permute-start | bytes 1794056 | tf_op jit(solution)/shard_map/ppermute | solution.py:403
  68.1 4.5 %collective-permute-start.11 = (f32[2,384,128]{2,1,0:T(8,128)S(1)}, f32[2,384,128]{2,1,0:T(8,128)S(1)}, u32[]{:S(2)}, u32[]{:S(2)}) collective-permute-start(f32[2,384,128]{2,1,0:T(8,128)S(1)} %get-tuple-element.94), channel_id=1, source_target_pairs={{0,1},{1,0},{2,3},{3,2},{4,5},{5,4},{6,7},{7,6},{8,9},{9,8},{10,11... | collective-permute-start | bytes 1179656 | tf_op jit(solution)/shard_map/ppermute | solution.py:403
  68.2 10.1 %collective-permute-start.16 = (f32[1,392,128]{2,1,0:T(8,128)S(1)}, f32[1,392,128]{2,1,0:T(8,128)S(1)}, u32[]{:S(2)}, u32[]{:S(2)}) collective-permute-start(f32[1,392,128]{2,1,0:T(8,128)S(1)} %get-tuple-element.100), channel_id=1, source_target_pairs={{0,4},{1,5},{2,6},{3,7},{4,0},{5,1},{6,2},{7,3},{8,12},{9,13},{10,... | collective-permute-start | bytes 602120 | tf_op jit(solution)/shard_map/ppermute | solution.py:403
  72.4 7.3 %collective-permute-start.10 = (f32[2,384,128]{2,1,0:T(8,128)S(1)}, f32[2,384,128]{2,1,0:T(8,128)S(1)}, u32[]{:S(2)}, u32[]{:S(2)}) collective-permute-start(f32[2,384,128]{2,1,0:T(8,128)S(1)} %get-tuple-element.92), channel_id=1, source_target_pairs={{0,1},{1,0},{2,3},{3,2},{4,5},{5,4},{6,7},{7,6},{8,9},{9,8},{10,11... | collective-permute-start | bytes 1179656 | tf_op jit(solution)/shard_map/ppermute | solution.py:403
  72.6 1.1 %copy-start.1 = (f32[128,9,128]{2,0,1:T(8,128)S(1)}, f32[128,9,128]{2,0,1:T(8,128)}, u32[]{:S(2)}) copy-start(f32[128,9,128]{2,0,1:T(8,128)} %param.6) | copy-start | bytes 1769476
  72.7 7.2 %collective-permute-start.13 = (f32[1,384,128]{2,1,0:T(8,128)S(1)}, f32[1,384,128]{2,1,0:T(8,128)S(1)}, u32[]{:S(2)}, u32[]{:S(2)}) collective-permute-start(f32[1,384,128]{2,1,0:T(8,128)S(1)} %get-tuple-element.107), channel_id=1, source_target_pairs={{0,2},{1,3},{2,0},{3,1},{4,6},{5,7},{6,4},{7,5},{8,10},{9,11},{10,... | collective-permute-start | bytes 589832 | tf_op jit(solution)/shard_map/ppermute | solution.py:403
  73.7 8.6 %collective-permute-start.15 = (f32[1,392,128]{2,1,0:T(8,128)S(1)}, f32[1,392,128]{2,1,0:T(8,128)S(1)}, u32[]{:S(2)}, u32[]{:S(2)}) collective-permute-start(f32[1,392,128]{2,1,0:T(8,128)S(1)} %get-tuple-element.98), channel_id=1, source_target_pairs={{0,4},{1,5},{2,6},{3,7},{4,0},{5,1},{6,2},{7,3},{8,12},{9,13},{10,... | collective-permute-start | bytes 602120 | tf_op jit(solution)/shard_map/ppermute | solution.py:403
  78.3 9.0 %collective-permute-start.17 = (f32[1,392,128]{2,1,0:T(8,128)S(1)}, f32[1,392,128]{2,1,0:T(8,128)S(1)}, u32[]{:S(2)}, u32[]{:S(2)}) collective-permute-start(f32[1,392,128]{2,1,0:T(8,128)S(1)} %add.54), channel_id=1, source_target_pairs={{0,8},{1,9},{2,10},{3,11},{4,12},{5,13},{6,14},{7,15},{8,0},{9,1},... | collective-permute-start | bytes 602120 | tf_op jit(solution)/shard_map/ppermute | solution.py:403
  78.4 8.9 %collective-permute-start.12 = (f32[1,384,128]{2,1,0:T(8,128)S(1)}, f32[1,384,128]{2,1,0:T(8,128)S(1)}, u32[]{:S(2)}, u32[]{:S(2)}) collective-permute-start(f32[1,384,128]{2,1,0:T(8,128)S(1)} %get-tuple-element.106), channel_id=1, source_target_pairs={{0,2},{1,3},{2,0},{3,1},{4,6},{5,7},{6,4},{7,5},{8,10},{9,11},{10,... | collective-permute-start | bytes 589832 | tf_op jit(solution)/shard_map/ppermute | solution.py:403
  79.9 11.5 %collective-permute-start.14 = (f32[1,384,128]{2,1,0:T(8,128)S(1)}, f32[1,384,128]{2,1,0:T(8,128)S(1)}, u32[]{:S(2)}, u32[]{:S(2)}) collective-permute-start(f32[1,384,128]{2,1,0:T(8,128)S(1)} %fusion), channel_id=1, source_target_pairs={{0,16},{1,17},{2,18},{3,19},{4,20},{5,21},{6,22},{7,23},{8,24},{9,... | collective-permute-start | bytes 589832 | tf_op jit(solution)/shard_map/ppermute | solution.py:403

commit v11 on v10

--- a/solution.py
+++ b/solution.py
@@ -49,8 +49,12 @@
 def products(sub, first, second, burgers):
     major = jnp.where(sub < 3, first[0], jnp.where(sub < 6, first[1], first[2]))
     minor = jnp.where(sub % 3 == 0, second[0], jnp.where(sub % 3 == 1, second[1], second[2]))
-    rest = place(sub, {0: first[2] * second[2], 1: burgers[0], 2: burgers[1], 3: burgers[2]}, 0.0)
-    return [head(major * minor), head(rest)], [major * minor - head(major * minor), rest - head(rest)]
+    rows = {0: first[2] * second[2], 1: burgers[0], 2: burgers[1]}
+    parts = []
+    for value in (major * minor, place(sub % 4, rows, burgers[2])):
+        high = head(value)
+        parts.append((high, value - high))
+    return parts
 
 
 def operands(near, far):
@@ -68,8 +72,9 @@
     left = [
         place(sub, {1: middle, 5: middle, 3: low, **end}, high) for (high, middle, low), end in zip(parts, ends)
     ]
-    high, low = products(sub, near[3:6], near[6:9], near[3:6])
-    left = tall(left + [zero] + high + low + high)
+    (main, main_low), (rest, rest_low) = products(sub, near[3:6], near[6:9], near[3:6])
+    half = sub < 4
+    left = tall(left + [main, jnp.where(half, rest, rest_low), main_low, main, jnp.where(half, rest, 0.0)])
 
     parts, square, far_sums, far_spot = tile_parts(sub, far)
     square = thirds(square + CORE)
@@ -78,8 +83,9 @@
         place(sub, {2: -2.0 * middle, 5: -2.0 * middle, 4: -2.0 * low, **end}, -2.0 * high)
         for (high, middle, low), end in zip(parts, ends)
     ]
-    high, low = products(sub, far[6:9], far[3:6], far[3:6])
-    return left.T, tall(spread + [zero]), tall(high + high + low), near_sums, near_spot, far_sums, far_spot
+    (main, main_low), (rest, rest_low) = products(sub, far[6:9], far[3:6], far[3:6])
+    numerator = tall([zero, main, rest, main, main_low, jnp.where(half, rest_low, 0.0)])
+    return left.T, tall(spread + [zero]), numerator, near_sums, near_spot, far_sums, far_spot
 
 
 def matmul(left, right, contract=(1, 0)):
@@ -207,7 +213,7 @@
             stash = lax.rem(group, 3)
             left_ref[k] = left
             right_ref[k, : spread.shape[0], :width] = spread
-            right_ref[k, spread.shape[0] :, width:] = numerator
+            right_ref[k, right_ref.shape[1] - numerator.shape[0] :, width:] = numerator
             sums_ref[stash, k, 0] = near_rows
             sums_ref[stash, k, 1] = far_rows
             spots_ref[stash, k, 0] = near_spot
@@ -265,7 +271,7 @@
         shapes += [(count, 3 * tiles + 8, width) for count in counts[1]]
     else:
         shapes = [(1, 3 * tiles, width)] * (near_number + far_number)
-    depth, sum_rows = 80, 16
+    depth, sum_rows = 64, 16
     share = len(near) * len(far) / (totals[0] * totals[1])
     elements = int(share * slot_count / 3) * width * width
 

time: 94.3 us -> 95.1 us (level); the launches traced: 93.1 us -> 95.6 us
  starting transfers between devices: 21.5 us -> 13.8 us
  Pallas kernels: 27.5 us -> 33.2 us
  waiting for transfers between devices: 39.4 us -> 43.6 us
    ppermute x18, starting transfers between devices: 21.5 us -> 13.8 us  [swap(): return lax.ppermute(value, AXES, [(k, k ^ mask) for k in range(devices)])]
    pallas_call x2, Pallas kernels: 26.8 us -> 32.4 us  [run_pairs(): pl.pallas_call(kernel, out_shape=[jax.ShapeDtypeStruct(shape, jnp.float32...]
    ppermute x18, waiting for transfers between devices: 39.4 us -> 43.6 us  [swap(): return lax.ppermute(value, AXES, [(k, k ^ mask) for k in range(devices)])]
  transfers between devices with their start and end apart: 18 -> 18, of which waited for: 9 -> 10; matrix products, arithmetic and copies ran while one was open for 0% -> 0% of each run, Pallas kernels for 14% -> 16%
where the time goes in v11:
time: 95.1 us; the launch traced here: 95.6 us
  waiting for transfers between devices  43.6 us (46%)
  Pallas kernels  33.2 us (35%)
  starting transfers between devices  13.8 us (15%)
  local copies, waits for them, and re-layouts  2.51 us (3%)
  other arithmetic  1.25 us (1%)
    ppermute x18, waiting for transfers between devices, swap(): return lax.ppermute(value, AXES, [(k, k ^ mask) for k in range(devices)])  43.6 us
    pallas_call x2, Pallas kernels, run_pairs(): pl.pallas_call(kernel, out_shape=[jax.ShapeDtypeStruct(shape, jnp.float32...  32.4 us
    ppermute x18, starting transfers between devices, swap(): return lax.ppermute(value, AXES, [(k, k ^ mask) for k in range(devices)])  13.8 us
    unnamed x12, local copies, waits for them, and re-layouts  2.39 us
  transfers between devices with their start and end apart: 18, of which 10 were waited for; matrix products, arithmetic and copies ran while one was open for 0% of the time, Pallas kernels for 16%

profile of v11, /device:TPU:0, one launch (start us, length us, event | category | flops | bytes accessed | tf_op | source)
XLA Modules:
  0.0 95.6 jit_solution(16765447744371388139)
XLA Ops:
  0.7 0.6 copy-done.4
  1.4 0.0 copy-done.3
  1.4 1.1 %copy-done = f32[128,9,128]{2,0,1:T(8,128)S(1)} copy-done((f32[128,9,128]{2,0,1:T(8,128)S(1)}, f32[128,9,128]{2,0,1:T(8,128)}, u32[]{:S(2)}) %copy-start) | copy-done | bytes 589848
  2.4 0.7 pack.1
  3.2 4.0 %collective-permute-start = (f32[146,8,128]{2,1,0:T(8,128)S(1)}, f32[146,8,128]{2,1,0:T(8,128)S(1)}, u32[]{:S(2)}, u32[]{:S(2)}) collective-permute-start(f32[146,8,128]{2,1,0:T(8,128)S(1)} %bitcast.28), channel_id=1, source_target_pairs={{0,16},{1,17},{2,18},{3,19},{4,20},{5,21},{6,22},{7,23},{8,24},{9,... | collective-permute-start | bytes 1794056 | tf_op jit(solution)/shard_map/ppermute | solution.py:409
  7.2 1.5 %collective-permute-start.1 = (f32[146,8,128]{2,1,0:T(8,128)S(1)}, f32[146,8,128]{2,1,0:T(8,128)S(1)}, u32[]{:S(2)}, u32[]{:S(2)}) collective-permute-start(f32[146,8,128]{2,1,0:T(8,128)S(1)} %bitcast.29), channel_id=1, source_target_pairs={{0,2},{1,3},{2,0},{3,1},{4,6},{5,7},{6,4},{7,5},{8,10},{9,11},{10,... | collective-permute-start | bytes 1794056 | tf_op jit(solution)/shard_map/ppermute | solution.py:409
  8.7 0.0 collective-permute-start.2
  8.7 1.6 %collective-permute-start.3 = (f32[146,8,128]{2,1,0:T(8,128)S(1)}, f32[146,8,128]{2,1,0:T(8,128)S(1)}, u32[]{:S(2)}, u32[]{:S(2)}) collective-permute-start(f32[146,8,128]{2,1,0:T(8,128)S(1)} %bitcast.31), channel_id=1, source_target_pairs={{0,8},{1,9},{2,10},{3,11},{4,12},{5,13},{6,14},{7,15},{8,0},{9,1},... | collective-permute-start | bytes 1794056 | tf_op jit(solution)/shard_map/ppermute | solution.py:409
  10.3 1.5 %collective-permute-start.4 = (f32[146,8,128]{2,1,0:T(8,128)S(1)}, f32[146,8,128]{2,1,0:T(8,128)S(1)}, u32[]{:S(2)}, u32[]{:S(2)}) collective-permute-start(f32[146,8,128]{2,1,0:T(8,128)S(1)} %bitcast.32), channel_id=1, source_target_pairs={{0,4},{1,5},{2,6},{3,7},{4,0},{5,1},{6,2},{7,3},{8,12},{9,13},{10,... | collective-permute-start | bytes 1794056 | tf_op jit(solution)/shard_map/ppermute | solution.py:409
  11.8 21.8 %collective-permute-done.refs_1_ = f32[146,8,128]{2,1,0:T(8,128)S(1)} collective-permute-done((f32[146,8,128]{2,1,0:T(8,128)S(1)}, f32[146,8,128]{2,1,0:T(8,128)S(1)}, u32[]{:S(2)}, u32[]{:S(2)}) %collective-permute-start) | collective-permute-done | bytes 598048 | tf_op jit(solution)/shard_map/ppermute | solution.py:409
  33.6 0.0 collective-permute-done.1.refs_2_
  33.6 0.0 collective-permute-done.2.refs_3_.refs_4_
  33.6 2.7 %collective-permute-done.3.refs_6_.refs_8_ = f32[146,8,128]{2,1,0:T(8,128)S(1)} collective-permute-done((f32[146,8,128]{2,1,0:T(8,128)S(1)}, f32[146,8,128]{2,1,0:T(8,128)S(1)}, u32[]{:S(2)}, u32[]{:S(2)}) %collective-permute-start.3) | collective-permute-done | bytes 598048 | tf_op jit(solution)/shard_map/ppermute | solution.py:409
  36.3 0.0 collective-permute-done.4.refs_7_.refs_9_
  36.3 0.0 collective-permute-start.7
  36.3 0.5 collective-permute-start.8
  36.8 0.6 collective-permute-start.5
  37.4 1.5 %collective-permute-start.6 = (f32[146,8,128]{2,1,0:T(8,128)S(1)}, f32[146,8,128]{2,1,0:T(8,128)S(1)}, u32[]{:S(2)}, u32[]{:S(2)}) collective-permute-start(f32[146,8,128]{2,1,0:T(8,128)S(1)} %collective-permute-done.3.refs_6_.refs_8_), channel_id=1, source_target_pairs={{0,4},{1,5},{2,6},{3,7},{4,0},{5,1},{6,2},{7,3},{8,12},{9,13},{10,... | collective-permute-start | bytes 1794056 | tf_op jit(solution)/shard_map/ppermute | solution.py:409
  38.9 0.0 collective-permute-done.7.refs_4_.refs_5_
  38.9 0.3 collective-permute-done.8.refs_5_.refs_6_
  39.2 14.8 %early_pairs.1 = (f32[1,384,128]{2,1,0:T(8,128)S(1)}, f32[1,384,128]{2,1,0:T(8,128)S(1)}, f32[1,384,128]{2,1,0:T(8,128)S(1)}, f32[1,384,128]{2,1,0:T(8,128)S(1)}...) custom-call(f32[146,8,128]{2,1,0:T(8,128)S(1)} %bitcast.33, ...), custom_call_target="tpu_custom_call" | custom-call | flops 1572864 | bytes 65536 | tf_op jit(solution)/shard_map/early_pairs/pallas_call | solution.py:304
  54.0 0.0 collective-permute-done.6.refs_10_
  54.0 0.2 collective-permute-start.9
  54.3 1.8 %collective-permute-done.9.refs_7_ = f32[146,8,128]{2,1,0:T(8,128)S(1)} collective-permute-done((f32[146,8,128]{2,1,0:T(8,128)S(1)}, f32[146,8,128]{2,1,0:T(8,128)S(1)}, u32[]{:S(2)}, u32[]{:S(2)}) %collective-permute-start.9) | collective-permute-done | bytes 598048 | tf_op jit(solution)/shard_map/ppermute | solution.py:409
  56.1 17.6 %pairs.1 = (f32[1,384,128]{2,1,0:T(8,128)S(1)}, f32[1,384,128]{2,1,0:T(8,128)S(1)}, f32[1,384,128]{2,1,0:T(8,128)S(1)}, f32[1,384,128]{2,1,0:T(8,128)S(1)}, f32[...) custom-call(f32[146,8,128]{2,1,0:T(8,128)S(1)} %bitcast.34, ...), custom_call_target="tpu_custom_call" | custom-call | flops 2785280000 | bytes 65536 | tf_op jit(solution)/shard_map/pairs/pallas_call | solution.py:304
  73.7 0.1 collective-permute-start.11
  73.8 0.1 collective-permute-start.16
  73.9 0.4 collective-permute-start.10
  74.3 1.2 %collective-permute-done.11 = f32[2,384,128]{2,1,0:T(8,128)S(1)} collective-permute-done((f32[2,384,128]{2,1,0:T(8,128)S(1)}, f32[2,384,128]{2,1,0:T(8,128)S(1)}, u32[]{:S(2)}, u32[]{:S(2)}) %collective-permute-start.11) | collective-permute-done | bytes 393248 | tf_op jit(solution)/shard_map/ppermute | solution.py:409
  75.6 0.4 collective-permute-start.13
  75.9 0.6 copy-done.1
  76.6 0.6 collective-permute-start.15
  77.2 4.4 %collective-permute-done.16 = f32[1,392,128]{2,1,0:T(8,128)S(1)} collective-permute-done((f32[1,392,128]{2,1,0:T(8,128)S(1)}, f32[1,392,128]{2,1,0:T(8,128)S(1)}, u32[]{:S(2)}, u32[]{:S(2)}) %collective-permute-start.16) | collective-permute-done | bytes 200736 | tf_op jit(solution)/shard_map/ppermute | solution.py:409
  81.7 0.1 collective-permute-start.17
  81.8 0.7 collective-permute-start.12
  82.5 0.0 collective-permute-done.10
  82.5 0.1 collective-permute-done.13
  82.6 0.1 collective-permute-start.14
  82.7 2.8 %collective-permute-done.15 = f32[1,392,128]{2,1,0:T(8,128)S(1)} collective-permute-done((f32[1,392,128]{2,1,0:T(8,128)S(1)}, f32[1,392,128]{2,1,0:T(8,128)S(1)}, u32[]{:S(2)}, u32[]{:S(2)}) %collective-permute-start.15) | collective-permute-done | bytes 200736 | tf_op jit(solution)/shard_map/ppermute | solution.py:409
  85.5 4.0 %collective-permute-done.17 = f32[1,392,128]{2,1,0:T(8,128)S(1)} collective-permute-done((f32[1,392,128]{2,1,0:T(8,128)S(1)}, f32[1,392,128]{2,1,0:T(8,128)S(1)}, u32[]{:S(2)}, u32[]{:S(2)}) %collective-permute-start.17) | collective-permute-done | bytes 200736 | tf_op jit(solution)/shard_map/ppermute | solution.py:409
  89.6 0.0 collective-permute-done.12
  89.6 4.3 %collective-permute-done.14 = f32[1,384,128]{2,1,0:T(8,128)S(1)} collective-permute-done((f32[1,384,128]{2,1,0:T(8,128)S(1)}, f32[1,384,128]{2,1,0:T(8,128)S(1)}, u32[]{:S(2)}, u32[]{:S(2)}) %collective-permute-start.14) | collective-permute-done | bytes 196640 | tf_op jit(solution)/shard_map/ppermute | solution.py:409
  93.9 0.1 fusion.3
  94.0 0.1 slice.61
  94.1 0.2 fusion.5
  94.3 0.2 fusion.4
  94.6 0.3 multiply_reduce_fusion
  94.9 0.7 maximum_add_fusion
  (23 shorter events, 0.3 us)
Async XLA Ops:
  0.0 0.7 copy-start.2
  0.7 0.7 copy-start.4
  0.7 0.7 copy-start.3
  0.7 0.7 copy-start.5
  1.4 1.1 %copy-start = (f32[128,9,128]{2,0,1:T(8,128)S(1)}, f32[128,9,128]{2,0,1:T(8,128)}, u32[]{:S(2)}) copy-start(f32[128,9,128]{2,0,1:T(8,128)} %param.6) | copy-start | bytes 1769476
  3.2 30.5 %collective-permute-start = (f32[146,8,128]{2,1,0:T(8,128)S(1)}, f32[146,8,128]{2,1,0:T(8,128)S(1)}, u32[]{:S(2)}, u32[]{:S(2)}) collective-permute-start(f32[146,8,128]{2,1,0:T(8,128)S(1)} %bitcast.28), channel_id=1, source_target_pairs={{0,16},{1,17},{2,18},{3,19},{4,20},{5,21},{6,22},{7,23},{8,24},{9,... | collective-permute-start | bytes 1794056 | tf_op jit(solution)/shard_map/ppermute | solution.py:409
  7.2 26.4 %collective-permute-start.1 = (f32[146,8,128]{2,1,0:T(8,128)S(1)}, f32[146,8,128]{2,1,0:T(8,128)S(1)}, u32[]{:S(2)}, u32[]{:S(2)}) collective-permute-start(f32[146,8,128]{2,1,0:T(8,128)S(1)} %bitcast.29), channel_id=1, source_target_pairs={{0,2},{1,3},{2,0},{3,1},{4,6},{5,7},{6,4},{7,5},{8,10},{9,11},{10,... | collective-permute-start | bytes 1794056 | tf_op jit(solution)/shard_map/ppermute | solution.py:409
  8.7 24.9 %collective-permute-start.2 = (f32[146,8,128]{2,1,0:T(8,128)S(1)}, f32[146,8,128]{2,1,0:T(8,128)S(1)}, u32[]{:S(2)}, u32[]{:S(2)}) collective-permute-start(f32[146,8,128]{2,1,0:T(8,128)S(1)} %bitcast.30), channel_id=1, source_target_pairs={{0,1},{1,0},{2,3},{3,2},{4,5},{5,4},{6,7},{7,6},{8,9},{9,8},{10,11... | collective-permute-start | bytes 1794056 | tf_op jit(solution)/shard_map/ppermute | solution.py:409
  8.7 27.6 %collective-permute-start.3 = (f32[146,8,128]{2,1,0:T(8,128)S(1)}, f32[146,8,128]{2,1,0:T(8,128)S(1)}, u32[]{:S(2)}, u32[]{:S(2)}) collective-permute-start(f32[146,8,128]{2,1,0:T(8,128)S(1)} %bitcast.31), channel_id=1, source_target_pairs={{0,8},{1,9},{2,10},{3,11},{4,12},{5,13},{6,14},{7,15},{8,0},{9,1},... | collective-permute-start | bytes 1794056 | tf_op jit(solution)/shard_map/ppermute | solution.py:409
  10.3 26.0 %collective-permute-start.4 = (f32[146,8,128]{2,1,0:T(8,128)S(1)}, f32[146,8,128]{2,1,0:T(8,128)S(1)}, u32[]{:S(2)}, u32[]{:S(2)}) collective-permute-start(f32[146,8,128]{2,1,0:T(8,128)S(1)} %bitcast.32), channel_id=1, source_target_pairs={{0,4},{1,5},{2,6},{3,7},{4,0},{5,1},{6,2},{7,3},{8,12},{9,13},{10,... | collective-permute-start | bytes 1794056 | tf_op jit(solution)/shard_map/ppermute | solution.py:409
  36.3 2.6 %collective-permute-start.7 = (f32[146,8,128]{2,1,0:T(8,128)S(1)}, f32[146,8,128]{2,1,0:T(8,128)S(1)}, u32[]{:S(2)}, u32[]{:S(2)}) collective-permute-start(f32[146,8,128]{2,1,0:T(8,128)S(1)} %collective-permute-done.refs_1_), channel_id=1, source_target_pairs={{0,1},{1,0},{2,3},{3,2},{4,5},{5,4},{6,7},{7,6},{8,9},{9,8},{10,11... | collective-permute-start | bytes 1794056 | tf_op jit(solution)/shard_map/ppermute | solution.py:409
  36.3 2.9 %collective-permute-start.8 = (f32[146,8,128]{2,1,0:T(8,128)S(1)}, f32[146,8,128]{2,1,0:T(8,128)S(1)}, u32[]{:S(2)}, u32[]{:S(2)}) collective-permute-start(f32[146,8,128]{2,1,0:T(8,128)S(1)} %collective-permute-done.1.refs_2_), channel_id=1, source_target_pairs={{0,1},{1,0},{2,3},{3,2},{4,5},{5,4},{6,7},{7,6},{8,9},{9,8},{10,11... | collective-permute-start | bytes 1794056 | tf_op jit(solution)/shard_map/ppermute | solution.py:409
  36.8 17.2 %collective-permute-start.5 = (f32[146,8,128]{2,1,0:T(8,128)S(1)}, f32[146,8,128]{2,1,0:T(8,128)S(1)}, u32[]{:S(2)}, u32[]{:S(2)}) collective-permute-start(f32[146,8,128]{2,1,0:T(8,128)S(1)} %collective-permute-done.refs_1_), channel_id=1, source_target_pairs={{0,2},{1,3},{2,0},{3,1},{4,6},{5,7},{6,4},{7,5},{8,10},{9,11},{10,... | collective-permute-start | bytes 1794056 | tf_op jit(solution)/shard_map/ppermute | solution.py:409
  37.4 16.7 %collective-permute-start.6 = (f32[146,8,128]{2,1,0:T(8,128)S(1)}, f32[146,8,128]{2,1,0:T(8,128)S(1)}, u32[]{:S(2)}, u32[]{:S(2)}) collective-permute-start(f32[146,8,128]{2,1,0:T(8,128)S(1)} %collective-permute-done.3.refs_6_.refs_8_), channel_id=1, source_target_pairs={{0,4},{1,5},{2,6},{3,7},{4,0},{5,1},{6,2},{7,3},{8,12},{9,13},{10,... | collective-permute-start | bytes 1794056 | tf_op jit(solution)/shard_map/ppermute | solution.py:409
  54.0 2.1 %collective-permute-start.9 = (f32[146,8,128]{2,1,0:T(8,128)S(1)}, f32[146,8,128]{2,1,0:T(8,128)S(1)}, u32[]{:S(2)}, u32[]{:S(2)}) collective-permute-start(f32[146,8,128]{2,1,0:T(8,128)S(1)} %collective-permute-done.5.refs_3_), channel_id=1, source_target_pairs={{0,1},{1,0},{2,3},{3,2},{4,5},{5,4},{6,7},{7,6},{8,9},{9,8},{10,11... | collective-permute-start | bytes 1794056 | tf_op jit(solution)/shard_map/ppermute | solution.py:409
  73.7 1.8 %collective-permute-start.11 = (f32[2,384,128]{2,1,0:T(8,128)S(1)}, f32[2,384,128]{2,1,0:T(8,128)S(1)}, u32[]{:S(2)}, u32[]{:S(2)}) collective-permute-start(f32[2,384,128]{2,1,0:T(8,128)S(1)} %get-tuple-element.94), channel_id=1, source_target_pairs={{0,1},{1,0},{2,3},{3,2},{4,5},{5,4},{6,7},{7,6},{8,9},{9,8},{10,11... | collective-permute-start | bytes 1179656 | tf_op jit(solution)/shard_map/ppermute | solution.py:409
  73.8 7.9 %collective-permute-start.16 = (f32[1,392,128]{2,1,0:T(8,128)S(1)}, f32[1,392,128]{2,1,0:T(8,128)S(1)}, u32[]{:S(2)}, u32[]{:S(2)}) collective-permute-start(f32[1,392,128]{2,1,0:T(8,128)S(1)} %get-tuple-element.100), channel_id=1, source_target_pairs={{0,4},{1,5},{2,6},{3,7},{4,0},{5,1},{6,2},{7,3},{8,12},{9,13},{10,... | collective-permute-start | bytes 602120 | tf_op jit(solution)/shard_map/ppermute | solution.py:409
  73.9 8.6 %collective-permute-start.10 = (f32[2,384,128]{2,1,0:T(8,128)S(1)}, f32[2,384,128]{2,1,0:T(8,128)S(1)}, u32[]{:S(2)}, u32[]{:S(2)}) collective-permute-start(f32[2,384,128]{2,1,0:T(8,128)S(1)} %get-tuple-element.92), channel_id=1, source_target_pairs={{0,1},{1,0},{2,3},{3,2},{4,5},{5,4},{6,7},{7,6},{8,9},{9,8},{10,11... | collective-permute-start | bytes 1179656 | tf_op jit(solution)/shard_map/ppermute | solution.py:409
  75.5 1.1 %copy-start.1 = (f32[128,9,128]{2,0,1:T(8,128)S(1)}, f32[128,9,128]{2,0,1:T(8,128)}, u32[]{:S(2)}) copy-start(f32[128,9,128]{2,0,1:T(8,128)} %param.6) | copy-start | bytes 1769476
  75.6 7.0 %collective-permute-start.13 = (f32[1,384,128]{2,1,0:T(8,128)S(1)}, f32[1,384,128]{2,1,0:T(8,128)S(1)}, u32[]{:S(2)}, u32[]{:S(2)}) collective-permute-start(f32[1,384,128]{2,1,0:T(8,128)S(1)} %get-tuple-element.107), channel_id=1, source_target_pairs={{0,2},{1,3},{2,0},{3,1},{4,6},{5,7},{6,4},{7,5},{8,10},{9,11},{10,... | collective-permute-start | bytes 589832 | tf_op jit(solution)/shard_map/ppermute | solution.py:409
  76.6 8.9 %collective-permute-start.15 = (f32[1,392,128]{2,1,0:T(8,128)S(1)}, f32[1,392,128]{2,1,0:T(8,128)S(1)}, u32[]{:S(2)}, u32[]{:S(2)}) collective-permute-start(f32[1,392,128]{2,1,0:T(8,128)S(1)} %get-tuple-element.98), channel_id=1, source_target_pairs={{0,4},{1,5},{2,6},{3,7},{4,0},{5,1},{6,2},{7,3},{8,12},{9,13},{10,... | collective-permute-start | bytes 602120 | tf_op jit(solution)/shard_map/ppermute | solution.py:409
  81.7 7.9 %collective-permute-start.17 = (f32[1,392,128]{2,1,0:T(8,128)S(1)}, f32[1,392,128]{2,1,0:T(8,128)S(1)}, u32[]{:S(2)}, u32[]{:S(2)}) collective-permute-start(f32[1,392,128]{2,1,0:T(8,128)S(1)} %add.54), channel_id=1, source_target_pairs={{0,8},{1,9},{2,10},{3,11},{4,12},{5,13},{6,14},{7,15},{8,0},{9,1},... | collective-permute-start | bytes 602120 | tf_op jit(solution)/shard_map/ppermute | solution.py:409
  81.8 7.8 %collective-permute-start.12 = (f32[1,384,128]{2,1,0:T(8,128)S(1)}, f32[1,384,128]{2,1,0:T(8,128)S(1)}, u32[]{:S(2)}, u32[]{:S(2)}) collective-permute-start(f32[1,384,128]{2,1,0:T(8,128)S(1)} %get-tuple-element.106), channel_id=1, source_target_pairs={{0,2},{1,3},{2,0},{3,1},{4,6},{5,7},{6,4},{7,5},{8,10},{9,11},{10,... | collective-permute-start | bytes 589832 | tf_op jit(solution)/shard_map/ppermute | solution.py:409
  82.6 11.3 %collective-permute-start.14 = (f32[1,384,128]{2,1,0:T(8,128)S(1)}, f32[1,384,128]{2,1,0:T(8,128)S(1)}, u32[]{:S(2)}, u32[]{:S(2)}) collective-permute-start(f32[1,384,128]{2,1,0:T(8,128)S(1)} %fusion), channel_id=1, source_target_pairs={{0,16},{1,17},{2,18},{3,19},{4,20},{5,21},{6,22},{7,23},{8,24},{9,... | collective-permute-start | bytes 589832 | tf_op jit(solution)/shard_map/ppermute | solution.py:409

commit v12 on v11

--- a/solution.py
+++ b/solution.py
@@ -466,6 +466,8 @@
             seen += count
         arrived = []
         for value, count in reversed(sent):
+            if arrived and step == steps[min(1, len(steps) - 1)]:
+                value, arrived[0] = lax.optimization_barrier((value, arrived[0]))
             got = swap(value, step)
             arrived = [got[k : k + 1] for k in range(count)] + arrived
         merged, at = [], 0

time: 95.1 us -> 94.2 us (level)
  Pallas kernels: 33.2 us -> 26.7 us
  starting transfers between devices: 13.8 us -> 19.3 us
    pallas_call x2, Pallas kernels: 32.4 us -> 25.9 us  [run_pairs(): pl.pallas_call(kernel, out_shape=[jax.ShapeDtypeStruct(shape, jnp.float32...]
    ppermute x18, starting transfers between devices: 13.8 us -> 19.3 us  [swap(): return lax.ppermute(value, AXES, [(k, k ^ mask) for k in range(devices)])]
  transfers between devices with their start and end apart: 18 -> 18, of which waited for: 10 -> 10; matrix products, arithmetic and copies ran while one was open for 0% -> 0% of each run, Pallas kernels for 16% -> 12%
where the time goes in v12:
time: 94.2 us
  waiting for transfers between devices  43 us (46%)
  Pallas kernels  26.7 us (28%)
  starting transfers between devices  19.3 us (20%)
  local copies, waits for them, and re-layouts  2.79 us (3%)
  other arithmetic  1.23 us (1%)
    ppermute x18, waiting for transfers between devices, swap(): return lax.ppermute(value, AXES, [(k, k ^ mask) for k in range(devices)])  43 us
    pallas_call x2, Pallas kernels, run_pairs(): pl.pallas_call(kernel, out_shape=[jax.ShapeDtypeStruct(shape, jnp.float32...  25.9 us
    ppermute x18, starting transfers between devices, swap(): return lax.ppermute(value, AXES, [(k, k ^ mask) for k in range(devices)])  19.3 us
    unnamed x12, local copies, waits for them, and re-layouts  2.67 us
  transfers between devices with their start and end apart: 18, of which 10 were waited for; matrix products, arithmetic and copies ran while one was open for 0% of the time, Pallas kernels for 12%

profile of v12, /device:TPU:0, one launch (start us, length us, event | category | flops | bytes accessed | tf_op | source)
XLA Modules:
  0.0 94.2 jit_solution(9782722287823535166)
XLA Ops:
  0.7 0.6 copy-done.4
  1.4 0.0 copy-done.3
  1.4 1.1 %copy-done = f32[128,9,128]{2,0,1:T(8,128)S(1)} copy-done((f32[128,9,128]{2,0,1:T(8,128)S(1)}, f32[128,9,128]{2,0,1:T(8,128)}, u32[]{:S(2)}) %copy-start) | copy-done | bytes 589848
  2.4 0.7 pack.1
  3.2 4.0 %collective-permute-start = (f32[146,8,128]{2,1,0:T(8,128)S(1)}, f32[146,8,128]{2,1,0:T(8,128)S(1)}, u32[]{:S(2)}, u32[]{:S(2)}) collective-permute-start(f32[146,8,128]{2,1,0:T(8,128)S(1)} %bitcast.28), channel_id=1, source_target_pairs={{0,16},{1,17},{2,18},{3,19},{4,20},{5,21},{6,22},{7,23},{8,24},{9,... | collective-permute-start | bytes 1794056 | tf_op jit(solution)/shard_map/ppermute | solution.py:409
  7.2 1.5 %collective-permute-start.1 = (f32[146,8,128]{2,1,0:T(8,128)S(1)}, f32[146,8,128]{2,1,0:T(8,128)S(1)}, u32[]{:S(2)}, u32[]{:S(2)}) collective-permute-start(f32[146,8,128]{2,1,0:T(8,128)S(1)} %bitcast.29), channel_id=1, source_target_pairs={{0,2},{1,3},{2,0},{3,1},{4,6},{5,7},{6,4},{7,5},{8,10},{9,11},{10,... | collective-permute-start | bytes 1794056 | tf_op jit(solution)/shard_map/ppermute | solution.py:409
  8.7 0.0 collective-permute-start.2
  8.7 1.6 %collective-permute-start.3 = (f32[146,8,128]{2,1,0:T(8,128)S(1)}, f32[146,8,128]{2,1,0:T(8,128)S(1)}, u32[]{:S(2)}, u32[]{:S(2)}) collective-permute-start(f32[146,8,128]{2,1,0:T(8,128)S(1)} %bitcast.31), channel_id=1, source_target_pairs={{0,8},{1,9},{2,10},{3,11},{4,12},{5,13},{6,14},{7,15},{8,0},{9,1},... | collective-permute-start | bytes 1794056 | tf_op jit(solution)/shard_map/ppermute | solution.py:409
  10.3 1.5 %collective-permute-start.4 = (f32[146,8,128]{2,1,0:T(8,128)S(1)}, f32[146,8,128]{2,1,0:T(8,128)S(1)}, u32[]{:S(2)}, u32[]{:S(2)}) collective-permute-start(f32[146,8,128]{2,1,0:T(8,128)S(1)} %bitcast.32), channel_id=1, source_target_pairs={{0,4},{1,5},{2,6},{3,7},{4,0},{5,1},{6,2},{7,3},{8,12},{9,13},{10,... | collective-permute-start | bytes 1794056 | tf_op jit(solution)/shard_map/ppermute | solution.py:409
  11.8 21.8 %collective-permute-done.refs_1_ = f32[146,8,128]{2,1,0:T(8,128)S(1)} collective-permute-done((f32[146,8,128]{2,1,0:T(8,128)S(1)}, f32[146,8,128]{2,1,0:T(8,128)S(1)}, u32[]{:S(2)}, u32[]{:S(2)}) %collective-permute-start) | collective-permute-done | bytes 598048 | tf_op jit(solution)/shard_map/ppermute | solution.py:409
  33.6 0.0 collective-permute-done.1.refs_2_
  33.6 0.0 collective-permute-done.2.refs_3_.refs_4_
  33.6 2.7 %collective-permute-done.3.refs_6_.refs_8_ = f32[146,8,128]{2,1,0:T(8,128)S(1)} collective-permute-done((f32[146,8,128]{2,1,0:T(8,128)S(1)}, f32[146,8,128]{2,1,0:T(8,128)S(1)}, u32[]{:S(2)}, u32[]{:S(2)}) %collective-permute-start.3) | collective-permute-done | bytes 598048 | tf_op jit(solution)/shard_map/ppermute | solution.py:409
  36.3 0.0 collective-permute-done.4.refs_7_.refs_9_
  36.3 0.0 collective-permute-start.7
  36.3 0.5 collective-permute-start.8
  36.8 0.6 collective-permute-start.5
  37.4 1.5 %collective-permute-start.6 = (f32[146,8,128]{2,1,0:T(8,128)S(1)}, f32[146,8,128]{2,1,0:T(8,128)S(1)}, u32[]{:S(2)}, u32[]{:S(2)}) collective-permute-start(f32[146,8,128]{2,1,0:T(8,128)S(1)} %collective-permute-done.3.refs_6_.refs_8_), channel_id=1, source_target_pairs={{0,4},{1,5},{2,6},{3,7},{4,0},{5,1},{6,2},{7,3},{8,12},{9,13},{10,... | collective-permute-start | bytes 1794056 | tf_op jit(solution)/shard_map/ppermute | solution.py:409
  38.9 0.0 collective-permute-done.7.refs_4_.refs_5_
  38.9 0.3 collective-permute-done.8.refs_5_.refs_6_
  39.2 11.2 %early_pairs.1 = (f32[1,384,128]{2,1,0:T(8,128)S(1)}, f32[1,384,128]{2,1,0:T(8,128)S(1)}, f32[1,384,128]{2,1,0:T(8,128)S(1)}, f32[1,384,128]{2,1,0:T(8,128)S(1)}...) custom-call(f32[146,8,128]{2,1,0:T(8,128)S(1)} %bitcast.33, ...), custom_call_target="tpu_custom_call" | custom-call | flops 1572864 | bytes 65536 | tf_op jit(solution)/shard_map/early_pairs/pallas_call | solution.py:304
  50.4 1.8 %collective-permute-done.5.refs_3_ = f32[146,8,128]{2,1,0:T(8,128)S(1)} collective-permute-done((f32[146,8,128]{2,1,0:T(8,128)S(1)}, f32[146,8,128]{2,1,0:T(8,128)S(1)}, u32[]{:S(2)}, u32[]{:S(2)}) %collective-permute-start.5) | collective-permute-done | bytes 598048 | tf_op jit(solution)/shard_map/ppermute | solution.py:409
  52.2 0.3 collective-permute-done.6.refs_10_
  52.5 0.0 collective-permute-start.9
  52.5 2.0 %collective-permute-done.9.refs_7_ = f32[146,8,128]{2,1,0:T(8,128)S(1)} collective-permute-done((f32[146,8,128]{2,1,0:T(8,128)S(1)}, f32[146,8,128]{2,1,0:T(8,128)S(1)}, u32[]{:S(2)}, u32[]{:S(2)}) %collective-permute-start.9) | collective-permute-done | bytes 598048 | tf_op jit(solution)/shard_map/ppermute | solution.py:409
  54.5 14.7 %pairs.1 = (f32[1,384,128]{2,1,0:T(8,128)S(1)}, f32[1,384,128]{2,1,0:T(8,128)S(1)}, f32[1,384,128]{2,1,0:T(8,128)S(1)}, f32[1,384,128]{2,1,0:T(8,128)S(1)}, f32[...) custom-call(f32[146,8,128]{2,1,0:T(8,128)S(1)} %bitcast.34, ...), custom_call_target="tpu_custom_call" | custom-call | flops 2785280000 | bytes 65536 | tf_op jit(solution)/shard_map/pairs/pallas_call | solution.py:304
  69.2 0.2 collective-permute-start.11
  69.4 0.0 collective-permute-start.15
  69.4 0.4 collective-permute-start.10
  69.8 1.2 %collective-permute-done.11 = f32[2,384,128]{2,1,0:T(8,128)S(1)} collective-permute-done((f32[2,384,128]{2,1,0:T(8,128)S(1)}, f32[2,384,128]{2,1,0:T(8,128)S(1)}, u32[]{:S(2)}, u32[]{:S(2)}) %collective-permute-start.11) | collective-permute-done | bytes 393248 | tf_op jit(solution)/shard_map/ppermute | solution.py:409
  71.1 0.1 collective-permute-start.12
  71.1 0.9 copy-done.1
  72.1 4.6 %collective-permute-done.15 = f32[1,392,128]{2,1,0:T(8,128)S(1)} collective-permute-done((f32[1,392,128]{2,1,0:T(8,128)S(1)}, f32[1,392,128]{2,1,0:T(8,128)S(1)}, u32[]{:S(2)}, u32[]{:S(2)}) %collective-permute-start.15) | collective-permute-done | bytes 200736 | tf_op jit(solution)/shard_map/ppermute | solution.py:409
  76.7 3.1 %collective-permute-start.17 = (f32[1,392,128]{2,1,0:T(8,128)S(1)}, f32[1,392,128]{2,1,0:T(8,128)S(1)}, u32[]{:S(2)}, u32[]{:S(2)}) collective-permute-start(f32[1,392,128]{2,1,0:T(8,128)S(1)} %add.54), channel_id=1, source_target_pairs={{0,8},{1,9},{2,10},{3,11},{4,12},{5,13},{6,14},{7,15},{8,0},{9,1},... | collective-permute-start | bytes 602120 | tf_op jit(solution)/shard_map/ppermute | solution.py:409
  79.8 0.3 collective-permute-start.16
  80.1 0.0 collective-permute-done.12
  80.1 0.0 collective-permute-done.10
  80.2 4.0 %collective-permute-start.14 = (f32[1,384,128]{2,1,0:T(8,128)S(1)}, f32[1,384,128]{2,1,0:T(8,128)S(1)}, u32[]{:S(2)}, u32[]{:S(2)}) collective-permute-start(f32[1,384,128]{2,1,0:T(8,128)S(1)} %fusion), channel_id=1, source_target_pairs={{0,16},{1,17},{2,18},{3,19},{4,20},{5,21},{6,22},{7,23},{8,24},{9,... | collective-permute-start | bytes 589832 | tf_op jit(solution)/shard_map/ppermute | solution.py:409
  84.2 0.0 collective-permute-start.13
  84.2 2.2 %collective-permute-done.17 = f32[1,392,128]{2,1,0:T(8,128)S(1)} collective-permute-done((f32[1,392,128]{2,1,0:T(8,128)S(1)}, f32[1,392,128]{2,1,0:T(8,128)S(1)}, u32[]{:S(2)}, u32[]{:S(2)}) %collective-permute-start.17) | collective-permute-done | bytes 200736 | tf_op jit(solution)/shard_map/ppermute | solution.py:409
  86.4 0.0 collective-permute-done.16
  86.4 6.1 %collective-permute-done.14 = f32[1,384,128]{2,1,0:T(8,128)S(1)} collective-permute-done((f32[1,384,128]{2,1,0:T(8,128)S(1)}, f32[1,384,128]{2,1,0:T(8,128)S(1)}, u32[]{:S(2)}, u32[]{:S(2)}) %collective-permute-start.14) | collective-permute-done | bytes 196640 | tf_op jit(solution)/shard_map/ppermute | solution.py:409
  92.5 0.0 collective-permute-done.13
  92.6 0.1 slice.61
  92.7 0.2 fusion.5
  92.9 0.2 fusion.4
  93.2 0.3 multiply_reduce_fusion
  93.5 0.7 maximum_add_fusion
  (23 shorter events, 0.3 us)
Async XLA Ops:
  0.0 0.7 copy-start.2
  0.7 0.7 copy-start.4
  0.7 0.7 copy-start.3
  0.7 0.7 copy-start.5
  1.4 1.1 %copy-start = (f32[128,9,128]{2,0,1:T(8,128)S(1)}, f32[128,9,128]{2,0,1:T(8,128)}, u32[]{:S(2)}) copy-start(f32[128,9,128]{2,0,1:T(8,128)} %param.6) | copy-start | bytes 1769476
  3.2 30.5 %collective-permute-start = (f32[146,8,128]{2,1,0:T(8,128)S(1)}, f32[146,8,128]{2,1,0:T(8,128)S(1)}, u32[]{:S(2)}, u32[]{:S(2)}) collective-permute-start(f32[146,8,128]{2,1,0:T(8,128)S(1)} %bitcast.28), channel_id=1, source_target_pairs={{0,16},{1,17},{2,18},{3,19},{4,20},{5,21},{6,22},{7,23},{8,24},{9,... | collective-permute-start | bytes 1794056 | tf_op jit(solution)/shard_map/ppermute | solution.py:409
  7.2 26.4 %collective-permute-start.1 = (f32[146,8,128]{2,1,0:T(8,128)S(1)}, f32[146,8,128]{2,1,0:T(8,128)S(1)}, u32[]{:S(2)}, u32[]{:S(2)}) collective-permute-start(f32[146,8,128]{2,1,0:T(8,128)S(1)} %bitcast.29), channel_id=1, source_target_pairs={{0,2},{1,3},{2,0},{3,1},{4,6},{5,7},{6,4},{7,5},{8,10},{9,11},{10,... | collective-permute-start | bytes 1794056 | tf_op jit(solution)/shard_map/ppermute | solution.py:409
  8.7 24.9 %collective-permute-start.2 = (f32[146,8,128]{2,1,0:T(8,128)S(1)}, f32[146,8,128]{2,1,0:T(8,128)S(1)}, u32[]{:S(2)}, u32[]{:S(2)}) collective-permute-start(f32[146,8,128]{2,1,0:T(8,128)S(1)} %bitcast.30), channel_id=1, source_target_pairs={{0,1},{1,0},{2,3},{3,2},{4,5},{5,4},{6,7},{7,6},{8,9},{9,8},{10,11... | collective-permute-start | bytes 1794056 | tf_op jit(solution)/shard_map/ppermute | solution.py:409
  8.7 27.6 %collective-permute-start.3 = (f32[146,8,128]{2,1,0:T(8,128)S(1)}, f32[146,8,128]{2,1,0:T(8,128)S(1)}, u32[]{:S(2)}, u32[]{:S(2)}) collective-permute-start(f32[146,8,128]{2,1,0:T(8,128)S(1)} %bitcast.31), channel_id=1, source_target_pairs={{0,8},{1,9},{2,10},{3,11},{4,12},{5,13},{6,14},{7,15},{8,0},{9,1},... | collective-permute-start | bytes 1794056 | tf_op jit(solution)/shard_map/ppermute | solution.py:409
  10.3 26.0 %collective-permute-start.4 = (f32[146,8,128]{2,1,0:T(8,128)S(1)}, f32[146,8,128]{2,1,0:T(8,128)S(1)}, u32[]{:S(2)}, u32[]{:S(2)}) collective-permute-start(f32[146,8,128]{2,1,0:T(8,128)S(1)} %bitcast.32), channel_id=1, source_target_pairs={{0,4},{1,5},{2,6},{3,7},{4,0},{5,1},{6,2},{7,3},{8,12},{9,13},{10,... | collective-permute-start | bytes 1794056 | tf_op jit(solution)/shard_map/ppermute | solution.py:409
  36.3 2.6 %collective-permute-start.7 = (f32[146,8,128]{2,1,0:T(8,128)S(1)}, f32[146,8,128]{2,1,0:T(8,128)S(1)}, u32[]{:S(2)}, u32[]{:S(2)}) collective-permute-start(f32[146,8,128]{2,1,0:T(8,128)S(1)} %collective-permute-done.refs_1_), channel_id=1, source_target_pairs={{0,1},{1,0},{2,3},{3,2},{4,5},{5,4},{6,7},{7,6},{8,9},{9,8},{10,11... | collective-permute-start | bytes 1794056 | tf_op jit(solution)/shard_map/ppermute | solution.py:409
  36.3 2.9 %collective-permute-start.8 = (f32[146,8,128]{2,1,0:T(8,128)S(1)}, f32[146,8,128]{2,1,0:T(8,128)S(1)}, u32[]{:S(2)}, u32[]{:S(2)}) collective-permute-start(f32[146,8,128]{2,1,0:T(8,128)S(1)} %collective-permute-done.1.refs_2_), channel_id=1, source_target_pairs={{0,1},{1,0},{2,3},{3,2},{4,5},{5,4},{6,7},{7,6},{8,9},{9,8},{10,11... | collective-permute-start | bytes 1794056 | tf_op jit(solution)/shard_map/ppermute | solution.py:409
  36.8 15.4 %collective-permute-start.5 = (f32[146,8,128]{2,1,0:T(8,128)S(1)}, f32[146,8,128]{2,1,0:T(8,128)S(1)}, u32[]{:S(2)}, u32[]{:S(2)}) collective-permute-start(f32[146,8,128]{2,1,0:T(8,128)S(1)} %collective-permute-done.refs_1_), channel_id=1, source_target_pairs={{0,2},{1,3},{2,0},{3,1},{4,6},{5,7},{6,4},{7,5},{8,10},{9,11},{10,... | collective-permute-start | bytes 1794056 | tf_op jit(solution)/shard_map/ppermute | solution.py:409
  37.4 15.1 %collective-permute-start.6 = (f32[146,8,128]{2,1,0:T(8,128)S(1)}, f32[146,8,128]{2,1,0:T(8,128)S(1)}, u32[]{:S(2)}, u32[]{:S(2)}) collective-permute-start(f32[146,8,128]{2,1,0:T(8,128)S(1)} %collective-permute-done.3.refs_6_.refs_8_), channel_id=1, source_target_pairs={{0,4},{1,5},{2,6},{3,7},{4,0},{5,1},{6,2},{7,3},{8,12},{9,13},{10,... | collective-permute-start | bytes 1794056 | tf_op jit(solution)/shard_map/ppermute | solution.py:409
  52.5 2.0 %collective-permute-start.9 = (f32[146,8,128]{2,1,0:T(8,128)S(1)}, f32[146,8,128]{2,1,0:T(8,128)S(1)}, u32[]{:S(2)}, u32[]{:S(2)}) collective-permute-start(f32[146,8,128]{2,1,0:T(8,128)S(1)} %collective-permute-done.5.refs_3_), channel_id=1, source_target_pairs={{0,1},{1,0},{2,3},{3,2},{4,5},{5,4},{6,7},{7,6},{8,9},{9,8},{10,11... | collective-permute-start | bytes 1794056 | tf_op jit(solution)/shard_map/ppermute | solution.py:409
  69.2 1.8 %collective-permute-start.11 = (f32[2,384,128]{2,1,0:T(8,128)S(1)}, f32[2,384,128]{2,1,0:T(8,128)S(1)}, u32[]{:S(2)}, u32[]{:S(2)}) collective-permute-start(f32[2,384,128]{2,1,0:T(8,128)S(1)} %get-tuple-element.98), channel_id=1, source_target_pairs={{0,1},{1,0},{2,3},{3,2},{4,5},{5,4},{6,7},{7,6},{8,9},{9,8},{10,11... | collective-permute-start | bytes 1179656 | tf_op jit(solution)/shard_map/ppermute | solution.py:409
  69.4 7.3 %collective-permute-start.15 = (f32[1,392,128]{2,1,0:T(8,128)S(1)}, f32[1,392,128]{2,1,0:T(8,128)S(1)}, u32[]{:S(2)}, u32[]{:S(2)}) collective-permute-start(f32[1,392,128]{2,1,0:T(8,128)S(1)} %get-tuple-element.105), channel_id=1, source_target_pairs={{0,4},{1,5},{2,6},{3,7},{4,0},{5,1},{6,2},{7,3},{8,12},{9,13},{10,... | collective-permute-start | bytes 602120 | tf_op jit(solution)/shard_map/ppermute | solution.py:409
  69.4 10.7 %collective-permute-start.10 = (f32[2,384,128]{2,1,0:T(8,128)S(1)}, f32[2,384,128]{2,1,0:T(8,128)S(1)}, u32[]{:S(2)}, u32[]{:S(2)}) collective-permute-start(f32[2,384,128]{2,1,0:T(8,128)S(1)} %get-tuple-element.96), channel_id=1, source_target_pairs={{0,1},{1,0},{2,3},{3,2},{4,5},{5,4},{6,7},{7,6},{8,9},{9,8},{10,11... | collective-permute-start | bytes 1179656 | tf_op jit(solution)/shard_map/ppermute | solution.py:409
  71.0 1.1 %copy-start.1 = (f32[128,9,128]{2,0,1:T(8,128)S(1)}, f32[128,9,128]{2,0,1:T(8,128)}, u32[]{:S(2)}) copy-start(f32[128,9,128]{2,0,1:T(8,128)} %param.6) | copy-start | bytes 1769476
  71.1 9.1 %collective-permute-start.12 = (f32[1,384,128]{2,1,0:T(8,128)S(1)}, f32[1,384,128]{2,1,0:T(8,128)S(1)}, u32[]{:S(2)}, u32[]{:S(2)}) collective-permute-start(f32[1,384,128]{2,1,0:T(8,128)S(1)} %get-tuple-element.114), channel_id=1, source_target_pairs={{0,2},{1,3},{2,0},{3,1},{4,6},{5,7},{6,4},{7,5},{8,10},{9,11},{10,... | collective-permute-start | bytes 589832 | tf_op jit(solution)/shard_map/ppermute | solution.py:409
  76.7 9.7 %collective-permute-start.17 = (f32[1,392,128]{2,1,0:T(8,128)S(1)}, f32[1,392,128]{2,1,0:T(8,128)S(1)}, u32[]{:S(2)}, u32[]{:S(2)}) collective-permute-start(f32[1,392,128]{2,1,0:T(8,128)S(1)} %add.54), channel_id=1, source_target_pairs={{0,8},{1,9},{2,10},{3,11},{4,12},{5,13},{6,14},{7,15},{8,0},{9,1},... | collective-permute-start | bytes 602120 | tf_op jit(solution)/shard_map/ppermute | solution.py:409
  79.8 6.5 %collective-permute-start.16 = (f32[1,392,128]{2,1,0:T(8,128)S(1)}, f32[1,392,128]{2,1,0:T(8,128)S(1)}, u32[]{:S(2)}, u32[]{:S(2)}) collective-permute-start(f32[1,392,128]{2,1,0:T(8,128)S(1)} %get-tuple-element.106), channel_id=1, source_target_pairs={{0,4},{1,5},{2,6},{3,7},{4,0},{5,1},{6,2},{7,3},{8,12},{9,13},{10,... | collective-permute-start | bytes 602120 | tf_op jit(solution)/shard_map/ppermute | solution.py:409
  80.2 12.4 %collective-permute-start.14 = (f32[1,384,128]{2,1,0:T(8,128)S(1)}, f32[1,384,128]{2,1,0:T(8,128)S(1)}, u32[]{:S(2)}, u32[]{:S(2)}) collective-permute-start(f32[1,384,128]{2,1,0:T(8,128)S(1)} %fusion), channel_id=1, source_target_pairs={{0,16},{1,17},{2,18},{3,19},{4,20},{5,21},{6,22},{7,23},{8,24},{9,... | collective-permute-start | bytes 589832 | tf_op jit(solution)/shard_map/ppermute | solution.py:409
  84.2 8.3 %collective-permute-start.13 = (f32[1,384,128]{2,1,0:T(8,128)S(1)}, f32[1,384,128]{2,1,0:T(8,128)S(1)}, u32[]{:S(2)}, u32[]{:S(2)}) collective-permute-start(f32[1,384,128]{2,1,0:T(8,128)S(1)} %get-tuple-element.100), channel_id=1, source_target_pairs={{0,2},{1,3},{2,0},{3,1},{4,6},{5,7},{6,4},{7,5},{8,10},{9,11},{10,... | collective-permute-start | bytes 589832 | tf_op jit(solution)/shard_map/ppermute | solution.py:409
